TPU v7x, 32 devices: a whole 2x2x4 slice. The times are simulated.
32 devices in a mesh: dp: 16 (over z, y, x), seq: 2 (over core).
Axes of the slice: x: 2, y: 2, z: 4, core: 2. Of those that a mesh axis runs over, the one named last changes fastest.
Arguments:
- patches: bfloat16 [64, 324, 512], P('dp', 'seq'), may hold values from -6 to 6
- resolution: int32 [64], P('dp'), may hold values from 0 to 2, as said below
- out_grad: bfloat16 [64, 324, 512], P('dp', 'seq'), may hold values from -6 to 6
- dense_in: float32 [512, 3072], P(('dp', 'seq')), may hold values from -0.25 to 0.25
- dense_out: float32 [1536, 512], P(('dp', 'seq')), may hold values from -0.15625 to 0.15625
- vectors: float32 [7680], P(('dp', 'seq')), may hold values from -1 to 2, as said below
- spatial: float32 [3, 324, 324], P(None, 'seq'), may hold values from -0.3125 to 0.3125
- spatial_bias: float32 [3, 324], P(None, 'seq'), may hold values from 0.5 to 1.5
- in_first: float32 [512, 3072], P(('dp', 'seq')), may hold values from -24 to 24
- in_second: float32 [512, 3072], P(('dp', 'seq')), may hold values from 11.904 to 47.616
- out_first: float32 [1536, 512], P(('dp', 'seq')), may hold values from -56 to 56
- out_second: float32 [1536, 512], P(('dp', 'seq')), may hold values from 67.456 to 265.856
- vec_first: float32 [7680], P(('dp', 'seq')), may hold values from -40 to 40
- vec_second: float32 [7680], P(('dp', 'seq')), may hold values from 32.9344 to 130.944
- spat_first: float32 [3, 324, 324], P(None, 'seq'), may hold values from -40 to 40
- spat_second: float32 [3, 324, 324], P(None, 'seq'), may hold values from 39.3216 to 157.2864
- bias_first: float32 [3, 324], P(None, 'seq'), may hold values from -40 to 40
- bias_second: float32 [3, 324], P(None, 'seq'), may hold values from 39.3216 to 157.2864
Outputs:
- mixed: bfloat16 [64, 324, 512], P('dp', 'seq')
- patches_grad: bfloat16 [64, 324, 512], P('dp', 'seq')
- next_dense_in: float32 [512, 3072], P(('dp', 'seq'))
- next_in_first: float32 [512, 3072], P(('dp', 'seq'))
- next_in_second: float32 [512, 3072], P(('dp', 'seq'))
- next_dense_out: float32 [1536, 512], P(('dp', 'seq'))
- next_out_first: float32 [1536, 512], P(('dp', 'seq'))
- next_out_second: float32 [1536, 512], P(('dp', 'seq'))
- next_vectors: float32 [7680], P(('dp', 'seq'))
- next_vec_first: float32 [7680], P(('dp', 'seq'))
- next_vec_second: float32 [7680], P(('dp', 'seq'))
- next_spatial: float32 [3, 324, 324], P(None, 'seq')
- next_spat_first: float32 [3, 324, 324], P(None, 'seq')
- next_spat_second: float32 [3, 324, 324], P(None, 'seq')
- next_spatial_bias: float32 [3, 324], P(None, 'seq')
- next_bias_first: float32 [3, 324], P(None, 'seq')
- next_bias_second: float32 [3, 324], P(None, 'seq')
Inputs may be any that keep to these rules, and one draw needn't show every extreme that they name: `resolution`: 0, 1, 2 name images of 100, 196 and 324 patches; among the 4 images of each index of dp at least one has index 2. `vectors`: gains and biases, gains near one.
All inputs are finite; a program needn't handle non-finite values.
Results may differ from a plain program's by a relative error of at most 0.012.
Values may be sent and summed in bfloat16 or wider, within the bound.
No kernel may reach another device: no remote copies, remote signals or barrier semaphores. Data moves between devices by JAX's collectives and lax.ppermute only.
A program may use at most 128 MiB of HBM per device.

v0:
```python
import jax
import jax.numpy as jnp
from jax import lax
from jax.sharding import PartitionSpec as P

D = 512
FF = 3072
HALF = 1536
PMAX = 324
P_MID = 196
P_LOW = 100
MB = 2
STEP = 10


NORM_EPS = 1e-05
BETA_ONE = 0.9
BETA_TWO = 0.99
ADAM_EPS = 1e-08
DENSE_RATE = 0.02
SMALL_RATE = 0.2
DENSE_DECAY = 0.05
HIGHEST = lax.Precision.HIGHEST


def shifted(block, axis, distance):
    devices = range(lax.axis_size(axis))
    route = [((i - distance) % len(devices), i) for i in devices]
    return lax.ppermute(block, axis, route)


def layer_norm(values, gain, shift):
    center = values - jnp.mean(values, axis=-1, keepdims=True)
    spread = jnp.mean(center * center, axis=-1, keepdims=True)
    return center * lax.rsqrt(spread + NORM_EPS) * gain + shift


def smooth_gate(values):
    return jax.nn.gelu(values, approximate=False)


def counts_of(levels):
    return jnp.where(levels == 0, P_LOW, jnp.where(levels == 1, P_MID, PMAX))


def split_vectors(vecs):
    gain_one = vecs[:D]
    shift_one = vecs[D : 2 * D]
    bias_in = vecs[2 * D : 2 * D + FF]
    gain_two = vecs[2 * D + FF : 2 * D + FF + HALF]
    shift_two = vecs[2 * D + FF + HALF : 2 * D + FF + 2 * HALF]
    bias_out = vecs[2 * D + FF + 2 * HALF :]
    return (gain_one, shift_one, bias_in, gain_two, shift_two, bias_out)


def select_level(levels, table):
    picked = jnp.zeros((levels.shape[0],) + table.shape[1:], jnp.float32)
    for level in range(3):
        hit = (levels == level).astype(jnp.float32).reshape((-1,) + (1,) * (table.ndim - 1))
        picked = picked + hit * table[level][None]
    return picked


def adamw(weight, grad, first, second, rate, decay):
    first = BETA_ONE * first + (1.0 - BETA_ONE) * grad
    second = BETA_TWO * second + (1.0 - BETA_TWO) * grad * grad
    first_hat = first / (1.0 - BETA_ONE**STEP)
    second_hat = second / (1.0 - BETA_TWO**STEP)
    weight = weight - rate * (first_hat / (jnp.sqrt(second_hat) + ADAM_EPS) + decay * weight)
    return (weight, first, second)


def local(
    patches,
    resolution,
    out_grad,
    dense_in,
    dense_out,
    vectors,
    spatial,
    spatial_bias,
    in_first,
    in_second,
    out_first,
    out_second,
    vec_first,
    vec_second,
    spat_first,
    spat_second,
    bias_first,
    bias_second,
):
    cycle = lax.axis_size("seq")
    place = lax.axis_index("seq")
    rows = patches.shape[1]
    per_batch = patches.shape[0] // MB
    own_rows = place * rows + jnp.arange(rows)
    every_row = jnp.arange(PMAX)
    shards = (
        dense_in.astype(jnp.bfloat16),
        dense_out.astype(jnp.bfloat16),
        vectors.astype(jnp.bfloat16),
    )
    summed = (jnp.zeros_like(dense_in), jnp.zeros_like(dense_out), jnp.zeros_like(vectors))
    grad_spat = jnp.zeros(spatial.shape, jnp.float32)
    grad_bias = jnp.zeros(spatial_bias.shape, jnp.float32)
    mixed_parts = []
    input_grads = []
    for batch in range(MB):
        gathered = (
            lax.all_gather(shards[0], ("dp", "seq"), axis=0, tiled=True),
            lax.all_gather(shards[1], ("dp", "seq"), axis=0, tiled=True),
            lax.all_gather(shards[2], ("dp", "seq"), axis=0, tiled=True),
        )
        weight_in, weight_out, vec_low = gathered
        gain_one, shift_one, bias_in, gain_two, shift_two, bias_out = split_vectors(
            vec_low.astype(jnp.float32)
        )
        lower = batch * per_batch
        levels = resolution[lower : lower + per_batch]
        inputs = patches[lower : lower + per_batch].astype(jnp.float32)
        upstream = out_grad[lower : lower + per_batch].astype(jnp.float32)
        counts = counts_of(levels)
        live_own = (own_rows[None, :] < counts[:, None]).astype(jnp.float32)
        live_all = (every_row[None, :] < counts[:, None]).astype(jnp.float32)
        mixing = (
            select_level(levels, spatial) * live_own[:, :, None] * live_all[:, None, :]
        ).astype(jnp.bfloat16)
        bias_rows = select_level(levels, spatial_bias)
        normed, norm_one_back = jax.vjp(layer_norm, inputs, gain_one, shift_one)
        normed_low = normed.astype(jnp.bfloat16)
        pre = (
            jnp.einsum("bpd,df->bpf", normed_low, weight_in, preferred_element_type=jnp.float32)
            + bias_in
        )
        act, gate_back = jax.vjp(smooth_gate, pre)
        left = act[..., :HALF]
        right = act[..., HALF:]
        gate_in, norm_two_back = jax.vjp(layer_norm, right, gain_two, shift_two)
        gate_low = gate_in.astype(jnp.bfloat16)
        blocks = [gate_low]
        current = gate_low
        mixed_sum = jnp.zeros((per_batch, rows, HALF), jnp.float32)
        for step in range(cycle):
            start = (place - step) % cycle * rows
            columns = lax.dynamic_slice_in_dim(mixing, start, rows, 2)
            mixed_sum = mixed_sum + jnp.einsum(
                "bij,bjf->bif", columns, current, preferred_element_type=jnp.float32
            )
            if step + 1 < cycle:
                current = shifted(current, "seq", 1)
                blocks.append(current)
        spat = live_own[:, :, None] * (mixed_sum + bias_rows[:, :, None])
        gated = (left * spat).astype(jnp.bfloat16)
        branch = (
            jnp.einsum("bpf,fd->bpd", gated, weight_out, preferred_element_type=jnp.float32)
            + bias_out
        )
        mixed_parts.append((inputs + live_own[:, :, None] * branch).astype(jnp.bfloat16))
        grad_branch = (live_own[:, :, None] * upstream).astype(jnp.bfloat16)
        grad_bias_out = jnp.sum(grad_branch.astype(jnp.float32), axis=(0, 1))
        grad_weight_out = jnp.einsum(
            "bpf,bpd->fd", gated, grad_branch, preferred_element_type=jnp.float32
        )
        grad_gated = jnp.einsum(
            "bpd,fd->bpf", grad_branch, weight_out, preferred_element_type=jnp.float32
        )
        grad_left = grad_gated * spat
        grad_mix = (grad_gated * left).astype(jnp.bfloat16) * live_own[:, :, None].astype(
            jnp.bfloat16
        )
        level_hits = (levels[:, None] == jnp.arange(3)[None, :]).astype(jnp.float32)
        row_totals = jnp.sum(grad_mix.astype(jnp.float32), axis=2)
        grad_bias = grad_bias + jnp.einsum("br,bi->ri", level_hits, row_totals, precision=HIGHEST)
        grad_cells = jnp.zeros((per_batch, rows, PMAX), jnp.float32)
        for step in range(len(blocks)):
            start = (place - step) % cycle * rows
            cell_block = jnp.einsum(
                "bif,bjf->bij", grad_mix, blocks[step], preferred_element_type=jnp.float32
            )
            grad_cells = lax.dynamic_update_slice_in_dim(grad_cells, cell_block, start, 2)
        grad_spat = grad_spat + jnp.einsum(
            "br,bij->rij", level_hits, grad_cells * live_all[:, None, :], precision=HIGHEST
        )

        def partial_term(dest):
            columns = lax.dynamic_slice_in_dim(mixing, dest * rows, rows, 2)
            return jnp.einsum("bij,bif->bjf", columns, grad_mix, preferred_element_type=jnp.float32)

        grad_gate = partial_term((place + 1) % cycle)
        step = 1
        grad_gate = shifted(grad_gate, "seq", -1)
        grad_gate = grad_gate + partial_term((place + 1 + step) % cycle)
        grad_right, grad_gain_two, grad_shift_two = norm_two_back(grad_gate)
        (grad_pre,) = gate_back(jnp.concatenate([grad_left, grad_right], axis=-1))
        grad_pre = grad_pre.astype(jnp.bfloat16)
        grad_bias_in = jnp.sum(grad_pre.astype(jnp.float32), axis=(0, 1))
        grad_weight_in = jnp.einsum(
            "bpd,bpf->df", normed_low, grad_pre, preferred_element_type=jnp.float32
        )
        grad_normed = jnp.einsum(
            "bpf,df->bpd", grad_pre, weight_in, preferred_element_type=jnp.float32
        )
        grad_inputs, grad_gain_one, grad_shift_one = norm_one_back(grad_normed)
        input_grads.append((upstream + grad_inputs).astype(jnp.bfloat16))
        grad_vec = jnp.concatenate(
            [
                grad_gain_one,
                grad_shift_one,
                grad_bias_in,
                grad_gain_two,
                grad_shift_two,
                grad_bias_out,
            ]
        )
        terms = (grad_weight_in, grad_weight_out, grad_vec)
        terms = (
            lax.psum_scatter(terms[0], ("dp", "seq"), scatter_dimension=0, tiled=True),
            lax.psum_scatter(terms[1], ("dp", "seq"), scatter_dimension=0, tiled=True),
            lax.psum_scatter(terms[2], ("dp", "seq"), scatter_dimension=0, tiled=True),
        )
        summed = (summed[0] + terms[0], summed[1] + terms[1], summed[2] + terms[2])
    grad_spat, grad_bias = lax.psum((grad_spat, grad_bias), "dp")
    new_in = adamw(dense_in, summed[0], in_first, in_second, DENSE_RATE, DENSE_DECAY)
    new_out = adamw(dense_out, summed[1], out_first, out_second, DENSE_RATE, DENSE_DECAY)
    new_vec = adamw(vectors, summed[2], vec_first, vec_second, SMALL_RATE, 0.0)
    new_spat = adamw(spatial, grad_spat, spat_first, spat_second, DENSE_RATE, DENSE_DECAY)
    new_bias = adamw(spatial_bias, grad_bias, bias_first, bias_second, SMALL_RATE, 0.0)
    return (
        jnp.concatenate(mixed_parts, axis=0),
        jnp.concatenate(input_grads, axis=0),
        new_in[0],
        new_in[1],
        new_in[2],
        new_out[0],
        new_out[1],
        new_out[2],
        new_vec[0],
        new_vec[1],
        new_vec[2],
        new_spat[0],
        new_spat[1],
        new_spat[2],
        new_bias[0],
        new_bias[1],
        new_bias[2],
    )


def solution(mesh):
    in_specs = (
        P("dp", "seq", None),
        P("dp"),
        P("dp", "seq", None),
        P(("dp", "seq"), None),
        P(("dp", "seq"), None),
        P(("dp", "seq")),
        P(None, "seq", None),
        P(None, "seq"),
        P(("dp", "seq"), None),
        P(("dp", "seq"), None),
        P(("dp", "seq"), None),
        P(("dp", "seq"), None),
        P(("dp", "seq")),
        P(("dp", "seq")),
        P(None, "seq", None),
        P(None, "seq", None),
        P(None, "seq"),
        P(None, "seq"),
    )
    out_specs = (
        P("dp", "seq", None),
        P("dp", "seq", None),
        P(("dp", "seq"), None),
        P(("dp", "seq"), None),
        P(("dp", "seq"), None),
        P(("dp", "seq"), None),
        P(("dp", "seq"), None),
        P(("dp", "seq"), None),
        P(("dp", "seq")),
        P(("dp", "seq")),
        P(("dp", "seq")),
        P(None, "seq", None),
        P(None, "seq", None),
        P(None, "seq", None),
        P(None, "seq"),
        P(None, "seq"),
        P(None, "seq"),
    )
    return jax.shard_map(local, mesh=mesh, in_specs=in_specs, out_specs=out_specs, check_vma=False)
```

profile of v0, /device:TPU:0, one launch (start us, length us, event | category | flops | bytes accessed | tf_op | source)
XLA Modules:
  0.0 548.6 jit_solution(3429012863449310262)
XLA Ops:
  13.2 42.4 %all-reduce = bf16[7680]{0:T(1024)(128)(2,1)S(1)} all-reduce(bf16[7680]{0:T(1024)(128)(2,1)S(1)} %dynamic-update-slice), channel_id=1, replica_groups=mesh['dp'=16,'seq'=2] {'dp','seq'}, use_global_device_ids=true, to_apply=%add | all-reduce | flops 7680 | bytes 30720
  55.6 2.2 fusion.168
  61.3 11.9 %all-gather.3.cloned.1.call-done = bf16[512,3072]{1,0:T(8,128)(2,1)} async-done(((bf16[16,3072]{1,0:T(8,128)(2,1)}), bf16[512,3072]{1,0:T(8,128)(2,1)}) %all-gather.3.cloned.1.call-update) | async-done | bytes 3145744 | tf_op jit(solution)/shard_map/all_gather | solution.py:111
  73.2 13.2 %multiply_multiply_fusion.10 = (f32[2,162,3072]{2,1,0:T(8,128)}, f32[2,162,3072]{2,1,0:T(8,128)}, f32[2,162,3072]{2,1,0:T(8,128)}) fusion(f32[3072]{0:T(1024)S(1)} %slice.102, bf16[512,3072]{1,0:T(8,128)(2,1)} %all-gather.3.cloned.1.call-done, f32[2,162]{1,0:T(2,128)S(1)} %fusion.144, f32[2,162]{1,0:T(2,128)S(1)} %broadcast_multiply_fusion.4, ...), kind=kOutput, calls=%fused_computation.39 | convolution fusion | flops 1084907520 | bytes 15440416 | tf_op jit(solution)/shard_map/bpd,df->bpf/dot_general | solution.py:133
  86.4 44.0 %all-gather.5.cloned.1.call-done = bf16[1536,512]{1,0:T(8,128)(2,1)} async-done(((bf16[48,512]{1,0:T(8,128)(2,1)}), bf16[1536,512]{1,0:T(8,128)(2,1)}) %all-gather.5.cloned.1.call-update) | async-done | bytes 1572880 | tf_op jit(solution)/shard_map/all_gather | solution.py:112
  130.4 5.3 convert_reduce_fusion.2
  136.4 2.9 copy.94
  139.5 13.3 %multiply_multiply_fusion.11 = (f32[2,162,3072]{2,1,0:T(8,128)S(1)}, f32[2,162,3072]{2,1,0:T(8,128)}, f32[2,162,3072]{2,1,0:T(8,128)}) fusion(f32[3072]{0:T(1024)S(1)} %slice.102, bf16[512,3072]{1,0:T(8,128)(2,1)S(1)} %copy-done.58, f32[512]{0:T(512)S(1)} %get-tuple-element.143, f32[512]{0:T(512)S(1)} %get-tuple-element.142, f32[2,162]{1,0:T(2,128)S(1)} %fusion.142, ...), kind=kOutput, calls=%fused_computation.40 | convolution fusion | flops 1084907520 | bytes 15440416 | tf_op jit(solution)/shard_map/bpd,df->bpf/dot_general | solution.py:133
  154.7 2.7 convert_reduce_fusion.3
  158.0 2.9 copy.89
  161.2 2.4 copy_add_fusion
  165.2 4.2 multiply_reduce_fusion.3
  171.4 3.3 broadcast_add_fusion
  180.8 1.9 dynamic_update_slice.14
  184.7 1.9 dynamic_update_slice.12
  186.6 2.8 fusion.119
  189.4 2.8 fusion.122
  196.5 2.4 fusion.68
  198.9 2.4 dynamic_update_slice.13
  201.4 2.4 fusion.90
  206.3 4.8 fusion.166
  212.0 3.4 fusion.165
  216.6 2.7 fusion.12
  219.4 5.3 convert_reduce_fusion.1
  224.8 2.0 fusion.101
  230.7 4.7 bitcast_add_fusion
  237.9 40.0 %psum.15 = f32[3,162]{1,0:T(4,128)S(1)} all-reduce(f32[3,162]{1,0:T(4,128)} %convolution_add_fusion.4), channel_id=1, replica_groups=mesh['dp'=16,'seq'=2] {'dp'}, use_global_device_ids=true, to_apply=%region_37.38 | all-reduce | flops 486 | bytes 3888 | tf_op jit(solution)/shard_map/psum | solution.py:223
  278.6 2.5 fusion.49
  289.7 37.3 %all-reduce.1 = f32[7680]{0:T(1024)S(1)} all-reduce(f32[7680]{0:T(1024)S(1)} %add.426), channel_id=7, replica_groups=mesh['dp'=16,'seq'=2] {'dp','seq'}, use_global_device_ids=true, to_apply=%region_26.27.clone | all-reduce | flops 7680 | bytes 61440
  327.7 3.4 multiply_subtract_fusion
  331.1 90.2 %reduce-scatter.5.cloned.1.call-done = f32[48,512]{1,0:T(8,128)} async-done(((f32[1536,512]{1,0:T(8,128)}), f32[48,512]{1,0:T(8,128)}) %reduce-scatter.5.cloned.1.call-update) | async-done | bytes 98320 | tf_op jit(solution)/shard_map/reduce_scatter | solution.py:219
  422.9 117.2 %reduce-scatter.3.cloned.1.call-done = f32[16,3072]{1,0:T(8,128)} async-done(((f32[512,3072]{1,0:T(8,128)}), f32[16,3072]{1,0:T(8,128)}) %reduce-scatter.3.cloned.1.call-update) | async-done | bytes 196624 | tf_op jit(solution)/shard_map/reduce_scatter | solution.py:218
  (221 shorter events, 53.1 us)
Async XLA Ops:
  7.2 53.6 %copy-start.36 = (bf16[4,162,512]{2,0,1:T(4,128)(2,1)S(1)}, bf16[4,162,512]{2,0,1:T(4,128)(2,1)}, u32[]{:S(2)}) copy-start(bf16[4,162,512]{2,0,1:T(4,128)(2,1)} %param.20) | copy-start | bytes 1990660
  7.2 66.0 %all-gather.3.cloned.1.call-start = ((), (), s32[]{:S(2)}) async-start(), calls=%async_computation.2 | async-start | bytes 3244032 | tf_op jit(solution)/shard_map/all_gather | solution.py:111
  8.9 121.5 %all-gather.5.cloned.1.call-start = ((), (), s32[]{:S(2)}) async-start(), calls=%async_computation.3 | async-start | bytes 1622016 | tf_op jit(solution)/shard_map/all_gather | solution.py:112
  10.5 317.2 %all-reduce.4.cloned.1.call-start = ((), (), s32[]{:S(2)}) async-start(), calls=%async_computation.4 | async-start | bytes 1548288 | tf_op jit(solution)/shard_map/psum | solution.py:223
  11.4 190.0 %copy-start.52 = (s32[2]{0:T(128)}, s32[2]{0:T(128)S(1)}, u32[]{:S(2)}) copy-start(s32[2]{0:T(128)S(1)} %get-tuple-element.170) | copy-start | bytes 28
  11.4 192.4 %copy-start.54 = (s32[2]{0:T(128)}, s32[2]{0:T(128)S(1)}, u32[]{:S(2)}) copy-start(s32[2]{0:T(128)S(1)} %get-tuple-element.167) | copy-start | bytes 28
  57.7 81.8 %copy-start.19 = (bf16[2,162,512]{2,0,1:T(2,128)(2,1)}, bf16[2,162,512]{2,0,1:T(2,128)(2,1)S(1)}, u32[]{:S(2)}) copy-start(bf16[2,162,512]{2,0,1:T(2,128)(2,1)S(1)} %get-tuple-element.133) | copy-start | bytes 995332
  58.9 165.8 %copy-start.44 = (f32[2,162]{1,0:T(2,128)}, f32[2,162]{1,0:T(2,128)S(1)}, u32[]{:S(2)}) copy-start(f32[2,162]{1,0:T(2,128)S(1)} %broadcast_multiply_fusion.5) | copy-start | bytes 3892
  60.8 100.5 %copy-start.28 = (bf16[2,162,324]{2,1,0:T(8,128)(2,1)}, bf16[2,162,324]{2,1,0:T(8,128)(2,1)S(1)}, u32[]{:S(2)}) copy-start(bf16[2,162,324]{2,1,0:T(8,128)(2,1)S(1)} %get-tuple-element.126) | copy-start | bytes 629860
  60.8 104.4 %copy-start.26 = (bf16[2,162,324]{2,1,0:T(8,128)(2,1)}, bf16[2,162,324]{2,1,0:T(8,128)(2,1)S(1)}, u32[]{:S(2)}) copy-start(bf16[2,162,324]{2,1,0:T(8,128)(2,1)S(1)} %get-tuple-element.127) | copy-start | bytes 629860
  60.8 163.9 %copy-start.48 = (f32[2,162]{1,0:T(2,128)}, f32[2,162]{1,0:T(2,128)S(1)}, u32[]{:S(2)}) copy-start(f32[2,162]{1,0:T(2,128)S(1)} %fusion.142) | copy-start | bytes 3892
  61.3 69.1 %copy-start.17 = (bf16[2,162,512]{2,0,1:T(2,128)(2,1)}, bf16[2,162,512]{2,0,1:T(2,128)(2,1)S(1)}, u32[]{:S(2)}) copy-start(bf16[2,162,512]{2,0,1:T(2,128)(2,1)S(1)} %get-tuple-element.131) | copy-start | bytes 995332
  61.3 91.5 %copy-start.15 = (bf16[2,162,512]{2,0,1:T(2,128)(2,1)}, bf16[2,162,512]{2,0,1:T(2,128)(2,1)S(1)}, u32[]{:S(2)}) copy-start(bf16[2,162,512]{2,0,1:T(2,128)(2,1)S(1)} %get-tuple-element.132) | copy-start | bytes 995332
  139.2 22.0 %collective-permute-start.3 = (f32[2,162,1536]{2,0,1:T(2,128)}, f32[2,162,1536]{2,0,1:T(2,128)}, u32[]{:S(2)}, u32[]{:S(2)}) collective-permute-start(f32[2,162,1536]{2,0,1:T(2,128)} %copy.94), channel_id=1, source_target_pairs={{1,0},{0,1},{3,2},{2,3},{5,4},{4,5},{7,6},{6,7},{9,8},{8,9},{11,10... | collective-permute-start | bytes 5971976 | tf_op jit(solution)/shard_map/ppermute | solution.py:29
  160.8 4.3 collective-permute-start.2
  176.5 15.7 %collective-permute-start.1 = (bf16[2,162,1536]{2,0,1:T(2,128)(2,1)}, bf16[2,162,1536]{2,0,1:T(2,128)(2,1)}, u32[]{:S(2)}, u32[]{:S(2)}) collective-permute-start(bf16[2,162,1536]{2,0,1:T(2,128)(2,1)} %copy.85), channel_id=1, source_target_pairs={{1,0},{0,1},{3,2},{2,3},{5,4},{4,5},{7,6},{6,7},{9,8},{8,9},{11,10... | collective-permute-start | bytes 2985992 | tf_op jit(solution)/shard_map/ppermute | solution.py:29
  179.7 16.9 %collective-permute-start = (bf16[2,162,1536]{2,0,1:T(2,128)(2,1)}, bf16[2,162,1536]{2,0,1:T(2,128)(2,1)}, u32[]{:S(2)}, u32[]{:S(2)}) collective-permute-start(bf16[2,162,1536]{2,0,1:T(2,128)(2,1)} %copy.82), channel_id=1, source_target_pairs={{1,0},{0,1},{3,2},{2,3},{5,4},{4,5},{7,6},{6,7},{9,8},{8,9},{11,10... | collective-permute-start | bytes 2985992 | tf_op jit(solution)/shard_map/ppermute | solution.py:29
  206.2 215.1 %reduce-scatter.5.cloned.1.call-start = ((), (), s32[]{:S(2)}) async-start(), calls=%async_computation.6 | async-start | bytes 3244032 | tf_op jit(solution)/shard_map/reduce_scatter | solution.py:219
  219.3 320.8 %reduce-scatter.3.cloned.1.call-start = ((), (), s32[]{:S(2)}) async-start(), calls=%async_computation.5 | async-start | bytes 6488064 | tf_op jit(solution)/shard_map/reduce_scatter | solution.py:218
  235.4 42.5 %copy-start.47 = (f32[3,162]{1,0:T(4,128)S(1)}, f32[3,162]{1,0:T(4,128)}, u32[]{:S(2)}) copy-start(f32[3,162]{1,0:T(4,128)} %param.25) | copy-start | bytes 5836
  235.4 42.5 %copy-start.50 = (f32[3,162]{1,0:T(4,128)S(1)}, f32[3,162]{1,0:T(4,128)}, u32[]{:S(2)}) copy-start(f32[3,162]{1,0:T(4,128)} %param.34) | copy-start | bytes 5836
  235.4 42.5 %copy-start.51 = (f32[3,162]{1,0:T(4,128)S(1)}, f32[3,162]{1,0:T(4,128)}, u32[]{:S(2)}) copy-start(f32[3,162]{1,0:T(4,128)} %param.35) | copy-start | bytes 5836
  287.0 40.0 %copy-start.55 = (f32[240]{0:T(256)S(1)}, f32[240]{0:T(256)}, u32[]{:S(2)}) copy-start(f32[240]{0:T(256)} %param.23) | copy-start | bytes 2884
  287.0 40.0 %copy-start.56 = (f32[240]{0:T(256)S(1)}, f32[240]{0:T(256)}, u32[]{:S(2)}) copy-start(f32[240]{0:T(256)} %param.30) | copy-start | bytes 2884
  287.0 40.0 %copy-start.57 = (f32[240]{0:T(256)S(1)}, f32[240]{0:T(256)}, u32[]{:S(2)}) copy-start(f32[240]{0:T(256)} %param.31) | copy-start | bytes 2884
  287.0 40.7 %copy-start.30 = (f32[3,162,324]{2,1,0:T(8,128)S(1)}, f32[3,162,324]{2,1,0:T(8,128)}, u32[]{:S(2)}) copy-start(f32[3,162,324]{2,1,0:T(8,128)} %param.24) | copy-start | bytes 1889572
  288.2 133.1 %copy-start.37 = (f32[48,512]{1,0:T(8,128)S(1)}, f32[48,512]{1,0:T(8,128)}, u32[]{:S(2)}) copy-start(f32[48,512]{1,0:T(8,128)} %param.22) | copy-start | bytes 294916
  288.2 133.1 %copy-start.40 = (f32[48,512]{1,0:T(8,128)S(1)}, f32[48,512]{1,0:T(8,128)}, u32[]{:S(2)}) copy-start(f32[48,512]{1,0:T(8,128)} %param.28) | copy-start | bytes 294916
  288.2 133.1 %copy-start.41 = (f32[48,512]{1,0:T(8,128)S(1)}, f32[48,512]{1,0:T(8,128)}, u32[]{:S(2)}) copy-start(f32[48,512]{1,0:T(8,128)} %param.29) | copy-start | bytes 294916
  288.3 251.8 %copy-start.35 = (f32[16,3072]{1,0:T(8,128)S(1)}, f32[16,3072]{1,0:T(8,128)}, u32[]{:S(2)}) copy-start(f32[16,3072]{1,0:T(8,128)} %param.21) | copy-start | bytes 589828
  288.3 251.8 %copy-start.38 = (f32[16,3072]{1,0:T(8,128)S(1)}, f32[16,3072]{1,0:T(8,128)}, u32[]{:S(2)}) copy-start(f32[16,3072]{1,0:T(8,128)} %param.26) | copy-start | bytes 589828
  288.3 251.8 %copy-start.39 = (f32[16,3072]{1,0:T(8,128)S(1)}, f32[16,3072]{1,0:T(8,128)}, u32[]{:S(2)}) copy-start(f32[16,3072]{1,0:T(8,128)} %param.27) | copy-start | bytes 589828
  (37 other events, 199.3 us)
Sparse Core Ops, SparseCore 0:
  11.5 61.7 all-gather.2
  76.7 53.7 all-gather.4
  206.3 108.8 all-reduce.3
  320.5 100.7 reduce-scatter.4
  426.8 113.2 reduce-scatter.2
where the time goes:
time: 558 us; the launch traced here: 549 us
  waiting for transfers between devices  265 us (47%)
  blocking collectives  120 us (22%)
  matrix products  86.2 us (15%)
  local copies, waits for them, and re-layouts  31.2 us (6%)
  other arithmetic  30.6 us (5%)
  between operations  14.9 us (3%)
    reduce_scatter x1, waiting for transfers between devices, local(): lax.psum_scatter(terms[0], ('dp', 'seq'), scatter_dimension=0, tiled=True)  117 us
    reduce_scatter x1, waiting for transfers between devices, local(): lax.psum_scatter(terms[1], ('dp', 'seq'), scatter_dimension=0, tiled=True)  90.2 us
    unnamed x2, blocking collectives  79.7 us
    all_gather x1, waiting for transfers between devices, local(): lax.all_gather(shards[1], ('dp', 'seq'), axis=0, tiled=True)  44 us
    psum x1, blocking collectives, local(): grad_spat, grad_bias = lax.psum((grad_spat, grad_bias), 'dp')  40 us
    dot_general x2, matrix products, local(): jnp.einsum('bpd,df->bpf', normed_low, weight_in, preferred_element_type=j...  26.5 us
    dot_general x4, matrix products, local(): jnp.einsum('bij,bjf->bif', columns, current, preferred_element_type=jnp.f...  13.8 us
    all_gather x1, waiting for transfers between devices, local(): lax.all_gather(shards[0], ('dp', 'seq'), axis=0, tiled=True)  11.9 us
  transfers between devices with their start and end apart: 9, of which 5 were waited for; matrix products, arithmetic and copies ran while one was open for 20% of the time, Pallas kernels for 0%

commit v1 on v0

v1 whole, which is shorter than its diff:
```python
import functools

import jax
import jax.numpy as jnp
from jax import lax
from jax.experimental import pallas as pl
from jax.experimental.pallas import tpu as pltpu
from jax.sharding import PartitionSpec as P

D = 512
FF = 3072
HALF = 1536
PMAX = 324
PPAD = 336
P_MID = 196
P_LOW = 100
VCOLS = 256
ROWS = 2 * PPAD
GROUPS = 16
DEVS = 2 * GROUPS
VPER = 240
SCOLS = 384
BIAS_AT = 336
TOTAL_AT = 324
LSTRIDE = 168
MIB = 1024 * 1024
STEP = 10

NORM_EPS = 1e-05
BETA_ONE = 0.9
BETA_TWO = 0.99
ADAM_EPS = 1e-08
DENSE_RATE = 0.02
SMALL_RATE = 0.2
DENSE_DECAY = 0.05

BF = jnp.bfloat16
F32 = jnp.float32
AXES = ("dp", "seq")
VM = pl.BlockSpec(memory_space=pltpu.VMEM)
SM = pl.BlockSpec(memory_space=pltpu.SMEM)
HB = pl.BlockSpec(memory_space=pl.ANY)


class Route:
    def __init__(self, n):
        bits = n.bit_length() - 1
        assert n == 1 << bits and bits >= 2
        self.n = n
        top = n // 4
        self.direct = [top, 2 * top, 3 * top]
        low = [1 << b for b in range(bits - 2)]
        self.low = list(zip(low[::-1], low))
        masks = [(0, 0)] + [(m, m) for m in self.direct]
        for step in self.low:
            masks = masks + [(m[0] ^ step[0], m[1] ^ step[1]) for m in masks]
        self.masks = masks

    def swap(self, block, mask):
        pairs = []
        for dp in range(self.n):
            for seq in range(2):
                pairs.append((dp * 2 + seq, (dp ^ mask[seq]) * 2 + seq))
        return lax.ppermute(block, AXES, pairs)

    def cross(self, block):
        pairs = []
        for dp in range(self.n):
            for seq in range(2):
                pairs.append((dp * 2 + seq, dp * 2 + 1 - seq))
        return lax.ppermute(block, AXES, pairs)

    def order(self, seq_flip):
        place = lax.axis_index("dp")
        seq = lax.axis_index("seq")
        if seq_flip:
            seq = 1 - seq
        zero = jnp.array([m[0] for m in self.masks], jnp.int32)
        one = jnp.array([m[1] for m in self.masks], jnp.int32)
        return place ^ jnp.where(seq == 0, zero, one), seq

    def table(self):
        mine, seq = self.order(False)
        other, flip = self.order(True)
        return jnp.concatenate([mine * 2 + seq, other * 2 + flip])

    def spread(self, shard):
        first = jnp.concatenate([shard] + [self.swap(shard, (m, m)) for m in self.direct], axis=0)
        return self.widen(first)

    def widen(self, first):
        blocks = [first]
        for step in self.low:
            blocks = blocks + [self.swap(b, step) for b in blocks]
        return blocks

    def gather(self, shard):
        blocks = self.spread(shard)
        return blocks + [self.cross(b) for b in blocks]

    def collect(self, terms):
        cur = terms[0].shape[0]
        rows = cur // self.n

        def part(lower, upper):
            total = terms[0][lower:upper].astype(F32)
            for t in terms[1:]:
                total = total + t[lower:upper].astype(F32)
            return total

        terms = list(terms)
        for step in reversed(self.low):
            half = cur // 2
            terms.append(self.swap(part(half, cur).astype(BF), step))
            cur = half
        got = []
        for j, m in enumerate(self.direct):
            got.append(self.swap(part((j + 1) * rows, (j + 2) * rows).astype(BF), (m, m)))
        total = part(0, rows)
        return (total + got[0].astype(F32)) + (got[1].astype(F32) + got[2].astype(F32))

    def next_term(self, terms, stage):
        cur = self.n * 16 >> stage
        half = cur // 2
        total = terms[0][half:cur].astype(F32)
        for t in terms[1:]:
            total = total + t[half:cur].astype(F32)
        total = total.astype(BF)
        return terms + [self.swap(total, self.low[-1 - stage])], [total]

    def scatter(self, keep, send):
        return self.collect([keep, self.cross(send)])


def dot(a, b, dims):
    return lax.dot_general(a, b, (dims, ((), ())), preferred_element_type=F32)


NN = ((1,), (0,))
NT = ((1,), (1,))
TN = ((0,), (0,))


def gelu_parts(p):
    bell = jnp.exp(p * p * -0.5)
    d = 1.0 + jnp.abs(p) * (0.3275911 * 0.7071067811865476)
    t = pl.reciprocal(d, approx=True)
    t = t * (2.0 - d * t)
    poly = t * (
        0.127414796
        + t * (-0.142248368 + t * (0.7107068705 + t * (-0.7265760135 + t * 0.5307027145)))
    )
    tail = poly * bell
    phi_sum = jnp.where(p >= 0.0, 1.0 - tail, tail)
    return p * phi_sum, phi_sum + p * bell * 0.3989422804014327


def count_of(level):
    return jnp.where(level == 0, P_LOW, jnp.where(level == 1, P_MID, PMAX))


def masked_mix(mix, count):
    i = lax.broadcasted_iota(jnp.int32, (PPAD, SCOLS), 0)
    j = lax.broadcasted_iota(jnp.int32, (PPAD, SCOLS), 1)
    return jnp.where((i < count) & (j < count), mix.astype(F32), 0.0).astype(BF)


def live_rows(count, shape, start=0):
    return lax.broadcasted_iota(jnp.int32, shape, 0) + start < count


def live_mask(levels_ref, b, width):
    return live_rows(count_of(levels_ref[b]), (PPAD, width))


def fold(value):
    total = value[:, 0:128]
    for n in range(128, value.shape[1], 128):
        total = total + value[:, n : n + 128]
    return total


def spread_sum(ref, factor):
    return jnp.broadcast_to(jnp.sum(ref[...], axis=-1, keepdims=True) * factor, ref.shape)


def wide(value, times):
    return jnp.concatenate([value] * times, axis=1)


def start_blocks(table_ref, pieces, rows, cols, target, sem, extra=0):
    copies = []
    k = 0
    for piece in pieces:
        for j in range(piece.shape[0] // 16):
            at = pl.multiple_of(table_ref[k] * rows, 16)
            c = pltpu.make_async_copy(
                piece.at[pl.ds(j * 16, 16), pl.ds(cols[0], cols[1])], target.at[pl.ds(at + extra, 16)], sem.at[k]
            )
            c.start()
            copies.append(c)
            k += 1
    return copies


def row_loop(step, body):
    def run(i, carry):
        body(pl.multiple_of(i * step, step))
        return carry

    lax.fori_loop(0, ROWS // step, run, 0)


def call(kernel, out_shape, in_specs, scratch, flops, nbytes, *args, room=12):
    vm = pl.BlockSpec(memory_space=pltpu.VMEM)
    return pl.pallas_call(
        kernel,
        out_shape=out_shape,
        in_specs=in_specs,
        out_specs=jax.tree.map(lambda _: vm, out_shape),
        scratch_shapes=scratch,
        compiler_params=pltpu.CompilerParams(vmem_limit_bytes=room * MIB),
        cost_estimate=pl.CostEstimate(flops=flops, bytes_accessed=nbytes, transcendentals=0),
    )(*args)


def norm_parts(values):
    center = values - jnp.mean(values, axis=-1, keepdims=True)
    scale = lax.rsqrt(jnp.mean(center * center, axis=-1, keepdims=True) + NORM_EPS)
    return center * scale, scale


VSEG = {
    "g1": (0, D),
    "b1": (D, D),
    "c1l": (2 * D, HALF),
    "c1r": (2 * D + HALF, HALF),
    "g2": (2 * D + FF, HALF),
    "b2": (2 * D + FF + HALF, HALF),
    "c2": (2 * D + FF + 2 * HALF, D),
}
VEC = 2 * D + FF + 2 * HALF + D


def seg(ref, name):
    start, size = VSEG[name]
    return ref[0:1, start : start + size]

def adamw(weight, grad, first, second, rate, decay):
    first = BETA_ONE * first + (1.0 - BETA_ONE) * grad
    second = BETA_TWO * second + (1.0 - BETA_TWO) * grad * grad
    first_hat = first / (1.0 - BETA_ONE**STEP)
    second_hat = second / (1.0 - BETA_TWO**STEP)
    weight = weight - rate * (first_hat / (jnp.sqrt(second_hat) + ADAM_EPS) + decay * weight)
    return (weight, first, second)


CHUNK = 16
TILE = 256
BODY = 32
STRIPE = 112
LO = 2 * HALF
SPC = 2 * SCOLS


def sds(shape, dtype):
    return jax.ShapeDtypeStruct(shape, dtype)


def pack_dense(dense_in, dense_out, vec_row):
    rows = dense_in.shape[0]
    per = vec_row.shape[1]

    def kernel(w_ref, o_ref, v_ref, out_ref, lo_ref, row):
        out_ref[:, 0:HALF] = w_ref[:, HALF:].astype(BF)
        row[...] = jnp.zeros_like(row)
        row[0:1, 0:per] = v_ref[...]
        out_ref[:, HALF:] = row[...].astype(BF)
        lo_ref[:, 0:HALF] = w_ref[:, 0:HALF].astype(BF)
        for g in range(3):
            lo_ref[:, HALF + g * D : HALF + (g + 1) * D] = o_ref[g * rows : (g + 1) * rows, :].astype(BF)

    scratch = [pltpu.VMEM((rows, VCOLS), F32)]
    shapes = (sds((rows, HALF + VCOLS), BF), sds((rows, LO), BF))
    return call(kernel, shapes, [VM] * 3, scratch, 1000, 600000, dense_in, dense_out, vec_row)


def pack_images(sides, spatial, bias_col, patches, out_grad):
    half = patches.shape[1]

    def kernel(sides_ref, s_ref, b_ref, x_ref, g_ref, spat_ref, xs_ref, gs_ref, buf):
        away = 2 - 2 * sides_ref[0]
        for b in range(2):
            xs_ref[b] = x_ref[away + b]
            gs_ref[b] = g_ref[away + b]
        buf[...] = jnp.zeros_like(buf)
        for level in range(3):
            buf[:, 0:PMAX] = s_ref[level]
            rest = b_ref[level]
            for c in range(3):
                piece = rest.astype(BF).astype(F32)
                buf[:, BIAS_AT + c : BIAS_AT + c + 1] = piece
                rest = rest - piece
            spat_ref[level] = buf[...].astype(BF)

    pair = sds((2, half, D), BF)
    return call(
        kernel,
        (sds((3, half, SCOLS), BF), pair, pair),
        [SM] + [VM] * 4,
        [pltpu.VMEM((half, SCOLS), F32)],
        1000,
        3000000,
        sides,
        spatial,
        bias_col,
        patches,
        out_grad,
    )


def stack(pieces, after):
    count = len(pieces)
    rows, cols = pieces[0].shape

    def kernel(*refs):
        for k in range(count):
            refs[count + 1][k * rows : (k + 1) * rows, :] = refs[k][...]

    return call(kernel, sds((count * rows, cols), BF), [VM] * count + [HB], [], 1000, 1000000, *pieces, after)


def two_halves(is_first, own, got):
    own = own.astype(F32)
    got = got.astype(F32)
    return jnp.where(is_first, own, got), jnp.where(is_first, got, own)


def spatial_mix(levels, sides, gate, spat_own, spat_got, after):
    half = spat_own.shape[1]
    count = len(after)

    def kernel(levels_ref, sides_ref, gate_ref, so_ref, sg_ref, *refs):
        spat_ref, mm_ref, mixf = refs[count:]
        is_first = sides_ref[0] == 0
        for b in range(2):
            level = levels_ref[b]
            live = count_of(level)
            one, two = two_halves(is_first, so_ref[level], sg_ref[level])
            mixf[0:half, :] = one
            mixf[half : 2 * half, :] = two
            mixf[2 * half :, :] = jnp.zeros((PPAD - 2 * half, SCOLS), F32)
            bias = jnp.sum(mixf[:, TOTAL_AT:], axis=-1, keepdims=True)
            mm_ref[b] = masked_mix(mixf[...], live)

            def mix_tile(n, carry):
                cols = pl.ds(pl.multiple_of(n * 512, 512), 512)
                got = dot(mm_ref[b], gate_ref[b * PPAD : b * PPAD + SCOLS, cols], NN) + bias
                got = jnp.where(live_rows(live, (PPAD, 512)), got, 0.0)
                spat_ref[b * PPAD : (b + 1) * PPAD, cols] = got.astype(BF)
                return carry

            lax.fori_loop(0, HALF // 512, mix_tile, 0)

    return call(
        kernel,
        (sds((ROWS, HALF), BF), sds((2, PPAD, SCOLS), BF)),
        [SM] * 2 + [VM] * 3 + [HB] * count,
        [pltpu.VMEM((PPAD, SCOLS), F32)],
        3000000000,
        6000000,
        levels,
        sides,
        gate,
        spat_own,
        spat_got,
        *after,
        room=14,
    )


def gate_forward(table, sides, patches, x_got, out_grad, g_got, pieces):
    count = len(pieces)
    half = patches.shape[1]

    def kernel(table_ref, sides_ref, p_ref, xg_ref, o_ref, gg_ref, *refs):
        ins = refs[:count]
        outs = refs[count : count + 9]
        x_ref, og_ref, h_ref, gate_ref, hat_ref, slope_ref, scale_ref, w_ref, vec_ref = outs
        vblk, xbuf, pre, part, mean, sem, vsem = refs[count + 9 :]
        vcopies = start_blocks(table_ref, ins, 16, (HALF, VCOLS), vblk, vsem)
        copies = start_blocks(table_ref, ins, 16, (0, HALF), w_ref, sem)
        me = sides_ref[0]
        is_first = me == 0

        for src, got, target in ((o_ref, gg_ref, og_ref), (p_ref, xg_ref, x_ref)):
            for b in range(2):
                one, two = two_halves(is_first, src[2 * me + b], got[b])
                xbuf[b * PPAD : b * PPAD + half, :] = one
                xbuf[b * PPAD + half : b * PPAD + 2 * half, :] = two
                xbuf[b * PPAD + 2 * half : (b + 1) * PPAD, :] = jnp.zeros((PPAD - 2 * half, D), F32)
            target[...] = xbuf[...].astype(BF)
        for c in vcopies:
            c.wait()
        for s in range(DEVS):
            row = vblk[16 * s : 16 * s + 16, :].astype(F32)[0:1, :VPER]
            vec_ref[0:1, VPER * s : VPER * s + VPER] = row

        def norm_one(r):
            hat, _ = norm_parts(xbuf[pl.ds(r, STRIPE), :])
            h_ref[pl.ds(r, STRIPE), :] = (hat * seg(vec_ref, "g1") + seg(vec_ref, "b1")).astype(BF)

        row_loop(STRIPE, norm_one)
        for c in copies:
            c.wait()
        c_start = VSEG["c1r"][0]
        g_start = VSEG["g2"][0]
        b_start = VSEG["b2"][0]

        def matmul(n, carry):
            at = pl.multiple_of(n * TILE, TILE)
            pre[:, pl.ds(at, TILE)] = dot(h_ref[...], w_ref[:, pl.ds(at, TILE)], NN)
            return carry

        lax.fori_loop(0, HALF // TILE, matmul, 0)

        def gelu_rows(r):
            for k in range(0, BODY, CHUNK):
                rows = pl.ds(r + k, CHUNK)
                total = jnp.zeros((CHUNK, 128), F32)
                for n in range(0, HALF, TILE):
                    v, slope = gelu_parts(pre[rows, n : n + TILE] + vec_ref[0:1, c_start + n : c_start + n + TILE])
                    pre[rows, n : n + TILE] = v
                    slope_ref[rows, n : n + TILE] = slope.astype(BF)
                    total = total + fold(v)
                part[rows, :] = total

        row_loop(BODY, gelu_rows)
        mean[...] = spread_sum(part, 1.0 / HALF)

        def square_rows(r):
            for k in range(0, BODY, CHUNK):
                rows = pl.ds(r + k, CHUNK)
                mid = mean[rows, :]
                total = jnp.zeros((CHUNK, 128), F32)
                for n in range(0, HALF, 128):
                    center = pre[rows, n : n + 128] - mid
                    total = total + center * center
                part[rows, :] = total

        row_loop(BODY, square_rows)
        scale_ref[...] = lax.rsqrt(spread_sum(part, 1.0 / HALF) + NORM_EPS)

        def gate_rows(r):
            for k in range(0, BODY, CHUNK):
                rows = pl.ds(r + k, CHUNK)
                mid = wide(mean[rows, :], 2)
                scale = wide(scale_ref[rows, :], 2)
                for n in range(0, HALF, TILE):
                    hat = (pre[rows, n : n + TILE] - mid) * scale
                    hat_ref[rows, n : n + TILE] = hat.astype(BF)
                    gate = hat * vec_ref[0:1, g_start + n : g_start + n + TILE]
                    gate = (gate + vec_ref[0:1, b_start + n : b_start + n + TILE]).astype(BF)
                    gate_ref[rows, n : n + TILE] = gate

        row_loop(BODY, gate_rows)
        gate_ref[ROWS:, :] = jnp.zeros((SCOLS - PPAD, HALF), BF)

    broad = sds((ROWS, HALF), BF)
    narrow = sds((ROWS, D), BF)
    out_shape = (
        narrow,
        narrow,
        narrow,
        sds((ROWS + SCOLS - PPAD, HALF), BF),
        broad,
        broad,
        sds((ROWS, 128), F32),
        sds((D, HALF), BF),
        sds((1, VEC), F32),
    )
    scratch = [
        pltpu.VMEM((D, VCOLS), BF),
        pltpu.VMEM((ROWS, D), F32),
        pltpu.VMEM((ROWS, HALF), F32),
        pltpu.VMEM((ROWS, 128), F32),
        pltpu.VMEM((ROWS, 128), F32),
        pltpu.SemaphoreType.DMA((DEVS,)),
        pltpu.SemaphoreType.DMA((DEVS,)),
    ]
    return call(
        kernel,
        out_shape,
        [SM] * 2 + [VM] * 4 + [HB] * count,
        scratch,
        10000000000,
        20000000,
        table,
        sides,
        patches,
        x_got,
        out_grad,
        g_got,
        *pieces,
        room=26,
    )


def split_rows(target, first, second, seq, value):
    half = first.shape[1]
    target[...] = value
    for b in range(2):
        one = target[b * PPAD : b * PPAD + half, :]
        two = target[b * PPAD + half : b * PPAD + 2 * half, :]
        first[b] = jnp.where(seq == 0, one, two).astype(BF)
        second[b] = jnp.where(seq == 0, two, one).astype(BF)


def middle(table, levels, sides, vec, h, spat, gate, grad_out, pieces):
    count = len(pieces)

    def kernel(table_ref, levels_ref, sides_ref, vec_ref, h_ref, spat_ref, gate_ref, og_ref, *refs):
        ins = refs[:count]
        gs_ref, gated_ref, q_ref, gb, wl, wo, keep, send, gsum_ref = refs[count : count + 9]
        pbuf, gbuf, cells, flat, sem = refs[count + 9 :]
        copies = start_blocks(table_ref, ins, 16, (0, HALF), wl, sem.at[0])
        for g in range(3):
            copies += start_blocks(table_ref, ins, 48, (HALF + g * D, D), wo, sem.at[1 + g], 16 * g)
        for b in range(2):
            rows = slice(b * PPAD, (b + 1) * PPAD)
            gb[rows, :] = jnp.where(live_mask(levels_ref, b, D), og_ref[rows, :].astype(F32), 0.0).astype(BF)
        gsum_ref[0:1, HALF : HALF + D] = jnp.sum(gb[...].astype(F32), axis=0, keepdims=True)
        cells[...] = jnp.zeros_like(cells)
        flat[...] = jnp.zeros_like(flat)
        for c in copies:
            c.wait()
        c_start = VSEG["c1l"][0]

        def tile(n, carry):
            at = pl.multiple_of(n * TILE, TILE)
            cols = pl.ds(at, TILE)
            pbuf[...] = dot(h_ref[...], wl[:, cols], NN)
            gbuf[...] = dot(gb[...], wo[cols, :], NT)
            shift = vec_ref[0:1, pl.ds(c_start + at, TILE)]
            total = jnp.zeros((CHUNK, TILE), F32)
            for k in range(0, ROWS, CHUNK):
                r = slice(k, k + CHUNK)
                u, slope = gelu_parts(pbuf[r, :] + shift)
                sp = spat_ref[r, cols].astype(F32)
                gg = gbuf[r, :]
                gated_ref[r, cols] = (u * sp).astype(BF)
                gs_ref[r, cols] = (gg * u).astype(BF)
                q = (gg * sp * slope).astype(BF)
                q_ref[r, cols] = q
                total = total + q.astype(F32)
            gsum_ref[0:1, cols] = jnp.sum(total, axis=0, keepdims=True)
            return carry

        lax.fori_loop(0, HALF // TILE, tile, 0)

        me = sides_ref[0]
        for b in range(2):
            level = levels_ref[b]
            count_b = count_of(level)
            gs = gs_ref[b * PPAD : (b + 1) * PPAD, :]
            got = dot(gs, gate_ref[b * PPAD : (b + 1) * PPAD, :], NT)
            sums = jnp.sum(gs.astype(F32), axis=-1, keepdims=True)
            j = lax.broadcasted_iota(jnp.int32, (PPAD, PPAD), 1)
            got = jnp.where(j < count_b, got, jnp.where(j == TOTAL_AT, sums, 0.0))
            cells[level, :, 0:PPAD] += got
        part = PMAX // 2
        for level in range(3):
            for k in range(2):
                flat[k, level * LSTRIDE : level * LSTRIDE + part, 0:PPAD] = cells[level, k * part : (k + 1) * part, 0:PPAD]
        for k in range(DEVS):
            target, side = (keep, me) if k < GROUPS else (send, 1 - me)
            r = pl.ds(k % GROUPS * 16, 16)
            block = flat[side, pl.ds(pl.multiple_of(sides_ref[1 + k] * 32, 32), 32), :].astype(BF)
            target[r, 0:SCOLS] = block[0:16]
            target[r, SCOLS:SPC] = block[16:32]

    broad = sds((ROWS, HALF), BF)
    payload = sds((D // 2, SPC), BF)
    out_shape = (
        broad,
        broad,
        broad,
        sds((ROWS, D), BF),
        sds((D, HALF), BF),
        sds((HALF, D), BF),
        payload,
        payload,
        sds((1, HALF + D), F32),
    )
    scratch = [
        pltpu.VMEM((ROWS, TILE), F32),
        pltpu.VMEM((ROWS, TILE), F32),
        pltpu.VMEM((3, PPAD, SCOLS), F32),
        pltpu.VMEM((2, 512, SCOLS), F32),
        pltpu.SemaphoreType.DMA((4, DEVS)),
    ]
    return call(
        kernel,
        out_shape,
        [SM] * 3 + [VM] * 5 + [HB] * count,
        scratch,
        8000000000,
        16000000,
        table,
        levels,
        sides,
        vec,
        h,
        spat,
        gate,
        grad_out,
        *pieces,
        room=28,
    )


def weight_grads(table, levels, sides, vec, gated, q, gb, h, wl, wo, x, half):
    def kernel(
        table_ref, levels_ref, sides_ref, vec_ref, t_ref, q_ref, gb_ref, h_ref, wl_ref, wo_ref, x_ref,
        keep, send, stay_ref, away_ref, gh_ref, branch, gwo, gwl,
    ):
        def out_tile(n, carry):
            cols = pl.ds(pl.multiple_of(n * TILE, TILE), TILE)
            gwo[cols, :] = dot(t_ref[:, cols], gb_ref[...], TN).astype(BF)
            return carry

        lax.fori_loop(0, HALF // TILE, out_tile, 0)

        def in_tile(n, carry):
            cols = pl.ds(pl.multiple_of(n * TILE, TILE), TILE)
            gwl[cols, :] = dot(h_ref[:, cols], q_ref[...], TN).astype(BF)
            branch[:, cols] = dot(t_ref[...], wo_ref[:, cols], NN)
            gh_ref[:, cols] = dot(q_ref[...], wl_ref[cols, :], NT)
            return carry

        lax.fori_loop(0, D // TILE, in_tile, 0)
        me = sides_ref[0]
        live = jnp.concatenate([live_mask(levels_ref, b, D) for b in range(2)], axis=0)
        out = branch[...] + seg(vec_ref, "c2")
        split_rows(branch, stay_ref, away_ref, me, x_ref[...].astype(F32) + jnp.where(live, out, 0.0))
        for k in range(DEVS):
            dev = table_ref[k]
            target = keep if k < GROUPS else send
            r = pl.ds(k % GROUPS * 16, 16)
            target[r, 0:HALF] = gwl[pl.ds(pl.multiple_of(dev * 16, 16), 16), :]
            for g in range(3):
                target[r, HALF + g * D : HALF + (g + 1) * D] = gwo[pl.ds(pl.multiple_of(dev * 48 + 16 * g, 16), 16), :]

    pair = sds((2, half, D), BF)
    payload = sds((D // 2, LO), BF)
    return call(
        kernel,
        (payload, payload, pair, pair, sds((ROWS, D), F32)),
        [SM] * 3 + [VM] * 8,
        [pltpu.VMEM((ROWS, D), F32), pltpu.VMEM((HALF, D), BF), pltpu.VMEM((D, HALF), BF)],
        5000000000,
        15000000,
        table,
        levels,
        sides,
        vec,
        gated,
        q,
        gb,
        h,
        wl,
        wo,
        x,
        room=24,
    )


def gate_backward(vec, gs, mm, hat, slope, scale):
    def kernel(vec_ref, gs_ref, mm_ref, hat_ref, slope_ref, scale_ref, gp, gsum_ref, dbuf, one, two, acc):
        for b in range(2):

            def mix_tile(n, carry):
                cols = pl.ds(pl.multiple_of(n * 512, 512), 512)
                got = dot(mm_ref[b], gs_ref[b * PPAD : (b + 1) * PPAD, cols], TN)
                dbuf[b * PPAD : (b + 1) * PPAD, cols] = got[0:PPAD]
                return carry

            lax.fori_loop(0, HALF // 512, mix_tile, 0)
        g_start = VSEG["g2"][0]

        def sum_rows(r):
            for k in range(0, BODY, CHUNK):
                rows = pl.ds(r + k, CHUNK)
                a = jnp.zeros((CHUNK, 128), F32)
                c = jnp.zeros((CHUNK, 128), F32)
                for n in range(0, HALF, TILE):
                    e = dbuf[rows, n : n + TILE] * vec_ref[0:1, g_start + n : g_start + n + TILE]
                    a = a + fold(e)
                    c = c + fold(e * hat_ref[rows, n : n + TILE].astype(F32))
                one[rows, :] = a
                two[rows, :] = c

        row_loop(BODY, sum_rows)
        one[...] = spread_sum(one, 1.0 / HALF)
        two[...] = spread_sum(two, 1.0 / HALF)
        acc[...] = jnp.zeros_like(acc)

        def grad_rows(r):
            for n in range(0, HALF, TILE):
                gain = vec_ref[0:1, g_start + n : g_start + n + TILE]
                sums = [jnp.zeros((CHUNK, TILE), F32) for _ in range(3)]
                for k in range(0, BODY, CHUNK):
                    rows = pl.ds(r + k, CHUNK)
                    d = dbuf[rows, n : n + TILE]
                    xh = hat_ref[rows, n : n + TILE].astype(F32)
                    inner = d * gain - wide(one[rows, :], 2) - xh * wide(two[rows, :], 2)
                    q = inner * wide(scale_ref[rows, :], 2) * slope_ref[rows, n : n + TILE].astype(F32)
                    q = q.astype(BF)
                    gp[rows, n : n + TILE] = q
                    sums = [sums[0] + d * xh, sums[1] + d, sums[2] + q.astype(F32)]
                for i in range(3):
                    acc[i, :, n : n + TILE] += sums[i]

        row_loop(BODY, grad_rows)
        for i in range(3):
            gsum_ref[0:1, i * HALF : (i + 1) * HALF] = jnp.sum(acc[i], axis=0, keepdims=True)

    return call(
        kernel,
        (sds((ROWS, HALF), BF), sds((1, 3 * HALF), F32)),
        [VM] * 6,
        [
            pltpu.VMEM((ROWS, HALF), F32),
            pltpu.VMEM((ROWS, 128), F32),
            pltpu.VMEM((ROWS, 128), F32),
            pltpu.VMEM((3, CHUNK, HALF), F32),
        ],
        3000000000,
        10000000,
        vec,
        gs,
        mm,
        hat,
        slope,
        scale,
        room=20,
    )


def in_grads(gp, h, w, gh, after):
    count = len(after)

    def kernel(gp_ref, h_ref, w_ref, gh_ref, *refs):
        gwr, ghb = refs[count:]

        def in_tile(n, carry):
            cols = pl.ds(pl.multiple_of(n * TILE, TILE), TILE)
            ghb[:, cols] = gh_ref[:, cols] + dot(gp_ref[...], w_ref[cols, :], NT)
            gwr[cols, :] = dot(h_ref[:, cols], gp_ref[...], TN).astype(BF)
            return carry

        lax.fori_loop(0, D // TILE, in_tile, 0)

    return call(
        kernel,
        (sds((D, HALF), BF), sds((ROWS, D), F32)),
        [VM] * 4 + [HB] * count,
        [],
        3000000000,
        8000000,
        gp,
        h,
        w,
        gh,
        *after,
        room=14,
    )


def in_backward(table, sides, vec, gsum, gate_sum, gwr, ghb, x, grad_out, half, after):
    count = len(after)

    def kernel(table_ref, sides_ref, vec_ref, gsum_ref, gate_ref, gwr, ghb, x_ref, og_ref, *refs):
        keep, send, stay_ref, away_ref, acc, gvec, blocks, pgb = refs[count:]

        def put(name, value):
            start, size = VSEG[name]
            gvec[0:1, start : start + size] = value

        put("g2", gate_ref[0:1, 0:HALF])
        put("b2", gate_ref[0:1, HALF : 2 * HALF])
        put("c1r", gate_ref[0:1, 2 * HALF : 3 * HALF])
        put("c1l", gsum_ref[0:1, 0:HALF])
        put("c2", gsum_ref[0:1, HALF : HALF + D])
        acc[...] = jnp.zeros_like(acc)
        def in_rows(r):
            rows = pl.ds(r, STRIPE)
            xh, scale = norm_parts(x_ref[rows, :].astype(F32))
            d = ghb[rows, :]
            e = d * seg(vec_ref, "g1")
            one = jnp.mean(e, axis=-1, keepdims=True)
            two = jnp.mean(e * xh, axis=-1, keepdims=True)
            pgb[rows, :] = og_ref[rows, :].astype(F32) + scale * (e - one - xh * two)
            acc[0:1, :] += jnp.sum(d * xh, axis=0, keepdims=True)
            acc[1:2, :] += jnp.sum(d, axis=0, keepdims=True)

        row_loop(STRIPE, in_rows)
        put("g1", acc[0:1, :])
        put("b1", acc[1:2, :])
        split_rows(pgb, stay_ref, away_ref, sides_ref[0], pgb[...])
        blocks[...] = jnp.zeros_like(blocks)
        for s in range(DEVS):
            blocks[s, 0:1, 0:VPER] = gvec[0:1, VPER * s : VPER * s + VPER]
        for k in range(DEVS):
            dev = table_ref[k]
            target = keep if k < GROUPS else send
            r = pl.ds(k % GROUPS * 16, 16)
            target[r, 0:HALF] = gwr[pl.ds(pl.multiple_of(dev * 16, 16), 16), :]
            target[r, HALF : HALF + VCOLS] = blocks[dev].astype(BF)

    payload = sds((D // 2, HALF + VCOLS), BF)
    pair = sds((2, half, D), BF)
    return call(
        kernel,
        (payload, payload, pair, pair),
        [SM] * 2 + [VM] * 7 + [HB] * count,
        [
            pltpu.VMEM((8, D), F32),
            pltpu.VMEM((1, VEC), F32),
            pltpu.VMEM((DEVS, 16, VCOLS), F32),
            pltpu.VMEM((ROWS, D), F32),
        ],
        2000000000,
        6000000,
        table,
        sides,
        vec,
        gsum,
        gate_sum,
        gwr,
        ghb,
        x,
        grad_out,
        *after,
        room=16,
    )


def line_parts(terms):
    cols = terms[0].shape[1]
    count = len(terms)

    def kernel(*refs):
        own, outs = refs[count], refs[count + 1 :]
        for m in range(4):
            rows = slice(16 * m, 16 * (m + 1))
            value = refs[0][rows, :].astype(F32)
            for t in refs[1:count]:
                value = value + t[rows, :].astype(F32)
            if m == 0:
                own[...] = value
            else:
                outs[m - 1][...] = value.astype(BF)

    block = pl.BlockSpec((64, cols), lambda i: (0, 0))
    one = pl.BlockSpec((16, cols), lambda i: (0, 0))
    return pl.pallas_call(
        kernel,
        grid=(1,),
        out_shape=[sds((16, cols), F32)] + [sds((16, cols), BF)] * 3,
        in_specs=[block] * count,
        out_specs=[one] * 4,
        compiler_params=pltpu.CompilerParams(vmem_limit_bytes=8 * MIB),
        cost_estimate=pl.CostEstimate(flops=1000000, bytes_accessed=3000000, transcendentals=0),
    )(*terms)


def line_sum(total, got):
    rows = total.shape[0]

    def kernel(own_ref, a_ref, b_ref, c_ref, out_ref):
        near = own_ref[...].astype(F32) + a_ref[...].astype(F32)
        far = b_ref[...].astype(F32) + c_ref[...].astype(F32)
        out_ref[...] = (near + far).astype(BF)

    return call(kernel, sds((rows, SPC), BF), [VM] * 4, [], 1000000, 500000, total, *got)


def line_spread(terms):
    count = len(terms)
    cols = terms[0].shape[1]

    def kernel(*refs):
        outs = refs[count:]
        for m in range(4):
            rows = slice(16 * m, 16 * (m + 1))
            value = refs[0][rows, :].astype(F32)
            for t in refs[1:count]:
                value = value + t[rows, :].astype(F32)
            value = value.astype(BF)
            for j in range(4):
                at = 16 * (m ^ j)
                outs[j][at : at + 16, :] = value

    block = pl.BlockSpec((64, cols), lambda i: (0, 0))
    return pl.pallas_call(
        kernel,
        grid=(1,),
        out_shape=[sds((64, cols), BF)] * 4,
        in_specs=[block] * count,
        out_specs=[block] * 4,
        compiler_params=pltpu.CompilerParams(vmem_limit_bytes=8 * MIB),
        cost_estimate=pl.CostEstimate(flops=1000000, bytes_accessed=1000000, transcendentals=0),
    )(*terms)


def finish_out(own, got, weight, first, second):
    def kernel(own_ref, a_ref, b_ref, c_ref, w_ref, m_ref, s_ref, left_ref, nw, nm, ns):
        total = own_ref[...] + a_ref[...].astype(F32)
        total = total + (b_ref[...].astype(F32) + c_ref[...].astype(F32))
        left_ref[...] = total[:, 0:HALF]
        for g in range(3):
            rows = slice(16 * g, 16 * (g + 1))
            grad = total[:, HALF + g * D : HALF + (g + 1) * D]
            new = adamw(w_ref[rows, :], grad, m_ref[rows, :], s_ref[rows, :], DENSE_RATE, DENSE_DECAY)
            nw[rows, :] = new[0]
            nm[rows, :] = new[1]
            ns[rows, :] = new[2]

    same = sds(weight.shape, F32)
    return call(
        kernel,
        (sds((16, HALF), F32), same, same, same),
        [VM] * 7,
        [],
        1000000,
        2000000,
        own,
        *got,
        weight,
        first,
        second,
    )


def finish_in(own, got, left, weight, first, second):
    def kernel(own_ref, a_ref, b_ref, c_ref, l_ref, w_ref, m_ref, s_ref, nw, nm, ns, vec_ref):
        total = own_ref[...] + a_ref[...].astype(F32)
        total = total + (b_ref[...].astype(F32) + c_ref[...].astype(F32))
        vec_ref[...] = total[0:1, HALF:]
        for cols, grad in ((slice(0, HALF), l_ref[...]), (slice(HALF, FF), total[:, 0:HALF])):
            new = adamw(w_ref[:, cols], grad, m_ref[:, cols], s_ref[:, cols], DENSE_RATE, DENSE_DECAY)
            nw[:, cols] = new[0]
            nm[:, cols] = new[1]
            ns[:, cols] = new[2]

    same = sds(weight.shape, F32)
    return call(
        kernel,
        (same, same, same, sds((1, VCOLS), F32)),
        [VM] * 8,
        [],
        1000000,
        2000000,
        own,
        *got,
        left,
        weight,
        first,
        second,
    )


def spatial_update(order, pieces, spatial, first, second):
    count = len(pieces)
    rows = spatial.shape[1]

    def kernel(order_ref, *refs):
        ins = refs[:count]
        w_ref, m_ref, s_ref, nw, nm, ns, nb, flat = refs[count:]
        k = 0
        for piece in ins:
            for j in range(piece.shape[0] // 16):
                at = pl.multiple_of(order_ref[k] * 32, 32)
                block = piece[16 * j : 16 * j + 16, :].astype(F32)
                flat[pl.ds(at, 16), :] = block[:, 0:SCOLS]
                flat[pl.ds(at + 16, 16), :] = block[:, SCOLS:]
                k += 1
        for level in range(3):
            got = flat[level * LSTRIDE : level * LSTRIDE + rows, :]
            new = adamw(w_ref[level], got[:, 0:PMAX], m_ref[level], s_ref[level], DENSE_RATE, DENSE_DECAY)
            nw[level] = new[0]
            nm[level] = new[1]
            ns[level] = new[2]
            nb[level] = got[:, TOTAL_AT : TOTAL_AT + 1]

    vm = pl.BlockSpec(memory_space=pltpu.VMEM)
    sm = pl.BlockSpec(memory_space=pltpu.SMEM)
    same = jax.ShapeDtypeStruct(spatial.shape, F32)
    return pl.pallas_call(
        kernel,
        out_shape=(same, same, same, jax.ShapeDtypeStruct((3, rows, 1), F32)),
        in_specs=[sm] + [vm] * (count + 3),
        out_specs=(vm,) * 4,
        scratch_shapes=[pltpu.VMEM((512, SCOLS), F32)],
        compiler_params=pltpu.CompilerParams(vmem_limit_bytes=12 * MIB),
        cost_estimate=pl.CostEstimate(flops=10000000, bytes_accessed=6000000, transcendentals=0),
    )(order, *pieces, spatial, first, second)


def in_order(blocks, table, rows):
    cols = blocks[0].shape[1]
    whole = jnp.concatenate(blocks, axis=0).reshape(-1, rows, cols)
    back = jnp.zeros_like(table).at[table].set(jnp.arange(table.shape[0], dtype=table.dtype))
    return jnp.take(whole, back, axis=0)


def local(
    patches,
    resolution,
    out_grad,
    dense_in,
    dense_out,
    vectors,
    spatial,
    spatial_bias,
    in_first,
    in_second,
    out_first,
    out_second,
    vec_first,
    vec_second,
    spat_first,
    spat_second,
    bias_first,
    bias_second,
):
    route = Route(lax.axis_size("dp"))
    ndev = 2 * route.n
    fits = route.n == GROUPS
    seq = lax.axis_index("seq").astype(jnp.int32)
    rows = patches.shape[1]
    table = route.table()
    order = route.order(False)[0]
    in_rows = dense_in.shape[0]
    out_rows = dense_out.shape[0]
    vec_len = vectors.shape[0]
    if fits:
        ktable = table
        korder = table // 2
    else:
        ktable = jnp.arange(DEVS, dtype=jnp.int32)
        korder = jnp.arange(DEVS, dtype=jnp.int32) % GROUPS
    sides = jnp.concatenate([seq[None], korder])
    levels = lax.dynamic_slice_in_dim(resolution, seq * 2, 2, 0)

    right_shard, lo_shard = pack_dense(dense_in, dense_out, vectors.reshape(1, vec_len))
    line = [route.swap(right_shard, (m, m)) for m in route.direct]
    lo_line = [route.swap(lo_shard, (m, m)) for m in route.direct]
    spat_own, x_send, g_send = pack_images(sides, spatial, spatial_bias.reshape(3, rows, 1), patches, out_grad)
    x_got = route.cross(x_send)
    g_got = route.cross(g_send)
    spat_got = route.cross(spat_own)
    right_blocks = route.widen(jnp.concatenate([right_shard] + line, axis=0))
    if fits:
        lo_first = stack([lo_shard] + lo_line, right_blocks[1])
    else:
        lo_first = jnp.concatenate([lo_shard] + lo_line, axis=0)
    lo_blocks = route.widen(lo_first)
    lo_second = lo_blocks[1]
    right_blocks = right_blocks + [route.cross(b) for b in right_blocks]
    lo_blocks = lo_blocks + [route.cross(b) for b in lo_blocks]
    if not fits:
        whole = in_order(right_blocks, table, in_rows)
        all_vec = whole[:, 0, HALF : HALF + vec_len].reshape(DEVS, 1, VPER)
        all_vec = jnp.pad(all_vec, ((0, 0), (0, 15), (0, VCOLS - VPER))).reshape(D, VCOLS)
        right_blocks = [jnp.concatenate([whole[:, :, :HALF].reshape(D, HALF), all_vec], axis=1)]
        whole = in_order(lo_blocks, table, in_rows)
        outs = whole[:, :, HALF:].reshape(ndev, in_rows, 3, D).transpose(0, 2, 1, 3).reshape(DEVS, 3, 16, D)
        outs = outs.transpose(0, 2, 1, 3).reshape(D, HALF)
        lo_blocks = [jnp.concatenate([whole[:, :, :HALF].reshape(D, HALF), outs], axis=1)]

    x, grad_out, h, gate, hat, slope, scale, weight_right, vec = gate_forward(
        ktable, sides, patches, x_got, out_grad, g_got, right_blocks
    )
    spat, mm = spatial_mix(levels, sides, gate, spat_own, spat_got, [lo_second])
    gs, gated, q, gb, wl, wo, sp_keep, sp_send, gsum = middle(ktable, levels, sides, vec, h, spat, gate, grad_out, lo_blocks)
    sp_got = route.cross(sp_send) if fits else sp_send
    lo_keep, lo_send, mixed_stay, mixed_away, gh = weight_grads(
        ktable, levels, sides, vec, gated, q, gb, h, wl, wo, x, rows
    )
    mixed_got = route.cross(mixed_away)
    gp, gate_sum = gate_backward(vec, gs, mm, hat, slope, scale)
    after = [[], []]
    if fits:
        terms = [lo_keep, route.cross(lo_send)]
        terms, lo_part = route.next_term(terms, 0)
        sp_terms = [sp_keep, sp_got]
        sp_terms, _ = route.next_term(sp_terms, 0)
        after[0] = [sp_terms[-1]]
        sp_terms, _ = route.next_term(sp_terms, 1)
        after[1] = [sp_terms[-1]] + lo_part
    gwr, ghb = in_grads(gp, h, weight_right, gh, after[0])
    right_keep, right_send, grad_stay, grad_away = in_backward(
        ktable, sides, vec, gsum, gate_sum, gwr, ghb, x, grad_out, rows, after[1]
    )
    if fits:
        sp_own, *sends = line_spread(sp_terms)
        got = [route.swap(p, (m, m)) for p, m in zip(sends, route.direct)]
        spat_pieces = route.widen(line_sum(sp_own, got))
        right_terms = [right_keep, route.cross(right_send)]
        terms, _ = route.next_term(terms, 1)
        right_terms, _ = route.next_term(right_terms, 0)
        own, *sends = line_parts(terms)
        got = [route.swap(p, (m, m)) for p, m in zip(sends, route.direct)]
        right_terms, _ = route.next_term(right_terms, 1)
        left_sum, *new_out = finish_out(own, got, dense_out, out_first, out_second)
        own, *sends = line_parts(right_terms)
        got = [route.swap(p, (m, m)) for p, m in zip(sends, route.direct)]
        *new_in, vec_sum = finish_in(own, got, left_sum, dense_in, in_first, in_second)
        vec_sum = vec_sum[0, :vec_len]
        korder = order
    else:
        both = jnp.concatenate([lo_keep, lo_send])
        outs = both[:, HALF:LO].reshape(DEVS, 16, 3, D).transpose(0, 2, 1, 3).reshape(ndev, out_rows, D)
        outs = jnp.take(outs, table, axis=0).reshape(HALF, D)
        out_sum = route.scatter(outs[: HALF // 2], outs[HALF // 2 :])
        lefts = jnp.take(both[:, :HALF].reshape(ndev, in_rows, HALF), table, axis=0).reshape(D, HALF)
        left_sum = route.scatter(lefts[: D // 2], lefts[D // 2 :])
        per = 512 // route.n

        def spat_blocks(part, flip):
            flat = part.reshape(GROUPS, 16, 2, SCOLS).transpose(0, 2, 1, 3).reshape(route.n, per, SCOLS)
            return jnp.take(flat, route.order(flip)[0], axis=0).reshape(512, SCOLS)

        spat_part = route.scatter(spat_blocks(sp_keep, False), spat_blocks(sp_send, True)).astype(BF)
        flat = in_order(route.spread(spat_part), order, per).reshape(GROUPS, 2, 16, SCOLS)
        spat_pieces = [flat.transpose(0, 2, 1, 3).reshape(GROUPS * 16, SPC)]
        korder = jnp.arange(GROUPS, dtype=jnp.int32)
        both = jnp.concatenate([right_keep, right_send])
        vecs = jnp.take(both[::16, HALF : HALF + VPER].reshape(ndev, vec_len), table, axis=0)
        vec_sum = route.scatter(vecs[: route.n], vecs[route.n :]).reshape(vec_len)
        rights = jnp.take(both[:, :HALF].reshape(ndev, in_rows, HALF), table, axis=0).reshape(D, HALF)
        right_sum = route.scatter(rights[: D // 2], rights[D // 2 :])
        in_sum = jnp.concatenate([left_sum, right_sum], axis=1)
        new_in = adamw(dense_in, in_sum, in_first, in_second, DENSE_RATE, DENSE_DECAY)
        new_out = adamw(dense_out, out_sum, out_first, out_second, DENSE_RATE, DENSE_DECAY)

    def whole_images(stays, came):
        return jnp.concatenate([jnp.where(seq == 0, stays, came), jnp.where(seq == 0, came, stays)], axis=0)

    mixed = whole_images(mixed_stay, mixed_got)
    patches_grad = whole_images(grad_stay, route.cross(grad_away))
    new_vec = adamw(vectors, vec_sum, vec_first, vec_second, SMALL_RATE, 0.0)
    spat_new = spatial_update(korder, spat_pieces, spatial, spat_first, spat_second)
    new_bias = adamw(spatial_bias, spat_new[3].reshape(3, rows), bias_first, bias_second, SMALL_RATE, 0.0)
    return (mixed, patches_grad) + tuple(new_in) + tuple(new_out) + new_vec + tuple(spat_new[:3]) + new_bias


def solution(mesh):
    rows3 = P("dp", "seq", None)
    dense = P(AXES, None)
    vec = P(AXES)
    spat = P(None, "seq", None)
    bias = P(None, "seq")
    in_specs = (rows3, P("dp"), rows3, dense, dense, vec, spat, bias)
    in_specs += (dense,) * 4 + (vec,) * 2 + (spat,) * 2 + (bias,) * 2
    out_specs = (rows3, rows3) + (dense,) * 6 + (vec,) * 3 + (spat,) * 3 + (bias,) * 3
    return jax.shard_map(local, mesh=mesh, in_specs=in_specs, out_specs=out_specs, check_vma=False)
```

time: 558 us -> 161 us (0.29); the launches traced: 549 us -> 161 us
  waiting for transfers between devices: 265 us -> 44.2 us
  blocking collectives: 120 us -> 0 us
  matrix products: 86.2 us -> 0 us
  Pallas kernels: 0 us -> 54.3 us
  starting transfers between devices: 1.22 us -> 43.7 us
  other arithmetic: 30.6 us -> 6.82 us
  local copies, waits for them, and re-layouts: 31.2 us -> 10.9 us
  between operations: 14.9 us -> 1.15 us
    reduce_scatter x2 -> x0, waiting for transfers between devices: 207 us -> none  [the longest x1 117 us: local(): lax.psum_scatter(terms[0], ('dp', 'seq'), scatter_dimension=0, tiled=True)]
    dot_general x28 -> x0, matrix products: 86.2 us -> none  [the longest x2 26.5 us: local(): jnp.einsum('bpd,df->bpf', normed_low, weight_in, preferred_element_type=j...]
    unnamed x2 -> x0, blocking collectives: 79.7 us -> none
    all_gather x2 -> x0, waiting for transfers between devices: 55.9 us -> none  [the longest x1 44 us: local(): lax.all_gather(shards[1], ('dp', 'seq'), axis=0, tiled=True)]
    pallas_call x0 -> x17, Pallas kernels: none -> 54.3 us  [the longest x13 50.5 us: call(): pl.pallas_call(kernel, out_shape=out_shape, in_specs=in_specs, out_specs=...]
    ppermute x4 -> x46, starting transfers between devices: 1.02 us -> 43.7 us  [the longest x30 39.6 us: swap(): return lax.ppermute(block, AXES, pairs)]
    ppermute x4 -> x46, waiting for transfers between devices: 1.56 us -> 44.2 us  [the longest x30 43 us: swap(): return lax.ppermute(block, AXES, pairs)]
    psum x1 -> x0, blocking collectives: 40 us -> none  [local(): grad_spat, grad_bias = lax.psum((grad_spat, grad_bias), 'dp')]
  transfers between devices with their start and end apart: 9 -> 46, of which waited for: 5 -> 18; matrix products, arithmetic and copies ran while one was open for 20% -> 6% of each run, Pallas kernels for 0% -> 20%
where the time goes in v1:
time: 161 us
  Pallas kernels  54.3 us (34%)
  waiting for transfers between devices  44.2 us (27%)
  starting transfers between devices  43.7 us (27%)
  local copies, waits for them, and re-layouts  10.9 us (7%)
  other arithmetic  6.82 us (4%)
    pallas_call x13, Pallas kernels, call(): pl.pallas_call(kernel, out_shape=out_shape, in_specs=in_specs, out_specs=...  50.5 us
    ppermute x30, waiting for transfers between devices, swap(): return lax.ppermute(block, AXES, pairs)  43 us
    ppermute x30, starting transfers between devices, swap(): return lax.ppermute(block, AXES, pairs)  39.6 us
    unnamed x77, local copies, waits for them, and re-layouts  10.6 us
    ppermute x16, starting transfers between devices, cross(): return lax.ppermute(block, AXES, pairs)  4.17 us
    convert_element_type x6, other arithmetic, next_term(): total = total.astype(BF)  3.38 us
  transfers between devices with their start and end apart: 46, of which 18 were waited for; matrix products, arithmetic and copies ran while one was open for 6% of the time, Pallas kernels for 20%

profile of v1, /device:TPU:0, one launch (start us, length us, event | category | flops | bytes accessed | tf_op | source)
XLA Modules:
  0.0 161.0 jit_solution(14522404046897490718)
XLA Ops:
  3.2 5.1 %collective-permute-start.4 = (bf16[16,1792]{1,0:T(8,128)(2,1)S(1)}, bf16[16,1792]{1,0:T(8,128)(2,1)S(1)}, u32[]{:S(2)}, u32[]{:S(2)}) collective-permute-start(bf16[16,1792]{1,0:T(8,128)(2,1)S(1)} %get-tuple-element.81), channel_id=1, source_target_pairs={{0,24},{1,25},{2,26},{3,27},{4,28},{5,29},{6,30},{7,31},{8,16},{9,... | collective-permute-start | bytes 172040 | tf_op jit(solution)/shard_map/ppermute | solution.py:64
  8.9 3.5 %collective-permute-done.2 = bf16[16,1792]{1,0:T(8,128)(2,1)S(1)} collective-permute-done((bf16[16,1792]{1,0:T(8,128)(2,1)S(1)}, bf16[16,1792]{1,0:T(8,128)(2,1)S(1)}, u32[]{:S(2)}, u32[]{:S(2)}) %collective-permute-start.2) | collective-permute-done | bytes 57376 | tf_op jit(solution)/shard_map/ppermute | solution.py:64
  13.4 1.6 %collective-permute-start.5 = (bf16[64,1792]{1,0:T(8,128)(2,1)S(1)}, bf16[64,1792]{1,0:T(8,128)(2,1)S(1)}, u32[]{:S(2)}, u32[]{:S(2)}) collective-permute-start(bf16[64,1792]{1,0:T(8,128)(2,1)S(1)} %constant_dynamic-update-slice_fusion.refs_0_), channel_id=1, source_target_pairs={{0,4},{1,3},{2,6},{3,1},{4,0},{5,7},{6,2},{7,5},{8,12},{9,11},{10,... | collective-permute-start | bytes 688136 | tf_op jit(solution)/shard_map/ppermute | solution.py:64
  15.0 2.6 %collective-permute-start.15 = (bf16[16,3072]{1,0:T(8,128)(2,1)S(1)}, bf16[16,3072]{1,0:T(8,128)(2,1)S(1)}, u32[]{:S(2)}, u32[]{:S(2)}) collective-permute-start(bf16[16,3072]{1,0:T(8,128)(2,1)S(1)} %get-tuple-element.86.refs_0_), channel_id=1, source_target_pairs={{0,24},{1,25},{2,26},{3,27},{4,28},{5,29},{6,30},{7,31},{8,16},{9,... | collective-permute-start | bytes 294920 | tf_op jit(solution)/shard_map/ppermute | solution.py:64
  17.6 1.8 %collective-permute-start.13 = (bf16[16,3072]{1,0:T(8,128)(2,1)S(1)}, bf16[16,3072]{1,0:T(8,128)(2,1)S(1)}, u32[]{:S(2)}, u32[]{:S(2)}) collective-permute-start(bf16[16,3072]{1,0:T(8,128)(2,1)S(1)} %get-tuple-element.86.refs_0_), channel_id=1, source_target_pairs={{0,8},{1,9},{2,10},{3,11},{4,12},{5,13},{6,14},{7,15},{8,0},{9,1},... | collective-permute-start | bytes 294920 | tf_op jit(solution)/shard_map/ppermute | solution.py:64
  20.1 2.4 %collective-permute-done.15.refs_3_ = bf16[16,3072]{1,0:T(8,128)(2,1)S(1)} collective-permute-done((bf16[16,3072]{1,0:T(8,128)(2,1)S(1)}, bf16[16,3072]{1,0:T(8,128)(2,1)S(1)}, u32[]{:S(2)}, u32[]{:S(2)}) %collective-permute-start.15) | collective-permute-done | bytes 98336 | tf_op jit(solution)/shard_map/ppermute | solution.py:64
  22.5 3.2 %collective-permute-done.14.refs_2_ = bf16[16,3072]{1,0:T(8,128)(2,1)S(1)} collective-permute-done((bf16[16,3072]{1,0:T(8,128)(2,1)S(1)}, bf16[16,3072]{1,0:T(8,128)(2,1)S(1)}, u32[]{:S(2)}, u32[]{:S(2)}) %collective-permute-start.14) | collective-permute-done | bytes 98336 | tf_op jit(solution)/shard_map/ppermute | solution.py:64
  32.9 2.0 %collective-permute-done.6.refs_2_ = bf16[64,1792]{1,0:T(8,128)(2,1)} collective-permute-done((bf16[64,1792]{1,0:T(8,128)(2,1)S(1)}, bf16[64,1792]{1,0:T(8,128)(2,1)}, u32[]{:S(2)}, u32[]{:S(2)}) %collective-permute-start.6) | collective-permute-done | bytes 229408 | tf_op jit(solution)/shard_map/ppermute | solution.py:64
  35.7 1.8 %collective-permute-done.16.refs_0_.refs_1_ = bf16[64,3072]{1,0:T(8,128)(2,1)} collective-permute-done((bf16[64,3072]{1,0:T(8,128)(2,1)S(1)}, bf16[64,3072]{1,0:T(8,128)(2,1)}, u32[]{:S(2)}, u32[]{:S(2)}) %collective-permute-start.16) | collective-permute-done | bytes 393248 | tf_op jit(solution)/shard_map/ppermute | solution.py:64
  40.4 2.2 %collective-permute-done.17.refs_2_ = bf16[64,3072]{1,0:T(8,128)(2,1)S(1)} collective-permute-done((bf16[64,3072]{1,0:T(8,128)(2,1)S(1)}, bf16[64,3072]{1,0:T(8,128)(2,1)S(1)}, u32[]{:S(2)}, u32[]{:S(2)}) %collective-permute-start.17) | collective-permute-done | bytes 393248 | tf_op jit(solution)/shard_map/ppermute | solution.py:64
  43.2 3.7 %collective-permute-done.18.refs_3_ = bf16[64,3072]{1,0:T(8,128)(2,1)S(1)} collective-permute-done((bf16[64,3072]{1,0:T(8,128)(2,1)}, bf16[64,3072]{1,0:T(8,128)(2,1)S(1)}, u32[]{:S(2)}, u32[]{:S(2)}) %collective-permute-start.18) | collective-permute-done | bytes 393248 | tf_op jit(solution)/shard_map/ppermute | solution.py:64
  47.9 12.1 %shard_map.361 = (bf16[672,512]{1,0:T(8,128)(2,1)S(1)}, bf16[672,512]{1,0:T(8,128)(2,1)S(1)}, bf16[672,512]{1,0:T(8,128)(2,1)S(1)}, bf16[720,1536]{1,0:T(8,128)(...) custom-call(s32[32]{0:T(128)S(1)} %get-tuple-element.182.table_ref, ...), custom_call_target="tpu_custom_call" | custom-call | flops 10000000000 | bytes 20000000 | tf_op jit(solution)/shard_map/pallas_call | solution.py:216
  60.0 3.2 %shard_map.363 = (bf16[672,1536]{1,0:T(8,128)(2,1)S(1)}, bf16[2,336,384]{2,1,0:T(8,128)(2,1)S(1)}) custom-call(s32[2]{0:T(128)S(1)} %dynamic_slice.3.levels_ref, s32[33]{0:T(128)S(1)} %pad_add_fusion.1.sides_ref, bf16[720,1536]{1,0:T(8,128)(2,1)S(1)} %get-tuple-element.84.gate_ref, bf16[3,162,384]{2,1,0:T(8,128)(2,1)S(1)} %copy-done.24, ...), custom_call_target="tpu_custom_call" | custom-call | flops 3000000000 | bytes 6000000 | tf_op jit(solution)/shard_map/pallas_call | solution.py:216
  63.2 13.8 %shard_map.364 = (bf16[672,1536]{1,0:T(8,128)(2,1)S(1)}, bf16[672,1536]{1,0:T(8,128)(2,1)S(1)}, bf16[672,1536]{1,0:T(8,128)(2,1)S(1)}, bf16[672,512]{1,0:T(8,128...) custom-call(s32[32]{0:T(128)S(1)} %get-tuple-element.182.table_ref, ...), custom_call_target="tpu_custom_call" | custom-call | flops 8000000000 | bytes 16000000 | tf_op jit(solution)/shard_map/pallas_call | solution.py:216
  77.0 7.5 %shard_map.365 = (bf16[256,3072]{1,0:T(8,128)(2,1)S(1)}, bf16[256,3072]{1,0:T(8,128)(2,1)S(1)}, bf16[2,162,512]{2,1,0:T(8,128)(2,1)S(1)}, bf16[2,162,512]{2,1,0:T(8,128)(2,1)S(1)}, f32[672,512]{1,0:T(8,128)S(1)}) custom-call(s32[32]{0:T(128)S(1)} %get-tuple-element.182.table_ref, s32[2]{0:T(128)S(1)} %dynamic_slice.3.levels_ref, ...), custom_call_target="tpu_custom_call" | custom-call | flops 5000000000 | bytes 15000000 | tf_op jit(solution)/shard_map/pallas_call | solution.py:216
  85.2 5.6 %shard_map.366 = (bf16[672,1536]{1,0:T(8,128)(2,1)S(1)}, f32[1,4608]{1,0:T(1,128)S(1)}) custom-call(f32[1,7680]{1,0:T(1,128)S(1)} %get-tuple-element.82.vec_ref, bf16[672,1536]{1,0:T(8,128)(2,1)S(1)} %get-tuple-element.98.gs_ref, bf16[2,336,384]{2,1,0:T(8,128)(2,1)S(1)} %get-tuple-element.99.mm_ref, bf16[672,1536]{1,0:T(8,128)(2,1)S(1)} %get-tuple-element.100.hat_ref, ...), custom_call_target="tpu_custom_call" | custom-call | flops 3000000000 | bytes 10000000 | tf_op jit(solution)/shard_map/pallas_call | solution.py:216
  93.3 3.4 %collective-permute-done.25.refs_0_.refs_2_ = bf16[128,768]{1,0:T(8,128)(2,1)S(1)} collective-permute-done((bf16[128,768]{1,0:T(8,128)(2,1)S(1)}, bf16[128,768]{1,0:T(8,128)(2,1)S(1)}, u32[]{:S(2)}, u32[]{:S(2)}) %collective-permute-start.25) | collective-permute-done | bytes 196640 | tf_op jit(solution)/shard_map/ppermute | solution.py:64
  97.8 2.7 %shard_map.367 = (bf16[512,1536]{1,0:T(8,128)(2,1)S(1)}, f32[672,512]{1,0:T(8,128)S(1)}) custom-call(bf16[672,1536]{1,0:T(8,128)(2,1)S(1)} %get-tuple-element.104.gp_ref, bf16[672,512]{1,0:T(8,128)(2,1)S(1)} %get-tuple-element.83.h_ref, bf16[512,1536]{1,0:T(8,128)(2,1)S(1)} %get-tuple-element.105.w_ref, f32[672,512]{1,0:T(8,128)S(1)} %get-tuple-element.106.gh_ref, ...), custom_call_target="tpu_custom_call" | custom-call | flops 3000000000 | bytes 8000000 | tf_op jit(solution)/shard_map/pallas_call | solution.py:216
  100.5 2.0 %collective-permute-done.26.refs_0_.refs_3_ = bf16[64,768]{1,0:T(8,128)(2,1)S(1)} collective-permute-done((bf16[64,768]{1,0:T(8,128)(2,1)S(1)}, bf16[64,768]{1,0:T(8,128)(2,1)S(1)}, u32[]{:S(2)}, u32[]{:S(2)}) %collective-permute-start.26) | collective-permute-done | bytes 98336 | tf_op jit(solution)/shard_map/ppermute | solution.py:64
  102.5 3.0 %shard_map.368 = (bf16[256,1792]{1,0:T(8,128)(2,1)S(1)}, bf16[256,1792]{1,0:T(8,128)(2,1)S(1)}, bf16[2,162,512]{2,1,0:T(8,128)(2,1)S(1)}, bf16[2,162,512]{2,1,0:T(8,128)(2,1)S(1)}) custom-call(s32[32]{0:T(128)S(1)} %get-tuple-element.182.table_ref, s32[33]{0:T(128)S(1)} %pad_add_fusion.1.sides_ref, f32[1,7680]{1,0:T(1,128)S(1)} %get-tuple-element.82.vec_ref, ...), custom_call_target="tpu_custom_call" | custom-call | flops 2000000000 | bytes 6000000 | tf_op jit(solution)/shard_map/pallas_call | solution.py:216
  105.8 2.8 %collective-permute-start.41 = (bf16[64,768]{1,0:T(8,128)(2,1)S(1)}, bf16[64,768]{1,0:T(8,128)(2,1)S(1)}, u32[]{:S(2)}, u32[]{:S(2)}) collective-permute-start(bf16[64,768]{1,0:T(8,128)(2,1)S(1)} %get-tuple-element.135), channel_id=1, source_target_pairs={{0,16},{1,17},{2,18},{3,19},{4,20},{5,21},{6,22},{7,23},{8,24},{9,... | collective-permute-start | bytes 294920 | tf_op jit(solution)/shard_map/ppermute | solution.py:64
  108.6 1.5 collective-permute-start.42
  110.1 2.5 %collective-permute-done.40.a_ref = bf16[64,768]{1,0:T(8,128)(2,1)S(1)} collective-permute-done((bf16[64,768]{1,0:T(8,128)(2,1)S(1)}, bf16[64,768]{1,0:T(8,128)(2,1)S(1)}, u32[]{:S(2)}, u32[]{:S(2)}) %collective-permute-start.40) | collective-permute-done | bytes 98336 | tf_op jit(solution)/shard_map/ppermute | solution.py:64
  112.7 3.9 %collective-permute-done.41.b_ref = bf16[64,768]{1,0:T(8,128)(2,1)S(1)} collective-permute-done((bf16[64,768]{1,0:T(8,128)(2,1)S(1)}, bf16[64,768]{1,0:T(8,128)(2,1)S(1)}, u32[]{:S(2)}, u32[]{:S(2)}) %collective-permute-start.41) | collective-permute-done | bytes 98336 | tf_op jit(solution)/shard_map/ppermute | solution.py:64
  125.1 5.5 %collective-permute-done.44.refs_2_ = bf16[64,768]{1,0:T(8,128)(2,1)S(1)} collective-permute-done((bf16[64,768]{1,0:T(8,128)(2,1)S(1)}, bf16[64,768]{1,0:T(8,128)(2,1)S(1)}, u32[]{:S(2)}, u32[]{:S(2)}) %collective-permute-start.44) | collective-permute-done | bytes 98336 | tf_op jit(solution)/shard_map/ppermute | solution.py:64
  131.6 2.5 %shard_map.375 = (f32[3,162,324]{2,1,0:T(8,128)}, f32[3,162,324]{2,1,0:T(8,128)}, f32[3,162,324]{2,1,0:T(8,128)}, f32[3,162,1]{2,1,0:T(8,128)S(1)}) custom-call(s32[16]{0:T(128)S(1)} %get-tuple-element.184.order_ref, bf16[64,768]{1,0:T(8,128)(2,1)S(1)} %shard_map.374.refs_0_, bf16[64,768]{1,0:T(8,128)(2,1)S(1)} %collective-permute-done.43.refs_1_, ...), custom_call_target="tpu_custom_call" | custom-call | flops 10000000 | bytes 6000000 | tf_op jit(solution)/shard_map/pallas_call | solution.py:1000
  139.3 3.0 %collective-permute-start.37 = (bf16[16,3072]{1,0:T(8,128)(2,1)S(1)}, bf16[16,3072]{1,0:T(8,128)(2,1)S(1)}, u32[]{:S(2)}, u32[]{:S(2)}) collective-permute-start(bf16[16,3072]{1,0:T(8,128)(2,1)S(1)} %get-tuple-element.122), channel_id=1, source_target_pairs={{0,8},{1,9},{2,10},{3,11},{4,12},{5,13},{6,14},{7,15},{8,0},{9,1},... | collective-permute-start | bytes 294920 | tf_op jit(solution)/shard_map/ppermute | solution.py:64
  145.4 1.5 collective-permute-start.39
  146.9 2.5 %collective-permute-done.31.refs_3_ = bf16[64,1792]{1,0:T(8,128)(2,1)S(1)} collective-permute-done((bf16[64,1792]{1,0:T(8,128)(2,1)S(1)}, bf16[64,1792]{1,0:T(8,128)(2,1)S(1)}, u32[]{:S(2)}, u32[]{:S(2)}) %collective-permute-start.31) | collective-permute-done | bytes 229408 | tf_op jit(solution)/shard_map/ppermute | solution.py:64
  150.6 2.7 %collective-permute-start.33 = (bf16[16,1792]{1,0:T(8,128)(2,1)S(1)}, bf16[16,1792]{1,0:T(8,128)(2,1)S(1)}, u32[]{:S(2)}, u32[]{:S(2)}) collective-permute-start(bf16[16,1792]{1,0:T(8,128)(2,1)S(1)} %get-tuple-element.119), channel_id=1, source_target_pairs={{0,16},{1,17},{2,18},{3,19},{4,20},{5,21},{6,22},{7,23},{8,24},{9,... | collective-permute-start | bytes 172040 | tf_op jit(solution)/shard_map/ppermute | solution.py:64
  153.3 1.7 %collective-permute-start.34 = (bf16[16,1792]{1,0:T(8,128)(2,1)S(1)}, bf16[16,1792]{1,0:T(8,128)(2,1)S(1)}, u32[]{:S(2)}, u32[]{:S(2)}) collective-permute-start(bf16[16,1792]{1,0:T(8,128)(2,1)S(1)} %get-tuple-element.120), channel_id=1, source_target_pairs={{0,24},{1,25},{2,26},{3,27},{4,28},{5,29},{6,30},{7,31},{8,16},{9,... | collective-permute-start | bytes 172040 | tf_op jit(solution)/shard_map/ppermute | solution.py:64
  157.1 2.4 %collective-permute-done.33.b_ref = bf16[16,1792]{1,0:T(8,128)(2,1)S(1)} collective-permute-done((bf16[16,1792]{1,0:T(8,128)(2,1)S(1)}, bf16[16,1792]{1,0:T(8,128)(2,1)S(1)}, u32[]{:S(2)}, u32[]{:S(2)}) %collective-permute-start.33) | collective-permute-done | bytes 57376 | tf_op jit(solution)/shard_map/ppermute | solution.py:64
  (173 shorter events, 44.0 us)
Async XLA Ops:
  3.2 10.2 %collective-permute-start.4 = (bf16[16,1792]{1,0:T(8,128)(2,1)S(1)}, bf16[16,1792]{1,0:T(8,128)(2,1)S(1)}, u32[]{:S(2)}, u32[]{:S(2)}) collective-permute-start(bf16[16,1792]{1,0:T(8,128)(2,1)S(1)} %get-tuple-element.81), channel_id=1, source_target_pairs={{0,24},{1,25},{2,26},{3,27},{4,28},{5,29},{6,30},{7,31},{8,16},{9,... | collective-permute-start | bytes 172040 | tf_op jit(solution)/shard_map/ppermute | solution.py:64
  13.4 12.3 %collective-permute-start.5 = (bf16[64,1792]{1,0:T(8,128)(2,1)S(1)}, bf16[64,1792]{1,0:T(8,128)(2,1)S(1)}, u32[]{:S(2)}, u32[]{:S(2)}) collective-permute-start(bf16[64,1792]{1,0:T(8,128)(2,1)S(1)} %constant_dynamic-update-slice_fusion.refs_0_), channel_id=1, source_target_pairs={{0,4},{1,3},{2,6},{3,1},{4,0},{5,7},{6,2},{7,5},{8,12},{9,11},{10,... | collective-permute-start | bytes 688136 | tf_op jit(solution)/shard_map/ppermute | solution.py:64
  15.0 7.5 %collective-permute-start.15 = (bf16[16,3072]{1,0:T(8,128)(2,1)S(1)}, bf16[16,3072]{1,0:T(8,128)(2,1)S(1)}, u32[]{:S(2)}, u32[]{:S(2)}) collective-permute-start(bf16[16,3072]{1,0:T(8,128)(2,1)S(1)} %get-tuple-element.86.refs_0_), channel_id=1, source_target_pairs={{0,24},{1,25},{2,26},{3,27},{4,28},{5,29},{6,30},{7,31},{8,16},{9,... | collective-permute-start | bytes 294920 | tf_op jit(solution)/shard_map/ppermute | solution.py:64
  17.6 8.1 %collective-permute-start.14 = (bf16[16,3072]{1,0:T(8,128)(2,1)S(1)}, bf16[16,3072]{1,0:T(8,128)(2,1)S(1)}, u32[]{:S(2)}, u32[]{:S(2)}) collective-permute-start(bf16[16,3072]{1,0:T(8,128)(2,1)S(1)} %get-tuple-element.86.refs_0_), channel_id=1, source_target_pairs={{0,16},{1,17},{2,18},{3,19},{4,20},{5,21},{6,22},{7,23},{8,24},{9,... | collective-permute-start | bytes 294920 | tf_op jit(solution)/shard_map/ppermute | solution.py:64
  17.6 8.1 %collective-permute-start.13 = (bf16[16,3072]{1,0:T(8,128)(2,1)S(1)}, bf16[16,3072]{1,0:T(8,128)(2,1)S(1)}, u32[]{:S(2)}, u32[]{:S(2)}) collective-permute-start(bf16[16,3072]{1,0:T(8,128)(2,1)S(1)} %get-tuple-element.86.refs_0_), channel_id=1, source_target_pairs={{0,8},{1,9},{2,10},{3,11},{4,12},{5,13},{6,14},{7,15},{8,0},{9,1},... | collective-permute-start | bytes 294920 | tf_op jit(solution)/shard_map/ppermute | solution.py:64
  20.1 11.6 %collective-permute-start.8 = (bf16[64,1792]{1,0:T(8,128)(2,1)S(1)}, bf16[64,1792]{1,0:T(8,128)(2,1)}, u32[]{:S(2)}, u32[]{:S(2)}) collective-permute-start(bf16[64,1792]{1,0:T(8,128)(2,1)S(1)} %constant_dynamic-update-slice_fusion.refs_0_), channel_id=1, source_target_pairs={{0,1},{1,0},{2,3},{3,2},{4,5},{5,4},{6,7},{7,6},{8,9},{9,8},{10,11... | collective-permute-start | bytes 688136 | tf_op jit(solution)/shard_map/ppermute | solution.py:71
  25.7 11.7 %collective-permute-start.16 = (bf16[64,3072]{1,0:T(8,128)(2,1)S(1)}, bf16[64,3072]{1,0:T(8,128)(2,1)}, u32[]{:S(2)}, u32[]{:S(2)}) collective-permute-start(bf16[64,3072]{1,0:T(8,128)(2,1)S(1)} %shard_map.362.refs_0_), channel_id=1, source_target_pairs={{0,4},{1,3},{2,6},{3,1},{4,0},{5,7},{6,2},{7,5},{8,12},{9,11},{10,... | collective-permute-start | bytes 1179656 | tf_op jit(solution)/shard_map/ppermute | solution.py:64
  31.7 7.0 %collective-permute-start.7 = (bf16[64,1792]{1,0:T(8,128)(2,1)S(1)}, bf16[64,1792]{1,0:T(8,128)(2,1)}, u32[]{:S(2)}, u32[]{:S(2)}) collective-permute-start(bf16[64,1792]{1,0:T(8,128)(2,1)S(1)} %collective-permute-done.5.refs_1_.refs_4_), channel_id=1, source_target_pairs={{0,2},{1,5},{2,0},{3,7},{4,6},{5,1},{6,4},{7,3},{8,10},{9,13},{10,... | collective-permute-start | bytes 688136 | tf_op jit(solution)/shard_map/ppermute | solution.py:64
  34.9 7.8 %collective-permute-start.17 = (bf16[64,3072]{1,0:T(8,128)(2,1)S(1)}, bf16[64,3072]{1,0:T(8,128)(2,1)S(1)}, u32[]{:S(2)}, u32[]{:S(2)}) collective-permute-start(bf16[64,3072]{1,0:T(8,128)(2,1)S(1)} %shard_map.362.refs_0_), channel_id=1, source_target_pairs={{0,2},{1,5},{2,0},{3,7},{4,6},{5,1},{6,4},{7,3},{8,10},{9,13},{10,... | collective-permute-start | bytes 1179656 | tf_op jit(solution)/shard_map/ppermute | solution.py:64
  37.5 9.4 %collective-permute-start.18 = (bf16[64,3072]{1,0:T(8,128)(2,1)}, bf16[64,3072]{1,0:T(8,128)(2,1)S(1)}, u32[]{:S(2)}, u32[]{:S(2)}) collective-permute-start(bf16[64,3072]{1,0:T(8,128)(2,1)} %collective-permute-done.16.refs_0_.refs_1_), channel_id=1, source_target_pairs={{0,2},{1,5},{2,0},{3,7},{4,6},{5,1},{6,4},{7,3},{8,10},{9,13},{10,... | collective-permute-start | bytes 1179656 | tf_op jit(solution)/shard_map/ppermute | solution.py:64
  39.3 20.7 %collective-permute-start.12 = (bf16[3,162,384]{2,1,0:T(8,128)(2,1)}, bf16[3,162,384]{2,1,0:T(8,128)(2,1)S(1)}, u32[]{:S(2)}, u32[]{:S(2)}) collective-permute-start(bf16[3,162,384]{2,1,0:T(8,128)(2,1)} %copy-done.23), channel_id=1, source_target_pairs={{0,1},{1,0},{2,3},{3,2},{4,5},{5,4},{6,7},{7,6},{8,9},{9,8},{10,11... | collective-permute-start | bytes 1119752 | tf_op jit(solution)/shard_map/ppermute | solution.py:71
  40.1 23.1 %collective-permute-start.19 = (bf16[64,3072]{1,0:T(8,128)(2,1)S(1)}, bf16[64,3072]{1,0:T(8,128)(2,1)S(1)}, u32[]{:S(2)}, u32[]{:S(2)}) collective-permute-start(bf16[64,3072]{1,0:T(8,128)(2,1)S(1)} %shard_map.362.refs_0_), channel_id=1, source_target_pairs={{0,1},{1,0},{2,3},{3,2},{4,5},{5,4},{6,7},{7,6},{8,9},{9,8},{10,11... | collective-permute-start | bytes 1179656 | tf_op jit(solution)/shard_map/ppermute | solution.py:71
  42.7 20.5 %collective-permute-start.20 = (bf16[64,3072]{1,0:T(8,128)(2,1)}, bf16[64,3072]{1,0:T(8,128)(2,1)S(1)}, u32[]{:S(2)}, u32[]{:S(2)}) collective-permute-start(bf16[64,3072]{1,0:T(8,128)(2,1)} %collective-permute-done.16.refs_0_.refs_1_), channel_id=1, source_target_pairs={{0,1},{1,0},{2,3},{3,2},{4,5},{5,4},{6,7},{7,6},{8,9},{9,8},{10,11... | collective-permute-start | bytes 1179656 | tf_op jit(solution)/shard_map/ppermute | solution.py:71
  42.7 20.5 %collective-permute-start.21 = (bf16[64,3072]{1,0:T(8,128)(2,1)S(1)}, bf16[64,3072]{1,0:T(8,128)(2,1)S(1)}, u32[]{:S(2)}, u32[]{:S(2)}) collective-permute-start(bf16[64,3072]{1,0:T(8,128)(2,1)S(1)} %collective-permute-done.17.refs_2_), channel_id=1, source_target_pairs={{0,1},{1,0},{2,3},{3,2},{4,5},{5,4},{6,7},{7,6},{8,9},{9,8},{10,11... | collective-permute-start | bytes 1179656 | tf_op jit(solution)/shard_map/ppermute | solution.py:71
  46.9 16.3 %collective-permute-start.22 = (bf16[64,3072]{1,0:T(8,128)(2,1)S(1)}, bf16[64,3072]{1,0:T(8,128)(2,1)S(1)}, u32[]{:S(2)}, u32[]{:S(2)}) collective-permute-start(bf16[64,3072]{1,0:T(8,128)(2,1)S(1)} %collective-permute-done.18.refs_3_), channel_id=1, source_target_pairs={{0,1},{1,0},{2,3},{3,2},{4,5},{5,4},{6,7},{7,6},{8,9},{9,8},{10,11... | collective-permute-start | bytes 1179656 | tf_op jit(solution)/shard_map/ppermute | solution.py:71
  84.6 7.2 %collective-permute-start.27 = (bf16[256,3072]{1,0:T(8,128)(2,1)S(1)}, bf16[256,3072]{1,0:T(8,128)(2,1)S(1)}, u32[]{:S(2)}, u32[]{:S(2)}) collective-permute-start(bf16[256,3072]{1,0:T(8,128)(2,1)S(1)} %get-tuple-element.112), channel_id=1, source_target_pairs={{0,1},{1,0},{2,3},{3,2},{4,5},{5,4},{6,7},{7,6},{8,9},{9,8},{10,11... | collective-permute-start | bytes 4718600 | tf_op jit(solution)/shard_map/ppermute | solution.py:71
  92.0 25.8 %collective-permute-start.35 = (bf16[128,3072]{1,0:T(8,128)(2,1)S(1)}, bf16[128,3072]{1,0:T(8,128)(2,1)S(1)}, u32[]{:S(2)}, u32[]{:S(2)}) collective-permute-start(bf16[128,3072]{1,0:T(8,128)(2,1)S(1)} %add_convert_fusion.refs_1_), channel_id=1, source_target_pairs={{0,2},{1,5},{2,0},{3,7},{4,6},{5,1},{6,4},{7,3},{8,10},{9,13},{10,... | collective-permute-start | bytes 2359304 | tf_op jit(solution)/shard_map/ppermute | solution.py:64
  105.5 14.3 %collective-permute-start.29 = (bf16[256,1792]{1,0:T(8,128)(2,1)S(1)}, bf16[256,1792]{1,0:T(8,128)(2,1)S(1)}, u32[]{:S(2)}, u32[]{:S(2)}) collective-permute-start(bf16[256,1792]{1,0:T(8,128)(2,1)S(1)} %get-tuple-element.116), channel_id=1, source_target_pairs={{0,1},{1,0},{2,3},{3,2},{4,5},{5,4},{6,7},{7,6},{8,9},{9,8},{10,11... | collective-permute-start | bytes 2752520 | tf_op jit(solution)/shard_map/ppermute | solution.py:71
  105.7 7.0 %collective-permute-start.40 = (bf16[64,768]{1,0:T(8,128)(2,1)S(1)}, bf16[64,768]{1,0:T(8,128)(2,1)S(1)}, u32[]{:S(2)}, u32[]{:S(2)}) collective-permute-start(bf16[64,768]{1,0:T(8,128)(2,1)S(1)} %get-tuple-element.134), channel_id=1, source_target_pairs={{0,8},{1,9},{2,10},{3,11},{4,12},{5,13},{6,14},{7,15},{8,0},{9,1},... | collective-permute-start | bytes 294920 | tf_op jit(solution)/shard_map/ppermute | solution.py:64
  105.8 10.8 %collective-permute-start.41 = (bf16[64,768]{1,0:T(8,128)(2,1)S(1)}, bf16[64,768]{1,0:T(8,128)(2,1)S(1)}, u32[]{:S(2)}, u32[]{:S(2)}) collective-permute-start(bf16[64,768]{1,0:T(8,128)(2,1)S(1)} %get-tuple-element.135), channel_id=1, source_target_pairs={{0,16},{1,17},{2,18},{3,19},{4,20},{5,21},{6,22},{7,23},{8,24},{9,... | collective-permute-start | bytes 294920 | tf_op jit(solution)/shard_map/ppermute | solution.py:64
  108.6 8.0 %collective-permute-start.42 = (bf16[64,768]{1,0:T(8,128)(2,1)S(1)}, bf16[64,768]{1,0:T(8,128)(2,1)S(1)}, u32[]{:S(2)}, u32[]{:S(2)}) collective-permute-start(bf16[64,768]{1,0:T(8,128)(2,1)S(1)} %get-tuple-element.136), channel_id=1, source_target_pairs={{0,24},{1,25},{2,26},{3,27},{4,28},{5,29},{6,30},{7,31},{8,16},{9,... | collective-permute-start | bytes 294920 | tf_op jit(solution)/shard_map/ppermute | solution.py:64
  112.7 8.9 %collective-permute-start.23 = (bf16[2,162,512]{2,1,0:T(8,128)(2,1)S(1)}, bf16[2,162,512]{2,1,0:T(8,128)(2,1)S(1)}, u32[]{:S(2)}, u32[]{:S(2)}) collective-permute-start(bf16[2,162,512]{2,1,0:T(8,128)(2,1)S(1)} %get-tuple-element.96), channel_id=1, source_target_pairs={{0,1},{1,0},{2,3},{3,2},{4,5},{5,4},{6,7},{7,6},{8,9},{9,8},{10,11... | collective-permute-start | bytes 995336 | tf_op jit(solution)/shard_map/ppermute | solution.py:71
  118.8 19.2 %collective-permute-start.36 = (bf16[64,3072]{1,0:T(8,128)(2,1)}, bf16[64,3072]{1,0:T(8,128)(2,1)S(1)}, u32[]{:S(2)}, u32[]{:S(2)}) collective-permute-start(bf16[64,3072]{1,0:T(8,128)(2,1)} %add_convert_fusion.2), channel_id=1, source_target_pairs={{0,4},{1,3},{2,6},{3,1},{4,0},{5,7},{6,2},{7,5},{8,12},{9,11},{10,... | collective-permute-start | bytes 1179656 | tf_op jit(solution)/shard_map/ppermute | solution.py:64
  120.8 21.5 %collective-permute-start.30 = (bf16[128,1792]{1,0:T(8,128)(2,1)}, bf16[128,1792]{1,0:T(8,128)(2,1)}, u32[]{:S(2)}, u32[]{:S(2)}) collective-permute-start(bf16[128,1792]{1,0:T(8,128)(2,1)} %add_convert_fusion.1), channel_id=1, source_target_pairs={{0,2},{1,5},{2,0},{3,7},{4,6},{5,1},{6,4},{7,3},{8,10},{9,13},{10,... | collective-permute-start | bytes 1376264 | tf_op jit(solution)/shard_map/ppermute | solution.py:64
  121.7 8.8 %collective-permute-start.44 = (bf16[64,768]{1,0:T(8,128)(2,1)S(1)}, bf16[64,768]{1,0:T(8,128)(2,1)S(1)}, u32[]{:S(2)}, u32[]{:S(2)}) collective-permute-start(bf16[64,768]{1,0:T(8,128)(2,1)S(1)} %shard_map.374.refs_0_), channel_id=1, source_target_pairs={{0,2},{1,5},{2,0},{3,7},{4,6},{5,1},{6,4},{7,3},{8,10},{9,13},{10,... | collective-permute-start | bytes 294920 | tf_op jit(solution)/shard_map/ppermute | solution.py:64
  123.1 8.6 %collective-permute-start.45 = (bf16[64,768]{1,0:T(8,128)(2,1)S(1)}, bf16[64,768]{1,0:T(8,128)(2,1)S(1)}, u32[]{:S(2)}, u32[]{:S(2)}) collective-permute-start(bf16[64,768]{1,0:T(8,128)(2,1)S(1)} %collective-permute-done.43.refs_1_), channel_id=1, source_target_pairs={{0,2},{1,5},{2,0},{3,7},{4,6},{5,1},{6,4},{7,3},{8,10},{9,13},{10,... | collective-permute-start | bytes 294920 | tf_op jit(solution)/shard_map/ppermute | solution.py:64
  136.6 7.8 %collective-permute-start.28 = (bf16[2,162,512]{2,1,0:T(8,128)(2,1)}, bf16[2,162,512]{2,1,0:T(8,128)(2,1)S(1)}, u32[]{:S(2)}, u32[]{:S(2)}) collective-permute-start(bf16[2,162,512]{2,1,0:T(8,128)(2,1)} %copy-done.25), channel_id=1, source_target_pairs={{0,1},{1,0},{2,3},{3,2},{4,5},{5,4},{6,7},{7,6},{8,9},{9,8},{10,11... | collective-permute-start | bytes 995336 | tf_op jit(solution)/shard_map/ppermute | solution.py:71
  139.3 14.0 %collective-permute-start.37 = (bf16[16,3072]{1,0:T(8,128)(2,1)S(1)}, bf16[16,3072]{1,0:T(8,128)(2,1)S(1)}, u32[]{:S(2)}, u32[]{:S(2)}) collective-permute-start(bf16[16,3072]{1,0:T(8,128)(2,1)S(1)} %get-tuple-element.122), channel_id=1, source_target_pairs={{0,8},{1,9},{2,10},{3,11},{4,12},{5,13},{6,14},{7,15},{8,0},{9,1},... | collective-permute-start | bytes 294920 | tf_op jit(solution)/shard_map/ppermute | solution.py:64
  144.4 11.8 %collective-permute-start.38 = (bf16[16,3072]{1,0:T(8,128)(2,1)S(1)}, bf16[16,3072]{1,0:T(8,128)(2,1)S(1)}, u32[]{:S(2)}, u32[]{:S(2)}) collective-permute-start(bf16[16,3072]{1,0:T(8,128)(2,1)S(1)} %get-tuple-element.123), channel_id=1, source_target_pairs={{0,16},{1,17},{2,18},{3,19},{4,20},{5,21},{6,22},{7,23},{8,24},{9,... | collective-permute-start | bytes 294920 | tf_op jit(solution)/shard_map/ppermute | solution.py:64
  145.4 10.9 %collective-permute-start.39 = (bf16[16,3072]{1,0:T(8,128)(2,1)S(1)}, bf16[16,3072]{1,0:T(8,128)(2,1)S(1)}, u32[]{:S(2)}, u32[]{:S(2)}) collective-permute-start(bf16[16,3072]{1,0:T(8,128)(2,1)S(1)} %get-tuple-element.124), channel_id=1, source_target_pairs={{0,24},{1,25},{2,26},{3,27},{4,28},{5,29},{6,30},{7,31},{8,16},{9,... | collective-permute-start | bytes 294920 | tf_op jit(solution)/shard_map/ppermute | solution.py:64
  150.5 6.6 %collective-permute-start.32 = (bf16[16,1792]{1,0:T(8,128)(2,1)S(1)}, bf16[16,1792]{1,0:T(8,128)(2,1)S(1)}, u32[]{:S(2)}, u32[]{:S(2)}) collective-permute-start(bf16[16,1792]{1,0:T(8,128)(2,1)S(1)} %get-tuple-element.118), channel_id=1, source_target_pairs={{0,8},{1,9},{2,10},{3,11},{4,12},{5,13},{6,14},{7,15},{8,0},{9,1},... | collective-permute-start | bytes 172040 | tf_op jit(solution)/shard_map/ppermute | solution.py:64
  150.6 8.9 %collective-permute-start.33 = (bf16[16,1792]{1,0:T(8,128)(2,1)S(1)}, bf16[16,1792]{1,0:T(8,128)(2,1)S(1)}, u32[]{:S(2)}, u32[]{:S(2)}) collective-permute-start(bf16[16,1792]{1,0:T(8,128)(2,1)S(1)} %get-tuple-element.119), channel_id=1, source_target_pairs={{0,16},{1,17},{2,18},{3,19},{4,20},{5,21},{6,22},{7,23},{8,24},{9,... | collective-permute-start | bytes 172040 | tf_op jit(solution)/shard_map/ppermute | solution.py:64
  (49 other events, 315.9 us)

commit v2 on v1

--- a/solution.py
+++ b/solution.py
@@ -94,6 +94,11 @@
             blocks = blocks + [self.swap(b, step) for b in blocks]
         return blocks
 
+    def widen_in_turn(self, first):
+        second = self.swap(first, self.low[0])
+        third = self.swap(first, self.low[1])
+        return [first, second, third, self.swap(stack([second], third), self.low[1])]
+
     def gather(self, shard):
         blocks = self.spread(shard)
         return blocks + [self.cross(b) for b in blocks]
@@ -118,15 +123,6 @@
             got.append(self.swap(part((j + 1) * rows, (j + 2) * rows).astype(BF), (m, m)))
         total = part(0, rows)
         return (total + got[0].astype(F32)) + (got[1].astype(F32) + got[2].astype(F32))
-
-    def next_term(self, terms, stage):
-        cur = self.n * 16 >> stage
-        half = cur // 2
-        total = terms[0][half:cur].astype(F32)
-        for t in terms[1:]:
-            total = total + t[half:cur].astype(F32)
-        total = total.astype(BF)
-        return terms + [self.swap(total, self.low[-1 - stage])], [total]
 
     def scatter(self, keep, send):
         return self.collect([keep, self.cross(send)])
@@ -271,18 +267,29 @@
     rows = dense_in.shape[0]
     per = vec_row.shape[1]
 
-    def kernel(w_ref, o_ref, v_ref, out_ref, lo_ref, row):
-        out_ref[:, 0:HALF] = w_ref[:, HALF:].astype(BF)
+    def kernel(w_hbm, o_hbm, v_ref, out_ref, lo_ref, w_ref, o_ref, row, sem):
+        first = pltpu.make_async_copy(w_hbm, w_ref, sem.at[0])
+        second = pltpu.make_async_copy(o_hbm, o_ref, sem.at[1])
+        first.start()
+        second.start()
         row[...] = jnp.zeros_like(row)
         row[0:1, 0:per] = v_ref[...]
         out_ref[:, HALF:] = row[...].astype(BF)
+        first.wait()
+        out_ref[:, 0:HALF] = w_ref[:, HALF:].astype(BF)
         lo_ref[:, 0:HALF] = w_ref[:, 0:HALF].astype(BF)
+        second.wait()
         for g in range(3):
             lo_ref[:, HALF + g * D : HALF + (g + 1) * D] = o_ref[g * rows : (g + 1) * rows, :].astype(BF)
 
-    scratch = [pltpu.VMEM((rows, VCOLS), F32)]
+    scratch = [
+        pltpu.VMEM(dense_in.shape, F32),
+        pltpu.VMEM(dense_out.shape, F32),
+        pltpu.VMEM((rows, VCOLS), F32),
+        pltpu.SemaphoreType.DMA((2,)),
+    ]
     shapes = (sds((rows, HALF + VCOLS), BF), sds((rows, LO), BF))
-    return call(kernel, shapes, [VM] * 3, scratch, 1000, 600000, dense_in, dense_out, vec_row)
+    return call(kernel, shapes, [HB, HB, VM], scratch, 1000, 600000, dense_in, dense_out, vec_row)
 
 
 def pack_images(sides, spatial, bias_col, patches, out_grad):
@@ -336,13 +343,44 @@
     return jnp.where(is_first, own, got), jnp.where(is_first, got, own)
 
 
-def spatial_mix(levels, sides, gate, spat_own, spat_got, after):
+def gate_norm(levels, sides, vec, v, part, spat_own, spat_got, after):
     half = spat_own.shape[1]
     count = len(after)
 
-    def kernel(levels_ref, sides_ref, gate_ref, so_ref, sg_ref, *refs):
-        spat_ref, mm_ref, mixf = refs[count:]
+    def kernel(levels_ref, sides_ref, vec_ref, v_ref, part_ref, so_ref, sg_ref, *refs):
+        gate_ref, hat_ref, scale_ref, spat_ref, mm_ref, mixf, mean, buf = refs[count:]
         is_first = sides_ref[0] == 0
+        g_start = VSEG["g2"][0]
+        b_start = VSEG["b2"][0]
+        mean[...] = spread_sum(part_ref, 1.0 / HALF)
+
+        def square_rows(r):
+            for k in range(0, BODY, CHUNK):
+                rows = pl.ds(r + k, CHUNK)
+                mid = mean[rows, :]
+                total = jnp.zeros((CHUNK, 128), F32)
+                for n in range(0, HALF, 128):
+                    center = v_ref[rows, n : n + 128] - mid
+                    total = total + center * center
+                buf[rows, :] = total
+
+        row_loop(BODY, square_rows)
+        scale_ref[...] = lax.rsqrt(spread_sum(buf, 1.0 / HALF) + NORM_EPS)
+
+        def gate_rows(r):
+            for k in range(0, BODY, CHUNK):
+                rows = pl.ds(r + k, CHUNK)
+                mid = wide(mean[rows, :], 2)
+                scale = wide(scale_ref[rows, :], 2)
+                for n in range(0, HALF, TILE):
+                    hat = (v_ref[rows, n : n + TILE] - mid) * scale
+                    hat_ref[rows, n : n + TILE] = hat.astype(BF)
+                    gate = hat * vec_ref[0:1, g_start + n : g_start + n + TILE]
+                    gate = (gate + vec_ref[0:1, b_start + n : b_start + n + TILE]).astype(BF)
+                    gate_ref[rows, n : n + TILE] = gate
+
+        row_loop(BODY, gate_rows)
+        gate_ref[ROWS:, :] = jnp.zeros((SCOLS - PPAD, HALF), BF)
         for b in range(2):
             level = levels_ref[b]
             live = count_of(level)
@@ -364,18 +402,26 @@
 
     return call(
         kernel,
-        (sds((ROWS, HALF), BF), sds((2, PPAD, SCOLS), BF)),
-        [SM] * 2 + [VM] * 3 + [HB] * count,
-        [pltpu.VMEM((PPAD, SCOLS), F32)],
-        3000000000,
-        6000000,
+        (
+            sds((ROWS + SCOLS - PPAD, HALF), BF),
+            sds((ROWS, HALF), BF),
+            sds((ROWS, 128), F32),
+            sds((ROWS, HALF), BF),
+            sds((2, PPAD, SCOLS), BF),
+        ),
+        [SM] * 2 + [VM] * 5 + [HB] * count,
+        [pltpu.VMEM((PPAD, SCOLS), F32), pltpu.VMEM((ROWS, 128), F32), pltpu.VMEM((ROWS, 128), F32)],
+        6000000000,
+        12000000,
         levels,
         sides,
-        gate,
+        vec,
+        v,
+        part,
         spat_own,
         spat_got,
         *after,
-        room=14,
+        room=22,
     )
 
 
@@ -385,9 +431,9 @@
 
     def kernel(table_ref, sides_ref, p_ref, xg_ref, o_ref, gg_ref, *refs):
         ins = refs[:count]
-        outs = refs[count : count + 9]
-        x_ref, og_ref, h_ref, gate_ref, hat_ref, slope_ref, scale_ref, w_ref, vec_ref = outs
-        vblk, xbuf, pre, part, mean, sem, vsem = refs[count + 9 :]
+        outs = refs[count : count + 8]
+        x_ref, og_ref, h_ref, pre, slope_ref, part, w_ref, vec_ref = outs
+        vblk, xbuf, sem, vsem = refs[count + 8 :]
         vcopies = start_blocks(table_ref, ins, 16, (HALF, VCOLS), vblk, vsem)
         copies = start_blocks(table_ref, ins, 16, (0, HALF), w_ref, sem)
         me = sides_ref[0]
@@ -414,8 +460,6 @@
         for c in copies:
             c.wait()
         c_start = VSEG["c1r"][0]
-        g_start = VSEG["g2"][0]
-        b_start = VSEG["b2"][0]
 
         def matmul(n, carry):
             at = pl.multiple_of(n * TILE, TILE)
@@ -436,35 +480,6 @@
                 part[rows, :] = total
 
         row_loop(BODY, gelu_rows)
-        mean[...] = spread_sum(part, 1.0 / HALF)
-
-        def square_rows(r):
-            for k in range(0, BODY, CHUNK):
-                rows = pl.ds(r + k, CHUNK)
-                mid = mean[rows, :]
-                total = jnp.zeros((CHUNK, 128), F32)
-                for n in range(0, HALF, 128):
-                    center = pre[rows, n : n + 128] - mid
-                    total = total + center * center
-                part[rows, :] = total
-
-        row_loop(BODY, square_rows)
-        scale_ref[...] = lax.rsqrt(spread_sum(part, 1.0 / HALF) + NORM_EPS)
-
-        def gate_rows(r):
-            for k in range(0, BODY, CHUNK):
-                rows = pl.ds(r + k, CHUNK)
-                mid = wide(mean[rows, :], 2)
-                scale = wide(scale_ref[rows, :], 2)
-                for n in range(0, HALF, TILE):
-                    hat = (pre[rows, n : n + TILE] - mid) * scale
-                    hat_ref[rows, n : n + TILE] = hat.astype(BF)
-                    gate = hat * vec_ref[0:1, g_start + n : g_start + n + TILE]
-                    gate = (gate + vec_ref[0:1, b_start + n : b_start + n + TILE]).astype(BF)
-                    gate_ref[rows, n : n + TILE] = gate
-
-        row_loop(BODY, gate_rows)
-        gate_ref[ROWS:, :] = jnp.zeros((SCOLS - PPAD, HALF), BF)
 
     broad = sds((ROWS, HALF), BF)
     narrow = sds((ROWS, D), BF)
@@ -472,8 +487,7 @@
         narrow,
         narrow,
         narrow,
-        sds((ROWS + SCOLS - PPAD, HALF), BF),
-        broad,
+        sds((ROWS, HALF), F32),
         broad,
         sds((ROWS, 128), F32),
         sds((D, HALF), BF),
@@ -482,9 +496,6 @@
     scratch = [
         pltpu.VMEM((D, VCOLS), BF),
         pltpu.VMEM((ROWS, D), F32),
-        pltpu.VMEM((ROWS, HALF), F32),
-        pltpu.VMEM((ROWS, 128), F32),
-        pltpu.VMEM((ROWS, 128), F32),
         pltpu.SemaphoreType.DMA((DEVS,)),
         pltpu.SemaphoreType.DMA((DEVS,)),
     ]
@@ -675,8 +686,12 @@
     )
 
 
-def gate_backward(vec, gs, mm, hat, slope, scale):
-    def kernel(vec_ref, gs_ref, mm_ref, hat_ref, slope_ref, scale_ref, gp, gsum_ref, dbuf, one, two, acc):
+def gate_backward(vec, gs, mm, hat, slope, scale, after):
+    count = len(after)
+
+    def kernel(vec_ref, gs_ref, mm_ref, hat_ref, slope_ref, scale_ref, *refs):
+        gp, gsum_ref, dbuf, one, two, acc = refs[count:]
+
         for b in range(2):
 
             def mix_tile(n, carry):
@@ -728,7 +743,7 @@
     return call(
         kernel,
         (sds((ROWS, HALF), BF), sds((1, 3 * HALF), F32)),
-        [VM] * 6,
+        [VM] * 6 + [HB] * count,
         [
             pltpu.VMEM((ROWS, HALF), F32),
             pltpu.VMEM((ROWS, 128), F32),
@@ -743,6 +758,7 @@
         hat,
         slope,
         scale,
+        *after,
         room=20,
     )
 
@@ -781,7 +797,7 @@
     count = len(after)
 
     def kernel(table_ref, sides_ref, vec_ref, gsum_ref, gate_ref, gwr, ghb, x_ref, og_ref, *refs):
-        keep, send, stay_ref, away_ref, acc, gvec, blocks, pgb = refs[count:]
+        keep, send, send_up, stay_ref, away_ref, acc, gvec, blocks, pgb = refs[count:]
 
         def put(name, value):
             start, size = VSEG[name]
@@ -813,16 +829,17 @@
             blocks[s, 0:1, 0:VPER] = gvec[0:1, VPER * s : VPER * s + VPER]
         for k in range(DEVS):
             dev = table_ref[k]
-            target = keep if k < GROUPS else send
-            r = pl.ds(k % GROUPS * 16, 16)
+            target = keep if k < GROUPS else send if k < GROUPS * 3 // 2 else send_up
+            r = pl.ds(k % (GROUPS if k < GROUPS else GROUPS // 2) * 16, 16)
             target[r, 0:HALF] = gwr[pl.ds(pl.multiple_of(dev * 16, 16), 16), :]
             target[r, HALF : HALF + VCOLS] = blocks[dev].astype(BF)
 
     payload = sds((D // 2, HALF + VCOLS), BF)
+    part = sds((D // 4, HALF + VCOLS), BF)
     pair = sds((2, half, D), BF)
     return call(
         kernel,
-        (payload, payload, pair, pair),
+        (payload, part, part, pair, pair),
         [SM] * 2 + [VM] * 7 + [HB] * count,
         [
             pltpu.VMEM((8, D), F32),
@@ -846,12 +863,37 @@
     )
 
 
-def line_parts(terms):
+def add_part(terms, size, after, places=None):
     cols = terms[0].shape[1]
     count = len(terms)
 
     def kernel(*refs):
-        own, outs = refs[count], refs[count + 1 :]
+        for r in range(0, size, 16):
+            rows = slice(r, r + 16)
+            value = refs[0][rows, :].astype(F32)
+            for t in refs[1:count]:
+                value = value + t[rows, :].astype(F32)
+            refs[count + len(after)][rows, :] = value.astype(BF)
+
+    places = places or [1] * count
+    blocks = [pl.BlockSpec((size, cols), lambda i, p=p: (p, 0)) for p in places]
+    return pl.pallas_call(
+        kernel,
+        grid=(1,),
+        out_shape=sds((size, cols), BF),
+        in_specs=blocks + [HB] * len(after),
+        out_specs=pl.BlockSpec((size, cols), lambda i: (0, 0)),
+        compiler_params=pltpu.CompilerParams(vmem_limit_bytes=10 * MIB),
+        cost_estimate=pl.CostEstimate(flops=1000000, bytes_accessed=3000000, transcendentals=0),
+    )(*terms, *after)
+
+
+def line_parts(terms, after):
+    cols = terms[0].shape[1]
+    count = len(terms)
+
+    def kernel(*refs):
+        own, outs = refs[count + 1], refs[count + 2 :]
         for m in range(4):
             rows = slice(16 * m, 16 * (m + 1))
             value = refs[0][rows, :].astype(F32)
@@ -868,30 +910,30 @@
         kernel,
         grid=(1,),
         out_shape=[sds((16, cols), F32)] + [sds((16, cols), BF)] * 3,
-        in_specs=[block] * count,
+        in_specs=[block] * count + [HB],
         out_specs=[one] * 4,
         compiler_params=pltpu.CompilerParams(vmem_limit_bytes=8 * MIB),
         cost_estimate=pl.CostEstimate(flops=1000000, bytes_accessed=3000000, transcendentals=0),
-    )(*terms)
-
-
-def line_sum(total, got):
+    )(*terms, after)
+
+
+def line_sum(total, got, after):
     rows = total.shape[0]
 
-    def kernel(own_ref, a_ref, b_ref, c_ref, out_ref):
+    def kernel(own_ref, a_ref, b_ref, c_ref, after_ref, out_ref):
         near = own_ref[...].astype(F32) + a_ref[...].astype(F32)
         far = b_ref[...].astype(F32) + c_ref[...].astype(F32)
         out_ref[...] = (near + far).astype(BF)
 
-    return call(kernel, sds((rows, SPC), BF), [VM] * 4, [], 1000000, 500000, total, *got)
-
-
-def line_spread(terms):
+    return call(kernel, sds((rows, SPC), BF), [VM] * 4 + [HB], [], 1000000, 500000, total, *got, after)
+
+
+def line_spread(terms, after):
     count = len(terms)
     cols = terms[0].shape[1]
 
     def kernel(*refs):
-        outs = refs[count:]
+        outs = refs[count + 1 :]
         for m in range(4):
             rows = slice(16 * m, 16 * (m + 1))
             value = refs[0][rows, :].astype(F32)
@@ -907,15 +949,15 @@
         kernel,
         grid=(1,),
         out_shape=[sds((64, cols), BF)] * 4,
-        in_specs=[block] * count,
+        in_specs=[block] * count + [HB],
         out_specs=[block] * 4,
         compiler_params=pltpu.CompilerParams(vmem_limit_bytes=8 * MIB),
         cost_estimate=pl.CostEstimate(flops=1000000, bytes_accessed=1000000, transcendentals=0),
-    )(*terms)
-
-
-def finish_out(own, got, weight, first, second):
-    def kernel(own_ref, a_ref, b_ref, c_ref, w_ref, m_ref, s_ref, left_ref, nw, nm, ns):
+    )(*terms, after)
+
+
+def finish_out(own, got, weight, first, second, after):
+    def kernel(own_ref, a_ref, b_ref, c_ref, w_ref, m_ref, s_ref, after_ref, left_ref, nw, nm, ns):
         total = own_ref[...] + a_ref[...].astype(F32)
         total = total + (b_ref[...].astype(F32) + c_ref[...].astype(F32))
         left_ref[...] = total[:, 0:HALF]
@@ -931,7 +973,7 @@
     return call(
         kernel,
         (sds((16, HALF), F32), same, same, same),
-        [VM] * 7,
+        [VM] * 7 + [HB],
         [],
         1000000,
         2000000,
@@ -940,11 +982,12 @@
         weight,
         first,
         second,
-    )
-
-
-def finish_in(own, got, left, weight, first, second):
-    def kernel(own_ref, a_ref, b_ref, c_ref, l_ref, w_ref, m_ref, s_ref, nw, nm, ns, vec_ref):
+        after,
+    )
+
+
+def finish_in(own, got, left, weight, first, second, after):
+    def kernel(own_ref, a_ref, b_ref, c_ref, l_ref, w_ref, m_ref, s_ref, after_ref, nw, nm, ns, vec_ref):
         total = own_ref[...] + a_ref[...].astype(F32)
         total = total + (b_ref[...].astype(F32) + c_ref[...].astype(F32))
         vec_ref[...] = total[0:1, HALF:]
@@ -958,7 +1001,7 @@
     return call(
         kernel,
         (same, same, same, sds((1, VCOLS), F32)),
-        [VM] * 8,
+        [VM] * 8 + [HB],
         [],
         1000000,
         2000000,
@@ -968,16 +1011,18 @@
         weight,
         first,
         second,
-    )
-
-
-def spatial_update(order, pieces, spatial, first, second):
+        after,
+    )
+
+
+def spatial_update(order, pieces, spatial, first, second, bias, bias_first, bias_second, after):
     count = len(pieces)
     rows = spatial.shape[1]
 
     def kernel(order_ref, *refs):
         ins = refs[:count]
-        w_ref, m_ref, s_ref, nw, nm, ns, nb, flat = refs[count:]
+        w_ref, m_ref, s_ref, bw, bm, bs = refs[count : count + 6]
+        nw, nm, ns, nbw, nbm, nbs, flat = refs[count + 6 + len(after) :]
         k = 0
         for piece in ins:
             for j in range(piece.shape[0] // 16):
@@ -986,26 +1031,40 @@
                 flat[pl.ds(at, 16), :] = block[:, 0:SCOLS]
                 flat[pl.ds(at + 16, 16), :] = block[:, SCOLS:]
                 k += 1
+        at = TOTAL_AT // 128 * 128
+        totals = flat[:, at : at + 128].T[TOTAL_AT - at : TOTAL_AT - at + 1, :]
         for level in range(3):
             got = flat[level * LSTRIDE : level * LSTRIDE + rows, :]
             new = adamw(w_ref[level], got[:, 0:PMAX], m_ref[level], s_ref[level], DENSE_RATE, DENSE_DECAY)
             nw[level] = new[0]
             nm[level] = new[1]
             ns[level] = new[2]
-            nb[level] = got[:, TOTAL_AT : TOTAL_AT + 1]
-
-    vm = pl.BlockSpec(memory_space=pltpu.VMEM)
-    sm = pl.BlockSpec(memory_space=pltpu.SMEM)
-    same = jax.ShapeDtypeStruct(spatial.shape, F32)
-    return pl.pallas_call(
-        kernel,
-        out_shape=(same, same, same, jax.ShapeDtypeStruct((3, rows, 1), F32)),
-        in_specs=[sm] + [vm] * (count + 3),
-        out_specs=(vm,) * 4,
-        scratch_shapes=[pltpu.VMEM((512, SCOLS), F32)],
-        compiler_params=pltpu.CompilerParams(vmem_limit_bytes=12 * MIB),
-        cost_estimate=pl.CostEstimate(flops=10000000, bytes_accessed=6000000, transcendentals=0),
-    )(order, *pieces, spatial, first, second)
+            got = totals[:, level * LSTRIDE : level * LSTRIDE + rows]
+            r = slice(level, level + 1)
+            new = adamw(bw[r, :], got, bm[r, :], bs[r, :], SMALL_RATE, 0.0)
+            nbw[r, :] = new[0]
+            nbm[r, :] = new[1]
+            nbs[r, :] = new[2]
+
+    same = sds(spatial.shape, F32)
+    small = sds(bias.shape, F32)
+    return call(
+        kernel,
+        (same, same, same, small, small, small),
+        [SM] + [VM] * (count + 6) + [HB] * len(after),
+        [pltpu.VMEM((512, SCOLS), F32)],
+        10000000,
+        6000000,
+        order,
+        *pieces,
+        spatial,
+        first,
+        second,
+        bias,
+        bias_first,
+        bias_second,
+        *after,
+    )
 
 
 def in_order(blocks, table, rows):
@@ -1061,12 +1120,12 @@
     x_got = route.cross(x_send)
     g_got = route.cross(g_send)
     spat_got = route.cross(spat_own)
-    right_blocks = route.widen(jnp.concatenate([right_shard] + line, axis=0))
     if fits:
-        lo_first = stack([lo_shard] + lo_line, right_blocks[1])
+        right_blocks = route.widen_in_turn(stack([right_shard] + line, lo_line[0]))
+        lo_blocks = route.widen_in_turn(stack([lo_shard] + lo_line, right_blocks[3]))
     else:
-        lo_first = jnp.concatenate([lo_shard] + lo_line, axis=0)
-    lo_blocks = route.widen(lo_first)
+        right_blocks = route.widen(jnp.concatenate([right_shard] + line, axis=0))
+        lo_blocks = route.widen(jnp.concatenate([lo_shard] + lo_line, axis=0))
     lo_second = lo_blocks[1]
     right_blocks = right_blocks + [route.cross(b) for b in right_blocks]
     lo_blocks = lo_blocks + [route.cross(b) for b in lo_blocks]
@@ -1080,46 +1139,59 @@
         outs = outs.transpose(0, 2, 1, 3).reshape(D, HALF)
         lo_blocks = [jnp.concatenate([whole[:, :, :HALF].reshape(D, HALF), outs], axis=1)]
 
-    x, grad_out, h, gate, hat, slope, scale, weight_right, vec = gate_forward(
+    x, grad_out, h, v, slope, part, weight_right, vec = gate_forward(
         ktable, sides, patches, x_got, out_grad, g_got, right_blocks
     )
-    spat, mm = spatial_mix(levels, sides, gate, spat_own, spat_got, [lo_second])
+    gate, hat, scale, spat, mm = gate_norm(levels, sides, vec, v, part, spat_own, spat_got, [lo_second])
     gs, gated, q, gb, wl, wo, sp_keep, sp_send, gsum = middle(ktable, levels, sides, vec, h, spat, gate, grad_out, lo_blocks)
-    sp_got = route.cross(sp_send) if fits else sp_send
+    near, far = route.low[-1], route.low[0]
+    if fits:
+        sp_terms = [sp_keep, route.cross(sp_send)]
     lo_keep, lo_send, mixed_stay, mixed_away, gh = weight_grads(
         ktable, levels, sides, vec, gated, q, gb, h, wl, wo, x, rows
     )
     mixed_got = route.cross(mixed_away)
-    gp, gate_sum = gate_backward(vec, gs, mm, hat, slope, scale)
     after = [[], []]
     if fits:
-        terms = [lo_keep, route.cross(lo_send)]
-        terms, lo_part = route.next_term(terms, 0)
-        sp_terms = [sp_keep, sp_got]
-        sp_terms, _ = route.next_term(sp_terms, 0)
+        sp_part = add_part(sp_terms, 128, [])
+        sp_terms.append(route.swap(sp_part, near))
+        lo_terms = [lo_keep, route.cross(lo_send)]
+        after[0] = [sp_part]
+    gp, gate_sum = gate_backward(vec, gs, mm, hat, slope, scale, after[0])
+    if fits:
+        lo_part = add_part(lo_terms, 128, [gate_sum])
+        lo_terms.append(route.swap(lo_part, near))
+        sp_part = add_part(sp_terms, 64, [lo_part])
+        sp_terms.append(route.swap(sp_part, far))
+        after[1] = [sp_part]
+    gwr, ghb = in_grads(gp, h, weight_right, gh, after[1])
+    if fits:
         after[0] = [sp_terms[-1]]
-        sp_terms, _ = route.next_term(sp_terms, 1)
-        after[1] = [sp_terms[-1]] + lo_part
-    gwr, ghb = in_grads(gp, h, weight_right, gh, after[0])
-    right_keep, right_send, grad_stay, grad_away = in_backward(
-        ktable, sides, vec, gsum, gate_sum, gwr, ghb, x, grad_out, rows, after[1]
+    else:
+        after[0] = []
+    right_keep, right_send, right_up, grad_stay, grad_away = in_backward(
+        ktable, sides, vec, gsum, gate_sum, gwr, ghb, x, grad_out, rows, after[0]
     )
     if fits:
-        sp_own, *sends = line_spread(sp_terms)
-        got = [route.swap(p, (m, m)) for p, m in zip(sends, route.direct)]
-        spat_pieces = route.widen(line_sum(sp_own, got))
+        right_up = route.cross(right_up)
         right_terms = [right_keep, route.cross(right_send)]
-        terms, _ = route.next_term(terms, 1)
-        right_terms, _ = route.next_term(right_terms, 0)
-        own, *sends = line_parts(terms)
-        got = [route.swap(p, (m, m)) for p, m in zip(sends, route.direct)]
-        right_terms, _ = route.next_term(right_terms, 1)
-        left_sum, *new_out = finish_out(own, got, dense_out, out_first, out_second)
-        own, *sends = line_parts(right_terms)
-        got = [route.swap(p, (m, m)) for p, m in zip(sends, route.direct)]
-        *new_in, vec_sum = finish_in(own, got, left_sum, dense_in, in_first, in_second)
-        vec_sum = vec_sum[0, :vec_len]
+        right_part = add_part([right_keep, right_up], 128, [], [1, 0])
+        right_terms.append(route.swap(right_part, near))
+        sp_own, *sends = line_spread(sp_terms, right_part)
+        sp_got = [route.swap(p, (m, m)) for p, m in zip(sends, route.direct)]
+        lo_part = add_part(lo_terms, 64, [sp_own])
+        lo_terms.append(route.swap(lo_part, far))
+        right_part = add_part(right_terms, 64, [lo_part])
+        right_terms.append(route.swap(right_part, far))
+        sp_sum = line_sum(sp_own, sp_got, right_part)
+        spat_pieces = route.widen(sp_sum)
+        lo_own, *sends = line_parts(lo_terms, sp_sum)
+        lo_got = [route.swap(p, (m, m)) for p, m in zip(sends, route.direct)]
+        right_own, *sends = line_parts(right_terms, lo_own)
+        right_got = [route.swap(p, (m, m)) for p, m in zip(sends, route.direct)]
+        left_sum, *new_out = finish_out(lo_own, lo_got, dense_out, out_first, out_second, right_own)
         korder = order
+        after = [left_sum]
     else:
         both = jnp.concatenate([lo_keep, lo_send])
         outs = both[:, HALF:LO].reshape(DEVS, 16, 3, D).transpose(0, 2, 1, 3).reshape(ndev, out_rows, D)
@@ -1137,7 +1209,8 @@
         flat = in_order(route.spread(spat_part), order, per).reshape(GROUPS, 2, 16, SCOLS)
         spat_pieces = [flat.transpose(0, 2, 1, 3).reshape(GROUPS * 16, SPC)]
         korder = jnp.arange(GROUPS, dtype=jnp.int32)
-        both = jnp.concatenate([right_keep, right_send])
+        after = []
+        both = jnp.concatenate([right_keep, right_send, right_up])
         vecs = jnp.take(both[::16, HALF : HALF + VPER].reshape(ndev, vec_len), table, axis=0)
         vec_sum = route.scatter(vecs[: route.n], vecs[route.n :]).reshape(vec_len)
         rights = jnp.take(both[:, :HALF].reshape(ndev, in_rows, HALF), table, axis=0).reshape(D, HALF)
@@ -1151,10 +1224,14 @@
 
     mixed = whole_images(mixed_stay, mixed_got)
     patches_grad = whole_images(grad_stay, route.cross(grad_away))
+    spat_new = spatial_update(
+        korder, spat_pieces, spatial, spat_first, spat_second, spatial_bias, bias_first, bias_second, after
+    )
+    if fits:
+        *new_in, vec_sum = finish_in(right_own, right_got, left_sum, dense_in, in_first, in_second, spat_new[0])
+        vec_sum = vec_sum[0, :vec_len]
     new_vec = adamw(vectors, vec_sum, vec_first, vec_second, SMALL_RATE, 0.0)
-    spat_new = spatial_update(korder, spat_pieces, spatial, spat_first, spat_second)
-    new_bias = adamw(spatial_bias, spat_new[3].reshape(3, rows), bias_first, bias_second, SMALL_RATE, 0.0)
-    return (mixed, patches_grad) + tuple(new_in) + tuple(new_out) + new_vec + tuple(spat_new[:3]) + new_bias
+    return (mixed, patches_grad) + tuple(new_in) + tuple(new_out) + new_vec + tuple(spat_new)
 
 
 def solution(mesh):

time: 161 us -> 151 us (0.938)
  waiting for transfers between devices: 44.2 us -> 37.2 us
  other arithmetic: 6.82 us -> 1.02 us
  Pallas kernels: 54.3 us -> 57.9 us
  local copies, waits for them, and re-layouts: 10.9 us -> 7.66 us
  starting transfers between devices: 43.7 us -> 45.7 us
    ppermute x30, waiting for transfers between devices: 43 us -> 32.4 us  [swap(): return lax.ppermute(block, AXES, pairs)]
    pallas_call x13 -> x17, Pallas kernels: 50.5 us -> 56.9 us  [call(): pl.pallas_call(kernel, out_shape=out_shape, in_specs=in_specs, out_specs=...]
    ppermute x16 -> x17, waiting for transfers between devices: 1.15 us -> 4.79 us  [cross(): return lax.ppermute(block, AXES, pairs)]
    convert_element_type x6 -> x0, other arithmetic: 3.38 us -> none  [next_term(): total = total.astype(BF)]
    unnamed x77 -> x54, local copies, waits for them, and re-layouts: 10.6 us -> 7.43 us
    ppermute x30, starting transfers between devices: 39.6 us -> 41.6 us  [swap(): return lax.ppermute(block, AXES, pairs)]
    pallas_call x1 -> x6, Pallas kernels: 2.48 us -> 0.6 us  [add_part(): pl.pallas_call(kernel, grid=(1,), out_shape=sds((size, cols), BF), in_spe...]
    ppermute x16 -> x17, starting transfers between devices: 4.17 us -> 4.04 us  [cross(): return lax.ppermute(block, AXES, pairs)]
  transfers between devices with their start and end apart: 46 -> 47, of which waited for: 18 -> 13; matrix products, arithmetic and copies ran while one was open for 6% -> 3% of each run, Pallas kernels for 20% -> 23%
where the time goes in v2:
time: 151 us
  Pallas kernels  57.9 us (38%)
  starting transfers between devices  45.7 us (30%)
  waiting for transfers between devices  37.2 us (25%)
  local copies, waits for them, and re-layouts  7.66 us (5%)
    pallas_call x17, Pallas kernels, call(): pl.pallas_call(kernel, out_shape=out_shape, in_specs=in_specs, out_specs=...  56.9 us
    ppermute x30, starting transfers between devices, swap(): return lax.ppermute(block, AXES, pairs)  41.6 us
    ppermute x30, waiting for transfers between devices, swap(): return lax.ppermute(block, AXES, pairs)  32.4 us
    unnamed x54, local copies, waits for them, and re-layouts  7.43 us
    ppermute x17, waiting for transfers between devices, cross(): return lax.ppermute(block, AXES, pairs)  4.79 us
    ppermute x17, starting transfers between devices, cross(): return lax.ppermute(block, AXES, pairs)  4.04 us
  transfers between devices with their start and end apart: 47, of which 13 were waited for; matrix products, arithmetic and copies ran while one was open for 3% of the time, Pallas kernels for 23%

profile of v2, /device:TPU:0, one launch (start us, length us, event | category | flops | bytes accessed | tf_op | source)
XLA Modules:
  0.0 150.6 jit_solution(14620939011405223711)
XLA Ops:
  3.6 3.1 %collective-permute-start.5 = (bf16[16,3072]{1,0:T(8,128)(2,1)S(1)}, bf16[16,3072]{1,0:T(8,128)(2,1)S(1)}, u32[]{:S(2)}, u32[]{:S(2)}) collective-permute-start(bf16[16,3072]{1,0:T(8,128)(2,1)S(1)} %get-tuple-element.87.refs_0_), channel_id=1, source_target_pairs={{0,8},{1,9},{2,10},{3,11},{4,12},{5,13},{6,14},{7,15},{8,0},{9,1},... | collective-permute-start | bytes 294920 | tf_op jit(solution)/shard_map/ppermute | solution.py:64
  6.7 2.5 %collective-permute-start.4 = (bf16[16,1792]{1,0:T(8,128)(2,1)S(1)}, bf16[16,1792]{1,0:T(8,128)(2,1)S(1)}, u32[]{:S(2)}, u32[]{:S(2)}) collective-permute-start(bf16[16,1792]{1,0:T(8,128)(2,1)S(1)} %get-tuple-element.86.refs_0_), channel_id=1, source_target_pairs={{0,24},{1,25},{2,26},{3,27},{4,28},{5,29},{6,30},{7,31},{8,16},{9,... | collective-permute-start | bytes 172040 | tf_op jit(solution)/shard_map/ppermute | solution.py:64
  9.3 1.8 %collective-permute-start.2 = (bf16[16,1792]{1,0:T(8,128)(2,1)S(1)}, bf16[16,1792]{1,0:T(8,128)(2,1)S(1)}, u32[]{:S(2)}, u32[]{:S(2)}) collective-permute-start(bf16[16,1792]{1,0:T(8,128)(2,1)S(1)} %get-tuple-element.86.refs_0_), channel_id=1, source_target_pairs={{0,8},{1,9},{2,10},{3,11},{4,12},{5,13},{6,14},{7,15},{8,0},{9,1},... | collective-permute-start | bytes 172040 | tf_op jit(solution)/shard_map/ppermute | solution.py:64
  11.1 2.7 %collective-permute-done.4.refs_3_ = bf16[16,1792]{1,0:T(8,128)(2,1)S(1)} collective-permute-done((bf16[16,1792]{1,0:T(8,128)(2,1)S(1)}, bf16[16,1792]{1,0:T(8,128)(2,1)S(1)}, u32[]{:S(2)}, u32[]{:S(2)}) %collective-permute-start.4) | collective-permute-done | bytes 57376 | tf_op jit(solution)/shard_map/ppermute | solution.py:64
  15.0 1.6 %collective-permute-start.7 = (bf16[64,1792]{1,0:T(8,128)(2,1)S(1)}, bf16[64,1792]{1,0:T(8,128)(2,1)}, u32[]{:S(2)}, u32[]{:S(2)}) collective-permute-start(bf16[64,1792]{1,0:T(8,128)(2,1)S(1)} %shard_map.361.refs_0_), channel_id=1, source_target_pairs={{0,2},{1,5},{2,0},{3,7},{4,6},{5,1},{6,4},{7,3},{8,10},{9,13},{10,... | collective-permute-start | bytes 688136 | tf_op jit(solution)/shard_map/ppermute | solution.py:64
  16.6 1.5 %collective-permute-start.6 = (bf16[64,1792]{1,0:T(8,128)(2,1)S(1)}, bf16[64,1792]{1,0:T(8,128)(2,1)}, u32[]{:S(2)}, u32[]{:S(2)}) collective-permute-start(bf16[64,1792]{1,0:T(8,128)(2,1)S(1)} %shard_map.361.refs_0_), channel_id=1, source_target_pairs={{0,4},{1,3},{2,6},{3,1},{4,0},{5,7},{6,2},{7,5},{8,12},{9,11},{10,... | collective-permute-start | bytes 688136 | tf_op jit(solution)/shard_map/ppermute | solution.py:64
  18.1 4.8 %collective-permute-done.7.refs_1_.refs_2_ = bf16[64,1792]{1,0:T(8,128)(2,1)} collective-permute-done((bf16[64,1792]{1,0:T(8,128)(2,1)S(1)}, bf16[64,1792]{1,0:T(8,128)(2,1)}, u32[]{:S(2)}, u32[]{:S(2)}) %collective-permute-start.7) | collective-permute-done | bytes 229408 | tf_op jit(solution)/shard_map/ppermute | solution.py:64
  23.8 1.6 %collective-permute-start.8 = (bf16[64,1792]{1,0:T(8,128)(2,1)S(1)}, bf16[64,1792]{1,0:T(8,128)(2,1)}, u32[]{:S(2)}, u32[]{:S(2)}) collective-permute-start(bf16[64,1792]{1,0:T(8,128)(2,1)S(1)} %shard_map.362), channel_id=1, source_target_pairs={{0,2},{1,5},{2,0},{3,7},{4,6},{5,1},{6,4},{7,3},{8,10},{9,13},{10,... | collective-permute-start | bytes 688136 | tf_op jit(solution)/shard_map/ppermute | solution.py:64
  25.4 2.7 %collective-permute-start.15 = (bf16[16,3072]{1,0:T(8,128)(2,1)S(1)}, bf16[16,3072]{1,0:T(8,128)(2,1)S(1)}, u32[]{:S(2)}, u32[]{:S(2)}) collective-permute-start(bf16[16,3072]{1,0:T(8,128)(2,1)S(1)} %get-tuple-element.87.refs_0_), channel_id=1, source_target_pairs={{0,24},{1,25},{2,26},{3,27},{4,28},{5,29},{6,30},{7,31},{8,16},{9,... | collective-permute-start | bytes 294920 | tf_op jit(solution)/shard_map/ppermute | solution.py:64
  28.1 3.8 %collective-permute-done.15.refs_3_ = bf16[16,3072]{1,0:T(8,128)(2,1)S(1)} collective-permute-done((bf16[16,3072]{1,0:T(8,128)(2,1)S(1)}, bf16[16,3072]{1,0:T(8,128)(2,1)S(1)}, u32[]{:S(2)}, u32[]{:S(2)}) %collective-permute-start.15) | collective-permute-done | bytes 98336 | tf_op jit(solution)/shard_map/ppermute | solution.py:64
  31.9 3.2 %collective-permute-done.14.refs_2_ = bf16[16,3072]{1,0:T(8,128)(2,1)S(1)} collective-permute-done((bf16[16,3072]{1,0:T(8,128)(2,1)S(1)}, bf16[16,3072]{1,0:T(8,128)(2,1)S(1)}, u32[]{:S(2)}, u32[]{:S(2)}) %collective-permute-start.14) | collective-permute-done | bytes 98336 | tf_op jit(solution)/shard_map/ppermute | solution.py:64
  39.9 1.5 %shard_map.359 = (bf16[3,162,384]{2,1,0:T(8,128)(2,1)S(1)}, bf16[2,162,512]{2,1,0:T(8,128)(2,1)}, bf16[2,162,512]{2,1,0:T(8,128)(2,1)}) custom-call(s32[33]{0:T(128)S(1)} %pad_add_fusion.1.sides_ref, f32[3,162,324]{2,1,0:T(8,128)S(1)} %copy-done, f32[3,162,1]{2,1,0:T(8,128)S(1)} %copy.47.b_ref, bf16[4,162,512]{2,1,0:T(8,128)(2,1)S(1)} %copy.50.x_ref.p_ref, ...), custom_call_target="tpu_custom_call" | custom-call | flops 1000 | bytes 3000000 | tf_op jit(solution)/shard_map/pallas_call | solution.py:212
  42.5 4.3 %collective-permute-done.17.refs_1_.refs_2_ = bf16[64,3072]{1,0:T(8,128)(2,1)S(1)} collective-permute-done((bf16[64,3072]{1,0:T(8,128)(2,1)S(1)}, bf16[64,3072]{1,0:T(8,128)(2,1)S(1)}, u32[]{:S(2)}, u32[]{:S(2)}) %collective-permute-start.17) | collective-permute-done | bytes 393248 | tf_op jit(solution)/shard_map/ppermute | solution.py:64
  50.5 10.7 %shard_map.363 = (bf16[672,512]{1,0:T(8,128)(2,1)S(1)}, bf16[672,512]{1,0:T(8,128)(2,1)S(1)}, bf16[672,512]{1,0:T(8,128)(2,1)S(1)}, f32[672,1536]{1,0:T(8,128)S(...) custom-call(s32[32]{0:T(128)S(1)} %get-tuple-element.189.table_ref, ...), custom_call_target="tpu_custom_call" | custom-call | flops 10000000000 | bytes 20000000 | tf_op jit(solution)/shard_map/pallas_call | solution.py:212
  61.8 5.1 %shard_map.365 = (bf16[720,1536]{1,0:T(8,128)(2,1)S(1)}, bf16[672,1536]{1,0:T(8,128)(2,1)S(1)}, f32[672,128]{1,0:T(8,128)S(1)}, bf16[672,1536]{1,0:T(8,128)(2,1)S(1)}, bf16[2,336,384]{2,1,0:T(8,128)(2,1)S(1)}) custom-call(s32[2]{0:T(128)S(1)} %dynamic_slice.3.levels_ref, s32[33]{0:T(128)S(1)} %pad_add_fusion.1.sides_ref, ...), custom_call_target="tpu_custom_call" | custom-call | flops 6000000000 | bytes 12000000 | tf_op jit(solution)/shard_map/pallas_call | solution.py:212
  66.9 13.8 %shard_map.367 = (bf16[672,1536]{1,0:T(8,128)(2,1)S(1)}, bf16[672,1536]{1,0:T(8,128)(2,1)S(1)}, bf16[672,1536]{1,0:T(8,128)(2,1)S(1)}, bf16[672,512]{1,0:T(8,128...) custom-call(s32[32]{0:T(128)S(1)} %get-tuple-element.189.table_ref, ...), custom_call_target="tpu_custom_call" | custom-call | flops 8000000000 | bytes 16000000 | tf_op jit(solution)/shard_map/pallas_call | solution.py:212
  80.7 7.7 %shard_map.368 = (bf16[256,3072]{1,0:T(8,128)(2,1)S(1)}, bf16[256,3072]{1,0:T(8,128)(2,1)S(1)}, bf16[2,162,512]{2,1,0:T(8,128)(2,1)S(1)}, bf16[2,162,512]{2,1,0:T(8,128)(2,1)S(1)}, f32[672,512]{1,0:T(8,128)S(1)}) custom-call(s32[32]{0:T(128)S(1)} %get-tuple-element.189.table_ref, s32[2]{0:T(128)S(1)} %dynamic_slice.3.levels_ref, ...), custom_call_target="tpu_custom_call" | custom-call | flops 5000000000 | bytes 15000000 | tf_op jit(solution)/shard_map/pallas_call | solution.py:212
  89.0 3.5 %collective-permute-done.24.refs_1_ = bf16[256,768]{1,0:T(8,128)(2,1)S(1)} collective-permute-done((bf16[256,768]{1,0:T(8,128)(2,1)S(1)}, bf16[256,768]{1,0:T(8,128)(2,1)S(1)}, u32[]{:S(2)}, u32[]{:S(2)}) %collective-permute-start.24) | collective-permute-done | bytes 393248 | tf_op jit(solution)/shard_map/ppermute | solution.py:71
  93.2 5.6 %shard_map.370 = (bf16[672,1536]{1,0:T(8,128)(2,1)S(1)}, f32[1,4608]{1,0:T(1,128)S(1)}) custom-call(f32[1,7680]{1,0:T(1,128)S(1)} %get-tuple-element.88.vec_ref, bf16[672,1536]{1,0:T(8,128)(2,1)S(1)} %get-tuple-element.105.gs_ref, bf16[2,336,384]{2,1,0:T(8,128)(2,1)S(1)} %get-tuple-element.106.mm_ref, bf16[672,1536]{1,0:T(8,128)(2,1)S(1)} %get-tuple-element.107.hat_ref, ...), custom_call_target="tpu_custom_call" | custom-call | flops 3000000000 | bytes 10000000 | tf_op jit(solution)/shard_map/pallas_call | solution.py:212
  99.0 1.6 %collective-permute-start.32 = (bf16[128,3072]{1,0:T(8,128)(2,1)S(1)}, bf16[128,3072]{1,0:T(8,128)(2,1)S(1)}, u32[]{:S(2)}, u32[]{:S(2)}) collective-permute-start(bf16[128,3072]{1,0:T(8,128)(2,1)S(1)} %shard_map.371.refs_3_), channel_id=1, source_target_pairs={{0,2},{1,5},{2,0},{3,7},{4,6},{5,1},{6,4},{7,3},{8,10},{9,13},{10,... | collective-permute-start | bytes 2359304 | tf_op jit(solution)/shard_map/ppermute | solution.py:64
  101.1 2.7 %shard_map.373 = (bf16[512,1536]{1,0:T(8,128)(2,1)S(1)}, f32[672,512]{1,0:T(8,128)S(1)}) custom-call(bf16[672,1536]{1,0:T(8,128)(2,1)S(1)} %get-tuple-element.113.gp_ref, bf16[672,512]{1,0:T(8,128)(2,1)S(1)} %get-tuple-element.89.h_ref, bf16[512,1536]{1,0:T(8,128)(2,1)S(1)} %get-tuple-element.114.w_ref, f32[672,512]{1,0:T(8,128)S(1)} %get-tuple-element.115.gh_ref, ...), custom_call_target="tpu_custom_call" | custom-call | flops 3000000000 | bytes 8000000 | tf_op jit(solution)/shard_map/pallas_call | solution.py:212
  103.8 2.7 %collective-permute-done.27.refs_0_.refs_3_ = bf16[64,768]{1,0:T(8,128)(2,1)S(1)} collective-permute-done((bf16[64,768]{1,0:T(8,128)(2,1)S(1)}, bf16[64,768]{1,0:T(8,128)(2,1)S(1)}, u32[]{:S(2)}, u32[]{:S(2)}) %collective-permute-start.27) | collective-permute-done | bytes 98336 | tf_op jit(solution)/shard_map/ppermute | solution.py:64
  106.4 2.8 %shard_map.374 = (bf16[256,1792]{1,0:T(8,128)(2,1)S(1)}, bf16[128,1792]{1,0:T(8,128)(2,1)S(1)}, bf16[128,1792]{1,0:T(8,128)(2,1)S(1)}, bf16[2,162,512]{2,1,0:T(8,128)(2,1)S(1)}, bf16[2,162,512]{2,1,0:T(8,128)(2,1)S(1)}) custom-call(s32[32]{0:T(128)S(1)} %get-tuple-element.189.table_ref, s32[33]{0:T(128)S(1)} %pad_add_fusion.1.sides_ref, ...), custom_call_target="tpu_custom_call" | custom-call | flops 2000000000 | bytes 6000000 | tf_op jit(solution)/shard_map/pallas_call | solution.py:212
  113.5 3.0 %collective-permute-start.36 = (bf16[64,768]{1,0:T(8,128)(2,1)S(1)}, bf16[64,768]{1,0:T(8,128)(2,1)S(1)}, u32[]{:S(2)}, u32[]{:S(2)}) collective-permute-start(bf16[64,768]{1,0:T(8,128)(2,1)S(1)} %get-tuple-element.127), channel_id=1, source_target_pairs={{0,16},{1,17},{2,18},{3,19},{4,20},{5,21},{6,22},{7,23},{8,24},{9,... | collective-permute-start | bytes 294920 | tf_op jit(solution)/shard_map/ppermute | solution.py:64
  116.5 7.0 %collective-permute-done.31.refs_2_ = bf16[128,1792]{1,0:T(8,128)(2,1)S(1)} collective-permute-done((bf16[128,1792]{1,0:T(8,128)(2,1)S(1)}, bf16[128,1792]{1,0:T(8,128)(2,1)S(1)}, u32[]{:S(2)}, u32[]{:S(2)}) %collective-permute-start.31) | collective-permute-done | bytes 458784 | tf_op jit(solution)/shard_map/ppermute | solution.py:64
  123.5 2.6 %collective-permute-start.37 = (bf16[64,768]{1,0:T(8,128)(2,1)S(1)}, bf16[64,768]{1,0:T(8,128)(2,1)S(1)}, u32[]{:S(2)}, u32[]{:S(2)}) collective-permute-start(bf16[64,768]{1,0:T(8,128)(2,1)S(1)} %get-tuple-element.128), channel_id=1, source_target_pairs={{0,24},{1,25},{2,26},{3,27},{4,28},{5,29},{6,30},{7,31},{8,16},{9,... | collective-permute-start | bytes 294920 | tf_op jit(solution)/shard_map/ppermute | solution.py:64
  128.3 1.6 %collective-permute-done.37.c_ref = bf16[64,768]{1,0:T(8,128)(2,1)S(1)} collective-permute-done((bf16[64,768]{1,0:T(8,128)(2,1)S(1)}, bf16[64,768]{1,0:T(8,128)(2,1)S(1)}, u32[]{:S(2)}, u32[]{:S(2)}) %collective-permute-start.37) | collective-permute-done | bytes 98336 | tf_op jit(solution)/shard_map/ppermute | solution.py:64
  131.0 3.2 %collective-permute-start.42 = (bf16[16,3072]{1,0:T(8,128)(2,1)S(1)}, bf16[16,3072]{1,0:T(8,128)(2,1)S(1)}, u32[]{:S(2)}, u32[]{:S(2)}) collective-permute-start(bf16[16,3072]{1,0:T(8,128)(2,1)S(1)} %get-tuple-element.135), channel_id=1, source_target_pairs={{0,16},{1,17},{2,18},{3,19},{4,20},{5,21},{6,22},{7,23},{8,24},{9,... | collective-permute-start | bytes 294920 | tf_op jit(solution)/shard_map/ppermute | solution.py:64
  135.4 1.6 %collective-permute-start.45 = (bf16[64,768]{1,0:T(8,128)(2,1)S(1)}, bf16[64,768]{1,0:T(8,128)(2,1)S(1)}, u32[]{:S(2)}, u32[]{:S(2)}) collective-permute-start(bf16[64,768]{1,0:T(8,128)(2,1)S(1)} %shard_map.379.refs_4_.refs_0_), channel_id=1, source_target_pairs={{0,2},{1,5},{2,0},{3,7},{4,6},{5,1},{6,4},{7,3},{8,10},{9,13},{10,... | collective-permute-start | bytes 294920 | tf_op jit(solution)/shard_map/ppermute | solution.py:64
  138.5 2.5 %collective-permute-start.39 = (bf16[16,1792]{1,0:T(8,128)(2,1)S(1)}, bf16[16,1792]{1,0:T(8,128)(2,1)S(1)}, u32[]{:S(2)}, u32[]{:S(2)}) collective-permute-start(bf16[16,1792]{1,0:T(8,128)(2,1)S(1)} %get-tuple-element.132), channel_id=1, source_target_pairs={{0,16},{1,17},{2,18},{3,19},{4,20},{5,21},{6,22},{7,23},{8,24},{9,... | collective-permute-start | bytes 172040 | tf_op jit(solution)/shard_map/ppermute | solution.py:64
  141.1 1.9 %collective-permute-start.40 = (bf16[16,1792]{1,0:T(8,128)(2,1)S(1)}, bf16[16,1792]{1,0:T(8,128)(2,1)S(1)}, u32[]{:S(2)}, u32[]{:S(2)}) collective-permute-start(bf16[16,1792]{1,0:T(8,128)(2,1)S(1)} %get-tuple-element.133), channel_id=1, source_target_pairs={{0,24},{1,25},{2,26},{3,27},{4,28},{5,29},{6,30},{7,31},{8,16},{9,... | collective-permute-start | bytes 172040 | tf_op jit(solution)/shard_map/ppermute | solution.py:64
  145.1 2.8 %shard_map.383 = (f32[3,162,324]{2,1,0:T(8,128)}, f32[3,162,324]{2,1,0:T(8,128)}, f32[3,162,324]{2,1,0:T(8,128)}, f32[3,162]{1,0:T(4,128)}, f32[3,162]{1,0:T(4,128)}, /*index=5*/f32[3,162]{1,0:T(4,128)}) custom-call(s32[16]{0:T(128)S(1)} %get-tuple-element.191.order_ref, bf16[64,768]{1,0:T(8,128)(2,1)S(1)} %shard_map.379.refs_4_.refs_0_, ...), custom_call_target="tpu_custom_call" | custom-call | flops 10000000 | bytes 6000000 | tf_op jit(solution)/shard_map/pallas_call | solution.py:212
  (152 shorter events, 32.1 us)
Async XLA Ops:
  3.6 11.4 %collective-permute-start.5 = (bf16[16,3072]{1,0:T(8,128)(2,1)S(1)}, bf16[16,3072]{1,0:T(8,128)(2,1)S(1)}, u32[]{:S(2)}, u32[]{:S(2)}) collective-permute-start(bf16[16,3072]{1,0:T(8,128)(2,1)S(1)} %get-tuple-element.87.refs_0_), channel_id=1, source_target_pairs={{0,8},{1,9},{2,10},{3,11},{4,12},{5,13},{6,14},{7,15},{8,0},{9,1},... | collective-permute-start | bytes 294920 | tf_op jit(solution)/shard_map/ppermute | solution.py:64
  6.7 7.1 %collective-permute-start.4 = (bf16[16,1792]{1,0:T(8,128)(2,1)S(1)}, bf16[16,1792]{1,0:T(8,128)(2,1)S(1)}, u32[]{:S(2)}, u32[]{:S(2)}) collective-permute-start(bf16[16,1792]{1,0:T(8,128)(2,1)S(1)} %get-tuple-element.86.refs_0_), channel_id=1, source_target_pairs={{0,24},{1,25},{2,26},{3,27},{4,28},{5,29},{6,30},{7,31},{8,16},{9,... | collective-permute-start | bytes 172040 | tf_op jit(solution)/shard_map/ppermute | solution.py:64
  15.0 7.8 %collective-permute-start.7 = (bf16[64,1792]{1,0:T(8,128)(2,1)S(1)}, bf16[64,1792]{1,0:T(8,128)(2,1)}, u32[]{:S(2)}, u32[]{:S(2)}) collective-permute-start(bf16[64,1792]{1,0:T(8,128)(2,1)S(1)} %shard_map.361.refs_0_), channel_id=1, source_target_pairs={{0,2},{1,5},{2,0},{3,7},{4,6},{5,1},{6,4},{7,3},{8,10},{9,13},{10,... | collective-permute-start | bytes 688136 | tf_op jit(solution)/shard_map/ppermute | solution.py:64
  23.8 11.2 %collective-permute-start.8 = (bf16[64,1792]{1,0:T(8,128)(2,1)S(1)}, bf16[64,1792]{1,0:T(8,128)(2,1)}, u32[]{:S(2)}, u32[]{:S(2)}) collective-permute-start(bf16[64,1792]{1,0:T(8,128)(2,1)S(1)} %shard_map.362), channel_id=1, source_target_pairs={{0,2},{1,5},{2,0},{3,7},{4,6},{5,1},{6,4},{7,3},{8,10},{9,13},{10,... | collective-permute-start | bytes 688136 | tf_op jit(solution)/shard_map/ppermute | solution.py:64
  25.4 6.5 %collective-permute-start.15 = (bf16[16,3072]{1,0:T(8,128)(2,1)S(1)}, bf16[16,3072]{1,0:T(8,128)(2,1)S(1)}, u32[]{:S(2)}, u32[]{:S(2)}) collective-permute-start(bf16[16,3072]{1,0:T(8,128)(2,1)S(1)} %get-tuple-element.87.refs_0_), channel_id=1, source_target_pairs={{0,24},{1,25},{2,26},{3,27},{4,28},{5,29},{6,30},{7,31},{8,16},{9,... | collective-permute-start | bytes 294920 | tf_op jit(solution)/shard_map/ppermute | solution.py:64
  28.1 7.0 %collective-permute-start.14 = (bf16[16,3072]{1,0:T(8,128)(2,1)S(1)}, bf16[16,3072]{1,0:T(8,128)(2,1)S(1)}, u32[]{:S(2)}, u32[]{:S(2)}) collective-permute-start(bf16[16,3072]{1,0:T(8,128)(2,1)S(1)} %get-tuple-element.87.refs_0_), channel_id=1, source_target_pairs={{0,16},{1,17},{2,18},{3,19},{4,20},{5,21},{6,22},{7,23},{8,24},{9,... | collective-permute-start | bytes 294920 | tf_op jit(solution)/shard_map/ppermute | solution.py:64
  35.1 11.6 %collective-permute-start.17 = (bf16[64,3072]{1,0:T(8,128)(2,1)S(1)}, bf16[64,3072]{1,0:T(8,128)(2,1)S(1)}, u32[]{:S(2)}, u32[]{:S(2)}) collective-permute-start(bf16[64,3072]{1,0:T(8,128)(2,1)S(1)} %shard_map.364.refs_0_), channel_id=1, source_target_pairs={{0,2},{1,5},{2,0},{3,7},{4,6},{5,1},{6,4},{7,3},{8,10},{9,13},{10,... | collective-permute-start | bytes 1179656 | tf_op jit(solution)/shard_map/ppermute | solution.py:64
  36.6 10.2 %collective-permute-start.16 = (bf16[64,3072]{1,0:T(8,128)(2,1)S(1)}, bf16[64,3072]{1,0:T(8,128)(2,1)}, u32[]{:S(2)}, u32[]{:S(2)}) collective-permute-start(bf16[64,3072]{1,0:T(8,128)(2,1)S(1)} %shard_map.364.refs_0_), channel_id=1, source_target_pairs={{0,4},{1,3},{2,6},{3,1},{4,0},{5,7},{6,2},{7,5},{8,12},{9,11},{10,... | collective-permute-start | bytes 1179656 | tf_op jit(solution)/shard_map/ppermute | solution.py:64
  41.4 6.9 %collective-permute-start = (bf16[2,162,512]{2,1,0:T(8,128)(2,1)}, bf16[2,162,512]{2,1,0:T(8,128)(2,1)}, u32[]{:S(2)}, u32[]{:S(2)}) collective-permute-start(bf16[2,162,512]{2,1,0:T(8,128)(2,1)} %get-tuple-element.84), channel_id=1, source_target_pairs={{0,1},{1,0},{2,3},{3,2},{4,5},{5,4},{6,7},{7,6},{8,9},{9,8},{10,11... | collective-permute-start | bytes 995336 | tf_op jit(solution)/shard_map/ppermute | solution.py:71
  41.9 6.6 %collective-permute-start.1 = (bf16[2,162,512]{2,1,0:T(8,128)(2,1)}, bf16[2,162,512]{2,1,0:T(8,128)(2,1)}, u32[]{:S(2)}, u32[]{:S(2)}) collective-permute-start(bf16[2,162,512]{2,1,0:T(8,128)(2,1)} %get-tuple-element.85), channel_id=1, source_target_pairs={{0,1},{1,0},{2,3},{3,2},{4,5},{5,4},{6,7},{7,6},{8,9},{9,8},{10,11... | collective-permute-start | bytes 995336 | tf_op jit(solution)/shard_map/ppermute | solution.py:71
  42.0 7.0 %collective-permute-start.11 = (bf16[64,1792]{1,0:T(8,128)(2,1)}, bf16[64,1792]{1,0:T(8,128)(2,1)S(1)}, u32[]{:S(2)}, u32[]{:S(2)}) collective-permute-start(bf16[64,1792]{1,0:T(8,128)(2,1)} %collective-permute-done.7.refs_1_.refs_2_), channel_id=1, source_target_pairs={{0,1},{1,0},{2,3},{3,2},{4,5},{5,4},{6,7},{7,6},{8,9},{9,8},{10,11... | collective-permute-start | bytes 688136 | tf_op jit(solution)/shard_map/ppermute | solution.py:71
  48.4 13.4 %collective-permute-start.13 = (bf16[3,162,384]{2,1,0:T(8,128)(2,1)}, bf16[3,162,384]{2,1,0:T(8,128)(2,1)S(1)}, u32[]{:S(2)}, u32[]{:S(2)}) collective-permute-start(bf16[3,162,384]{2,1,0:T(8,128)(2,1)} %copy-done.17), channel_id=1, source_target_pairs={{0,1},{1,0},{2,3},{3,2},{4,5},{5,4},{6,7},{7,6},{8,9},{9,8},{10,11... | collective-permute-start | bytes 1119752 | tf_op jit(solution)/shard_map/ppermute | solution.py:71
  48.5 18.4 %collective-permute-start.19 = (bf16[64,3072]{1,0:T(8,128)(2,1)S(1)}, bf16[64,3072]{1,0:T(8,128)(2,1)S(1)}, u32[]{:S(2)}, u32[]{:S(2)}) collective-permute-start(bf16[64,3072]{1,0:T(8,128)(2,1)S(1)} %shard_map.364.refs_0_), channel_id=1, source_target_pairs={{0,1},{1,0},{2,3},{3,2},{4,5},{5,4},{6,7},{7,6},{8,9},{9,8},{10,11... | collective-permute-start | bytes 1179656 | tf_op jit(solution)/shard_map/ppermute | solution.py:71
  48.9 12.8 %collective-permute-start.18 = (bf16[64,3072]{1,0:T(8,128)(2,1)S(1)}, bf16[64,3072]{1,0:T(8,128)(2,1)S(1)}, u32[]{:S(2)}, u32[]{:S(2)}) collective-permute-start(bf16[64,3072]{1,0:T(8,128)(2,1)S(1)} %shard_map.366), channel_id=1, source_target_pairs={{0,2},{1,5},{2,0},{3,7},{4,6},{5,1},{6,4},{7,3},{8,10},{9,13},{10,... | collective-permute-start | bytes 1179656 | tf_op jit(solution)/shard_map/ppermute | solution.py:64
  88.4 10.4 %collective-permute-start.26 = (bf16[256,3072]{1,0:T(8,128)(2,1)S(1)}, bf16[256,3072]{1,0:T(8,128)(2,1)S(1)}, u32[]{:S(2)}, u32[]{:S(2)}) collective-permute-start(bf16[256,3072]{1,0:T(8,128)(2,1)S(1)} %get-tuple-element.117), channel_id=1, source_target_pairs={{0,1},{1,0},{2,3},{3,2},{4,5},{5,4},{6,7},{7,6},{8,9},{9,8},{10,11... | collective-permute-start | bytes 4718600 | tf_op jit(solution)/shard_map/ppermute | solution.py:71
  92.6 8.0 %collective-permute-start.25 = (bf16[128,768]{1,0:T(8,128)(2,1)S(1)}, bf16[128,768]{1,0:T(8,128)(2,1)S(1)}, u32[]{:S(2)}, u32[]{:S(2)}) collective-permute-start(bf16[128,768]{1,0:T(8,128)(2,1)S(1)} %shard_map.369.refs_0_), channel_id=1, source_target_pairs={{0,2},{1,5},{2,0},{3,7},{4,6},{5,1},{6,4},{7,3},{8,10},{9,13},{10,... | collective-permute-start | bytes 589832 | tf_op jit(solution)/shard_map/ppermute | solution.py:64
  99.0 13.1 %collective-permute-start.32 = (bf16[128,3072]{1,0:T(8,128)(2,1)S(1)}, bf16[128,3072]{1,0:T(8,128)(2,1)S(1)}, u32[]{:S(2)}, u32[]{:S(2)}) collective-permute-start(bf16[128,3072]{1,0:T(8,128)(2,1)S(1)} %shard_map.371.refs_3_), channel_id=1, source_target_pairs={{0,2},{1,5},{2,0},{3,7},{4,6},{5,1},{6,4},{7,3},{8,10},{9,13},{10,... | collective-permute-start | bytes 2359304 | tf_op jit(solution)/shard_map/ppermute | solution.py:64
  111.2 12.3 %collective-permute-start.31 = (bf16[128,1792]{1,0:T(8,128)(2,1)S(1)}, bf16[128,1792]{1,0:T(8,128)(2,1)S(1)}, u32[]{:S(2)}, u32[]{:S(2)}) collective-permute-start(bf16[128,1792]{1,0:T(8,128)(2,1)S(1)} %shard_map.375.refs_4_), channel_id=1, source_target_pairs={{0,2},{1,5},{2,0},{3,7},{4,6},{5,1},{6,4},{7,3},{8,10},{9,13},{10,... | collective-permute-start | bytes 1376264 | tf_op jit(solution)/shard_map/ppermute | solution.py:64
  112.3 18.4 %collective-permute-start.34 = (bf16[64,3072]{1,0:T(8,128)(2,1)S(1)}, bf16[64,3072]{1,0:T(8,128)(2,1)S(1)}, u32[]{:S(2)}, u32[]{:S(2)}) collective-permute-start(bf16[64,3072]{1,0:T(8,128)(2,1)S(1)} %shard_map.377.refs_3_), channel_id=1, source_target_pairs={{0,4},{1,3},{2,6},{3,1},{4,0},{5,7},{6,2},{7,5},{8,12},{9,11},{10,... | collective-permute-start | bytes 1179656 | tf_op jit(solution)/shard_map/ppermute | solution.py:64
  113.3 20.9 %collective-permute-start.28 = (bf16[2,162,512]{2,1,0:T(8,128)(2,1)S(1)}, bf16[2,162,512]{2,1,0:T(8,128)(2,1)S(1)}, u32[]{:S(2)}, u32[]{:S(2)}) collective-permute-start(bf16[2,162,512]{2,1,0:T(8,128)(2,1)S(1)} %get-tuple-element.121), channel_id=1, source_target_pairs={{0,1},{1,0},{2,3},{3,2},{4,5},{5,4},{6,7},{7,6},{8,9},{9,8},{10,11... | collective-permute-start | bytes 995336 | tf_op jit(solution)/shard_map/ppermute | solution.py:71
  113.4 14.0 %collective-permute-start.35 = (bf16[64,768]{1,0:T(8,128)(2,1)S(1)}, bf16[64,768]{1,0:T(8,128)(2,1)S(1)}, u32[]{:S(2)}, u32[]{:S(2)}) collective-permute-start(bf16[64,768]{1,0:T(8,128)(2,1)S(1)} %get-tuple-element.126), channel_id=1, source_target_pairs={{0,8},{1,9},{2,10},{3,11},{4,12},{5,13},{6,14},{7,15},{8,0},{9,1},... | collective-permute-start | bytes 294920 | tf_op jit(solution)/shard_map/ppermute | solution.py:64
  113.5 14.8 %collective-permute-start.36 = (bf16[64,768]{1,0:T(8,128)(2,1)S(1)}, bf16[64,768]{1,0:T(8,128)(2,1)S(1)}, u32[]{:S(2)}, u32[]{:S(2)}) collective-permute-start(bf16[64,768]{1,0:T(8,128)(2,1)S(1)} %get-tuple-element.127), channel_id=1, source_target_pairs={{0,16},{1,17},{2,18},{3,19},{4,20},{5,21},{6,22},{7,23},{8,24},{9,... | collective-permute-start | bytes 294920 | tf_op jit(solution)/shard_map/ppermute | solution.py:64
  123.5 6.4 %collective-permute-start.37 = (bf16[64,768]{1,0:T(8,128)(2,1)S(1)}, bf16[64,768]{1,0:T(8,128)(2,1)S(1)}, u32[]{:S(2)}, u32[]{:S(2)}) collective-permute-start(bf16[64,768]{1,0:T(8,128)(2,1)S(1)} %get-tuple-element.128), channel_id=1, source_target_pairs={{0,24},{1,25},{2,26},{3,27},{4,28},{5,29},{6,30},{7,31},{8,16},{9,... | collective-permute-start | bytes 294920 | tf_op jit(solution)/shard_map/ppermute | solution.py:64
  127.4 9.6 %collective-permute-start.33 = (bf16[64,1792]{1,0:T(8,128)(2,1)S(1)}, bf16[64,1792]{1,0:T(8,128)(2,1)S(1)}, u32[]{:S(2)}, u32[]{:S(2)}) collective-permute-start(bf16[64,1792]{1,0:T(8,128)(2,1)S(1)} %shard_map.378.after_ref), channel_id=1, source_target_pairs={{0,4},{1,3},{2,6},{3,1},{4,0},{5,7},{6,2},{7,5},{8,12},{9,11},{10,... | collective-permute-start | bytes 688136 | tf_op jit(solution)/shard_map/ppermute | solution.py:64
  130.9 7.6 %collective-permute-start.41 = (bf16[16,3072]{1,0:T(8,128)(2,1)S(1)}, bf16[16,3072]{1,0:T(8,128)(2,1)S(1)}, u32[]{:S(2)}, u32[]{:S(2)}) collective-permute-start(bf16[16,3072]{1,0:T(8,128)(2,1)S(1)} %get-tuple-element.134), channel_id=1, source_target_pairs={{0,8},{1,9},{2,10},{3,11},{4,12},{5,13},{6,14},{7,15},{8,0},{9,1},... | collective-permute-start | bytes 294920 | tf_op jit(solution)/shard_map/ppermute | solution.py:64
  131.0 7.5 %collective-permute-start.42 = (bf16[16,3072]{1,0:T(8,128)(2,1)S(1)}, bf16[16,3072]{1,0:T(8,128)(2,1)S(1)}, u32[]{:S(2)}, u32[]{:S(2)}) collective-permute-start(bf16[16,3072]{1,0:T(8,128)(2,1)S(1)} %get-tuple-element.135), channel_id=1, source_target_pairs={{0,16},{1,17},{2,18},{3,19},{4,20},{5,21},{6,22},{7,23},{8,24},{9,... | collective-permute-start | bytes 294920 | tf_op jit(solution)/shard_map/ppermute | solution.py:64
  134.2 6.8 %collective-permute-start.43 = (bf16[16,3072]{1,0:T(8,128)(2,1)S(1)}, bf16[16,3072]{1,0:T(8,128)(2,1)S(1)}, u32[]{:S(2)}, u32[]{:S(2)}) collective-permute-start(bf16[16,3072]{1,0:T(8,128)(2,1)S(1)} %get-tuple-element.136), channel_id=1, source_target_pairs={{0,24},{1,25},{2,26},{3,27},{4,28},{5,29},{6,30},{7,31},{8,16},{9,... | collective-permute-start | bytes 294920 | tf_op jit(solution)/shard_map/ppermute | solution.py:64
  135.4 9.6 %collective-permute-start.45 = (bf16[64,768]{1,0:T(8,128)(2,1)S(1)}, bf16[64,768]{1,0:T(8,128)(2,1)S(1)}, u32[]{:S(2)}, u32[]{:S(2)}) collective-permute-start(bf16[64,768]{1,0:T(8,128)(2,1)S(1)} %shard_map.379.refs_4_.refs_0_), channel_id=1, source_target_pairs={{0,2},{1,5},{2,0},{3,7},{4,6},{5,1},{6,4},{7,3},{8,10},{9,13},{10,... | collective-permute-start | bytes 294920 | tf_op jit(solution)/shard_map/ppermute | solution.py:64
  137.0 8.0 %collective-permute-start.46 = (bf16[64,768]{1,0:T(8,128)(2,1)S(1)}, bf16[64,768]{1,0:T(8,128)(2,1)S(1)}, u32[]{:S(2)}, u32[]{:S(2)}) collective-permute-start(bf16[64,768]{1,0:T(8,128)(2,1)S(1)} %collective-permute-done.44.refs_1_), channel_id=1, source_target_pairs={{0,2},{1,5},{2,0},{3,7},{4,6},{5,1},{6,4},{7,3},{8,10},{9,13},{10,... | collective-permute-start | bytes 294920 | tf_op jit(solution)/shard_map/ppermute | solution.py:64
  138.5 9.3 %collective-permute-start.38 = (bf16[16,1792]{1,0:T(8,128)(2,1)S(1)}, bf16[16,1792]{1,0:T(8,128)(2,1)S(1)}, u32[]{:S(2)}, u32[]{:S(2)}) collective-permute-start(bf16[16,1792]{1,0:T(8,128)(2,1)S(1)} %get-tuple-element.131), channel_id=1, source_target_pairs={{0,8},{1,9},{2,10},{3,11},{4,12},{5,13},{6,14},{7,15},{8,0},{9,1},... | collective-permute-start | bytes 172040 | tf_op jit(solution)/shard_map/ppermute | solution.py:64
  138.5 9.3 %collective-permute-start.39 = (bf16[16,1792]{1,0:T(8,128)(2,1)S(1)}, bf16[16,1792]{1,0:T(8,128)(2,1)S(1)}, u32[]{:S(2)}, u32[]{:S(2)}) collective-permute-start(bf16[16,1792]{1,0:T(8,128)(2,1)S(1)} %get-tuple-element.132), channel_id=1, source_target_pairs={{0,16},{1,17},{2,18},{3,19},{4,20},{5,21},{6,22},{7,23},{8,24},{9,... | collective-permute-start | bytes 172040 | tf_op jit(solution)/shard_map/ppermute | solution.py:64
  141.1 6.8 %collective-permute-start.40 = (bf16[16,1792]{1,0:T(8,128)(2,1)S(1)}, bf16[16,1792]{1,0:T(8,128)(2,1)S(1)}, u32[]{:S(2)}, u32[]{:S(2)}) collective-permute-start(bf16[16,1792]{1,0:T(8,128)(2,1)S(1)} %get-tuple-element.133), channel_id=1, source_target_pairs={{0,24},{1,25},{2,26},{3,27},{4,28},{5,29},{6,30},{7,31},{8,16},{9,... | collective-permute-start | bytes 172040 | tf_op jit(solution)/shard_map/ppermute | solution.py:64
  (40 other events, 335.6 us)

commit v3 on v2

--- a/solution.py
+++ b/solution.py
@@ -94,10 +94,9 @@
             blocks = blocks + [self.swap(b, step) for b in blocks]
         return blocks
 
-    def widen_in_turn(self, first):
-        second = self.swap(first, self.low[0])
-        third = self.swap(first, self.low[1])
-        return [first, second, third, self.swap(stack([second], third), self.low[1])]
+    def widen_direct(self, first):
+        one, two = self.low
+        return [first] + [self.swap(first, m) for m in (one, two, (one[0] ^ two[0], one[1] ^ two[1]))]
 
     def gather(self, shard):
         blocks = self.spread(shard)
@@ -267,29 +266,34 @@
     rows = dense_in.shape[0]
     per = vec_row.shape[1]
 
-    def kernel(w_hbm, o_hbm, v_ref, out_ref, lo_ref, w_ref, o_ref, row, sem):
-        first = pltpu.make_async_copy(w_hbm, w_ref, sem.at[0])
-        second = pltpu.make_async_copy(o_hbm, o_ref, sem.at[1])
-        first.start()
-        second.start()
+    def kernel(w_hbm, o_hbm, v_hbm, out_ref, w_ref, o_ref, v_ref, row, sem):
+        copies = [
+            pltpu.make_async_copy(src, dst, sem.at[k])
+            for k, (src, dst) in enumerate(((w_hbm, w_ref), (o_hbm, o_ref), (v_hbm, v_ref)))
+        ]
+        for c in copies:
+            c.start()
         row[...] = jnp.zeros_like(row)
+        for c in copies:
+            c.wait()
+        out_ref[:, 0:HALF] = w_ref[:, HALF:].astype(BF)
         row[0:1, 0:per] = v_ref[...]
-        out_ref[:, HALF:] = row[...].astype(BF)
-        first.wait()
-        out_ref[:, 0:HALF] = w_ref[:, HALF:].astype(BF)
-        lo_ref[:, 0:HALF] = w_ref[:, 0:HALF].astype(BF)
-        second.wait()
+        out_ref[:, HALF : HALF + VCOLS] = row[...].astype(BF)
+        start = HALF + VCOLS
+        out_ref[:, start : start + HALF] = w_ref[:, 0:HALF].astype(BF)
+        start += HALF
         for g in range(3):
-            lo_ref[:, HALF + g * D : HALF + (g + 1) * D] = o_ref[g * rows : (g + 1) * rows, :].astype(BF)
+            out_ref[:, start + g * D : start + (g + 1) * D] = o_ref[g * rows : (g + 1) * rows, :].astype(BF)
 
     scratch = [
         pltpu.VMEM(dense_in.shape, F32),
         pltpu.VMEM(dense_out.shape, F32),
+        pltpu.VMEM(vec_row.shape, F32),
         pltpu.VMEM((rows, VCOLS), F32),
-        pltpu.SemaphoreType.DMA((2,)),
+        pltpu.SemaphoreType.DMA((3,)),
     ]
-    shapes = (sds((rows, HALF + VCOLS), BF), sds((rows, LO), BF))
-    return call(kernel, shapes, [HB, HB, VM], scratch, 1000, 600000, dense_in, dense_out, vec_row)
+    shape = sds((rows, HALF + VCOLS + LO), BF)
+    return call(kernel, shape, [HB] * 3, scratch, 1000, 600000, dense_in, dense_out, vec_row, room=60)
 
 
 def pack_images(sides, spatial, bias_col, patches, out_grad):
@@ -326,15 +330,17 @@
     )
 
 
-def stack(pieces, after):
+def stack(pieces, start, width, after):
     count = len(pieces)
-    rows, cols = pieces[0].shape
+    rows = pieces[0].shape[0]
 
     def kernel(*refs):
+        out = refs[count + len(after)]
         for k in range(count):
-            refs[count + 1][k * rows : (k + 1) * rows, :] = refs[k][...]
-
-    return call(kernel, sds((count * rows, cols), BF), [VM] * count + [HB], [], 1000, 1000000, *pieces, after)
+            out[k * rows : (k + 1) * rows, :] = refs[k][:, start : start + width]
+
+    specs = [VM] * count + [HB] * len(after)
+    return call(kernel, sds((count * rows, width), BF), specs, [], 1000, 1000000, *pieces, *after)
 
 
 def two_halves(is_first, own, got):
@@ -1113,20 +1119,20 @@
     sides = jnp.concatenate([seq[None], korder])
     levels = lax.dynamic_slice_in_dim(resolution, seq * 2, 2, 0)
 
-    right_shard, lo_shard = pack_dense(dense_in, dense_out, vectors.reshape(1, vec_len))
-    line = [route.swap(right_shard, (m, m)) for m in route.direct]
-    lo_line = [route.swap(lo_shard, (m, m)) for m in route.direct]
+    shard = pack_dense(dense_in, dense_out, vectors.reshape(1, vec_len))
+    line = [shard] + [route.swap(shard, (m, m)) for m in route.direct]
     spat_own, x_send, g_send = pack_images(sides, spatial, spatial_bias.reshape(3, rows, 1), patches, out_grad)
     x_got = route.cross(x_send)
     g_got = route.cross(g_send)
     spat_got = route.cross(spat_own)
+    first_cols = HALF + VCOLS
     if fits:
-        right_blocks = route.widen_in_turn(stack([right_shard] + line, lo_line[0]))
-        lo_blocks = route.widen_in_turn(stack([lo_shard] + lo_line, right_blocks[3]))
+        right_blocks = route.widen_direct(stack(line, 0, first_cols, [x_send]))
+        lo_blocks = route.widen_direct(stack(line, first_cols, LO, [right_blocks[1]]))
     else:
-        right_blocks = route.widen(jnp.concatenate([right_shard] + line, axis=0))
-        lo_blocks = route.widen(jnp.concatenate([lo_shard] + lo_line, axis=0))
-    lo_second = lo_blocks[1]
+        whole = jnp.concatenate(line, axis=0)
+        right_blocks = route.widen(whole[:, :first_cols])
+        lo_blocks = route.widen(whole[:, first_cols:])
     right_blocks = right_blocks + [route.cross(b) for b in right_blocks]
     lo_blocks = lo_blocks + [route.cross(b) for b in lo_blocks]
     if not fits:
@@ -1142,7 +1148,7 @@
     x, grad_out, h, v, slope, part, weight_right, vec = gate_forward(
         ktable, sides, patches, x_got, out_grad, g_got, right_blocks
     )
-    gate, hat, scale, spat, mm = gate_norm(levels, sides, vec, v, part, spat_own, spat_got, [lo_second])
+    gate, hat, scale, spat, mm = gate_norm(levels, sides, vec, v, part, spat_own, spat_got, [])
     gs, gated, q, gb, wl, wo, sp_keep, sp_send, gsum = middle(ktable, levels, sides, vec, h, spat, gate, grad_out, lo_blocks)
     near, far = route.low[-1], route.low[0]
     if fits:

time: 151 us -> 146 us (0.967)
  starting transfers between devices: 45.7 us -> 40.3 us
  Pallas kernels: 57.9 us -> 56.3 us
    ppermute x30 -> x27, starting transfers between devices: 41.6 us -> 36.8 us  [swap(): return lax.ppermute(block, AXES, pairs)]
    pallas_call x17 -> x15, Pallas kernels: 56.9 us -> 55.4 us  [call(): pl.pallas_call(kernel, out_shape=out_shape, in_specs=in_specs, out_specs=...]
    unnamed x54 -> x48, local copies, waits for them, and re-layouts: 7.43 us -> 7.75 us
    ppermute x30 -> x27, waiting for transfers between devices: 32.4 us -> 32.4 us  [swap(): return lax.ppermute(block, AXES, pairs)]
  transfers between devices with their start and end apart: 47 -> 44, of which waited for: 13 -> 10; matrix products, arithmetic and copies ran while one was open for 3% -> 5% of each run, Pallas kernels for 23% -> 22%
where the time goes in v3:
time: 146 us; the launch traced here: 145 us
  Pallas kernels  56.3 us (39%)
  starting transfers between devices  40.3 us (28%)
  waiting for transfers between devices  37.1 us (25%)
  local copies, waits for them, and re-layouts  8.67 us (6%)
  other arithmetic  1.66 us (1%)
    pallas_call x15, Pallas kernels, call(): pl.pallas_call(kernel, out_shape=out_shape, in_specs=in_specs, out_specs=...  55.4 us
    ppermute x27, starting transfers between devices, swap(): return lax.ppermute(block, AXES, pairs)  36.8 us
    ppermute x27, waiting for transfers between devices, swap(): return lax.ppermute(block, AXES, pairs)  32.4 us
    unnamed x48, local copies, waits for them, and re-layouts  7.75 us
    ppermute x17, waiting for transfers between devices, cross(): return lax.ppermute(block, AXES, pairs)  4.73 us
    ppermute x17, starting transfers between devices, cross(): return lax.ppermute(block, AXES, pairs)  3.47 us
  transfers between devices with their start and end apart: 44, of which 10 were waited for; matrix products, arithmetic and copies ran while one was open for 5% of the time, Pallas kernels for 22%

profile of v3, /device:TPU:0, one launch (start us, length us, event | category | flops | bytes accessed | tf_op | source)
XLA Modules:
  0.0 145.3 jit_solution(3082825962581510123)
XLA Ops:
  0.7 1.8 %shard_map.360.refs_0_ = bf16[16,4864]{1,0:T(8,128)(2,1)} custom-call(f32[16,3072]{1,0:T(8,128)} %w_ref.3, f32[48,512]{1,0:T(8,128)} %w_ref.2, f32[1,240]{1,0:T(1,128)} %bitcast.7), custom_call_target="tpu_custom_call" | custom-call | flops 1000 | bytes 600000 | tf_op jit(solution)/shard_map/pallas_call | solution.py:211
  2.4 5.1 %collective-permute-start.4 = (bf16[16,4864]{1,0:T(8,128)(2,1)}, bf16[16,4864]{1,0:T(8,128)(2,1)S(1)}, u32[]{:S(2)}, u32[]{:S(2)}) collective-permute-start(bf16[16,4864]{1,0:T(8,128)(2,1)} %shard_map.360.refs_0_), channel_id=1, source_target_pairs={{0,24},{1,25},{2,26},{3,27},{4,28},{5,29},{6,30},{7,31},{8,16},{9,... | collective-permute-start | bytes 466952 | tf_op jit(solution)/shard_map/ppermute | solution.py:64
  9.9 1.2 copy.50.x_ref.p_ref
  11.1 1.2 copy.49.g_ref.o_ref
  13.3 7.7 %collective-permute-done.3.refs_2_ = bf16[16,4864]{1,0:T(8,128)(2,1)S(1)} collective-permute-done((bf16[16,4864]{1,0:T(8,128)(2,1)}, bf16[16,4864]{1,0:T(8,128)(2,1)S(1)}, u32[]{:S(2)}, u32[]{:S(2)}) %collective-permute-start.3) | collective-permute-done | bytes 155680 | tf_op jit(solution)/shard_map/ppermute | solution.py:64
  21.0 2.5 %collective-permute-start.7 = (bf16[64,1792]{1,0:T(8,128)(2,1)S(1)}, bf16[64,1792]{1,0:T(8,128)(2,1)}, u32[]{:S(2)}, u32[]{:S(2)}) collective-permute-start(bf16[64,1792]{1,0:T(8,128)(2,1)S(1)} %shard_map.361.refs_0_), channel_id=1, source_target_pairs={{0,6},{1,7},{2,4},{3,5},{4,2},{5,3},{6,0},{7,1},{8,14},{9,15},{10,... | collective-permute-start | bytes 688136 | tf_op jit(solution)/shard_map/ppermute | solution.py:64
  25.8 4.8 %collective-permute-done.7.refs_3_ = bf16[64,1792]{1,0:T(8,128)(2,1)} collective-permute-done((bf16[64,1792]{1,0:T(8,128)(2,1)S(1)}, bf16[64,1792]{1,0:T(8,128)(2,1)}, u32[]{:S(2)}, u32[]{:S(2)}) %collective-permute-start.7) | collective-permute-done | bytes 229408 | tf_op jit(solution)/shard_map/ppermute | solution.py:64
  30.6 3.1 %collective-permute-done.6.refs_2_ = bf16[64,1792]{1,0:T(8,128)(2,1)} collective-permute-done((bf16[64,1792]{1,0:T(8,128)(2,1)S(1)}, bf16[64,1792]{1,0:T(8,128)(2,1)}, u32[]{:S(2)}, u32[]{:S(2)}) %collective-permute-start.6) | collective-permute-done | bytes 229408 | tf_op jit(solution)/shard_map/ppermute | solution.py:64
  34.9 1.4 collective-permute-start.15
  39.4 10.4 %shard_map.362 = (bf16[672,512]{1,0:T(8,128)(2,1)S(1)}, bf16[672,512]{1,0:T(8,128)(2,1)S(1)}, bf16[672,512]{1,0:T(8,128)(2,1)S(1)}, f32[672,1536]{1,0:T(8,128)S(...) custom-call(s32[32]{0:T(128)S(1)} %get-tuple-element.185.table_ref, ...), custom_call_target="tpu_custom_call" | custom-call | flops 10000000000 | bytes 20000000 | tf_op jit(solution)/shard_map/pallas_call | solution.py:211
  49.9 5.4 %collective-permute-done.14.refs_2_ = bf16[64,3072]{1,0:T(8,128)(2,1)S(1)} collective-permute-done((bf16[64,3072]{1,0:T(8,128)(2,1)S(1)}, bf16[64,3072]{1,0:T(8,128)(2,1)S(1)}, u32[]{:S(2)}, u32[]{:S(2)}) %collective-permute-start.14) | collective-permute-done | bytes 393248 | tf_op jit(solution)/shard_map/ppermute | solution.py:64
  55.8 5.0 %shard_map.363 = (bf16[720,1536]{1,0:T(8,128)(2,1)S(1)}, bf16[672,1536]{1,0:T(8,128)(2,1)S(1)}, f32[672,128]{1,0:T(8,128)S(1)}, bf16[672,1536]{1,0:T(8,128)(2,1)S(1)}, bf16[2,336,384]{2,1,0:T(8,128)(2,1)S(1)}) custom-call(s32[2]{0:T(128)S(1)} %dynamic_slice.3.levels_ref, s32[33]{0:T(128)S(1)} %pad_add_fusion.1.sides_ref, ...), custom_call_target="tpu_custom_call" | custom-call | flops 6000000000 | bytes 12000000 | tf_op jit(solution)/shard_map/pallas_call | solution.py:211
  60.9 14.1 %shard_map.365 = (bf16[672,1536]{1,0:T(8,128)(2,1)S(1)}, bf16[672,1536]{1,0:T(8,128)(2,1)S(1)}, bf16[672,1536]{1,0:T(8,128)(2,1)S(1)}, bf16[672,512]{1,0:T(8,128...) custom-call(s32[32]{0:T(128)S(1)} %get-tuple-element.185.table_ref, ...), custom_call_target="tpu_custom_call" | custom-call | flops 8000000000 | bytes 16000000 | tf_op jit(solution)/shard_map/pallas_call | solution.py:211
  75.0 7.5 %shard_map.366 = (bf16[256,3072]{1,0:T(8,128)(2,1)S(1)}, bf16[256,3072]{1,0:T(8,128)(2,1)S(1)}, bf16[2,162,512]{2,1,0:T(8,128)(2,1)S(1)}, bf16[2,162,512]{2,1,0:T(8,128)(2,1)S(1)}, f32[672,512]{1,0:T(8,128)S(1)}) custom-call(s32[32]{0:T(128)S(1)} %get-tuple-element.185.table_ref, s32[2]{0:T(128)S(1)} %dynamic_slice.3.levels_ref, ...), custom_call_target="tpu_custom_call" | custom-call | flops 5000000000 | bytes 15000000 | tf_op jit(solution)/shard_map/pallas_call | solution.py:211
  83.2 3.5 %collective-permute-done.21.refs_1_ = bf16[256,768]{1,0:T(8,128)(2,1)S(1)} collective-permute-done((bf16[256,768]{1,0:T(8,128)(2,1)S(1)}, bf16[256,768]{1,0:T(8,128)(2,1)S(1)}, u32[]{:S(2)}, u32[]{:S(2)}) %collective-permute-start.21) | collective-permute-done | bytes 393248 | tf_op jit(solution)/shard_map/ppermute | solution.py:71
  86.7 1.3 collective-permute-start.22
  87.9 5.6 %shard_map.368 = (bf16[672,1536]{1,0:T(8,128)(2,1)S(1)}, f32[1,4608]{1,0:T(1,128)S(1)}) custom-call(f32[1,7680]{1,0:T(1,128)S(1)} %get-tuple-element.84.vec_ref, bf16[672,1536]{1,0:T(8,128)(2,1)S(1)} %get-tuple-element.101.gs_ref, bf16[2,336,384]{2,1,0:T(8,128)(2,1)S(1)} %get-tuple-element.102.mm_ref, bf16[672,1536]{1,0:T(8,128)(2,1)S(1)} %get-tuple-element.103.hat_ref, ...), custom_call_target="tpu_custom_call" | custom-call | flops 3000000000 | bytes 10000000 | tf_op jit(solution)/shard_map/pallas_call | solution.py:211
  95.9 2.7 %shard_map.371 = (bf16[512,1536]{1,0:T(8,128)(2,1)S(1)}, f32[672,512]{1,0:T(8,128)S(1)}) custom-call(bf16[672,1536]{1,0:T(8,128)(2,1)S(1)} %get-tuple-element.109.gp_ref, bf16[672,512]{1,0:T(8,128)(2,1)S(1)} %get-tuple-element.85.h_ref, bf16[512,1536]{1,0:T(8,128)(2,1)S(1)} %get-tuple-element.110.w_ref, f32[672,512]{1,0:T(8,128)S(1)} %get-tuple-element.111.gh_ref, ...), custom_call_target="tpu_custom_call" | custom-call | flops 3000000000 | bytes 8000000 | tf_op jit(solution)/shard_map/pallas_call | solution.py:211
  98.6 2.0 %collective-permute-done.24.refs_0_.refs_3_ = bf16[64,768]{1,0:T(8,128)(2,1)S(1)} collective-permute-done((bf16[64,768]{1,0:T(8,128)(2,1)S(1)}, bf16[64,768]{1,0:T(8,128)(2,1)S(1)}, u32[]{:S(2)}, u32[]{:S(2)}) %collective-permute-start.24) | collective-permute-done | bytes 98336 | tf_op jit(solution)/shard_map/ppermute | solution.py:64
  100.5 2.8 %shard_map.372 = (bf16[256,1792]{1,0:T(8,128)(2,1)S(1)}, bf16[128,1792]{1,0:T(8,128)(2,1)S(1)}, bf16[128,1792]{1,0:T(8,128)(2,1)S(1)}, bf16[2,162,512]{2,1,0:T(8,128)(2,1)S(1)}, bf16[2,162,512]{2,1,0:T(8,128)(2,1)S(1)}) custom-call(s32[32]{0:T(128)S(1)} %get-tuple-element.185.table_ref, s32[33]{0:T(128)S(1)} %pad_add_fusion.1.sides_ref, ...), custom_call_target="tpu_custom_call" | custom-call | flops 2000000000 | bytes 6000000 | tf_op jit(solution)/shard_map/pallas_call | solution.py:211
  104.0 1.2 collective-permute-done.27.refs_1_
  105.3 1.2 collective-permute-start.28
  108.1 2.8 %collective-permute-start.33 = (bf16[64,768]{1,0:T(8,128)(2,1)S(1)}, bf16[64,768]{1,0:T(8,128)(2,1)S(1)}, u32[]{:S(2)}, u32[]{:S(2)}) collective-permute-start(bf16[64,768]{1,0:T(8,128)(2,1)S(1)} %get-tuple-element.123), channel_id=1, source_target_pairs={{0,16},{1,17},{2,18},{3,19},{4,20},{5,21},{6,22},{7,23},{8,24},{9,... | collective-permute-start | bytes 294920 | tf_op jit(solution)/shard_map/ppermute | solution.py:64
  110.9 7.2 %collective-permute-done.28.refs_2_ = bf16[128,1792]{1,0:T(8,128)(2,1)S(1)} collective-permute-done((bf16[128,1792]{1,0:T(8,128)(2,1)S(1)}, bf16[128,1792]{1,0:T(8,128)(2,1)S(1)}, u32[]{:S(2)}, u32[]{:S(2)}) %collective-permute-start.28) | collective-permute-done | bytes 458784 | tf_op jit(solution)/shard_map/ppermute | solution.py:64
  118.1 2.3 %collective-permute-start.34 = (bf16[64,768]{1,0:T(8,128)(2,1)S(1)}, bf16[64,768]{1,0:T(8,128)(2,1)S(1)}, u32[]{:S(2)}, u32[]{:S(2)}) collective-permute-start(bf16[64,768]{1,0:T(8,128)(2,1)S(1)} %get-tuple-element.124), channel_id=1, source_target_pairs={{0,24},{1,25},{2,26},{3,27},{4,28},{5,29},{6,30},{7,31},{8,16},{9,... | collective-permute-start | bytes 294920 | tf_op jit(solution)/shard_map/ppermute | solution.py:64
  122.8 1.7 %collective-permute-done.34.c_ref = bf16[64,768]{1,0:T(8,128)(2,1)S(1)} collective-permute-done((bf16[64,768]{1,0:T(8,128)(2,1)S(1)}, bf16[64,768]{1,0:T(8,128)(2,1)S(1)}, u32[]{:S(2)}, u32[]{:S(2)}) %collective-permute-start.34) | collective-permute-done | bytes 98336 | tf_op jit(solution)/shard_map/ppermute | solution.py:64
  126.0 2.8 %collective-permute-start.39 = (bf16[16,3072]{1,0:T(8,128)(2,1)S(1)}, bf16[16,3072]{1,0:T(8,128)(2,1)S(1)}, u32[]{:S(2)}, u32[]{:S(2)}) collective-permute-start(bf16[16,3072]{1,0:T(8,128)(2,1)S(1)} %get-tuple-element.131), channel_id=1, source_target_pairs={{0,16},{1,17},{2,18},{3,19},{4,20},{5,21},{6,22},{7,23},{8,24},{9,... | collective-permute-start | bytes 294920 | tf_op jit(solution)/shard_map/ppermute | solution.py:64
  128.8 1.6 %collective-permute-start.40 = (bf16[16,3072]{1,0:T(8,128)(2,1)S(1)}, bf16[16,3072]{1,0:T(8,128)(2,1)S(1)}, u32[]{:S(2)}, u32[]{:S(2)}) collective-permute-start(bf16[16,3072]{1,0:T(8,128)(2,1)S(1)} %get-tuple-element.132), channel_id=1, source_target_pairs={{0,24},{1,25},{2,26},{3,27},{4,28},{5,29},{6,30},{7,31},{8,16},{9,... | collective-permute-start | bytes 294920 | tf_op jit(solution)/shard_map/ppermute | solution.py:64
  133.3 2.3 %collective-permute-start.36 = (bf16[16,1792]{1,0:T(8,128)(2,1)S(1)}, bf16[16,1792]{1,0:T(8,128)(2,1)S(1)}, u32[]{:S(2)}, u32[]{:S(2)}) collective-permute-start(bf16[16,1792]{1,0:T(8,128)(2,1)S(1)} %get-tuple-element.128), channel_id=1, source_target_pairs={{0,16},{1,17},{2,18},{3,19},{4,20},{5,21},{6,22},{7,23},{8,24},{9,... | collective-permute-start | bytes 172040 | tf_op jit(solution)/shard_map/ppermute | solution.py:64
  135.6 2.1 %collective-permute-start.37 = (bf16[16,1792]{1,0:T(8,128)(2,1)S(1)}, bf16[16,1792]{1,0:T(8,128)(2,1)S(1)}, u32[]{:S(2)}, u32[]{:S(2)}) collective-permute-start(bf16[16,1792]{1,0:T(8,128)(2,1)S(1)} %get-tuple-element.129), channel_id=1, source_target_pairs={{0,24},{1,25},{2,26},{3,27},{4,28},{5,29},{6,30},{7,31},{8,16},{9,... | collective-permute-start | bytes 172040 | tf_op jit(solution)/shard_map/ppermute | solution.py:64
  137.7 1.2 copy.53
  139.8 2.8 %shard_map.381 = (f32[3,162,324]{2,1,0:T(8,128)}, f32[3,162,324]{2,1,0:T(8,128)}, f32[3,162,324]{2,1,0:T(8,128)}, f32[3,162]{1,0:T(4,128)}, f32[3,162]{1,0:T(4,128)}, /*index=5*/f32[3,162]{1,0:T(4,128)}) custom-call(s32[16]{0:T(128)S(1)} %get-tuple-element.187.order_ref, bf16[64,768]{1,0:T(8,128)(2,1)S(1)} %shard_map.377.refs_4_.refs_0_, ...), custom_call_target="tpu_custom_call" | custom-call | flops 10000000 | bytes 6000000 | tf_op jit(solution)/shard_map/pallas_call | solution.py:211
  (138 shorter events, 25.8 us)
Async XLA Ops:
  2.4 10.8 %collective-permute-start.4 = (bf16[16,4864]{1,0:T(8,128)(2,1)}, bf16[16,4864]{1,0:T(8,128)(2,1)S(1)}, u32[]{:S(2)}, u32[]{:S(2)}) collective-permute-start(bf16[16,4864]{1,0:T(8,128)(2,1)} %shard_map.360.refs_0_), channel_id=1, source_target_pairs={{0,24},{1,25},{2,26},{3,27},{4,28},{5,29},{6,30},{7,31},{8,16},{9,... | collective-permute-start | bytes 466952 | tf_op jit(solution)/shard_map/ppermute | solution.py:64
  7.6 13.4 %collective-permute-start.3 = (bf16[16,4864]{1,0:T(8,128)(2,1)}, bf16[16,4864]{1,0:T(8,128)(2,1)S(1)}, u32[]{:S(2)}, u32[]{:S(2)}) collective-permute-start(bf16[16,4864]{1,0:T(8,128)(2,1)} %shard_map.360.refs_0_), channel_id=1, source_target_pairs={{0,16},{1,17},{2,18},{3,19},{4,20},{5,21},{6,22},{7,23},{8,24},{9,... | collective-permute-start | bytes 466952 | tf_op jit(solution)/shard_map/ppermute | solution.py:64
  7.6 13.4 %collective-permute-start.2 = (bf16[16,4864]{1,0:T(8,128)(2,1)}, bf16[16,4864]{1,0:T(8,128)(2,1)S(1)}, u32[]{:S(2)}, u32[]{:S(2)}) collective-permute-start(bf16[16,4864]{1,0:T(8,128)(2,1)} %shard_map.360.refs_0_), channel_id=1, source_target_pairs={{0,8},{1,9},{2,10},{3,11},{4,12},{5,13},{6,14},{7,15},{8,0},{9,1},... | collective-permute-start | bytes 466952 | tf_op jit(solution)/shard_map/ppermute | solution.py:64
  13.2 11.3 %collective-permute-start.1 = (bf16[2,162,512]{2,1,0:T(8,128)(2,1)S(1)}, bf16[2,162,512]{2,1,0:T(8,128)(2,1)S(1)}, u32[]{:S(2)}, u32[]{:S(2)}) collective-permute-start(bf16[2,162,512]{2,1,0:T(8,128)(2,1)S(1)} %get-tuple-element.83), channel_id=1, source_target_pairs={{0,1},{1,0},{2,3},{3,2},{4,5},{5,4},{6,7},{7,6},{8,9},{9,8},{10,11... | collective-permute-start | bytes 995336 | tf_op jit(solution)/shard_map/ppermute | solution.py:71
  21.0 9.6 %collective-permute-start.7 = (bf16[64,1792]{1,0:T(8,128)(2,1)S(1)}, bf16[64,1792]{1,0:T(8,128)(2,1)}, u32[]{:S(2)}, u32[]{:S(2)}) collective-permute-start(bf16[64,1792]{1,0:T(8,128)(2,1)S(1)} %shard_map.361.refs_0_), channel_id=1, source_target_pairs={{0,6},{1,7},{2,4},{3,5},{4,2},{5,3},{6,0},{7,1},{8,14},{9,15},{10,... | collective-permute-start | bytes 688136 | tf_op jit(solution)/shard_map/ppermute | solution.py:64
  23.5 10.2 %collective-permute-start.6 = (bf16[64,1792]{1,0:T(8,128)(2,1)S(1)}, bf16[64,1792]{1,0:T(8,128)(2,1)}, u32[]{:S(2)}, u32[]{:S(2)}) collective-permute-start(bf16[64,1792]{1,0:T(8,128)(2,1)S(1)} %shard_map.361.refs_0_), channel_id=1, source_target_pairs={{0,2},{1,5},{2,0},{3,7},{4,6},{5,1},{6,4},{7,3},{8,10},{9,13},{10,... | collective-permute-start | bytes 688136 | tf_op jit(solution)/shard_map/ppermute | solution.py:64
  24.0 9.7 %collective-permute-start.5 = (bf16[64,1792]{1,0:T(8,128)(2,1)S(1)}, bf16[64,1792]{1,0:T(8,128)(2,1)}, u32[]{:S(2)}, u32[]{:S(2)}) collective-permute-start(bf16[64,1792]{1,0:T(8,128)(2,1)S(1)} %shard_map.361.refs_0_), channel_id=1, source_target_pairs={{0,4},{1,3},{2,6},{3,1},{4,0},{5,7},{6,2},{7,5},{8,12},{9,11},{10,... | collective-permute-start | bytes 688136 | tf_op jit(solution)/shard_map/ppermute | solution.py:64
  24.5 9.8 %collective-permute-start = (bf16[2,162,512]{2,1,0:T(8,128)(2,1)S(1)}, bf16[2,162,512]{2,1,0:T(8,128)(2,1)}, u32[]{:S(2)}, u32[]{:S(2)}) collective-permute-start(bf16[2,162,512]{2,1,0:T(8,128)(2,1)S(1)} %get-tuple-element.82.refs_4_), channel_id=1, source_target_pairs={{0,1},{1,0},{2,3},{3,2},{4,5},{5,4},{6,7},{7,6},{8,9},{9,8},{10,11... | collective-permute-start | bytes 995336 | tf_op jit(solution)/shard_map/ppermute | solution.py:71
  25.3 9.2 %collective-permute-start.8 = (bf16[64,1792]{1,0:T(8,128)(2,1)S(1)}, bf16[64,1792]{1,0:T(8,128)(2,1)}, u32[]{:S(2)}, u32[]{:S(2)}) collective-permute-start(bf16[64,1792]{1,0:T(8,128)(2,1)S(1)} %shard_map.361.refs_0_), channel_id=1, source_target_pairs={{0,1},{1,0},{2,3},{3,2},{4,5},{5,4},{6,7},{7,6},{8,9},{9,8},{10,11... | collective-permute-start | bytes 688136 | tf_op jit(solution)/shard_map/ppermute | solution.py:71
  34.4 21.5 %collective-permute-start.12 = (bf16[3,162,384]{2,1,0:T(8,128)(2,1)}, bf16[3,162,384]{2,1,0:T(8,128)(2,1)S(1)}, u32[]{:S(2)}, u32[]{:S(2)}) collective-permute-start(bf16[3,162,384]{2,1,0:T(8,128)(2,1)} %copy-done.14), channel_id=1, source_target_pairs={{0,1},{1,0},{2,3},{3,2},{4,5},{5,4},{6,7},{7,6},{8,9},{9,8},{10,11... | collective-permute-start | bytes 1119752 | tf_op jit(solution)/shard_map/ppermute | solution.py:71
  34.5 26.4 %collective-permute-start.16 = (bf16[64,3072]{1,0:T(8,128)(2,1)S(1)}, bf16[64,3072]{1,0:T(8,128)(2,1)S(1)}, u32[]{:S(2)}, u32[]{:S(2)}) collective-permute-start(bf16[64,3072]{1,0:T(8,128)(2,1)S(1)} %shard_map.364.refs_0_), channel_id=1, source_target_pairs={{0,1},{1,0},{2,3},{3,2},{4,5},{5,4},{6,7},{7,6},{8,9},{9,8},{10,11... | collective-permute-start | bytes 1179656 | tf_op jit(solution)/shard_map/ppermute | solution.py:71
  34.9 14.9 %collective-permute-start.15 = (bf16[64,3072]{1,0:T(8,128)(2,1)S(1)}, bf16[64,3072]{1,0:T(8,128)(2,1)S(1)}, u32[]{:S(2)}, u32[]{:S(2)}) collective-permute-start(bf16[64,3072]{1,0:T(8,128)(2,1)S(1)} %shard_map.364.refs_0_), channel_id=1, source_target_pairs={{0,6},{1,7},{2,4},{3,5},{4,2},{5,3},{6,0},{7,1},{8,14},{9,15},{10,... | collective-permute-start | bytes 1179656 | tf_op jit(solution)/shard_map/ppermute | solution.py:64
  36.4 18.9 %collective-permute-start.14 = (bf16[64,3072]{1,0:T(8,128)(2,1)S(1)}, bf16[64,3072]{1,0:T(8,128)(2,1)S(1)}, u32[]{:S(2)}, u32[]{:S(2)}) collective-permute-start(bf16[64,3072]{1,0:T(8,128)(2,1)S(1)} %shard_map.364.refs_0_), channel_id=1, source_target_pairs={{0,2},{1,5},{2,0},{3,7},{4,6},{5,1},{6,4},{7,3},{8,10},{9,13},{10,... | collective-permute-start | bytes 1179656 | tf_op jit(solution)/shard_map/ppermute | solution.py:64
  37.4 18.0 %collective-permute-start.13 = (bf16[64,3072]{1,0:T(8,128)(2,1)S(1)}, bf16[64,3072]{1,0:T(8,128)(2,1)S(1)}, u32[]{:S(2)}, u32[]{:S(2)}) collective-permute-start(bf16[64,3072]{1,0:T(8,128)(2,1)S(1)} %shard_map.364.refs_0_), channel_id=1, source_target_pairs={{0,4},{1,3},{2,6},{3,1},{4,0},{5,7},{6,2},{7,5},{8,12},{9,11},{10,... | collective-permute-start | bytes 1179656 | tf_op jit(solution)/shard_map/ppermute | solution.py:64
  49.9 11.1 %collective-permute-start.19 = (bf16[64,3072]{1,0:T(8,128)(2,1)S(1)}, bf16[64,3072]{1,0:T(8,128)(2,1)S(1)}, u32[]{:S(2)}, u32[]{:S(2)}) collective-permute-start(bf16[64,3072]{1,0:T(8,128)(2,1)S(1)} %collective-permute-done.15.refs_3_), channel_id=1, source_target_pairs={{0,1},{1,0},{2,3},{3,2},{4,5},{5,4},{6,7},{7,6},{8,9},{9,8},{10,11... | collective-permute-start | bytes 1179656 | tf_op jit(solution)/shard_map/ppermute | solution.py:71
  82.6 11.0 %collective-permute-start.23 = (bf16[256,3072]{1,0:T(8,128)(2,1)S(1)}, bf16[256,3072]{1,0:T(8,128)(2,1)S(1)}, u32[]{:S(2)}, u32[]{:S(2)}) collective-permute-start(bf16[256,3072]{1,0:T(8,128)(2,1)S(1)} %get-tuple-element.113), channel_id=1, source_target_pairs={{0,1},{1,0},{2,3},{3,2},{4,5},{5,4},{6,7},{7,6},{8,9},{9,8},{10,11... | collective-permute-start | bytes 4718600 | tf_op jit(solution)/shard_map/ppermute | solution.py:71
  86.7 8.0 %collective-permute-start.22 = (bf16[128,768]{1,0:T(8,128)(2,1)S(1)}, bf16[128,768]{1,0:T(8,128)(2,1)S(1)}, u32[]{:S(2)}, u32[]{:S(2)}) collective-permute-start(bf16[128,768]{1,0:T(8,128)(2,1)S(1)} %shard_map.367.refs_0_), channel_id=1, source_target_pairs={{0,2},{1,5},{2,0},{3,7},{4,6},{5,1},{6,4},{7,3},{8,10},{9,13},{10,... | collective-permute-start | bytes 589832 | tf_op jit(solution)/shard_map/ppermute | solution.py:64
  93.8 12.9 %collective-permute-start.29 = (bf16[128,3072]{1,0:T(8,128)(2,1)S(1)}, bf16[128,3072]{1,0:T(8,128)(2,1)S(1)}, u32[]{:S(2)}, u32[]{:S(2)}) collective-permute-start(bf16[128,3072]{1,0:T(8,128)(2,1)S(1)} %shard_map.369.refs_3_), channel_id=1, source_target_pairs={{0,2},{1,5},{2,0},{3,7},{4,6},{5,1},{6,4},{7,3},{8,10},{9,13},{10,... | collective-permute-start | bytes 2359304 | tf_op jit(solution)/shard_map/ppermute | solution.py:64
  105.3 12.8 %collective-permute-start.28 = (bf16[128,1792]{1,0:T(8,128)(2,1)S(1)}, bf16[128,1792]{1,0:T(8,128)(2,1)S(1)}, u32[]{:S(2)}, u32[]{:S(2)}) collective-permute-start(bf16[128,1792]{1,0:T(8,128)(2,1)S(1)} %shard_map.373.refs_4_), channel_id=1, source_target_pairs={{0,2},{1,5},{2,0},{3,7},{4,6},{5,1},{6,4},{7,3},{8,10},{9,13},{10,... | collective-permute-start | bytes 1376264 | tf_op jit(solution)/shard_map/ppermute | solution.py:64
  106.8 18.9 %collective-permute-start.31 = (bf16[64,3072]{1,0:T(8,128)(2,1)S(1)}, bf16[64,3072]{1,0:T(8,128)(2,1)S(1)}, u32[]{:S(2)}, u32[]{:S(2)}) collective-permute-start(bf16[64,3072]{1,0:T(8,128)(2,1)S(1)} %shard_map.375.refs_3_), channel_id=1, source_target_pairs={{0,4},{1,3},{2,6},{3,1},{4,0},{5,7},{6,2},{7,5},{8,12},{9,11},{10,... | collective-permute-start | bytes 1179656 | tf_op jit(solution)/shard_map/ppermute | solution.py:64
  108.0 20.8 %collective-permute-start.25 = (bf16[2,162,512]{2,1,0:T(8,128)(2,1)S(1)}, bf16[2,162,512]{2,1,0:T(8,128)(2,1)S(1)}, u32[]{:S(2)}, u32[]{:S(2)}) collective-permute-start(bf16[2,162,512]{2,1,0:T(8,128)(2,1)S(1)} %get-tuple-element.117), channel_id=1, source_target_pairs={{0,1},{1,0},{2,3},{3,2},{4,5},{5,4},{6,7},{7,6},{8,9},{9,8},{10,11... | collective-permute-start | bytes 995336 | tf_op jit(solution)/shard_map/ppermute | solution.py:71
  108.0 13.7 %collective-permute-start.32 = (bf16[64,768]{1,0:T(8,128)(2,1)S(1)}, bf16[64,768]{1,0:T(8,128)(2,1)S(1)}, u32[]{:S(2)}, u32[]{:S(2)}) collective-permute-start(bf16[64,768]{1,0:T(8,128)(2,1)S(1)} %get-tuple-element.122), channel_id=1, source_target_pairs={{0,8},{1,9},{2,10},{3,11},{4,12},{5,13},{6,14},{7,15},{8,0},{9,1},... | collective-permute-start | bytes 294920 | tf_op jit(solution)/shard_map/ppermute | solution.py:64
  108.1 14.7 %collective-permute-start.33 = (bf16[64,768]{1,0:T(8,128)(2,1)S(1)}, bf16[64,768]{1,0:T(8,128)(2,1)S(1)}, u32[]{:S(2)}, u32[]{:S(2)}) collective-permute-start(bf16[64,768]{1,0:T(8,128)(2,1)S(1)} %get-tuple-element.123), channel_id=1, source_target_pairs={{0,16},{1,17},{2,18},{3,19},{4,20},{5,21},{6,22},{7,23},{8,24},{9,... | collective-permute-start | bytes 294920 | tf_op jit(solution)/shard_map/ppermute | solution.py:64
  121.7 9.9 %collective-permute-start.30 = (bf16[64,1792]{1,0:T(8,128)(2,1)S(1)}, bf16[64,1792]{1,0:T(8,128)(2,1)S(1)}, u32[]{:S(2)}, u32[]{:S(2)}) collective-permute-start(bf16[64,1792]{1,0:T(8,128)(2,1)S(1)} %shard_map.376.after_ref), channel_id=1, source_target_pairs={{0,4},{1,3},{2,6},{3,1},{4,0},{5,7},{6,2},{7,5},{8,12},{9,11},{10,... | collective-permute-start | bytes 688136 | tf_op jit(solution)/shard_map/ppermute | solution.py:64
  125.9 7.4 %collective-permute-start.38 = (bf16[16,3072]{1,0:T(8,128)(2,1)S(1)}, bf16[16,3072]{1,0:T(8,128)(2,1)S(1)}, u32[]{:S(2)}, u32[]{:S(2)}) collective-permute-start(bf16[16,3072]{1,0:T(8,128)(2,1)S(1)} %get-tuple-element.130), channel_id=1, source_target_pairs={{0,8},{1,9},{2,10},{3,11},{4,12},{5,13},{6,14},{7,15},{8,0},{9,1},... | collective-permute-start | bytes 294920 | tf_op jit(solution)/shard_map/ppermute | solution.py:64
  126.0 7.3 %collective-permute-start.39 = (bf16[16,3072]{1,0:T(8,128)(2,1)S(1)}, bf16[16,3072]{1,0:T(8,128)(2,1)S(1)}, u32[]{:S(2)}, u32[]{:S(2)}) collective-permute-start(bf16[16,3072]{1,0:T(8,128)(2,1)S(1)} %get-tuple-element.131), channel_id=1, source_target_pairs={{0,16},{1,17},{2,18},{3,19},{4,20},{5,21},{6,22},{7,23},{8,24},{9,... | collective-permute-start | bytes 294920 | tf_op jit(solution)/shard_map/ppermute | solution.py:64
  128.8 6.8 %collective-permute-start.40 = (bf16[16,3072]{1,0:T(8,128)(2,1)S(1)}, bf16[16,3072]{1,0:T(8,128)(2,1)S(1)}, u32[]{:S(2)}, u32[]{:S(2)}) collective-permute-start(bf16[16,3072]{1,0:T(8,128)(2,1)S(1)} %get-tuple-element.132), channel_id=1, source_target_pairs={{0,24},{1,25},{2,26},{3,27},{4,28},{5,29},{6,30},{7,31},{8,16},{9,... | collective-permute-start | bytes 294920 | tf_op jit(solution)/shard_map/ppermute | solution.py:64
  130.4 9.3 %collective-permute-start.42 = (bf16[64,768]{1,0:T(8,128)(2,1)S(1)}, bf16[64,768]{1,0:T(8,128)(2,1)S(1)}, u32[]{:S(2)}, u32[]{:S(2)}) collective-permute-start(bf16[64,768]{1,0:T(8,128)(2,1)S(1)} %shard_map.377.refs_4_.refs_0_), channel_id=1, source_target_pairs={{0,2},{1,5},{2,0},{3,7},{4,6},{5,1},{6,4},{7,3},{8,10},{9,13},{10,... | collective-permute-start | bytes 294920 | tf_op jit(solution)/shard_map/ppermute | solution.py:64
  131.6 8.2 %collective-permute-start.43 = (bf16[64,768]{1,0:T(8,128)(2,1)S(1)}, bf16[64,768]{1,0:T(8,128)(2,1)S(1)}, u32[]{:S(2)}, u32[]{:S(2)}) collective-permute-start(bf16[64,768]{1,0:T(8,128)(2,1)S(1)} %collective-permute-done.41.refs_1_), channel_id=1, source_target_pairs={{0,2},{1,5},{2,0},{3,7},{4,6},{5,1},{6,4},{7,3},{8,10},{9,13},{10,... | collective-permute-start | bytes 294920 | tf_op jit(solution)/shard_map/ppermute | solution.py:64
  133.3 9.3 %collective-permute-start.35 = (bf16[16,1792]{1,0:T(8,128)(2,1)S(1)}, bf16[16,1792]{1,0:T(8,128)(2,1)S(1)}, u32[]{:S(2)}, u32[]{:S(2)}) collective-permute-start(bf16[16,1792]{1,0:T(8,128)(2,1)S(1)} %get-tuple-element.127), channel_id=1, source_target_pairs={{0,8},{1,9},{2,10},{3,11},{4,12},{5,13},{6,14},{7,15},{8,0},{9,1},... | collective-permute-start | bytes 172040 | tf_op jit(solution)/shard_map/ppermute | solution.py:64
  133.3 9.3 %collective-permute-start.36 = (bf16[16,1792]{1,0:T(8,128)(2,1)S(1)}, bf16[16,1792]{1,0:T(8,128)(2,1)S(1)}, u32[]{:S(2)}, u32[]{:S(2)}) collective-permute-start(bf16[16,1792]{1,0:T(8,128)(2,1)S(1)} %get-tuple-element.128), channel_id=1, source_target_pairs={{0,16},{1,17},{2,18},{3,19},{4,20},{5,21},{6,22},{7,23},{8,24},{9,... | collective-permute-start | bytes 172040 | tf_op jit(solution)/shard_map/ppermute | solution.py:64
  135.6 7.0 %collective-permute-start.37 = (bf16[16,1792]{1,0:T(8,128)(2,1)S(1)}, bf16[16,1792]{1,0:T(8,128)(2,1)S(1)}, u32[]{:S(2)}, u32[]{:S(2)}) collective-permute-start(bf16[16,1792]{1,0:T(8,128)(2,1)S(1)} %get-tuple-element.129), channel_id=1, source_target_pairs={{0,24},{1,25},{2,26},{3,27},{4,28},{5,29},{6,30},{7,31},{8,16},{9,... | collective-permute-start | bytes 172040 | tf_op jit(solution)/shard_map/ppermute | solution.py:64
  (34 other events, 218.3 us)

commit v4 on v3

--- a/solution.py
+++ b/solution.py
@@ -266,7 +266,7 @@
     rows = dense_in.shape[0]
     per = vec_row.shape[1]
 
-    def kernel(w_hbm, o_hbm, v_hbm, out_ref, w_ref, o_ref, v_ref, row, sem):
+    def kernel(w_hbm, o_hbm, v_hbm, out_ref, lo_ref, w_ref, o_ref, v_ref, row, sem):
         copies = [
             pltpu.make_async_copy(src, dst, sem.at[k])
             for k, (src, dst) in enumerate(((w_hbm, w_ref), (o_hbm, o_ref), (v_hbm, v_ref)))
@@ -279,11 +279,9 @@
         out_ref[:, 0:HALF] = w_ref[:, HALF:].astype(BF)
         row[0:1, 0:per] = v_ref[...]
         out_ref[:, HALF : HALF + VCOLS] = row[...].astype(BF)
-        start = HALF + VCOLS
-        out_ref[:, start : start + HALF] = w_ref[:, 0:HALF].astype(BF)
-        start += HALF
+        lo_ref[:, 0:HALF] = w_ref[:, 0:HALF].astype(BF)
         for g in range(3):
-            out_ref[:, start + g * D : start + (g + 1) * D] = o_ref[g * rows : (g + 1) * rows, :].astype(BF)
+            lo_ref[:, HALF + g * D : HALF + (g + 1) * D] = o_ref[g * rows : (g + 1) * rows, :].astype(BF)
 
     scratch = [
         pltpu.VMEM(dense_in.shape, F32),
@@ -292,7 +290,7 @@
         pltpu.VMEM((rows, VCOLS), F32),
         pltpu.SemaphoreType.DMA((3,)),
     ]
-    shape = sds((rows, HALF + VCOLS + LO), BF)
+    shape = (sds((rows, HALF + VCOLS), BF), sds((rows, LO), BF))
     return call(kernel, shape, [HB] * 3, scratch, 1000, 600000, dense_in, dense_out, vec_row, room=60)
 
 
@@ -330,17 +328,17 @@
     )
 
 
-def stack(pieces, start, width, after):
+def stack(pieces, after):
     count = len(pieces)
-    rows = pieces[0].shape[0]
+    rows, cols = pieces[0].shape
 
     def kernel(*refs):
         out = refs[count + len(after)]
         for k in range(count):
-            out[k * rows : (k + 1) * rows, :] = refs[k][:, start : start + width]
+            out[k * rows : (k + 1) * rows, :] = refs[k][...]
 
     specs = [VM] * count + [HB] * len(after)
-    return call(kernel, sds((count * rows, width), BF), specs, [], 1000, 1000000, *pieces, *after)
+    return call(kernel, sds((count * rows, cols), BF), specs, [], 1000, 1000000, *pieces, *after)
 
 
 def two_halves(is_first, own, got):
@@ -636,11 +634,14 @@
     )
 
 
-def weight_grads(table, levels, sides, vec, gated, q, gb, h, wl, wo, x, half):
+def weight_grads(table, levels, sides, vec, gated, q, gb, h, wl, wo, x, half, after):
+    count = len(after)
+
     def kernel(
-        table_ref, levels_ref, sides_ref, vec_ref, t_ref, q_ref, gb_ref, h_ref, wl_ref, wo_ref, x_ref,
-        keep, send, stay_ref, away_ref, gh_ref, branch, gwo, gwl,
+        table_ref, levels_ref, sides_ref, vec_ref, t_ref, q_ref, gb_ref, h_ref, wl_ref, wo_ref, x_ref, *refs
     ):
+        keep, send, send_up, stay_ref, away_ref, gh_ref, branch, gwo, gwl = refs[count:]
+
         def out_tile(n, carry):
             cols = pl.ds(pl.multiple_of(n * TILE, TILE), TILE)
             gwo[cols, :] = dot(t_ref[:, cols], gb_ref[...], TN).astype(BF)
@@ -662,18 +663,19 @@
         split_rows(branch, stay_ref, away_ref, me, x_ref[...].astype(F32) + jnp.where(live, out, 0.0))
         for k in range(DEVS):
             dev = table_ref[k]
-            target = keep if k < GROUPS else send
-            r = pl.ds(k % GROUPS * 16, 16)
+            target = keep if k < GROUPS else send if k < GROUPS * 3 // 2 else send_up
+            r = pl.ds(k % (GROUPS if k < GROUPS else GROUPS // 2) * 16, 16)
             target[r, 0:HALF] = gwl[pl.ds(pl.multiple_of(dev * 16, 16), 16), :]
             for g in range(3):
                 target[r, HALF + g * D : HALF + (g + 1) * D] = gwo[pl.ds(pl.multiple_of(dev * 48 + 16 * g, 16), 16), :]
 
     pair = sds((2, half, D), BF)
     payload = sds((D // 2, LO), BF)
+    part = sds((D // 4, LO), BF)
     return call(
         kernel,
-        (payload, payload, pair, pair, sds((ROWS, D), F32)),
-        [SM] * 3 + [VM] * 8,
+        (payload, part, part, pair, pair, sds((ROWS, D), F32)),
+        [SM] * 3 + [VM] * 8 + [HB] * count,
         [pltpu.VMEM((ROWS, D), F32), pltpu.VMEM((HALF, D), BF), pltpu.VMEM((D, HALF), BF)],
         5000000000,
         15000000,
@@ -688,6 +690,7 @@
         wl,
         wo,
         x,
+        *after,
         room=24,
     )
 
@@ -1119,20 +1122,19 @@
     sides = jnp.concatenate([seq[None], korder])
     levels = lax.dynamic_slice_in_dim(resolution, seq * 2, 2, 0)
 
-    shard = pack_dense(dense_in, dense_out, vectors.reshape(1, vec_len))
-    line = [shard] + [route.swap(shard, (m, m)) for m in route.direct]
+    right_shard, lo_shard = pack_dense(dense_in, dense_out, vectors.reshape(1, vec_len))
+    line = [right_shard] + [route.swap(right_shard, (m, m)) for m in route.direct]
+    lo_line = [lo_shard] + [route.swap(lo_shard, (m, m)) for m in route.direct]
     spat_own, x_send, g_send = pack_images(sides, spatial, spatial_bias.reshape(3, rows, 1), patches, out_grad)
     x_got = route.cross(x_send)
     g_got = route.cross(g_send)
     spat_got = route.cross(spat_own)
-    first_cols = HALF + VCOLS
     if fits:
-        right_blocks = route.widen_direct(stack(line, 0, first_cols, [x_send]))
-        lo_blocks = route.widen_direct(stack(line, first_cols, LO, [right_blocks[1]]))
+        right_blocks = route.widen_direct(stack(line, []))
+        lo_blocks = route.widen_direct(stack(lo_line, [right_blocks[1]]))
     else:
-        whole = jnp.concatenate(line, axis=0)
-        right_blocks = route.widen(whole[:, :first_cols])
-        lo_blocks = route.widen(whole[:, first_cols:])
+        right_blocks = route.widen(jnp.concatenate(line, axis=0))
+        lo_blocks = route.widen(jnp.concatenate(lo_line, axis=0))
     right_blocks = right_blocks + [route.cross(b) for b in right_blocks]
     lo_blocks = lo_blocks + [route.cross(b) for b in lo_blocks]
     if not fits:
@@ -1151,55 +1153,55 @@
     gate, hat, scale, spat, mm = gate_norm(levels, sides, vec, v, part, spat_own, spat_got, [])
     gs, gated, q, gb, wl, wo, sp_keep, sp_send, gsum = middle(ktable, levels, sides, vec, h, spat, gate, grad_out, lo_blocks)
     near, far = route.low[-1], route.low[0]
+    after = [[], [], [], []]
     if fits:
-        sp_terms = [sp_keep, route.cross(sp_send)]
-    lo_keep, lo_send, mixed_stay, mixed_away, gh = weight_grads(
-        ktable, levels, sides, vec, gated, q, gb, h, wl, wo, x, rows
-    )
+        sp_got = route.cross(sp_send)
+        sp_part = add_part([sp_keep, sp_got], 128, [])
+        sp_terms = [sp_keep, sp_got, route.swap(sp_part, near)]
+        after[0] = [sp_part]
+    lo_keep, lo_send, lo_up, mixed_stay, mixed_away, gh = weight_grads(
+        ktable, levels, sides, vec, gated, q, gb, h, wl, wo, x, rows, after[0]
+    )
+    if fits:
+        lo_up = route.cross(lo_up)
+        lo_terms = [lo_keep, route.cross(lo_send)]
+        sp_part = add_part(sp_terms, 64, [lo_keep])
+        sp_terms.append(route.swap(sp_part, far))
+        lo_part = add_part([lo_keep, lo_up], 128, [sp_part], [1, 0])
+        lo_terms.append(route.swap(lo_part, near))
+        after[1] = [lo_part]
     mixed_got = route.cross(mixed_away)
-    after = [[], []]
+    gp, gate_sum = gate_backward(vec, gs, mm, hat, slope, scale, after[1])
     if fits:
-        sp_part = add_part(sp_terms, 128, [])
-        sp_terms.append(route.swap(sp_part, near))
-        lo_terms = [lo_keep, route.cross(lo_send)]
-        after[0] = [sp_part]
-    gp, gate_sum = gate_backward(vec, gs, mm, hat, slope, scale, after[0])
+        sp_own, *sends = line_spread(sp_terms, gate_sum)
+        sp_got = [route.swap(p, (m, m)) for p, m in zip(sends, route.direct)]
+        after[2] = [sp_own]
+    gwr, ghb = in_grads(gp, h, weight_right, gh, after[2])
     if fits:
-        lo_part = add_part(lo_terms, 128, [gate_sum])
-        lo_terms.append(route.swap(lo_part, near))
-        sp_part = add_part(sp_terms, 64, [lo_part])
-        sp_terms.append(route.swap(sp_part, far))
-        after[1] = [sp_part]
-    gwr, ghb = in_grads(gp, h, weight_right, gh, after[1])
-    if fits:
-        after[0] = [sp_terms[-1]]
-    else:
-        after[0] = []
+        lo_part = add_part(lo_terms, 64, [gwr])
+        lo_terms.append(route.swap(lo_part, far))
+        after[3] = [lo_part]
     right_keep, right_send, right_up, grad_stay, grad_away = in_backward(
-        ktable, sides, vec, gsum, gate_sum, gwr, ghb, x, grad_out, rows, after[0]
+        ktable, sides, vec, gsum, gate_sum, gwr, ghb, x, grad_out, rows, after[3]
     )
     if fits:
         right_up = route.cross(right_up)
         right_terms = [right_keep, route.cross(right_send)]
         right_part = add_part([right_keep, right_up], 128, [], [1, 0])
         right_terms.append(route.swap(right_part, near))
-        sp_own, *sends = line_spread(sp_terms, right_part)
-        sp_got = [route.swap(p, (m, m)) for p, m in zip(sends, route.direct)]
-        lo_part = add_part(lo_terms, 64, [sp_own])
-        lo_terms.append(route.swap(lo_part, far))
-        right_part = add_part(right_terms, 64, [lo_part])
+        lo_own, *sends = line_parts(lo_terms, right_part)
+        lo_got = [route.swap(p, (m, m)) for p, m in zip(sends, route.direct)]
+        sp_sum = line_sum(sp_own, sp_got, lo_own)
+        spat_pieces = route.widen(sp_sum)
+        right_part = add_part(right_terms, 64, [sp_sum])
         right_terms.append(route.swap(right_part, far))
-        sp_sum = line_sum(sp_own, sp_got, right_part)
-        spat_pieces = route.widen(sp_sum)
-        lo_own, *sends = line_parts(lo_terms, sp_sum)
-        lo_got = [route.swap(p, (m, m)) for p, m in zip(sends, route.direct)]
-        right_own, *sends = line_parts(right_terms, lo_own)
+        right_own, *sends = line_parts(right_terms, right_part)
         right_got = [route.swap(p, (m, m)) for p, m in zip(sends, route.direct)]
         left_sum, *new_out = finish_out(lo_own, lo_got, dense_out, out_first, out_second, right_own)
         korder = order
         after = [left_sum]
     else:
-        both = jnp.concatenate([lo_keep, lo_send])
+        both = jnp.concatenate([lo_keep, lo_send, lo_up])
         outs = both[:, HALF:LO].reshape(DEVS, 16, 3, D).transpose(0, 2, 1, 3).reshape(ndev, out_rows, D)
         outs = jnp.take(outs, table, axis=0).reshape(HALF, D)
         out_sum = route.scatter(outs[: HALF // 2], outs[HALF // 2 :])

time: 146 us -> 150 us (1.027)
  starting transfers between devices: 40.3 us -> 42.9 us
    ppermute x27 -> x30, waiting for transfers between devices: 32.4 us -> 35.9 us  [swap(): return lax.ppermute(block, AXES, pairs)]
    ppermute x17 -> x18, waiting for transfers between devices: 4.73 us -> 1.91 us  [cross(): return lax.ppermute(block, AXES, pairs)]
    ppermute x27 -> x30, starting transfers between devices: 36.8 us -> 39.5 us  [swap(): return lax.ppermute(block, AXES, pairs)]
    unnamed x48 -> x46, local copies, waits for them, and re-layouts: 7.75 us -> 7.58 us
    ppermute x17 -> x18, starting transfers between devices: 3.47 us -> 3.39 us  [cross(): return lax.ppermute(block, AXES, pairs)]
  transfers between devices with their start and end apart: 44 -> 48, of which waited for: 10 -> 14; matrix products, arithmetic and copies ran while one was open for 5% -> 5% of each run, Pallas kernels for 22% -> 20%
where the time goes in v4:
time: 150 us
  Pallas kernels  57.7 us (38%)
  starting transfers between devices  42.9 us (29%)
  waiting for transfers between devices  37.8 us (25%)
  local copies, waits for them, and re-layouts  8.49 us (6%)
  other arithmetic  1.67 us (1%)
    pallas_call x15, Pallas kernels, call(): pl.pallas_call(kernel, out_shape=out_shape, in_specs=in_specs, out_specs=...  56.7 us
    ppermute x30, starting transfers between devices, swap(): return lax.ppermute(block, AXES, pairs)  39.5 us
    ppermute x30, waiting for transfers between devices, swap(): return lax.ppermute(block, AXES, pairs)  35.9 us
    unnamed x46, local copies, waits for them, and re-layouts  7.58 us
    ppermute x18, starting transfers between devices, cross(): return lax.ppermute(block, AXES, pairs)  3.39 us
  transfers between devices with their start and end apart: 48, of which 14 were waited for; matrix products, arithmetic and copies ran while one was open for 5% of the time, Pallas kernels for 20%

profile of v4, /device:TPU:0, one launch (start us, length us, event | category | flops | bytes accessed | tf_op | source)
XLA Modules:
  0.0 149.9 jit_solution(14873388484641740618)
XLA Ops:
  0.7 1.8 %shard_map.360 = (bf16[16,1792]{1,0:T(8,128)(2,1)}, bf16[16,3072]{1,0:T(8,128)(2,1)}) custom-call(f32[16,3072]{1,0:T(8,128)} %w_ref.3, f32[48,512]{1,0:T(8,128)} %w_ref.2, f32[1,240]{1,0:T(1,128)} %bitcast.7), custom_call_target="tpu_custom_call" | custom-call | flops 1000 | bytes 600000 | tf_op jit(solution)/shard_map/pallas_call | solution.py:211
  2.4 5.1 %collective-permute-start.4 = (bf16[16,1792]{1,0:T(8,128)(2,1)}, bf16[16,1792]{1,0:T(8,128)(2,1)S(1)}, u32[]{:S(2)}, u32[]{:S(2)}) collective-permute-start(bf16[16,1792]{1,0:T(8,128)(2,1)} %get-tuple-element.87.refs_0_), channel_id=1, source_target_pairs={{0,24},{1,25},{2,26},{3,27},{4,28},{5,29},{6,30},{7,31},{8,16},{9,... | collective-permute-start | bytes 172040 | tf_op jit(solution)/shard_map/ppermute | solution.py:64
  8.2 3.7 %collective-permute-start.15 = (bf16[16,3072]{1,0:T(8,128)(2,1)}, bf16[16,3072]{1,0:T(8,128)(2,1)S(1)}, u32[]{:S(2)}, u32[]{:S(2)}) collective-permute-start(bf16[16,3072]{1,0:T(8,128)(2,1)} %get-tuple-element.96.refs_0_), channel_id=1, source_target_pairs={{0,24},{1,25},{2,26},{3,27},{4,28},{5,29},{6,30},{7,31},{8,16},{9,... | collective-permute-start | bytes 294920 | tf_op jit(solution)/shard_map/ppermute | solution.py:64
  12.0 5.8 %collective-permute-done.3.refs_2_ = bf16[16,1792]{1,0:T(8,128)(2,1)S(1)} collective-permute-done((bf16[16,1792]{1,0:T(8,128)(2,1)}, bf16[16,1792]{1,0:T(8,128)(2,1)S(1)}, u32[]{:S(2)}, u32[]{:S(2)}) %collective-permute-start.3) | collective-permute-done | bytes 57376 | tf_op jit(solution)/shard_map/ppermute | solution.py:64
  19.3 2.4 %collective-permute-start.7 = (bf16[64,1792]{1,0:T(8,128)(2,1)S(1)}, bf16[64,1792]{1,0:T(8,128)(2,1)}, u32[]{:S(2)}, u32[]{:S(2)}) collective-permute-start(bf16[64,1792]{1,0:T(8,128)(2,1)S(1)} %shard_map.361.refs_0_), channel_id=1, source_target_pairs={{0,6},{1,7},{2,4},{3,5},{4,2},{5,3},{6,0},{7,1},{8,14},{9,15},{10,... | collective-permute-start | bytes 688136 | tf_op jit(solution)/shard_map/ppermute | solution.py:64
  26.4 1.5 %shard_map.359 = (bf16[3,162,384]{2,1,0:T(8,128)(2,1)S(1)}, bf16[2,162,512]{2,1,0:T(8,128)(2,1)}, bf16[2,162,512]{2,1,0:T(8,128)(2,1)}) custom-call(s32[33]{0:T(128)S(1)} %pad_add_fusion.1.sides_ref, f32[3,162,324]{2,1,0:T(8,128)S(1)} %copy-done, f32[3,162,1]{2,1,0:T(8,128)S(1)} %copy.47.b_ref, bf16[4,162,512]{2,1,0:T(8,128)(2,1)S(1)} %copy.50.x_ref.p_ref, ...), custom_call_target="tpu_custom_call" | custom-call | flops 1000 | bytes 3000000 | tf_op jit(solution)/shard_map/pallas_call | solution.py:211
  28.7 2.2 %collective-permute-done.13.refs_1_ = bf16[16,3072]{1,0:T(8,128)(2,1)S(1)} collective-permute-done((bf16[16,3072]{1,0:T(8,128)(2,1)S(1)}, bf16[16,3072]{1,0:T(8,128)(2,1)S(1)}, u32[]{:S(2)}, u32[]{:S(2)}) %collective-permute-start.13) | collective-permute-done | bytes 98336 | tf_op jit(solution)/shard_map/ppermute | solution.py:64
  31.5 1.9 %collective-permute-done.6.refs_2_ = bf16[64,1792]{1,0:T(8,128)(2,1)} collective-permute-done((bf16[64,1792]{1,0:T(8,128)(2,1)S(1)}, bf16[64,1792]{1,0:T(8,128)(2,1)}, u32[]{:S(2)}, u32[]{:S(2)}) %collective-permute-start.6) | collective-permute-done | bytes 229408 | tf_op jit(solution)/shard_map/ppermute | solution.py:64
  34.6 1.6 %collective-permute-start.18 = (bf16[64,3072]{1,0:T(8,128)(2,1)S(1)}, bf16[64,3072]{1,0:T(8,128)(2,1)S(1)}, u32[]{:S(2)}, u32[]{:S(2)}) collective-permute-start(bf16[64,3072]{1,0:T(8,128)(2,1)S(1)} %shard_map.364.refs_0_), channel_id=1, source_target_pairs={{0,6},{1,7},{2,4},{3,5},{4,2},{5,3},{6,0},{7,1},{8,14},{9,15},{10,... | collective-permute-start | bytes 1179656 | tf_op jit(solution)/shard_map/ppermute | solution.py:64
  38.1 10.7 %shard_map.362 = (bf16[672,512]{1,0:T(8,128)(2,1)S(1)}, bf16[672,512]{1,0:T(8,128)(2,1)S(1)}, bf16[672,512]{1,0:T(8,128)(2,1)S(1)}, f32[672,1536]{1,0:T(8,128)S(...) custom-call(s32[32]{0:T(128)S(1)} %get-tuple-element.191.table_ref, ...), custom_call_target="tpu_custom_call" | custom-call | flops 10000000000 | bytes 20000000 | tf_op jit(solution)/shard_map/pallas_call | solution.py:211
  48.9 6.0 %collective-permute-done.17.refs_2_ = bf16[64,3072]{1,0:T(8,128)(2,1)S(1)} collective-permute-done((bf16[64,3072]{1,0:T(8,128)(2,1)S(1)}, bf16[64,3072]{1,0:T(8,128)(2,1)S(1)}, u32[]{:S(2)}, u32[]{:S(2)}) %collective-permute-start.17) | collective-permute-done | bytes 393248 | tf_op jit(solution)/shard_map/ppermute | solution.py:64
  55.4 5.1 %shard_map.363 = (bf16[720,1536]{1,0:T(8,128)(2,1)S(1)}, bf16[672,1536]{1,0:T(8,128)(2,1)S(1)}, f32[672,128]{1,0:T(8,128)S(1)}, bf16[672,1536]{1,0:T(8,128)(2,1)S(1)}, bf16[2,336,384]{2,1,0:T(8,128)(2,1)S(1)}) custom-call(s32[2]{0:T(128)S(1)} %dynamic_slice.3.levels_ref, s32[33]{0:T(128)S(1)} %pad_add_fusion.1.sides_ref, ...), custom_call_target="tpu_custom_call" | custom-call | flops 6000000000 | bytes 12000000 | tf_op jit(solution)/shard_map/pallas_call | solution.py:211
  60.5 14.1 %shard_map.365 = (bf16[672,1536]{1,0:T(8,128)(2,1)S(1)}, bf16[672,1536]{1,0:T(8,128)(2,1)S(1)}, bf16[672,1536]{1,0:T(8,128)(2,1)S(1)}, bf16[672,512]{1,0:T(8,128...) custom-call(s32[32]{0:T(128)S(1)} %get-tuple-element.191.table_ref, ...), custom_call_target="tpu_custom_call" | custom-call | flops 8000000000 | bytes 16000000 | tf_op jit(solution)/shard_map/pallas_call | solution.py:211
  74.8 1.5 %collective-permute-done.23.refs_1_ = bf16[256,768]{1,0:T(8,128)(2,1)S(1)} collective-permute-done((bf16[256,768]{1,0:T(8,128)(2,1)S(1)}, bf16[256,768]{1,0:T(8,128)(2,1)S(1)}, u32[]{:S(2)}, u32[]{:S(2)}) %collective-permute-start.23) | collective-permute-done | bytes 393248 | tf_op jit(solution)/shard_map/ppermute | solution.py:71
  76.5 7.5 %shard_map.367 = (bf16[256,3072]{1,0:T(8,128)(2,1)S(1)}, bf16[128,3072]{1,0:T(8,128)(2,1)S(1)}, bf16[128,3072]{1,0:T(8,128)(2,1)S(1)}, bf16[2,162,512]{2,1,0:T(8...) custom-call(s32[32]{0:T(128)S(1)} %get-tuple-element.191.table_ref, ...), custom_call_target="tpu_custom_call" | custom-call | flops 5000000000 | bytes 15000000 | tf_op jit(solution)/shard_map/pallas_call | solution.py:211
  84.2 1.5 %collective-permute-start.26 = (bf16[128,768]{1,0:T(8,128)(2,1)S(1)}, bf16[128,768]{1,0:T(8,128)(2,1)S(1)}, u32[]{:S(2)}, u32[]{:S(2)}) collective-permute-start(bf16[128,768]{1,0:T(8,128)(2,1)S(1)} %shard_map.366.refs_0_), channel_id=1, source_target_pairs={{0,2},{1,5},{2,0},{3,7},{4,6},{5,1},{6,4},{7,3},{8,10},{9,13},{10,... | collective-permute-start | bytes 589832 | tf_op jit(solution)/shard_map/ppermute | solution.py:64
  85.8 4.2 %collective-permute-done.26.refs_2_ = bf16[128,768]{1,0:T(8,128)(2,1)S(1)} collective-permute-done((bf16[128,768]{1,0:T(8,128)(2,1)S(1)}, bf16[128,768]{1,0:T(8,128)(2,1)S(1)}, u32[]{:S(2)}, u32[]{:S(2)}) %collective-permute-start.26) | collective-permute-done | bytes 196640 | tf_op jit(solution)/shard_map/ppermute | solution.py:64
  90.2 1.6 %collective-permute-start.29 = (bf16[128,3072]{1,0:T(8,128)(2,1)S(1)}, bf16[128,3072]{1,0:T(8,128)(2,1)S(1)}, u32[]{:S(2)}, u32[]{:S(2)}) collective-permute-start(bf16[128,3072]{1,0:T(8,128)(2,1)S(1)} %shard_map.369.refs_0_), channel_id=1, source_target_pairs={{0,2},{1,5},{2,0},{3,7},{4,6},{5,1},{6,4},{7,3},{8,10},{9,13},{10,... | collective-permute-start | bytes 2359304 | tf_op jit(solution)/shard_map/ppermute | solution.py:64
  92.5 5.6 %shard_map.370 = (bf16[672,1536]{1,0:T(8,128)(2,1)S(1)}, f32[1,4608]{1,0:T(1,128)S(1)}) custom-call(f32[1,7680]{1,0:T(1,128)S(1)} %get-tuple-element.88.vec_ref, bf16[672,1536]{1,0:T(8,128)(2,1)S(1)} %get-tuple-element.108.gs_ref, bf16[2,336,384]{2,1,0:T(8,128)(2,1)S(1)} %get-tuple-element.109.mm_ref, bf16[672,1536]{1,0:T(8,128)(2,1)S(1)} %get-tuple-element.110.hat_ref, ...), custom_call_target="tpu_custom_call" | custom-call | flops 3000000000 | bytes 10000000 | tf_op jit(solution)/shard_map/pallas_call | solution.py:211
  98.2 2.9 %shard_map.372 = (bf16[512,1536]{1,0:T(8,128)(2,1)S(1)}, f32[672,512]{1,0:T(8,128)S(1)}) custom-call(bf16[672,1536]{1,0:T(8,128)(2,1)S(1)} %get-tuple-element.116.gp_ref, bf16[672,512]{1,0:T(8,128)(2,1)S(1)} %get-tuple-element.89.h_ref, bf16[512,1536]{1,0:T(8,128)(2,1)S(1)} %get-tuple-element.117.w_ref, f32[672,512]{1,0:T(8,128)S(1)} %get-tuple-element.118.gh_ref, ...), custom_call_target="tpu_custom_call" | custom-call | flops 3000000000 | bytes 8000000 | tf_op jit(solution)/shard_map/pallas_call | solution.py:211
  101.1 1.4 collective-permute-done.29.refs_2_
  102.7 2.8 %shard_map.374 = (bf16[256,1792]{1,0:T(8,128)(2,1)S(1)}, bf16[128,1792]{1,0:T(8,128)(2,1)S(1)}, bf16[128,1792]{1,0:T(8,128)(2,1)S(1)}, bf16[2,162,512]{2,1,0:T(8,128)(2,1)S(1)}, bf16[2,162,512]{2,1,0:T(8,128)(2,1)S(1)}) custom-call(s32[32]{0:T(128)S(1)} %get-tuple-element.191.table_ref, s32[33]{0:T(128)S(1)} %pad_add_fusion.1.sides_ref, ...), custom_call_target="tpu_custom_call" | custom-call | flops 2000000000 | bytes 6000000 | tf_op jit(solution)/shard_map/pallas_call | solution.py:211
  108.9 4.5 %collective-permute-done.34.a_ref = bf16[64,768]{1,0:T(8,128)(2,1)S(1)} collective-permute-done((bf16[64,768]{1,0:T(8,128)(2,1)S(1)}, bf16[64,768]{1,0:T(8,128)(2,1)S(1)}, u32[]{:S(2)}, u32[]{:S(2)}) %collective-permute-start.34) | collective-permute-done | bytes 98336 | tf_op jit(solution)/shard_map/ppermute | solution.py:64
  114.7 2.8 %collective-permute-done.37.refs_3_ = bf16[64,3072]{1,0:T(8,128)(2,1)S(1)} collective-permute-done((bf16[64,3072]{1,0:T(8,128)(2,1)S(1)}, bf16[64,3072]{1,0:T(8,128)(2,1)S(1)}, u32[]{:S(2)}, u32[]{:S(2)}) %collective-permute-start.37) | collective-permute-done | bytes 393248 | tf_op jit(solution)/shard_map/ppermute | solution.py:64
  117.5 2.6 %collective-permute-start.36 = (bf16[64,768]{1,0:T(8,128)(2,1)S(1)}, bf16[64,768]{1,0:T(8,128)(2,1)S(1)}, u32[]{:S(2)}, u32[]{:S(2)}) collective-permute-start(bf16[64,768]{1,0:T(8,128)(2,1)S(1)} %get-tuple-element.130), channel_id=1, source_target_pairs={{0,24},{1,25},{2,26},{3,27},{4,28},{5,29},{6,30},{7,31},{8,16},{9,... | collective-permute-start | bytes 294920 | tf_op jit(solution)/shard_map/ppermute | solution.py:64
  122.0 2.8 %collective-permute-done.36.c_ref = bf16[64,768]{1,0:T(8,128)(2,1)S(1)} collective-permute-done((bf16[64,768]{1,0:T(8,128)(2,1)S(1)}, bf16[64,768]{1,0:T(8,128)(2,1)S(1)}, u32[]{:S(2)}, u32[]{:S(2)}) %collective-permute-start.36) | collective-permute-done | bytes 98336 | tf_op jit(solution)/shard_map/ppermute | solution.py:64
  129.1 2.3 %collective-permute-done.45.refs_1_ = bf16[64,768]{1,0:T(8,128)(2,1)S(1)} collective-permute-done((bf16[64,768]{1,0:T(8,128)(2,1)S(1)}, bf16[64,768]{1,0:T(8,128)(2,1)S(1)}, u32[]{:S(2)}, u32[]{:S(2)}) %collective-permute-start.45) | collective-permute-done | bytes 98336 | tf_op jit(solution)/shard_map/ppermute | solution.py:64
  131.4 1.9 %collective-permute-start.46 = (bf16[64,768]{1,0:T(8,128)(2,1)S(1)}, bf16[64,768]{1,0:T(8,128)(2,1)S(1)}, u32[]{:S(2)}, u32[]{:S(2)}) collective-permute-start(bf16[64,768]{1,0:T(8,128)(2,1)S(1)} %shard_map.377.refs_3_.refs_0_), channel_id=1, source_target_pairs={{0,2},{1,5},{2,0},{3,7},{4,6},{5,1},{6,4},{7,3},{8,10},{9,13},{10,... | collective-permute-start | bytes 294920 | tf_op jit(solution)/shard_map/ppermute | solution.py:64
  133.3 1.7 %collective-permute-done.38.refs_3_ = bf16[64,1792]{1,0:T(8,128)(2,1)S(1)} collective-permute-done((bf16[64,1792]{1,0:T(8,128)(2,1)S(1)}, bf16[64,1792]{1,0:T(8,128)(2,1)S(1)}, u32[]{:S(2)}, u32[]{:S(2)}) %collective-permute-start.38) | collective-permute-done | bytes 229408 | tf_op jit(solution)/shard_map/ppermute | solution.py:64
  135.0 2.6 %collective-permute-start.47 = (bf16[64,768]{1,0:T(8,128)(2,1)S(1)}, bf16[64,768]{1,0:T(8,128)(2,1)S(1)}, u32[]{:S(2)}, u32[]{:S(2)}) collective-permute-start(bf16[64,768]{1,0:T(8,128)(2,1)S(1)} %collective-permute-done.45.refs_1_), channel_id=1, source_target_pairs={{0,2},{1,5},{2,0},{3,7},{4,6},{5,1},{6,4},{7,3},{8,10},{9,13},{10,... | collective-permute-start | bytes 294920 | tf_op jit(solution)/shard_map/ppermute | solution.py:64
  138.6 2.5 %collective-permute-start.40 = (bf16[16,1792]{1,0:T(8,128)(2,1)S(1)}, bf16[16,1792]{1,0:T(8,128)(2,1)S(1)}, u32[]{:S(2)}, u32[]{:S(2)}) collective-permute-start(bf16[16,1792]{1,0:T(8,128)(2,1)S(1)} %get-tuple-element.134), channel_id=1, source_target_pairs={{0,16},{1,17},{2,18},{3,19},{4,20},{5,21},{6,22},{7,23},{8,24},{9,... | collective-permute-start | bytes 172040 | tf_op jit(solution)/shard_map/ppermute | solution.py:64
  144.4 2.8 %shard_map.381 = (f32[3,162,324]{2,1,0:T(8,128)}, f32[3,162,324]{2,1,0:T(8,128)}, f32[3,162,324]{2,1,0:T(8,128)}, f32[3,162]{1,0:T(4,128)}, f32[3,162]{1,0:T(4,128)}, /*index=5*/f32[3,162]{1,0:T(4,128)}) custom-call(s32[16]{0:T(128)S(1)} %get-tuple-element.193.order_ref, bf16[64,768]{1,0:T(8,128)(2,1)S(1)} %shard_map.377.refs_3_.refs_0_, ...), custom_call_target="tpu_custom_call" | custom-call | flops 10000000 | bytes 6000000 | tf_op jit(solution)/shard_map/pallas_call | solution.py:211
  (144 shorter events, 31.0 us)
Async XLA Ops:
  2.4 9.5 %collective-permute-start.4 = (bf16[16,1792]{1,0:T(8,128)(2,1)}, bf16[16,1792]{1,0:T(8,128)(2,1)S(1)}, u32[]{:S(2)}, u32[]{:S(2)}) collective-permute-start(bf16[16,1792]{1,0:T(8,128)(2,1)} %get-tuple-element.87.refs_0_), channel_id=1, source_target_pairs={{0,24},{1,25},{2,26},{3,27},{4,28},{5,29},{6,30},{7,31},{8,16},{9,... | collective-permute-start | bytes 172040 | tf_op jit(solution)/shard_map/ppermute | solution.py:64
  7.6 10.2 %collective-permute-start.3 = (bf16[16,1792]{1,0:T(8,128)(2,1)}, bf16[16,1792]{1,0:T(8,128)(2,1)S(1)}, u32[]{:S(2)}, u32[]{:S(2)}) collective-permute-start(bf16[16,1792]{1,0:T(8,128)(2,1)} %get-tuple-element.87.refs_0_), channel_id=1, source_target_pairs={{0,16},{1,17},{2,18},{3,19},{4,20},{5,21},{6,22},{7,23},{8,24},{9,... | collective-permute-start | bytes 172040 | tf_op jit(solution)/shard_map/ppermute | solution.py:64
  7.6 10.2 %collective-permute-start.2 = (bf16[16,1792]{1,0:T(8,128)(2,1)}, bf16[16,1792]{1,0:T(8,128)(2,1)S(1)}, u32[]{:S(2)}, u32[]{:S(2)}) collective-permute-start(bf16[16,1792]{1,0:T(8,128)(2,1)} %get-tuple-element.87.refs_0_), channel_id=1, source_target_pairs={{0,8},{1,9},{2,10},{3,11},{4,12},{5,13},{6,14},{7,15},{8,0},{9,1},... | collective-permute-start | bytes 172040 | tf_op jit(solution)/shard_map/ppermute | solution.py:64
  8.2 14.1 %collective-permute-start.15 = (bf16[16,3072]{1,0:T(8,128)(2,1)}, bf16[16,3072]{1,0:T(8,128)(2,1)S(1)}, u32[]{:S(2)}, u32[]{:S(2)}) collective-permute-start(bf16[16,3072]{1,0:T(8,128)(2,1)} %get-tuple-element.96.refs_0_), channel_id=1, source_target_pairs={{0,24},{1,25},{2,26},{3,27},{4,28},{5,29},{6,30},{7,31},{8,16},{9,... | collective-permute-start | bytes 294920 | tf_op jit(solution)/shard_map/ppermute | solution.py:64
  11.9 14.3 %collective-permute-start.14 = (bf16[16,3072]{1,0:T(8,128)(2,1)}, bf16[16,3072]{1,0:T(8,128)(2,1)S(1)}, u32[]{:S(2)}, u32[]{:S(2)}) collective-permute-start(bf16[16,3072]{1,0:T(8,128)(2,1)} %get-tuple-element.96.refs_0_), channel_id=1, source_target_pairs={{0,16},{1,17},{2,18},{3,19},{4,20},{5,21},{6,22},{7,23},{8,24},{9,... | collective-permute-start | bytes 294920 | tf_op jit(solution)/shard_map/ppermute | solution.py:64
  18.6 12.3 %collective-permute-start.8 = (bf16[64,1792]{1,0:T(8,128)(2,1)S(1)}, bf16[64,1792]{1,0:T(8,128)(2,1)}, u32[]{:S(2)}, u32[]{:S(2)}) collective-permute-start(bf16[64,1792]{1,0:T(8,128)(2,1)S(1)} %shard_map.361.refs_0_), channel_id=1, source_target_pairs={{0,1},{1,0},{2,3},{3,2},{4,5},{5,4},{6,7},{7,6},{8,9},{9,8},{10,11... | collective-permute-start | bytes 688136 | tf_op jit(solution)/shard_map/ppermute | solution.py:71
  19.3 12.1 %collective-permute-start.7 = (bf16[64,1792]{1,0:T(8,128)(2,1)S(1)}, bf16[64,1792]{1,0:T(8,128)(2,1)}, u32[]{:S(2)}, u32[]{:S(2)}) collective-permute-start(bf16[64,1792]{1,0:T(8,128)(2,1)S(1)} %shard_map.361.refs_0_), channel_id=1, source_target_pairs={{0,6},{1,7},{2,4},{3,5},{4,2},{5,3},{6,0},{7,1},{8,14},{9,15},{10,... | collective-permute-start | bytes 688136 | tf_op jit(solution)/shard_map/ppermute | solution.py:64
  21.8 11.6 %collective-permute-start.6 = (bf16[64,1792]{1,0:T(8,128)(2,1)S(1)}, bf16[64,1792]{1,0:T(8,128)(2,1)}, u32[]{:S(2)}, u32[]{:S(2)}) collective-permute-start(bf16[64,1792]{1,0:T(8,128)(2,1)S(1)} %shard_map.361.refs_0_), channel_id=1, source_target_pairs={{0,2},{1,5},{2,0},{3,7},{4,6},{5,1},{6,4},{7,3},{8,10},{9,13},{10,... | collective-permute-start | bytes 688136 | tf_op jit(solution)/shard_map/ppermute | solution.py:64
  22.3 11.0 %collective-permute-start.5 = (bf16[64,1792]{1,0:T(8,128)(2,1)S(1)}, bf16[64,1792]{1,0:T(8,128)(2,1)S(1)}, u32[]{:S(2)}, u32[]{:S(2)}) collective-permute-start(bf16[64,1792]{1,0:T(8,128)(2,1)S(1)} %shard_map.361.refs_0_), channel_id=1, source_target_pairs={{0,4},{1,3},{2,6},{3,1},{4,0},{5,7},{6,2},{7,5},{8,12},{9,11},{10,... | collective-permute-start | bytes 688136 | tf_op jit(solution)/shard_map/ppermute | solution.py:64
  34.0 21.4 %collective-permute-start.12 = (bf16[3,162,384]{2,1,0:T(8,128)(2,1)}, bf16[3,162,384]{2,1,0:T(8,128)(2,1)S(1)}, u32[]{:S(2)}, u32[]{:S(2)}) collective-permute-start(bf16[3,162,384]{2,1,0:T(8,128)(2,1)} %copy-done.15), channel_id=1, source_target_pairs={{0,1},{1,0},{2,3},{3,2},{4,5},{5,4},{6,7},{7,6},{8,9},{9,8},{10,11... | collective-permute-start | bytes 1119752 | tf_op jit(solution)/shard_map/ppermute | solution.py:71
  34.1 26.4 %collective-permute-start.19 = (bf16[64,3072]{1,0:T(8,128)(2,1)S(1)}, bf16[64,3072]{1,0:T(8,128)(2,1)S(1)}, u32[]{:S(2)}, u32[]{:S(2)}) collective-permute-start(bf16[64,3072]{1,0:T(8,128)(2,1)S(1)} %shard_map.364.refs_0_), channel_id=1, source_target_pairs={{0,1},{1,0},{2,3},{3,2},{4,5},{5,4},{6,7},{7,6},{8,9},{9,8},{10,11... | collective-permute-start | bytes 1179656 | tf_op jit(solution)/shard_map/ppermute | solution.py:71
  34.6 14.2 %collective-permute-start.18 = (bf16[64,3072]{1,0:T(8,128)(2,1)S(1)}, bf16[64,3072]{1,0:T(8,128)(2,1)S(1)}, u32[]{:S(2)}, u32[]{:S(2)}) collective-permute-start(bf16[64,3072]{1,0:T(8,128)(2,1)S(1)} %shard_map.364.refs_0_), channel_id=1, source_target_pairs={{0,6},{1,7},{2,4},{3,5},{4,2},{5,3},{6,0},{7,1},{8,14},{9,15},{10,... | collective-permute-start | bytes 1179656 | tf_op jit(solution)/shard_map/ppermute | solution.py:64
  36.2 18.7 %collective-permute-start.17 = (bf16[64,3072]{1,0:T(8,128)(2,1)S(1)}, bf16[64,3072]{1,0:T(8,128)(2,1)S(1)}, u32[]{:S(2)}, u32[]{:S(2)}) collective-permute-start(bf16[64,3072]{1,0:T(8,128)(2,1)S(1)} %shard_map.364.refs_0_), channel_id=1, source_target_pairs={{0,2},{1,5},{2,0},{3,7},{4,6},{5,1},{6,4},{7,3},{8,10},{9,13},{10,... | collective-permute-start | bytes 1179656 | tf_op jit(solution)/shard_map/ppermute | solution.py:64
  36.9 18.1 %collective-permute-start.16 = (bf16[64,3072]{1,0:T(8,128)(2,1)S(1)}, bf16[64,3072]{1,0:T(8,128)(2,1)S(1)}, u32[]{:S(2)}, u32[]{:S(2)}) collective-permute-start(bf16[64,3072]{1,0:T(8,128)(2,1)S(1)} %shard_map.364.refs_0_), channel_id=1, source_target_pairs={{0,4},{1,3},{2,6},{3,1},{4,0},{5,7},{6,2},{7,5},{8,12},{9,11},{10,... | collective-permute-start | bytes 1179656 | tf_op jit(solution)/shard_map/ppermute | solution.py:64
  48.8 11.7 %collective-permute-start.22 = (bf16[64,3072]{1,0:T(8,128)(2,1)S(1)}, bf16[64,3072]{1,0:T(8,128)(2,1)S(1)}, u32[]{:S(2)}, u32[]{:S(2)}) collective-permute-start(bf16[64,3072]{1,0:T(8,128)(2,1)S(1)} %collective-permute-done.18.refs_3_), channel_id=1, source_target_pairs={{0,1},{1,0},{2,3},{3,2},{4,5},{5,4},{6,7},{7,6},{8,9},{9,8},{10,11... | collective-permute-start | bytes 1179656 | tf_op jit(solution)/shard_map/ppermute | solution.py:71
  85.8 15.4 %collective-permute-start.28 = (bf16[128,3072]{1,0:T(8,128)(2,1)S(1)}, bf16[128,3072]{1,0:T(8,128)(2,1)S(1)}, u32[]{:S(2)}, u32[]{:S(2)}) collective-permute-start(bf16[128,3072]{1,0:T(8,128)(2,1)S(1)} %get-tuple-element.122), channel_id=1, source_target_pairs={{0,1},{1,0},{2,3},{3,2},{4,5},{5,4},{6,7},{7,6},{8,9},{9,8},{10,11... | collective-permute-start | bytes 2359304 | tf_op jit(solution)/shard_map/ppermute | solution.py:71
  90.2 12.4 %collective-permute-start.29 = (bf16[128,3072]{1,0:T(8,128)(2,1)S(1)}, bf16[128,3072]{1,0:T(8,128)(2,1)S(1)}, u32[]{:S(2)}, u32[]{:S(2)}) collective-permute-start(bf16[128,3072]{1,0:T(8,128)(2,1)S(1)} %shard_map.369.refs_0_), channel_id=1, source_target_pairs={{0,2},{1,5},{2,0},{3,7},{4,6},{5,1},{6,4},{7,3},{8,10},{9,13},{10,... | collective-permute-start | bytes 2359304 | tf_op jit(solution)/shard_map/ppermute | solution.py:64
  91.7 6.4 %collective-permute-start.27 = (bf16[64,768]{1,0:T(8,128)(2,1)S(1)}, bf16[64,768]{1,0:T(8,128)(2,1)S(1)}, u32[]{:S(2)}, u32[]{:S(2)}) collective-permute-start(bf16[64,768]{1,0:T(8,128)(2,1)S(1)} %shard_map.368.refs_2_), channel_id=1, source_target_pairs={{0,4},{1,3},{2,6},{3,1},{4,0},{5,7},{6,2},{7,5},{8,12},{9,11},{10,... | collective-permute-start | bytes 294920 | tf_op jit(solution)/shard_map/ppermute | solution.py:64
  106.1 11.4 %collective-permute-start.37 = (bf16[64,3072]{1,0:T(8,128)(2,1)S(1)}, bf16[64,3072]{1,0:T(8,128)(2,1)S(1)}, u32[]{:S(2)}, u32[]{:S(2)}) collective-permute-start(bf16[64,3072]{1,0:T(8,128)(2,1)S(1)} %shard_map.373.refs_0_), channel_id=1, source_target_pairs={{0,4},{1,3},{2,6},{3,1},{4,0},{5,7},{6,2},{7,5},{8,12},{9,11},{10,... | collective-permute-start | bytes 1179656 | tf_op jit(solution)/shard_map/ppermute | solution.py:64
  107.1 18.9 %collective-permute-start.31 = (bf16[128,1792]{1,0:T(8,128)(2,1)S(1)}, bf16[128,1792]{1,0:T(8,128)(2,1)S(1)}, u32[]{:S(2)}, u32[]{:S(2)}) collective-permute-start(bf16[128,1792]{1,0:T(8,128)(2,1)S(1)} %get-tuple-element.126), channel_id=1, source_target_pairs={{0,1},{1,0},{2,3},{3,2},{4,5},{5,4},{6,7},{7,6},{8,9},{9,8},{10,11... | collective-permute-start | bytes 1376264 | tf_op jit(solution)/shard_map/ppermute | solution.py:71
  107.6 19.2 %collective-permute-start.33 = (bf16[128,1792]{1,0:T(8,128)(2,1)S(1)}, bf16[128,1792]{1,0:T(8,128)(2,1)S(1)}, u32[]{:S(2)}, u32[]{:S(2)}) collective-permute-start(bf16[128,1792]{1,0:T(8,128)(2,1)S(1)} %shard_map.375.refs_4_), channel_id=1, source_target_pairs={{0,2},{1,5},{2,0},{3,7},{4,6},{5,1},{6,4},{7,3},{8,10},{9,13},{10,... | collective-permute-start | bytes 1376264 | tf_op jit(solution)/shard_map/ppermute | solution.py:64
  108.8 19.0 %collective-permute-start.30 = (bf16[2,162,512]{2,1,0:T(8,128)(2,1)S(1)}, bf16[2,162,512]{2,1,0:T(8,128)(2,1)S(1)}, u32[]{:S(2)}, u32[]{:S(2)}) collective-permute-start(bf16[2,162,512]{2,1,0:T(8,128)(2,1)S(1)} %get-tuple-element.124), channel_id=1, source_target_pairs={{0,1},{1,0},{2,3},{3,2},{4,5},{5,4},{6,7},{7,6},{8,9},{9,8},{10,11... | collective-permute-start | bytes 995336 | tf_op jit(solution)/shard_map/ppermute | solution.py:71
  113.4 8.5 %collective-permute-start.35 = (bf16[64,768]{1,0:T(8,128)(2,1)S(1)}, bf16[64,768]{1,0:T(8,128)(2,1)S(1)}, u32[]{:S(2)}, u32[]{:S(2)}) collective-permute-start(bf16[64,768]{1,0:T(8,128)(2,1)S(1)} %get-tuple-element.129), channel_id=1, source_target_pairs={{0,16},{1,17},{2,18},{3,19},{4,20},{5,21},{6,22},{7,23},{8,24},{9,... | collective-permute-start | bytes 294920 | tf_op jit(solution)/shard_map/ppermute | solution.py:64
  117.5 7.2 %collective-permute-start.36 = (bf16[64,768]{1,0:T(8,128)(2,1)S(1)}, bf16[64,768]{1,0:T(8,128)(2,1)S(1)}, u32[]{:S(2)}, u32[]{:S(2)}) collective-permute-start(bf16[64,768]{1,0:T(8,128)(2,1)S(1)} %get-tuple-element.130), channel_id=1, source_target_pairs={{0,24},{1,25},{2,26},{3,27},{4,28},{5,29},{6,30},{7,31},{8,16},{9,... | collective-permute-start | bytes 294920 | tf_op jit(solution)/shard_map/ppermute | solution.py:64
  122.0 15.8 %collective-permute-start.42 = (bf16[16,3072]{1,0:T(8,128)(2,1)S(1)}, bf16[16,3072]{1,0:T(8,128)(2,1)S(1)}, u32[]{:S(2)}, u32[]{:S(2)}) collective-permute-start(bf16[16,3072]{1,0:T(8,128)(2,1)S(1)} %get-tuple-element.136), channel_id=1, source_target_pairs={{0,8},{1,9},{2,10},{3,11},{4,12},{5,13},{6,14},{7,15},{8,0},{9,1},... | collective-permute-start | bytes 294920 | tf_op jit(solution)/shard_map/ppermute | solution.py:64
  124.7 13.9 %collective-permute-start.43 = (bf16[16,3072]{1,0:T(8,128)(2,1)S(1)}, bf16[16,3072]{1,0:T(8,128)(2,1)S(1)}, u32[]{:S(2)}, u32[]{:S(2)}) collective-permute-start(bf16[16,3072]{1,0:T(8,128)(2,1)S(1)} %get-tuple-element.137), channel_id=1, source_target_pairs={{0,16},{1,17},{2,18},{3,19},{4,20},{5,21},{6,22},{7,23},{8,24},{9,... | collective-permute-start | bytes 294920 | tf_op jit(solution)/shard_map/ppermute | solution.py:64
  126.0 15.1 %collective-permute-start.44 = (bf16[16,3072]{1,0:T(8,128)(2,1)S(1)}, bf16[16,3072]{1,0:T(8,128)(2,1)S(1)}, u32[]{:S(2)}, u32[]{:S(2)}) collective-permute-start(bf16[16,3072]{1,0:T(8,128)(2,1)S(1)} %get-tuple-element.138), channel_id=1, source_target_pairs={{0,24},{1,25},{2,26},{3,27},{4,28},{5,29},{6,30},{7,31},{8,16},{9,... | collective-permute-start | bytes 294920 | tf_op jit(solution)/shard_map/ppermute | solution.py:64
  127.9 7.1 %collective-permute-start.38 = (bf16[64,1792]{1,0:T(8,128)(2,1)S(1)}, bf16[64,1792]{1,0:T(8,128)(2,1)S(1)}, u32[]{:S(2)}, u32[]{:S(2)}) collective-permute-start(bf16[64,1792]{1,0:T(8,128)(2,1)S(1)} %shard_map.378.refs_4_), channel_id=1, source_target_pairs={{0,4},{1,3},{2,6},{3,1},{4,0},{5,7},{6,2},{7,5},{8,12},{9,11},{10,... | collective-permute-start | bytes 688136 | tf_op jit(solution)/shard_map/ppermute | solution.py:64
  131.4 12.9 %collective-permute-start.46 = (bf16[64,768]{1,0:T(8,128)(2,1)S(1)}, bf16[64,768]{1,0:T(8,128)(2,1)S(1)}, u32[]{:S(2)}, u32[]{:S(2)}) collective-permute-start(bf16[64,768]{1,0:T(8,128)(2,1)S(1)} %shard_map.377.refs_3_.refs_0_), channel_id=1, source_target_pairs={{0,2},{1,5},{2,0},{3,7},{4,6},{5,1},{6,4},{7,3},{8,10},{9,13},{10,... | collective-permute-start | bytes 294920 | tf_op jit(solution)/shard_map/ppermute | solution.py:64
  135.0 9.3 %collective-permute-start.47 = (bf16[64,768]{1,0:T(8,128)(2,1)S(1)}, bf16[64,768]{1,0:T(8,128)(2,1)S(1)}, u32[]{:S(2)}, u32[]{:S(2)}) collective-permute-start(bf16[64,768]{1,0:T(8,128)(2,1)S(1)} %collective-permute-done.45.refs_1_), channel_id=1, source_target_pairs={{0,2},{1,5},{2,0},{3,7},{4,6},{5,1},{6,4},{7,3},{8,10},{9,13},{10,... | collective-permute-start | bytes 294920 | tf_op jit(solution)/shard_map/ppermute | solution.py:64
  137.7 9.4 %collective-permute-start.39 = (bf16[16,1792]{1,0:T(8,128)(2,1)S(1)}, bf16[16,1792]{1,0:T(8,128)(2,1)S(1)}, u32[]{:S(2)}, u32[]{:S(2)}) collective-permute-start(bf16[16,1792]{1,0:T(8,128)(2,1)S(1)} %get-tuple-element.133), channel_id=1, source_target_pairs={{0,8},{1,9},{2,10},{3,11},{4,12},{5,13},{6,14},{7,15},{8,0},{9,1},... | collective-permute-start | bytes 172040 | tf_op jit(solution)/shard_map/ppermute | solution.py:64
  138.6 8.6 %collective-permute-start.40 = (bf16[16,1792]{1,0:T(8,128)(2,1)S(1)}, bf16[16,1792]{1,0:T(8,128)(2,1)S(1)}, u32[]{:S(2)}, u32[]{:S(2)}) collective-permute-start(bf16[16,1792]{1,0:T(8,128)(2,1)S(1)} %get-tuple-element.134), channel_id=1, source_target_pairs={{0,16},{1,17},{2,18},{3,19},{4,20},{5,21},{6,22},{7,23},{8,24},{9,... | collective-permute-start | bytes 172040 | tf_op jit(solution)/shard_map/ppermute | solution.py:64
  (37 other events, 246.0 us)

commit v5 on v4

--- a/solution.py
+++ b/solution.py
@@ -634,13 +634,11 @@
     )
 
 
-def weight_grads(table, levels, sides, vec, gated, q, gb, h, wl, wo, x, half, after):
+def out_grads(gated, gb, after):
     count = len(after)
 
-    def kernel(
-        table_ref, levels_ref, sides_ref, vec_ref, t_ref, q_ref, gb_ref, h_ref, wl_ref, wo_ref, x_ref, *refs
-    ):
-        keep, send, send_up, stay_ref, away_ref, gh_ref, branch, gwo, gwl = refs[count:]
+    def kernel(t_ref, gb_ref, *refs):
+        gwo = refs[count]
 
         def out_tile(n, carry):
             cols = pl.ds(pl.multiple_of(n * TILE, TILE), TILE)
@@ -648,6 +646,19 @@
             return carry
 
         lax.fori_loop(0, HALF // TILE, out_tile, 0)
+
+    return call(
+        kernel, sds((HALF, D), BF), [VM] * 2 + [HB] * count, [], 1000000000, 5000000, gated, gb, *after, room=10
+    )
+
+
+def weight_grads(table, levels, sides, vec, gated, q, gwo, h, wl, wo, x, half, after):
+    count = len(after)
+
+    def kernel(
+        table_ref, levels_ref, sides_ref, vec_ref, t_ref, q_ref, gwo, h_ref, wl_ref, wo_ref, x_ref, *refs
+    ):
+        keep, send, send_up, stay_ref, away_ref, gh_ref, branch, gwl = refs[count:]
 
         def in_tile(n, carry):
             cols = pl.ds(pl.multiple_of(n * TILE, TILE), TILE)
@@ -676,7 +687,7 @@
         kernel,
         (payload, part, part, pair, pair, sds((ROWS, D), F32)),
         [SM] * 3 + [VM] * 8 + [HB] * count,
-        [pltpu.VMEM((ROWS, D), F32), pltpu.VMEM((HALF, D), BF), pltpu.VMEM((D, HALF), BF)],
+        [pltpu.VMEM((ROWS, D), F32), pltpu.VMEM((D, HALF), BF)],
         5000000000,
         15000000,
         table,
@@ -685,7 +696,7 @@
         vec,
         gated,
         q,
-        gb,
+        gwo,
         h,
         wl,
         wo,
@@ -902,7 +913,7 @@
     count = len(terms)
 
     def kernel(*refs):
-        own, outs = refs[count + 1], refs[count + 2 :]
+        own, *outs = refs[count + len(after) :]
         for m in range(4):
             rows = slice(16 * m, 16 * (m + 1))
             value = refs[0][rows, :].astype(F32)
@@ -919,50 +930,41 @@
         kernel,
         grid=(1,),
         out_shape=[sds((16, cols), F32)] + [sds((16, cols), BF)] * 3,
-        in_specs=[block] * count + [HB],
+        in_specs=[block] * count + [HB] * len(after),
         out_specs=[one] * 4,
         compiler_params=pltpu.CompilerParams(vmem_limit_bytes=8 * MIB),
         cost_estimate=pl.CostEstimate(flops=1000000, bytes_accessed=3000000, transcendentals=0),
-    )(*terms, after)
-
-
-def line_sum(total, got, after):
-    rows = total.shape[0]
-
-    def kernel(own_ref, a_ref, b_ref, c_ref, after_ref, out_ref):
-        near = own_ref[...].astype(F32) + a_ref[...].astype(F32)
-        far = b_ref[...].astype(F32) + c_ref[...].astype(F32)
-        out_ref[...] = (near + far).astype(BF)
-
-    return call(kernel, sds((rows, SPC), BF), [VM] * 4 + [HB], [], 1000000, 500000, total, *got, after)
-
-
-def line_spread(terms, after):
+    )(*terms, *after)
+
+
+def line_turn(terms, flip, after):
     count = len(terms)
     cols = terms[0].shape[1]
 
     def kernel(*refs):
-        outs = refs[count + 1 :]
+        outs = refs[count + len(after) :]
         for m in range(4):
             rows = slice(16 * m, 16 * (m + 1))
             value = refs[0][rows, :].astype(F32)
             for t in refs[1:count]:
                 value = value + t[rows, :].astype(F32)
             value = value.astype(BF)
-            for j in range(4):
-                at = 16 * (m ^ j)
-                outs[j][at : at + 16, :] = value
+            outs[0][rows, :] = value
+            if flip:
+                at = 16 * (m ^ flip)
+                outs[1][at : at + 16, :] = value
 
     block = pl.BlockSpec((64, cols), lambda i: (0, 0))
+    number = 2 if flip else 1
     return pl.pallas_call(
         kernel,
         grid=(1,),
-        out_shape=[sds((64, cols), BF)] * 4,
-        in_specs=[block] * count + [HB],
-        out_specs=[block] * 4,
+        out_shape=[sds((64, cols), BF)] * number,
+        in_specs=[block] * count + [HB] * len(after),
+        out_specs=[block] * number,
         compiler_params=pltpu.CompilerParams(vmem_limit_bytes=8 * MIB),
         cost_estimate=pl.CostEstimate(flops=1000000, bytes_accessed=1000000, transcendentals=0),
-    )(*terms, after)
+    )(*terms, *after)
 
 
 def finish_out(own, got, weight, first, second, after):
@@ -1153,49 +1155,55 @@
     gate, hat, scale, spat, mm = gate_norm(levels, sides, vec, v, part, spat_own, spat_got, [])
     gs, gated, q, gb, wl, wo, sp_keep, sp_send, gsum = middle(ktable, levels, sides, vec, h, spat, gate, grad_out, lo_blocks)
     near, far = route.low[-1], route.low[0]
-    after = [[], [], [], []]
+    after = [[] for _ in range(5)]
     if fits:
         sp_got = route.cross(sp_send)
         sp_part = add_part([sp_keep, sp_got], 128, [])
         sp_terms = [sp_keep, sp_got, route.swap(sp_part, near)]
         after[0] = [sp_part]
+    gwo = out_grads(gated, gb, after[0])
+    if fits:
+        sp_part = add_part(sp_terms, 64, [gwo])
+        sp_terms.append(route.swap(sp_part, far))
+        after[1] = [sp_part]
     lo_keep, lo_send, lo_up, mixed_stay, mixed_away, gh = weight_grads(
-        ktable, levels, sides, vec, gated, q, gb, h, wl, wo, x, rows, after[0]
-    )
+        ktable, levels, sides, vec, gated, q, gwo, h, wl, wo, x, rows, after[1]
+    )
+    mixed_got = route.cross(mixed_away)
     if fits:
         lo_up = route.cross(lo_up)
         lo_terms = [lo_keep, route.cross(lo_send)]
-        sp_part = add_part(sp_terms, 64, [lo_keep])
-        sp_terms.append(route.swap(sp_part, far))
-        lo_part = add_part([lo_keep, lo_up], 128, [sp_part], [1, 0])
+        sp_own, sp_out = line_turn(sp_terms, 1, [lo_keep])
+        sp_terms = [sp_own, route.swap(sp_out, (route.direct[0],) * 2)]
+        lo_part = add_part([lo_keep, lo_up], 128, [sp_own], [1, 0])
         lo_terms.append(route.swap(lo_part, near))
-        after[1] = [lo_part]
-    mixed_got = route.cross(mixed_away)
-    gp, gate_sum = gate_backward(vec, gs, mm, hat, slope, scale, after[1])
+        after[2] = [lo_part]
+    gp, gate_sum = gate_backward(vec, gs, mm, hat, slope, scale, after[2])
     if fits:
-        sp_own, *sends = line_spread(sp_terms, gate_sum)
-        sp_got = [route.swap(p, (m, m)) for p, m in zip(sends, route.direct)]
-        after[2] = [sp_own]
-    gwr, ghb = in_grads(gp, h, weight_right, gh, after[2])
+        sp_own, sp_out = line_turn(sp_terms, 2, [gate_sum])
+        sp_terms = [sp_own, route.swap(sp_out, (route.direct[1],) * 2)]
+        after[3] = [sp_own, mixed_got]
+    gwr, ghb = in_grads(gp, h, weight_right, gh, after[3])
     if fits:
         lo_part = add_part(lo_terms, 64, [gwr])
         lo_terms.append(route.swap(lo_part, far))
-        after[3] = [lo_part]
+        after[4] = [lo_part]
     right_keep, right_send, right_up, grad_stay, grad_away = in_backward(
-        ktable, sides, vec, gsum, gate_sum, gwr, ghb, x, grad_out, rows, after[3]
-    )
+        ktable, sides, vec, gsum, gate_sum, gwr, ghb, x, grad_out, rows, after[4]
+    )
+    grad_got = route.cross(grad_away)
     if fits:
         right_up = route.cross(right_up)
         right_terms = [right_keep, route.cross(right_send)]
         right_part = add_part([right_keep, right_up], 128, [], [1, 0])
         right_terms.append(route.swap(right_part, near))
-        lo_own, *sends = line_parts(lo_terms, right_part)
+        (sp_sum,) = line_turn(sp_terms, 0, [right_part])
+        spat_pieces = route.widen(sp_sum)
+        lo_own, *sends = line_parts(lo_terms, [sp_sum, grad_got])
         lo_got = [route.swap(p, (m, m)) for p, m in zip(sends, route.direct)]
-        sp_sum = line_sum(sp_own, sp_got, lo_own)
-        spat_pieces = route.widen(sp_sum)
-        right_part = add_part(right_terms, 64, [sp_sum])
+        right_part = add_part(right_terms, 64, [lo_own])
         right_terms.append(route.swap(right_part, far))
-        right_own, *sends = line_parts(right_terms, right_part)
+        right_own, *sends = line_parts(right_terms, [right_part])
         right_got = [route.swap(p, (m, m)) for p, m in zip(sends, route.direct)]
         left_sum, *new_out = finish_out(lo_own, lo_got, dense_out, out_first, out_second, right_own)
         korder = order
@@ -1231,7 +1239,7 @@
         return jnp.concatenate([jnp.where(seq == 0, stays, came), jnp.where(seq == 0, came, stays)], axis=0)
 
     mixed = whole_images(mixed_stay, mixed_got)
-    patches_grad = whole_images(grad_stay, route.cross(grad_away))
+    patches_grad = whole_images(grad_stay, grad_got)
     spat_new = spatial_update(
         korder, spat_pieces, spatial, spat_first, spat_second, spatial_bias, bias_first, bias_second, after
     )

time: 150 us -> 149 us (level)
  starting transfers between devices: 42.9 us -> 40.4 us
  local copies, waits for them, and re-layouts: 8.49 us -> 10.7 us
    ppermute x30 -> x29, starting transfers between devices: 39.5 us -> 36.8 us  [swap(): return lax.ppermute(block, AXES, pairs)]
    ppermute x30 -> x29, waiting for transfers between devices: 35.9 us -> 33.6 us  [swap(): return lax.ppermute(block, AXES, pairs)]
    unnamed x46 -> x50, local copies, waits for them, and re-layouts: 7.58 us -> 9.78 us
  transfers between devices with their start and end apart: 48 -> 47, of which waited for: 14 -> 12; matrix products, arithmetic and copies ran while one was open for 5% -> 5% of each run, Pallas kernels for 20% -> 22%
where the time goes in v5:
time: 149 us
  Pallas kernels  58.2 us (39%)
  starting transfers between devices  40.4 us (27%)
  waiting for transfers between devices  36.5 us (24%)
  local copies, waits for them, and re-layouts  10.7 us (7%)
  other arithmetic  1.67 us (1%)
    pallas_call x15, Pallas kernels, call(): pl.pallas_call(kernel, out_shape=out_shape, in_specs=in_specs, out_specs=...  57.1 us
    ppermute x29, starting transfers between devices, swap(): return lax.ppermute(block, AXES, pairs)  36.8 us
    ppermute x29, waiting for transfers between devices, swap(): return lax.ppermute(block, AXES, pairs)  33.6 us
    unnamed x50, local copies, waits for them, and re-layouts  9.78 us
    ppermute x18, starting transfers between devices, cross(): return lax.ppermute(block, AXES, pairs)  3.58 us
  transfers between devices with their start and end apart: 47, of which 12 were waited for; matrix products, arithmetic and copies ran while one was open for 5% of the time, Pallas kernels for 22%

profile of v5, /device:TPU:0, one launch (start us, length us, event | category | flops | bytes accessed | tf_op | source)
XLA Modules:
  0.0 148.7 jit_solution(9371997794262045012)
XLA Ops:
  0.7 1.8 %shard_map.360 = (bf16[16,1792]{1,0:T(8,128)(2,1)}, bf16[16,3072]{1,0:T(8,128)(2,1)}) custom-call(f32[16,3072]{1,0:T(8,128)} %w_ref.3, f32[48,512]{1,0:T(8,128)} %w_ref.2, f32[1,240]{1,0:T(1,128)} %bitcast.7), custom_call_target="tpu_custom_call" | custom-call | flops 1000 | bytes 600000 | tf_op jit(solution)/shard_map/pallas_call | solution.py:211
  2.4 5.1 %collective-permute-start.4 = (bf16[16,1792]{1,0:T(8,128)(2,1)}, bf16[16,1792]{1,0:T(8,128)(2,1)S(1)}, u32[]{:S(2)}, u32[]{:S(2)}) collective-permute-start(bf16[16,1792]{1,0:T(8,128)(2,1)} %get-tuple-element.87.refs_0_), channel_id=1, source_target_pairs={{0,24},{1,25},{2,26},{3,27},{4,28},{5,29},{6,30},{7,31},{8,16},{9,... | collective-permute-start | bytes 172040 | tf_op jit(solution)/shard_map/ppermute | solution.py:64
  8.2 3.7 %collective-permute-start.15 = (bf16[16,3072]{1,0:T(8,128)(2,1)}, bf16[16,3072]{1,0:T(8,128)(2,1)S(1)}, u32[]{:S(2)}, u32[]{:S(2)}) collective-permute-start(bf16[16,3072]{1,0:T(8,128)(2,1)} %get-tuple-element.96.refs_0_), channel_id=1, source_target_pairs={{0,24},{1,25},{2,26},{3,27},{4,28},{5,29},{6,30},{7,31},{8,16},{9,... | collective-permute-start | bytes 294920 | tf_op jit(solution)/shard_map/ppermute | solution.py:64
  12.0 5.8 %collective-permute-done.3.refs_2_ = bf16[16,1792]{1,0:T(8,128)(2,1)S(1)} collective-permute-done((bf16[16,1792]{1,0:T(8,128)(2,1)}, bf16[16,1792]{1,0:T(8,128)(2,1)S(1)}, u32[]{:S(2)}, u32[]{:S(2)}) %collective-permute-start.3) | collective-permute-done | bytes 57376 | tf_op jit(solution)/shard_map/ppermute | solution.py:64
  19.3 2.4 %collective-permute-start.7 = (bf16[64,1792]{1,0:T(8,128)(2,1)S(1)}, bf16[64,1792]{1,0:T(8,128)(2,1)}, u32[]{:S(2)}, u32[]{:S(2)}) collective-permute-start(bf16[64,1792]{1,0:T(8,128)(2,1)S(1)} %shard_map.361.refs_0_), channel_id=1, source_target_pairs={{0,6},{1,7},{2,4},{3,5},{4,2},{5,3},{6,0},{7,1},{8,14},{9,15},{10,... | collective-permute-start | bytes 688136 | tf_op jit(solution)/shard_map/ppermute | solution.py:64
  26.4 1.5 %shard_map.359 = (bf16[3,162,384]{2,1,0:T(8,128)(2,1)S(1)}, bf16[2,162,512]{2,1,0:T(8,128)(2,1)}, bf16[2,162,512]{2,1,0:T(8,128)(2,1)}) custom-call(s32[33]{0:T(128)S(1)} %pad_add_fusion.1.sides_ref, f32[3,162,324]{2,1,0:T(8,128)S(1)} %copy-done, f32[3,162,1]{2,1,0:T(8,128)S(1)} %copy.47.b_ref, bf16[4,162,512]{2,1,0:T(8,128)(2,1)S(1)} %copy.50.x_ref.p_ref, ...), custom_call_target="tpu_custom_call" | custom-call | flops 1000 | bytes 3000000 | tf_op jit(solution)/shard_map/pallas_call | solution.py:211
  27.9 3.0 %collective-permute-done.13.refs_1_ = bf16[16,3072]{1,0:T(8,128)(2,1)S(1)} collective-permute-done((bf16[16,3072]{1,0:T(8,128)(2,1)S(1)}, bf16[16,3072]{1,0:T(8,128)(2,1)S(1)}, u32[]{:S(2)}, u32[]{:S(2)}) %collective-permute-start.13) | collective-permute-done | bytes 98336 | tf_op jit(solution)/shard_map/ppermute | solution.py:64
  31.5 1.9 %collective-permute-done.6.refs_2_ = bf16[64,1792]{1,0:T(8,128)(2,1)} collective-permute-done((bf16[64,1792]{1,0:T(8,128)(2,1)S(1)}, bf16[64,1792]{1,0:T(8,128)(2,1)}, u32[]{:S(2)}, u32[]{:S(2)}) %collective-permute-start.6) | collective-permute-done | bytes 229408 | tf_op jit(solution)/shard_map/ppermute | solution.py:64
  34.6 1.5 collective-permute-start.18
  38.1 11.2 %shard_map.362 = (bf16[672,512]{1,0:T(8,128)(2,1)S(1)}, bf16[672,512]{1,0:T(8,128)(2,1)S(1)}, bf16[672,512]{1,0:T(8,128)(2,1)S(1)}, f32[672,1536]{1,0:T(8,128)S(...) custom-call(s32[32]{0:T(128)S(1)} %get-tuple-element.191.table_ref, ...), custom_call_target="tpu_custom_call" | custom-call | flops 10000000000 | bytes 20000000 | tf_op jit(solution)/shard_map/pallas_call | solution.py:211
  49.4 5.5 %collective-permute-done.17.refs_2_ = bf16[64,3072]{1,0:T(8,128)(2,1)S(1)} collective-permute-done((bf16[64,3072]{1,0:T(8,128)(2,1)S(1)}, bf16[64,3072]{1,0:T(8,128)(2,1)S(1)}, u32[]{:S(2)}, u32[]{:S(2)}) %collective-permute-start.17) | collective-permute-done | bytes 393248 | tf_op jit(solution)/shard_map/ppermute | solution.py:64
  55.4 5.1 %shard_map.363 = (bf16[720,1536]{1,0:T(8,128)(2,1)S(1)}, bf16[672,1536]{1,0:T(8,128)(2,1)S(1)}, f32[672,128]{1,0:T(8,128)S(1)}, bf16[672,1536]{1,0:T(8,128)(2,1)S(1)}, bf16[2,336,384]{2,1,0:T(8,128)(2,1)S(1)}) custom-call(s32[2]{0:T(128)S(1)} %dynamic_slice.3.levels_ref, s32[33]{0:T(128)S(1)} %pad_add_fusion.1.sides_ref, ...), custom_call_target="tpu_custom_call" | custom-call | flops 6000000000 | bytes 12000000 | tf_op jit(solution)/shard_map/pallas_call | solution.py:211
  60.5 1.3 copy-done.17
  61.8 1.6 %copy-done.18 = bf16[720,1536]{1,0:T(8,128)(2,1)S(1)} copy-done((bf16[720,1536]{1,0:T(8,128)(2,1)S(1)}, bf16[720,1536]{1,0:T(8,128)(2,1)}, u32[]{:S(2)}) %copy-start.18) | copy-done | bytes 2211864
  63.4 14.1 %shard_map.365 = (bf16[672,1536]{1,0:T(8,128)(2,1)S(1)}, bf16[672,1536]{1,0:T(8,128)(2,1)S(1)}, bf16[672,1536]{1,0:T(8,128)(2,1)S(1)}, bf16[672,512]{1,0:T(8,128...) custom-call(s32[32]{0:T(128)S(1)} %get-tuple-element.191.table_ref, ...), custom_call_target="tpu_custom_call" | custom-call | flops 8000000000 | bytes 16000000 | tf_op jit(solution)/shard_map/pallas_call | solution.py:211
  77.8 1.5 %collective-permute-done.23.refs_1_ = bf16[256,768]{1,0:T(8,128)(2,1)S(1)} collective-permute-done((bf16[256,768]{1,0:T(8,128)(2,1)S(1)}, bf16[256,768]{1,0:T(8,128)(2,1)S(1)}, u32[]{:S(2)}, u32[]{:S(2)}) %collective-permute-start.23) | collective-permute-done | bytes 393248 | tf_op jit(solution)/shard_map/ppermute | solution.py:71
  79.4 1.4 collective-permute-start.24
  80.7 2.4 %shard_map.367.refs_3_.gwo = bf16[1536,512]{1,0:T(8,128)(2,1)S(1)} custom-call(bf16[672,1536]{1,0:T(8,128)(2,1)S(1)} %get-tuple-element.97.t_ref, bf16[672,512]{1,0:T(8,128)(2,1)S(1)} %get-tuple-element.99.gb_ref, bf16[128,768]{1,0:T(8,128)(2,1)S(1)} %shard_map.366.refs_0_), custom_call_target="tpu_custom_call" | custom-call | flops 1000000000 | bytes 5000000 | tf_op jit(solution)/shard_map/pallas_call | solution.py:211
  83.2 2.0 %collective-permute-done.24.refs_2_ = bf16[128,768]{1,0:T(8,128)(2,1)S(1)} collective-permute-done((bf16[128,768]{1,0:T(8,128)(2,1)S(1)}, bf16[128,768]{1,0:T(8,128)(2,1)S(1)}, u32[]{:S(2)}, u32[]{:S(2)}) %collective-permute-start.24) | collective-permute-done | bytes 196640 | tf_op jit(solution)/shard_map/ppermute | solution.py:64
  85.2 5.1 %shard_map.369 = (bf16[256,3072]{1,0:T(8,128)(2,1)S(1)}, bf16[128,3072]{1,0:T(8,128)(2,1)S(1)}, bf16[128,3072]{1,0:T(8,128)(2,1)S(1)}, bf16[2,162,512]{2,1,0:T(8...) custom-call(s32[32]{0:T(128)S(1)} %get-tuple-element.191.table_ref, ...), custom_call_target="tpu_custom_call" | custom-call | flops 5000000000 | bytes 15000000 | tf_op jit(solution)/shard_map/pallas_call | solution.py:211
  91.9 3.2 %collective-permute-done.27.refs_3_ = bf16[64,768]{1,0:T(8,128)(2,1)S(1)} collective-permute-done((bf16[64,768]{1,0:T(8,128)(2,1)S(1)}, bf16[64,768]{1,0:T(8,128)(2,1)S(1)}, u32[]{:S(2)}, u32[]{:S(2)}) %collective-permute-start.27) | collective-permute-done | bytes 98336 | tf_op jit(solution)/shard_map/ppermute | solution.py:64
  95.3 1.4 collective-permute-start.30
  96.7 5.6 %shard_map.372 = (bf16[672,1536]{1,0:T(8,128)(2,1)S(1)}, f32[1,4608]{1,0:T(1,128)S(1)}) custom-call(f32[1,7680]{1,0:T(1,128)S(1)} %get-tuple-element.88.vec_ref, bf16[672,1536]{1,0:T(8,128)(2,1)S(1)} %get-tuple-element.108.gs_ref, bf16[2,336,384]{2,1,0:T(8,128)(2,1)S(1)} %get-tuple-element.109.mm_ref, bf16[672,1536]{1,0:T(8,128)(2,1)S(1)} %get-tuple-element.110.hat_ref, ...), custom_call_target="tpu_custom_call" | custom-call | flops 3000000000 | bytes 10000000 | tf_op jit(solution)/shard_map/pallas_call | solution.py:211
  102.4 2.9 %shard_map.374 = (bf16[512,1536]{1,0:T(8,128)(2,1)S(1)}, f32[672,512]{1,0:T(8,128)S(1)}) custom-call(bf16[672,1536]{1,0:T(8,128)(2,1)S(1)} %get-tuple-element.117.gp_ref, bf16[672,512]{1,0:T(8,128)(2,1)S(1)} %get-tuple-element.89.h_ref, bf16[512,1536]{1,0:T(8,128)(2,1)S(1)} %get-tuple-element.118.w_ref, f32[672,512]{1,0:T(8,128)S(1)} %get-tuple-element.119.gh_ref, ...), custom_call_target="tpu_custom_call" | custom-call | flops 3000000000 | bytes 8000000 | tf_op jit(solution)/shard_map/pallas_call | solution.py:211
  105.4 2.0 %collective-permute-done.30.refs_2_ = bf16[128,3072]{1,0:T(8,128)(2,1)S(1)} collective-permute-done((bf16[128,3072]{1,0:T(8,128)(2,1)S(1)}, bf16[128,3072]{1,0:T(8,128)(2,1)S(1)}, u32[]{:S(2)}, u32[]{:S(2)}) %collective-permute-start.30) | collective-permute-done | bytes 786464 | tf_op jit(solution)/shard_map/ppermute | solution.py:64
  107.5 2.8 %shard_map.376 = (bf16[256,1792]{1,0:T(8,128)(2,1)S(1)}, bf16[128,1792]{1,0:T(8,128)(2,1)S(1)}, bf16[128,1792]{1,0:T(8,128)(2,1)S(1)}, bf16[2,162,512]{2,1,0:T(8,128)(2,1)S(1)}, bf16[2,162,512]{2,1,0:T(8,128)(2,1)S(1)}) custom-call(s32[32]{0:T(128)S(1)} %get-tuple-element.191.table_ref, s32[33]{0:T(128)S(1)} %pad_add_fusion.1.sides_ref, ...), custom_call_target="tpu_custom_call" | custom-call | flops 2000000000 | bytes 6000000 | tf_op jit(solution)/shard_map/pallas_call | solution.py:211
  112.3 1.4 collective-permute-start.34
  116.7 6.3 %collective-permute-done.36.refs_1_ = bf16[64,768]{1,0:T(8,128)(2,1)S(1)} collective-permute-done((bf16[64,768]{1,0:T(8,128)(2,1)S(1)}, bf16[64,768]{1,0:T(8,128)(2,1)S(1)}, u32[]{:S(2)}, u32[]{:S(2)}) %collective-permute-start.36) | collective-permute-done | bytes 98336 | tf_op jit(solution)/shard_map/ppermute | solution.py:64
  124.6 3.1 %collective-permute-start.42 = (bf16[16,3072]{1,0:T(8,128)(2,1)S(1)}, bf16[16,3072]{1,0:T(8,128)(2,1)S(1)}, u32[]{:S(2)}, u32[]{:S(2)}) collective-permute-start(bf16[16,3072]{1,0:T(8,128)(2,1)S(1)} %get-tuple-element.137), channel_id=1, source_target_pairs={{0,16},{1,17},{2,18},{3,19},{4,20},{5,21},{6,22},{7,23},{8,24},{9,... | collective-permute-start | bytes 294920 | tf_op jit(solution)/shard_map/ppermute | solution.py:64
  131.5 4.0 %collective-permute-done.37.refs_3_ = bf16[64,1792]{1,0:T(8,128)(2,1)S(1)} collective-permute-done((bf16[64,1792]{1,0:T(8,128)(2,1)S(1)}, bf16[64,1792]{1,0:T(8,128)(2,1)S(1)}, u32[]{:S(2)}, u32[]{:S(2)}) %collective-permute-start.37) | collective-permute-done | bytes 229408 | tf_op jit(solution)/shard_map/ppermute | solution.py:64
  136.7 3.2 %collective-permute-start.39 = (bf16[16,1792]{1,0:T(8,128)(2,1)S(1)}, bf16[16,1792]{1,0:T(8,128)(2,1)S(1)}, u32[]{:S(2)}, u32[]{:S(2)}) collective-permute-start(bf16[16,1792]{1,0:T(8,128)(2,1)S(1)} %get-tuple-element.134), channel_id=1, source_target_pairs={{0,16},{1,17},{2,18},{3,19},{4,20},{5,21},{6,22},{7,23},{8,24},{9,... | collective-permute-start | bytes 172040 | tf_op jit(solution)/shard_map/ppermute | solution.py:64
  143.2 2.8 %shard_map.383 = (f32[3,162,324]{2,1,0:T(8,128)}, f32[3,162,324]{2,1,0:T(8,128)}, f32[3,162,324]{2,1,0:T(8,128)}, f32[3,162]{1,0:T(4,128)}, f32[3,162]{1,0:T(4,128)}, /*index=5*/f32[3,162]{1,0:T(4,128)}) custom-call(s32[16]{0:T(128)S(1)} %get-tuple-element.193.order_ref, bf16[64,768]{1,0:T(8,128)(2,1)S(1)} %shard_map.378.refs_4_.refs_0_, ...), custom_call_target="tpu_custom_call" | custom-call | flops 10000000 | bytes 6000000 | tf_op jit(solution)/shard_map/pallas_call | solution.py:211
  (148 shorter events, 31.0 us)
Async XLA Ops:
  2.4 9.5 %collective-permute-start.4 = (bf16[16,1792]{1,0:T(8,128)(2,1)}, bf16[16,1792]{1,0:T(8,128)(2,1)S(1)}, u32[]{:S(2)}, u32[]{:S(2)}) collective-permute-start(bf16[16,1792]{1,0:T(8,128)(2,1)} %get-tuple-element.87.refs_0_), channel_id=1, source_target_pairs={{0,24},{1,25},{2,26},{3,27},{4,28},{5,29},{6,30},{7,31},{8,16},{9,... | collective-permute-start | bytes 172040 | tf_op jit(solution)/shard_map/ppermute | solution.py:64
  7.6 10.2 %collective-permute-start.3 = (bf16[16,1792]{1,0:T(8,128)(2,1)}, bf16[16,1792]{1,0:T(8,128)(2,1)S(1)}, u32[]{:S(2)}, u32[]{:S(2)}) collective-permute-start(bf16[16,1792]{1,0:T(8,128)(2,1)} %get-tuple-element.87.refs_0_), channel_id=1, source_target_pairs={{0,16},{1,17},{2,18},{3,19},{4,20},{5,21},{6,22},{7,23},{8,24},{9,... | collective-permute-start | bytes 172040 | tf_op jit(solution)/shard_map/ppermute | solution.py:64
  7.6 10.2 %collective-permute-start.2 = (bf16[16,1792]{1,0:T(8,128)(2,1)}, bf16[16,1792]{1,0:T(8,128)(2,1)S(1)}, u32[]{:S(2)}, u32[]{:S(2)}) collective-permute-start(bf16[16,1792]{1,0:T(8,128)(2,1)} %get-tuple-element.87.refs_0_), channel_id=1, source_target_pairs={{0,8},{1,9},{2,10},{3,11},{4,12},{5,13},{6,14},{7,15},{8,0},{9,1},... | collective-permute-start | bytes 172040 | tf_op jit(solution)/shard_map/ppermute | solution.py:64
  8.2 14.1 %collective-permute-start.15 = (bf16[16,3072]{1,0:T(8,128)(2,1)}, bf16[16,3072]{1,0:T(8,128)(2,1)S(1)}, u32[]{:S(2)}, u32[]{:S(2)}) collective-permute-start(bf16[16,3072]{1,0:T(8,128)(2,1)} %get-tuple-element.96.refs_0_), channel_id=1, source_target_pairs={{0,24},{1,25},{2,26},{3,27},{4,28},{5,29},{6,30},{7,31},{8,16},{9,... | collective-permute-start | bytes 294920 | tf_op jit(solution)/shard_map/ppermute | solution.py:64
  11.9 14.3 %collective-permute-start.14 = (bf16[16,3072]{1,0:T(8,128)(2,1)}, bf16[16,3072]{1,0:T(8,128)(2,1)S(1)}, u32[]{:S(2)}, u32[]{:S(2)}) collective-permute-start(bf16[16,3072]{1,0:T(8,128)(2,1)} %get-tuple-element.96.refs_0_), channel_id=1, source_target_pairs={{0,16},{1,17},{2,18},{3,19},{4,20},{5,21},{6,22},{7,23},{8,24},{9,... | collective-permute-start | bytes 294920 | tf_op jit(solution)/shard_map/ppermute | solution.py:64
  18.6 12.3 %collective-permute-start.8 = (bf16[64,1792]{1,0:T(8,128)(2,1)S(1)}, bf16[64,1792]{1,0:T(8,128)(2,1)S(1)}, u32[]{:S(2)}, u32[]{:S(2)}) collective-permute-start(bf16[64,1792]{1,0:T(8,128)(2,1)S(1)} %shard_map.361.refs_0_), channel_id=1, source_target_pairs={{0,1},{1,0},{2,3},{3,2},{4,5},{5,4},{6,7},{7,6},{8,9},{9,8},{10,11... | collective-permute-start | bytes 688136 | tf_op jit(solution)/shard_map/ppermute | solution.py:71
  19.3 12.1 %collective-permute-start.7 = (bf16[64,1792]{1,0:T(8,128)(2,1)S(1)}, bf16[64,1792]{1,0:T(8,128)(2,1)}, u32[]{:S(2)}, u32[]{:S(2)}) collective-permute-start(bf16[64,1792]{1,0:T(8,128)(2,1)S(1)} %shard_map.361.refs_0_), channel_id=1, source_target_pairs={{0,6},{1,7},{2,4},{3,5},{4,2},{5,3},{6,0},{7,1},{8,14},{9,15},{10,... | collective-permute-start | bytes 688136 | tf_op jit(solution)/shard_map/ppermute | solution.py:64
  21.8 11.6 %collective-permute-start.6 = (bf16[64,1792]{1,0:T(8,128)(2,1)S(1)}, bf16[64,1792]{1,0:T(8,128)(2,1)}, u32[]{:S(2)}, u32[]{:S(2)}) collective-permute-start(bf16[64,1792]{1,0:T(8,128)(2,1)S(1)} %shard_map.361.refs_0_), channel_id=1, source_target_pairs={{0,2},{1,5},{2,0},{3,7},{4,6},{5,1},{6,4},{7,3},{8,10},{9,13},{10,... | collective-permute-start | bytes 688136 | tf_op jit(solution)/shard_map/ppermute | solution.py:64
  22.3 11.0 %collective-permute-start.5 = (bf16[64,1792]{1,0:T(8,128)(2,1)S(1)}, bf16[64,1792]{1,0:T(8,128)(2,1)S(1)}, u32[]{:S(2)}, u32[]{:S(2)}) collective-permute-start(bf16[64,1792]{1,0:T(8,128)(2,1)S(1)} %shard_map.361.refs_0_), channel_id=1, source_target_pairs={{0,4},{1,3},{2,6},{3,1},{4,0},{5,7},{6,2},{7,5},{8,12},{9,11},{10,... | collective-permute-start | bytes 688136 | tf_op jit(solution)/shard_map/ppermute | solution.py:64
  34.0 21.4 %collective-permute-start.12 = (bf16[3,162,384]{2,1,0:T(8,128)(2,1)}, bf16[3,162,384]{2,1,0:T(8,128)(2,1)S(1)}, u32[]{:S(2)}, u32[]{:S(2)}) collective-permute-start(bf16[3,162,384]{2,1,0:T(8,128)(2,1)} %copy-done.15), channel_id=1, source_target_pairs={{0,1},{1,0},{2,3},{3,2},{4,5},{5,4},{6,7},{7,6},{8,9},{9,8},{10,11... | collective-permute-start | bytes 1119752 | tf_op jit(solution)/shard_map/ppermute | solution.py:71
  34.1 27.7 %collective-permute-start.19 = (bf16[64,3072]{1,0:T(8,128)(2,1)S(1)}, bf16[64,3072]{1,0:T(8,128)(2,1)S(1)}, u32[]{:S(2)}, u32[]{:S(2)}) collective-permute-start(bf16[64,3072]{1,0:T(8,128)(2,1)S(1)} %shard_map.364.refs_0_), channel_id=1, source_target_pairs={{0,1},{1,0},{2,3},{3,2},{4,5},{5,4},{6,7},{7,6},{8,9},{9,8},{10,11... | collective-permute-start | bytes 1179656 | tf_op jit(solution)/shard_map/ppermute | solution.py:71
  34.6 14.7 %collective-permute-start.18 = (bf16[64,3072]{1,0:T(8,128)(2,1)S(1)}, bf16[64,3072]{1,0:T(8,128)(2,1)S(1)}, u32[]{:S(2)}, u32[]{:S(2)}) collective-permute-start(bf16[64,3072]{1,0:T(8,128)(2,1)S(1)} %shard_map.364.refs_0_), channel_id=1, source_target_pairs={{0,6},{1,7},{2,4},{3,5},{4,2},{5,3},{6,0},{7,1},{8,14},{9,15},{10,... | collective-permute-start | bytes 1179656 | tf_op jit(solution)/shard_map/ppermute | solution.py:64
  36.0 18.8 %collective-permute-start.17 = (bf16[64,3072]{1,0:T(8,128)(2,1)S(1)}, bf16[64,3072]{1,0:T(8,128)(2,1)S(1)}, u32[]{:S(2)}, u32[]{:S(2)}) collective-permute-start(bf16[64,3072]{1,0:T(8,128)(2,1)S(1)} %shard_map.364.refs_0_), channel_id=1, source_target_pairs={{0,2},{1,5},{2,0},{3,7},{4,6},{5,1},{6,4},{7,3},{8,10},{9,13},{10,... | collective-permute-start | bytes 1179656 | tf_op jit(solution)/shard_map/ppermute | solution.py:64
  37.0 18.1 %collective-permute-start.16 = (bf16[64,3072]{1,0:T(8,128)(2,1)S(1)}, bf16[64,3072]{1,0:T(8,128)(2,1)S(1)}, u32[]{:S(2)}, u32[]{:S(2)}) collective-permute-start(bf16[64,3072]{1,0:T(8,128)(2,1)S(1)} %shard_map.364.refs_0_), channel_id=1, source_target_pairs={{0,4},{1,3},{2,6},{3,1},{4,0},{5,7},{6,2},{7,5},{8,12},{9,11},{10,... | collective-permute-start | bytes 1179656 | tf_op jit(solution)/shard_map/ppermute | solution.py:64
  49.3 12.5 %collective-permute-start.22 = (bf16[64,3072]{1,0:T(8,128)(2,1)S(1)}, bf16[64,3072]{1,0:T(8,128)(2,1)S(1)}, u32[]{:S(2)}, u32[]{:S(2)}) collective-permute-start(bf16[64,3072]{1,0:T(8,128)(2,1)S(1)} %collective-permute-done.18.refs_3_), channel_id=1, source_target_pairs={{0,1},{1,0},{2,3},{3,2},{4,5},{5,4},{6,7},{7,6},{8,9},{9,8},{10,11... | collective-permute-start | bytes 1179656 | tf_op jit(solution)/shard_map/ppermute | solution.py:71
  54.8 7.0 %collective-permute-start.21 = (bf16[64,3072]{1,0:T(8,128)(2,1)S(1)}, bf16[64,3072]{1,0:T(8,128)(2,1)S(1)}, u32[]{:S(2)}, u32[]{:S(2)}) collective-permute-start(bf16[64,3072]{1,0:T(8,128)(2,1)S(1)} %collective-permute-done.17.refs_2_), channel_id=1, source_target_pairs={{0,1},{1,0},{2,3},{3,2},{4,5},{5,4},{6,7},{7,6},{8,9},{9,8},{10,11... | collective-permute-start | bytes 1179656 | tf_op jit(solution)/shard_map/ppermute | solution.py:71
  55.0 6.8 %collective-permute-start.20 = (bf16[64,3072]{1,0:T(8,128)(2,1)S(1)}, bf16[64,3072]{1,0:T(8,128)(2,1)S(1)}, u32[]{:S(2)}, u32[]{:S(2)}) collective-permute-start(bf16[64,3072]{1,0:T(8,128)(2,1)S(1)} %collective-permute-done.16.refs_1_), channel_id=1, source_target_pairs={{0,1},{1,0},{2,3},{3,2},{4,5},{5,4},{6,7},{7,6},{8,9},{9,8},{10,11... | collective-permute-start | bytes 1179656 | tf_op jit(solution)/shard_map/ppermute | solution.py:71
  91.5 13.8 %collective-permute-start.29 = (bf16[128,3072]{1,0:T(8,128)(2,1)S(1)}, bf16[128,3072]{1,0:T(8,128)(2,1)S(1)}, u32[]{:S(2)}, u32[]{:S(2)}) collective-permute-start(bf16[128,3072]{1,0:T(8,128)(2,1)S(1)} %get-tuple-element.124), channel_id=1, source_target_pairs={{0,1},{1,0},{2,3},{3,2},{4,5},{5,4},{6,7},{7,6},{8,9},{9,8},{10,11... | collective-permute-start | bytes 2359304 | tf_op jit(solution)/shard_map/ppermute | solution.py:71
  95.3 12.1 %collective-permute-start.30 = (bf16[128,3072]{1,0:T(8,128)(2,1)S(1)}, bf16[128,3072]{1,0:T(8,128)(2,1)S(1)}, u32[]{:S(2)}, u32[]{:S(2)}) collective-permute-start(bf16[128,3072]{1,0:T(8,128)(2,1)S(1)} %shard_map.371.refs_0_), channel_id=1, source_target_pairs={{0,2},{1,5},{2,0},{3,7},{4,6},{5,1},{6,4},{7,3},{8,10},{9,13},{10,... | collective-permute-start | bytes 2359304 | tf_op jit(solution)/shard_map/ppermute | solution.py:64
  110.4 17.3 %collective-permute-start.32 = (bf16[128,1792]{1,0:T(8,128)(2,1)S(1)}, bf16[128,1792]{1,0:T(8,128)(2,1)S(1)}, u32[]{:S(2)}, u32[]{:S(2)}) collective-permute-start(bf16[128,1792]{1,0:T(8,128)(2,1)S(1)} %get-tuple-element.128), channel_id=1, source_target_pairs={{0,1},{1,0},{2,3},{3,2},{4,5},{5,4},{6,7},{7,6},{8,9},{9,8},{10,11... | collective-permute-start | bytes 1376264 | tf_op jit(solution)/shard_map/ppermute | solution.py:71
  112.3 16.6 %collective-permute-start.34 = (bf16[128,1792]{1,0:T(8,128)(2,1)S(1)}, bf16[128,1792]{1,0:T(8,128)(2,1)S(1)}, u32[]{:S(2)}, u32[]{:S(2)}) collective-permute-start(bf16[128,1792]{1,0:T(8,128)(2,1)S(1)} %shard_map.377.refs_2_), channel_id=1, source_target_pairs={{0,2},{1,5},{2,0},{3,7},{4,6},{5,1},{6,4},{7,3},{8,10},{9,13},{10,... | collective-permute-start | bytes 1376264 | tf_op jit(solution)/shard_map/ppermute | solution.py:64
  113.7 10.6 %collective-permute-start.35 = (bf16[64,3072]{1,0:T(8,128)(2,1)S(1)}, bf16[64,3072]{1,0:T(8,128)(2,1)S(1)}, u32[]{:S(2)}, u32[]{:S(2)}) collective-permute-start(bf16[64,3072]{1,0:T(8,128)(2,1)S(1)} %shard_map.375.refs_0_), channel_id=1, source_target_pairs={{0,4},{1,3},{2,6},{3,1},{4,0},{5,7},{6,2},{7,5},{8,12},{9,11},{10,... | collective-permute-start | bytes 1179656 | tf_op jit(solution)/shard_map/ppermute | solution.py:64
  114.7 9.5 %collective-permute-start.31 = (bf16[2,162,512]{2,1,0:T(8,128)(2,1)S(1)}, bf16[2,162,512]{2,1,0:T(8,128)(2,1)S(1)}, u32[]{:S(2)}, u32[]{:S(2)}) collective-permute-start(bf16[2,162,512]{2,1,0:T(8,128)(2,1)S(1)} %get-tuple-element.126), channel_id=1, source_target_pairs={{0,1},{1,0},{2,3},{3,2},{4,5},{5,4},{6,7},{7,6},{8,9},{9,8},{10,11... | collective-permute-start | bytes 995336 | tf_op jit(solution)/shard_map/ppermute | solution.py:71
  114.7 8.3 %collective-permute-start.36 = (bf16[64,768]{1,0:T(8,128)(2,1)S(1)}, bf16[64,768]{1,0:T(8,128)(2,1)S(1)}, u32[]{:S(2)}, u32[]{:S(2)}) collective-permute-start(bf16[64,768]{1,0:T(8,128)(2,1)S(1)} %get-tuple-element.130), channel_id=1, source_target_pairs={{0,16},{1,17},{2,18},{3,19},{4,20},{5,21},{6,22},{7,23},{8,24},{9,... | collective-permute-start | bytes 294920 | tf_op jit(solution)/shard_map/ppermute | solution.py:64
  123.0 7.2 %collective-permute-start.44 = (bf16[64,768]{1,0:T(8,128)(2,1)S(1)}, bf16[64,768]{1,0:T(8,128)(2,1)S(1)}, u32[]{:S(2)}, u32[]{:S(2)}) collective-permute-start(bf16[64,768]{1,0:T(8,128)(2,1)S(1)} %shard_map.378.refs_4_.refs_0_), channel_id=1, source_target_pairs={{0,4},{1,3},{2,6},{3,1},{4,0},{5,7},{6,2},{7,5},{8,12},{9,11},{10,... | collective-permute-start | bytes 294920 | tf_op jit(solution)/shard_map/ppermute | solution.py:64
  124.5 12.1 %collective-permute-start.41 = (bf16[16,3072]{1,0:T(8,128)(2,1)S(1)}, bf16[16,3072]{1,0:T(8,128)(2,1)S(1)}, u32[]{:S(2)}, u32[]{:S(2)}) collective-permute-start(bf16[16,3072]{1,0:T(8,128)(2,1)S(1)} %get-tuple-element.136), channel_id=1, source_target_pairs={{0,8},{1,9},{2,10},{3,11},{4,12},{5,13},{6,14},{7,15},{8,0},{9,1},... | collective-permute-start | bytes 294920 | tf_op jit(solution)/shard_map/ppermute | solution.py:64
  124.6 12.1 %collective-permute-start.42 = (bf16[16,3072]{1,0:T(8,128)(2,1)S(1)}, bf16[16,3072]{1,0:T(8,128)(2,1)S(1)}, u32[]{:S(2)}, u32[]{:S(2)}) collective-permute-start(bf16[16,3072]{1,0:T(8,128)(2,1)S(1)} %get-tuple-element.137), channel_id=1, source_target_pairs={{0,16},{1,17},{2,18},{3,19},{4,20},{5,21},{6,22},{7,23},{8,24},{9,... | collective-permute-start | bytes 294920 | tf_op jit(solution)/shard_map/ppermute | solution.py:64
  127.7 12.1 %collective-permute-start.43 = (bf16[16,3072]{1,0:T(8,128)(2,1)S(1)}, bf16[16,3072]{1,0:T(8,128)(2,1)S(1)}, u32[]{:S(2)}, u32[]{:S(2)}) collective-permute-start(bf16[16,3072]{1,0:T(8,128)(2,1)S(1)} %get-tuple-element.138), channel_id=1, source_target_pairs={{0,24},{1,25},{2,26},{3,27},{4,28},{5,29},{6,30},{7,31},{8,16},{9,... | collective-permute-start | bytes 294920 | tf_op jit(solution)/shard_map/ppermute | solution.py:64
  130.3 12.8 %collective-permute-start.45 = (bf16[64,768]{1,0:T(8,128)(2,1)S(1)}, bf16[64,768]{1,0:T(8,128)(2,1)S(1)}, u32[]{:S(2)}, u32[]{:S(2)}) collective-permute-start(bf16[64,768]{1,0:T(8,128)(2,1)S(1)} %shard_map.378.refs_4_.refs_0_), channel_id=1, source_target_pairs={{0,2},{1,5},{2,0},{3,7},{4,6},{5,1},{6,4},{7,3},{8,10},{9,13},{10,... | collective-permute-start | bytes 294920 | tf_op jit(solution)/shard_map/ppermute | solution.py:64
  135.5 7.6 %collective-permute-start.46 = (bf16[64,768]{1,0:T(8,128)(2,1)S(1)}, bf16[64,768]{1,0:T(8,128)(2,1)S(1)}, u32[]{:S(2)}, u32[]{:S(2)}) collective-permute-start(bf16[64,768]{1,0:T(8,128)(2,1)S(1)} %collective-permute-done.44.refs_1_), channel_id=1, source_target_pairs={{0,2},{1,5},{2,0},{3,7},{4,6},{5,1},{6,4},{7,3},{8,10},{9,13},{10,... | collective-permute-start | bytes 294920 | tf_op jit(solution)/shard_map/ppermute | solution.py:64
  136.6 9.4 %collective-permute-start.38 = (bf16[16,1792]{1,0:T(8,128)(2,1)S(1)}, bf16[16,1792]{1,0:T(8,128)(2,1)S(1)}, u32[]{:S(2)}, u32[]{:S(2)}) collective-permute-start(bf16[16,1792]{1,0:T(8,128)(2,1)S(1)} %get-tuple-element.133), channel_id=1, source_target_pairs={{0,8},{1,9},{2,10},{3,11},{4,12},{5,13},{6,14},{7,15},{8,0},{9,1},... | collective-permute-start | bytes 172040 | tf_op jit(solution)/shard_map/ppermute | solution.py:64
  136.7 9.3 %collective-permute-start.39 = (bf16[16,1792]{1,0:T(8,128)(2,1)S(1)}, bf16[16,1792]{1,0:T(8,128)(2,1)S(1)}, u32[]{:S(2)}, u32[]{:S(2)}) collective-permute-start(bf16[16,1792]{1,0:T(8,128)(2,1)S(1)} %get-tuple-element.134), channel_id=1, source_target_pairs={{0,16},{1,17},{2,18},{3,19},{4,20},{5,21},{6,22},{7,23},{8,24},{9,... | collective-permute-start | bytes 172040 | tf_op jit(solution)/shard_map/ppermute | solution.py:64
  (38 other events, 244.5 us)

commit v6 on v5

--- a/solution.py
+++ b/solution.py
@@ -94,9 +94,18 @@
             blocks = blocks + [self.swap(b, step) for b in blocks]
         return blocks
 
+    def widen_in_turn(self, first):
+        second = self.swap(first, self.low[0])
+        third = self.swap(first, self.low[1])
+        passed = stack([second], [third])
+        return [first, second, third, self.swap(passed, self.low[1])], passed
+
     def widen_direct(self, first):
+        return [first] + [self.swap(first, m) for m in self.plane()]
+
+    def plane(self):
         one, two = self.low
-        return [first] + [self.swap(first, m) for m in (one, two, (one[0] ^ two[0], one[1] ^ two[1]))]
+        return [one, two, (one[0] ^ two[0], one[1] ^ two[1])]
 
     def gather(self, shard):
         blocks = self.spread(shard)
@@ -817,7 +826,7 @@
     count = len(after)
 
     def kernel(table_ref, sides_ref, vec_ref, gsum_ref, gate_ref, gwr, ghb, x_ref, og_ref, *refs):
-        keep, send, send_up, stay_ref, away_ref, acc, gvec, blocks, pgb = refs[count:]
+        keep, send, up_a, up_b, stay_ref, away_ref, acc, gvec, blocks, pgb = refs[count:]
 
         def put(name, value):
             start, size = VSEG[name]
@@ -849,17 +858,18 @@
             blocks[s, 0:1, 0:VPER] = gvec[0:1, VPER * s : VPER * s + VPER]
         for k in range(DEVS):
             dev = table_ref[k]
-            target = keep if k < GROUPS else send if k < GROUPS * 3 // 2 else send_up
-            r = pl.ds(k % (GROUPS if k < GROUPS else GROUPS // 2) * 16, 16)
+            target, first = next((t, f) for t, f in ((up_b, 28), (up_a, 24), (send, GROUPS), (keep, 0)) if k >= f)
+            r = pl.ds((k - first) * 16, 16)
             target[r, 0:HALF] = gwr[pl.ds(pl.multiple_of(dev * 16, 16), 16), :]
             target[r, HALF : HALF + VCOLS] = blocks[dev].astype(BF)
 
     payload = sds((D // 2, HALF + VCOLS), BF)
     part = sds((D // 4, HALF + VCOLS), BF)
+    eighth = sds((D // 8, HALF + VCOLS), BF)
     pair = sds((2, half, D), BF)
     return call(
         kernel,
-        (payload, part, part, pair, pair),
+        (payload, part, eighth, eighth, pair, pair),
         [SM] * 2 + [VM] * 7 + [HB] * count,
         [
             pltpu.VMEM((8, D), F32),
@@ -881,6 +891,28 @@
         *after,
         room=16,
     )
+
+
+def add_upper(keep, upper, after):
+    cols = keep.shape[1]
+    size = keep.shape[0] // 2
+
+    def kernel(keep_ref, a_ref, b_ref, *refs):
+        for r in range(0, size, 16):
+            piece = a_ref if r < size // 2 else b_ref
+            value = keep_ref[r : r + 16, :].astype(F32) + piece[r % (size // 2) : r % (size // 2) + 16, :].astype(F32)
+            refs[len(after)][r : r + 16, :] = value.astype(BF)
+
+    specs = [pl.BlockSpec((size, cols), lambda i: (1, 0))] + [pl.BlockSpec((size // 2, cols), lambda i: (0, 0))] * 2
+    return pl.pallas_call(
+        kernel,
+        grid=(1,),
+        out_shape=sds((size, cols), BF),
+        in_specs=specs + [HB] * len(after),
+        out_specs=pl.BlockSpec((size, cols), lambda i: (0, 0)),
+        compiler_params=pltpu.CompilerParams(vmem_limit_bytes=10 * MIB),
+        cost_estimate=pl.CostEstimate(flops=1000000, bytes_accessed=2000000, transcendentals=0),
+    )(keep, *upper, *after)
 
 
 def add_part(terms, size, after, places=None):
@@ -1132,13 +1164,14 @@
     g_got = route.cross(g_send)
     spat_got = route.cross(spat_own)
     if fits:
-        right_blocks = route.widen_direct(stack(line, []))
-        lo_blocks = route.widen_direct(stack(lo_line, [right_blocks[1]]))
+        right_blocks, passed = route.widen_in_turn(stack(line, []))
+        lo_blocks = route.widen_direct(stack(lo_line, [passed]))
     else:
         right_blocks = route.widen(jnp.concatenate(line, axis=0))
         lo_blocks = route.widen(jnp.concatenate(lo_line, axis=0))
     right_blocks = right_blocks + [route.cross(b) for b in right_blocks]
-    lo_blocks = lo_blocks + [route.cross(b) for b in lo_blocks]
+    if not fits:
+        lo_blocks = lo_blocks + [route.cross(b) for b in lo_blocks]
     if not fits:
         whole = in_order(right_blocks, table, in_rows)
         all_vec = whole[:, 0, HALF : HALF + vec_len].reshape(DEVS, 1, VPER)
@@ -1153,6 +1186,8 @@
         ktable, sides, patches, x_got, out_grad, g_got, right_blocks
     )
     gate, hat, scale, spat, mm = gate_norm(levels, sides, vec, v, part, spat_own, spat_got, [])
+    if fits:
+        lo_blocks = lo_blocks + [route.cross(lo_blocks[0]), route.cross(stack(lo_blocks[1:], [mm]))]
     gs, gated, q, gb, wl, wo, sp_keep, sp_send, gsum = middle(ktable, levels, sides, vec, h, spat, gate, grad_out, lo_blocks)
     near, far = route.low[-1], route.low[0]
     after = [[] for _ in range(5)]
@@ -1173,11 +1208,11 @@
     if fits:
         lo_up = route.cross(lo_up)
         lo_terms = [lo_keep, route.cross(lo_send)]
-        sp_own, sp_out = line_turn(sp_terms, 1, [lo_keep])
+        lo_part = add_part([lo_keep, lo_up], 128, [], [1, 0])
+        lo_terms.append(route.swap(lo_part, near))
+        sp_own, sp_out = line_turn(sp_terms, 1, [lo_part])
         sp_terms = [sp_own, route.swap(sp_out, (route.direct[0],) * 2)]
-        lo_part = add_part([lo_keep, lo_up], 128, [sp_own], [1, 0])
-        lo_terms.append(route.swap(lo_part, near))
-        after[2] = [lo_part]
+        after[2] = [sp_own]
     gp, gate_sum = gate_backward(vec, gs, mm, hat, slope, scale, after[2])
     if fits:
         sp_own, sp_out = line_turn(sp_terms, 2, [gate_sum])
@@ -1188,20 +1223,20 @@
         lo_part = add_part(lo_terms, 64, [gwr])
         lo_terms.append(route.swap(lo_part, far))
         after[4] = [lo_part]
-    right_keep, right_send, right_up, grad_stay, grad_away = in_backward(
+    right_keep, right_send, up_a, up_b, grad_stay, grad_away = in_backward(
         ktable, sides, vec, gsum, gate_sum, gwr, ghb, x, grad_out, rows, after[4]
     )
     grad_got = route.cross(grad_away)
     if fits:
-        right_up = route.cross(right_up)
+        upper = [route.cross(up_a), route.cross(up_b)]
         right_terms = [right_keep, route.cross(right_send)]
-        right_part = add_part([right_keep, right_up], 128, [], [1, 0])
+        lo_own, *sends = line_parts(lo_terms, [right_keep])
+        lo_got = [route.swap(p, (m, m)) for p, m in zip(sends, route.direct)]
+        right_part = add_upper(right_keep, upper, [lo_own])
         right_terms.append(route.swap(right_part, near))
-        (sp_sum,) = line_turn(sp_terms, 0, [right_part])
+        (sp_sum,) = line_turn(sp_terms, 0, [right_part, grad_got])
         spat_pieces = route.widen(sp_sum)
-        lo_own, *sends = line_parts(lo_terms, [sp_sum, grad_got])
-        lo_got = [route.swap(p, (m, m)) for p, m in zip(sends, route.direct)]
-        right_part = add_part(right_terms, 64, [lo_own])
+        right_part = add_part(right_terms, 64, [sp_sum])
         right_terms.append(route.swap(right_part, far))
         right_own, *sends = line_parts(right_terms, [right_part])
         right_got = [route.swap(p, (m, m)) for p, m in zip(sends, route.direct)]
@@ -1226,7 +1261,7 @@
         spat_pieces = [flat.transpose(0, 2, 1, 3).reshape(GROUPS * 16, SPC)]
         korder = jnp.arange(GROUPS, dtype=jnp.int32)
         after = []
-        both = jnp.concatenate([right_keep, right_send, right_up])
+        both = jnp.concatenate([right_keep, right_send, up_a, up_b])
         vecs = jnp.take(both[::16, HALF : HALF + VPER].reshape(ndev, vec_len), table, axis=0)
         vec_sum = route.scatter(vecs[: route.n], vecs[route.n :]).reshape(vec_len)
         rights = jnp.take(both[:, :HALF].reshape(ndev, in_rows, HALF), table, axis=0).reshape(D, HALF)

time: 149 us -> 147 us (0.987)
  local copies, waits for them, and re-layouts: 10.7 us -> 7.25 us
    unnamed x50, local copies, waits for them, and re-layouts: 9.78 us -> 6.33 us
    ppermute x18 -> x17, waiting for transfers between devices: 2.9 us -> 6.29 us  [cross(): return lax.ppermute(block, AXES, pairs)]
    ppermute x29, waiting for transfers between devices: 33.6 us -> 30.7 us  [swap(): return lax.ppermute(block, AXES, pairs)]
    pallas_call x15 -> x17, Pallas kernels: 57.1 us -> 57.7 us  [call(): pl.pallas_call(kernel, out_shape=out_shape, in_specs=in_specs, out_specs=...]
    ppermute x18 -> x17, starting transfers between devices: 3.58 us -> 3.59 us  [cross(): return lax.ppermute(block, AXES, pairs)]
  transfers between devices with their start and end apart: 47 -> 46, of which waited for: 12 -> 14; matrix products, arithmetic and copies ran while one was open for 5% -> 3% of each run, Pallas kernels for 22% -> 25%
where the time goes in v6:
time: 147 us
  Pallas kernels  58.7 us (40%)
  starting transfers between devices  41.1 us (28%)
  waiting for transfers between devices  37 us (25%)
  local copies, waits for them, and re-layouts  7.25 us (5%)
  other arithmetic  1.66 us (1%)
    pallas_call x17, Pallas kernels, call(): pl.pallas_call(kernel, out_shape=out_shape, in_specs=in_specs, out_specs=...  57.7 us
    ppermute x29, starting transfers between devices, swap(): return lax.ppermute(block, AXES, pairs)  37.5 us
    ppermute x29, waiting for transfers between devices, swap(): return lax.ppermute(block, AXES, pairs)  30.7 us
    unnamed x50, local copies, waits for them, and re-layouts  6.33 us
    ppermute x17, waiting for transfers between devices, cross(): return lax.ppermute(block, AXES, pairs)  6.29 us
    ppermute x17, starting transfers between devices, cross(): return lax.ppermute(block, AXES, pairs)  3.59 us
  transfers between devices with their start and end apart: 46, of which 14 were waited for; matrix products, arithmetic and copies ran while one was open for 3% of the time, Pallas kernels for 25%

profile of v6, /device:TPU:0, one launch (start us, length us, event | category | flops | bytes accessed | tf_op | source)
XLA Modules:
  0.0 146.9 jit_solution(13263485535552393658)
XLA Ops:
  0.7 1.7 %shard_map.360 = (bf16[16,1792]{1,0:T(8,128)(2,1)}, bf16[16,3072]{1,0:T(8,128)(2,1)}) custom-call(f32[16,3072]{1,0:T(8,128)} %w_ref.3, f32[48,512]{1,0:T(8,128)} %w_ref.2, f32[1,240]{1,0:T(1,128)} %bitcast.7), custom_call_target="tpu_custom_call" | custom-call | flops 1000 | bytes 600000 | tf_op jit(solution)/shard_map/pallas_call | solution.py:220
  2.4 5.1 %collective-permute-start.4 = (bf16[16,1792]{1,0:T(8,128)(2,1)}, bf16[16,1792]{1,0:T(8,128)(2,1)S(1)}, u32[]{:S(2)}, u32[]{:S(2)}) collective-permute-start(bf16[16,1792]{1,0:T(8,128)(2,1)} %get-tuple-element.88.refs_0_), channel_id=1, source_target_pairs={{0,24},{1,25},{2,26},{3,27},{4,28},{5,29},{6,30},{7,31},{8,16},{9,... | collective-permute-start | bytes 172040 | tf_op jit(solution)/shard_map/ppermute | solution.py:64
  8.1 2.0 %collective-permute-done.4.refs_3_ = bf16[16,1792]{1,0:T(8,128)(2,1)S(1)} collective-permute-done((bf16[16,1792]{1,0:T(8,128)(2,1)}, bf16[16,1792]{1,0:T(8,128)(2,1)S(1)}, u32[]{:S(2)}, u32[]{:S(2)}) %collective-permute-start.4) | collective-permute-done | bytes 57376 | tf_op jit(solution)/shard_map/ppermute | solution.py:64
  10.1 2.6 %collective-permute-done.3.refs_2_ = bf16[16,1792]{1,0:T(8,128)(2,1)S(1)} collective-permute-done((bf16[16,1792]{1,0:T(8,128)(2,1)}, bf16[16,1792]{1,0:T(8,128)(2,1)S(1)}, u32[]{:S(2)}, u32[]{:S(2)}) %collective-permute-start.3) | collective-permute-done | bytes 57376 | tf_op jit(solution)/shard_map/ppermute | solution.py:64
  13.6 1.6 %collective-permute-start.6 = (bf16[64,1792]{1,0:T(8,128)(2,1)S(1)}, bf16[64,1792]{1,0:T(8,128)(2,1)S(1)}, u32[]{:S(2)}, u32[]{:S(2)}) collective-permute-start(bf16[64,1792]{1,0:T(8,128)(2,1)S(1)} %shard_map.361.refs_0_), channel_id=1, source_target_pairs={{0,2},{1,5},{2,0},{3,7},{4,6},{5,1},{6,4},{7,3},{8,10},{9,13},{10,... | collective-permute-start | bytes 688136 | tf_op jit(solution)/shard_map/ppermute | solution.py:64
  16.7 2.6 %collective-permute-start.15 = (bf16[16,3072]{1,0:T(8,128)(2,1)}, bf16[16,3072]{1,0:T(8,128)(2,1)S(1)}, u32[]{:S(2)}, u32[]{:S(2)}) collective-permute-start(bf16[16,3072]{1,0:T(8,128)(2,1)} %get-tuple-element.97.refs_0_), channel_id=1, source_target_pairs={{0,24},{1,25},{2,26},{3,27},{4,28},{5,29},{6,30},{7,31},{8,16},{9,... | collective-permute-start | bytes 294920 | tf_op jit(solution)/shard_map/ppermute | solution.py:64
  20.0 1.6 %collective-permute-done.6.refs_1_.refs_2_ = bf16[64,1792]{1,0:T(8,128)(2,1)S(1)} collective-permute-done((bf16[64,1792]{1,0:T(8,128)(2,1)S(1)}, bf16[64,1792]{1,0:T(8,128)(2,1)S(1)}, u32[]{:S(2)}, u32[]{:S(2)}) %collective-permute-start.6) | collective-permute-done | bytes 229408 | tf_op jit(solution)/shard_map/ppermute | solution.py:64
  21.7 1.6 %collective-permute-start.7 = (bf16[64,1792]{1,0:T(8,128)(2,1)S(1)}, bf16[64,1792]{1,0:T(8,128)(2,1)}, u32[]{:S(2)}, u32[]{:S(2)}) collective-permute-start(bf16[64,1792]{1,0:T(8,128)(2,1)S(1)} %shard_map.362.refs_4_), channel_id=1, source_target_pairs={{0,2},{1,5},{2,0},{3,7},{4,6},{5,1},{6,4},{7,3},{8,10},{9,13},{10,... | collective-permute-start | bytes 688136 | tf_op jit(solution)/shard_map/ppermute | solution.py:64
  25.5 1.5 %shard_map.359 = (bf16[3,162,384]{2,1,0:T(8,128)(2,1)S(1)}, bf16[2,162,512]{2,1,0:T(8,128)(2,1)}, bf16[2,162,512]{2,1,0:T(8,128)(2,1)}) custom-call(s32[33]{0:T(128)S(1)} %pad_add_fusion.1.sides_ref, f32[3,162,324]{2,1,0:T(8,128)S(1)} %copy-done, f32[3,162,1]{2,1,0:T(8,128)S(1)} %copy.47.b_ref, bf16[4,162,512]{2,1,0:T(8,128)(2,1)S(1)} %copy.50.x_ref.p_ref, ...), custom_call_target="tpu_custom_call" | custom-call | flops 1000 | bytes 3000000 | tf_op jit(solution)/shard_map/pallas_call | solution.py:220
  28.9 4.2 %collective-permute-done.13.refs_1_ = bf16[16,3072]{1,0:T(8,128)(2,1)S(1)} collective-permute-done((bf16[16,3072]{1,0:T(8,128)(2,1)S(1)}, bf16[16,3072]{1,0:T(8,128)(2,1)S(1)}, u32[]{:S(2)}, u32[]{:S(2)}) %collective-permute-start.13) | collective-permute-done | bytes 98336 | tf_op jit(solution)/shard_map/ppermute | solution.py:64
  38.7 11.0 %shard_map.363 = (bf16[672,512]{1,0:T(8,128)(2,1)S(1)}, bf16[672,512]{1,0:T(8,128)(2,1)S(1)}, bf16[672,512]{1,0:T(8,128)(2,1)S(1)}, f32[672,1536]{1,0:T(8,128)S(...) custom-call(s32[32]{0:T(128)S(1)} %get-tuple-element.193.table_ref, ...), custom_call_target="tpu_custom_call" | custom-call | flops 10000000000 | bytes 20000000 | tf_op jit(solution)/shard_map/pallas_call | solution.py:220
  49.7 5.0 %shard_map.364 = (bf16[720,1536]{1,0:T(8,128)(2,1)S(1)}, bf16[672,1536]{1,0:T(8,128)(2,1)S(1)}, f32[672,128]{1,0:T(8,128)S(1)}, bf16[672,1536]{1,0:T(8,128)(2,1)S(1)}, bf16[2,336,384]{2,1,0:T(8,128)(2,1)S(1)}) custom-call(s32[2]{0:T(128)S(1)} %dynamic_slice.3.levels_ref, s32[33]{0:T(128)S(1)} %pad_add_fusion.1.sides_ref, ...), custom_call_target="tpu_custom_call" | custom-call | flops 6000000000 | bytes 12000000 | tf_op jit(solution)/shard_map/pallas_call | solution.py:220
  56.1 2.9 %collective-permute-done.19.refs_4_ = bf16[64,3072]{1,0:T(8,128)(2,1)S(1)} collective-permute-done((bf16[64,3072]{1,0:T(8,128)(2,1)S(1)}, bf16[64,3072]{1,0:T(8,128)(2,1)S(1)}, u32[]{:S(2)}, u32[]{:S(2)}) %collective-permute-start.19) | collective-permute-done | bytes 393248 | tf_op jit(solution)/shard_map/ppermute | solution.py:71
  59.0 14.0 %shard_map.367 = (bf16[672,1536]{1,0:T(8,128)(2,1)S(1)}, bf16[672,1536]{1,0:T(8,128)(2,1)S(1)}, bf16[672,1536]{1,0:T(8,128)(2,1)S(1)}, bf16[672,512]{1,0:T(8,128...) custom-call(s32[32]{0:T(128)S(1)} %get-tuple-element.193.table_ref, ...), custom_call_target="tpu_custom_call" | custom-call | flops 8000000000 | bytes 16000000 | tf_op jit(solution)/shard_map/pallas_call | solution.py:220
  73.3 1.6 %collective-permute-done.21.refs_1_ = bf16[256,768]{1,0:T(8,128)(2,1)S(1)} collective-permute-done((bf16[256,768]{1,0:T(8,128)(2,1)S(1)}, bf16[256,768]{1,0:T(8,128)(2,1)S(1)}, u32[]{:S(2)}, u32[]{:S(2)}) %collective-permute-start.21) | collective-permute-done | bytes 393248 | tf_op jit(solution)/shard_map/ppermute | solution.py:71
  75.6 2.4 %shard_map.369.refs_3_.gwo = bf16[1536,512]{1,0:T(8,128)(2,1)S(1)} custom-call(bf16[672,1536]{1,0:T(8,128)(2,1)S(1)} %get-tuple-element.99.t_ref, bf16[672,512]{1,0:T(8,128)(2,1)S(1)} %get-tuple-element.101.gb_ref, bf16[128,768]{1,0:T(8,128)(2,1)S(1)} %shard_map.368.refs_0_), custom_call_target="tpu_custom_call" | custom-call | flops 1000000000 | bytes 5000000 | tf_op jit(solution)/shard_map/pallas_call | solution.py:220
  78.0 2.6 %collective-permute-done.22.refs_2_ = bf16[128,768]{1,0:T(8,128)(2,1)S(1)} collective-permute-done((bf16[128,768]{1,0:T(8,128)(2,1)S(1)}, bf16[128,768]{1,0:T(8,128)(2,1)S(1)}, u32[]{:S(2)}, u32[]{:S(2)}) %collective-permute-start.22) | collective-permute-done | bytes 196640 | tf_op jit(solution)/shard_map/ppermute | solution.py:64
  80.7 5.1 %shard_map.371 = (bf16[256,3072]{1,0:T(8,128)(2,1)S(1)}, bf16[128,3072]{1,0:T(8,128)(2,1)S(1)}, bf16[128,3072]{1,0:T(8,128)(2,1)S(1)}, bf16[2,162,512]{2,1,0:T(8...) custom-call(s32[32]{0:T(128)S(1)} %get-tuple-element.193.table_ref, ...), custom_call_target="tpu_custom_call" | custom-call | flops 5000000000 | bytes 15000000 | tf_op jit(solution)/shard_map/pallas_call | solution.py:220
  86.4 1.8 %collective-permute-done.25.refs_1_ = bf16[128,3072]{1,0:T(8,128)(2,1)S(1)} collective-permute-done((bf16[128,3072]{1,0:T(8,128)(2,1)S(1)}, bf16[128,3072]{1,0:T(8,128)(2,1)S(1)}, u32[]{:S(2)}, u32[]{:S(2)}) %collective-permute-start.25) | collective-permute-done | bytes 786464 | tf_op jit(solution)/shard_map/ppermute | solution.py:71
  90.1 4.7 %collective-permute-done.24.refs_3_ = bf16[64,768]{1,0:T(8,128)(2,1)S(1)} collective-permute-done((bf16[64,768]{1,0:T(8,128)(2,1)S(1)}, bf16[64,768]{1,0:T(8,128)(2,1)S(1)}, u32[]{:S(2)}, u32[]{:S(2)}) %collective-permute-start.24) | collective-permute-done | bytes 98336 | tf_op jit(solution)/shard_map/ppermute | solution.py:64
  95.6 5.7 %shard_map.374 = (bf16[672,1536]{1,0:T(8,128)(2,1)S(1)}, f32[1,4608]{1,0:T(1,128)S(1)}) custom-call(f32[1,7680]{1,0:T(1,128)S(1)} %get-tuple-element.89.vec_ref, bf16[672,1536]{1,0:T(8,128)(2,1)S(1)} %get-tuple-element.110.gs_ref, bf16[2,336,384]{2,1,0:T(8,128)(2,1)S(1)} %get-tuple-element.98.refs_3_.mm_ref, ...), custom_call_target="tpu_custom_call" | custom-call | flops 3000000000 | bytes 10000000 | tf_op jit(solution)/shard_map/pallas_call | solution.py:220
  101.4 2.9 %shard_map.376 = (bf16[512,1536]{1,0:T(8,128)(2,1)S(1)}, f32[672,512]{1,0:T(8,128)S(1)}) custom-call(bf16[672,1536]{1,0:T(8,128)(2,1)S(1)} %get-tuple-element.118.gp_ref, bf16[672,512]{1,0:T(8,128)(2,1)S(1)} %get-tuple-element.90.h_ref, bf16[512,1536]{1,0:T(8,128)(2,1)S(1)} %get-tuple-element.119.w_ref, f32[672,512]{1,0:T(8,128)S(1)} %get-tuple-element.120.gh_ref, ...), custom_call_target="tpu_custom_call" | custom-call | flops 3000000000 | bytes 8000000 | tf_op jit(solution)/shard_map/pallas_call | solution.py:220
  106.0 2.8 %shard_map.378 = (bf16[256,1792]{1,0:T(8,128)(2,1)S(1)}, bf16[128,1792]{1,0:T(8,128)(2,1)S(1)}, bf16[64,1792]{1,0:T(8,128)(2,1)S(1)}, bf16[64,1792]{1,0:T(8,128)...) custom-call(s32[32]{0:T(128)S(1)} %get-tuple-element.193.table_ref, ...), custom_call_target="tpu_custom_call" | custom-call | flops 2000000000 | bytes 6000000 | tf_op jit(solution)/shard_map/pallas_call | solution.py:220
  109.4 2.9 %collective-permute-done.33.refs_3_ = bf16[64,3072]{1,0:T(8,128)(2,1)S(1)} collective-permute-done((bf16[64,3072]{1,0:T(8,128)(2,1)S(1)}, bf16[64,3072]{1,0:T(8,128)(2,1)S(1)}, u32[]{:S(2)}, u32[]{:S(2)}) %collective-permute-start.33) | collective-permute-done | bytes 393248 | tf_op jit(solution)/shard_map/ppermute | solution.py:64
  114.1 2.1 %collective-permute-start.35 = (bf16[64,768]{1,0:T(8,128)(2,1)S(1)}, bf16[64,768]{1,0:T(8,128)(2,1)S(1)}, u32[]{:S(2)}, u32[]{:S(2)}) collective-permute-start(bf16[64,768]{1,0:T(8,128)(2,1)S(1)} %get-tuple-element.133), channel_id=1, source_target_pairs={{0,16},{1,17},{2,18},{3,19},{4,20},{5,21},{6,22},{7,23},{8,24},{9,... | collective-permute-start | bytes 294920 | tf_op jit(solution)/shard_map/ppermute | solution.py:64
  118.1 4.4 %collective-permute-done.35.refs_1_ = bf16[64,768]{1,0:T(8,128)(2,1)S(1)} collective-permute-done((bf16[64,768]{1,0:T(8,128)(2,1)S(1)}, bf16[64,768]{1,0:T(8,128)(2,1)S(1)}, u32[]{:S(2)}, u32[]{:S(2)}) %collective-permute-start.35) | collective-permute-done | bytes 98336 | tf_op jit(solution)/shard_map/ppermute | solution.py:64
  122.8 1.9 %collective-permute-start.42 = (bf16[16,3072]{1,0:T(8,128)(2,1)S(1)}, bf16[16,3072]{1,0:T(8,128)(2,1)S(1)}, u32[]{:S(2)}, u32[]{:S(2)}) collective-permute-start(bf16[16,3072]{1,0:T(8,128)(2,1)S(1)} %get-tuple-element.140), channel_id=1, source_target_pairs={{0,24},{1,25},{2,26},{3,27},{4,28},{5,29},{6,30},{7,31},{8,16},{9,... | collective-permute-start | bytes 294920 | tf_op jit(solution)/shard_map/ppermute | solution.py:64
  127.0 2.4 %collective-permute-done.43.refs_1_ = bf16[64,768]{1,0:T(8,128)(2,1)S(1)} collective-permute-done((bf16[64,768]{1,0:T(8,128)(2,1)S(1)}, bf16[64,768]{1,0:T(8,128)(2,1)S(1)}, u32[]{:S(2)}, u32[]{:S(2)}) %collective-permute-start.43) | collective-permute-done | bytes 98336 | tf_op jit(solution)/shard_map/ppermute | solution.py:64
  130.3 2.5 %collective-permute-done.36.refs_3_ = bf16[64,1792]{1,0:T(8,128)(2,1)S(1)} collective-permute-done((bf16[64,1792]{1,0:T(8,128)(2,1)S(1)}, bf16[64,1792]{1,0:T(8,128)(2,1)S(1)}, u32[]{:S(2)}, u32[]{:S(2)}) %collective-permute-start.36) | collective-permute-done | bytes 229408 | tf_op jit(solution)/shard_map/ppermute | solution.py:64
  132.8 1.7 %collective-permute-start.45 = (bf16[64,768]{1,0:T(8,128)(2,1)S(1)}, bf16[64,768]{1,0:T(8,128)(2,1)S(1)}, u32[]{:S(2)}, u32[]{:S(2)}) collective-permute-start(bf16[64,768]{1,0:T(8,128)(2,1)S(1)} %collective-permute-done.43.refs_1_), channel_id=1, source_target_pairs={{0,2},{1,5},{2,0},{3,7},{4,6},{5,1},{6,4},{7,3},{8,10},{9,13},{10,... | collective-permute-start | bytes 294920 | tf_op jit(solution)/shard_map/ppermute | solution.py:64
  137.4 1.8 %collective-permute-start.39 = (bf16[16,1792]{1,0:T(8,128)(2,1)S(1)}, bf16[16,1792]{1,0:T(8,128)(2,1)S(1)}, u32[]{:S(2)}, u32[]{:S(2)}) collective-permute-start(bf16[16,1792]{1,0:T(8,128)(2,1)S(1)} %get-tuple-element.137), channel_id=1, source_target_pairs={{0,24},{1,25},{2,26},{3,27},{4,28},{5,29},{6,30},{7,31},{8,16},{9,... | collective-permute-start | bytes 172040 | tf_op jit(solution)/shard_map/ppermute | solution.py:64
  141.4 2.8 %shard_map.385 = (f32[3,162,324]{2,1,0:T(8,128)}, f32[3,162,324]{2,1,0:T(8,128)}, f32[3,162,324]{2,1,0:T(8,128)}, f32[3,162]{1,0:T(4,128)}, f32[3,162]{1,0:T(4,128)}, /*index=5*/f32[3,162]{1,0:T(4,128)}) custom-call(s32[16]{0:T(128)S(1)} %get-tuple-element.195.order_ref, bf16[64,768]{1,0:T(8,128)(2,1)S(1)} %shard_map.381.refs_3_.refs_0_, ...), custom_call_target="tpu_custom_call" | custom-call | flops 10000000 | bytes 6000000 | tf_op jit(solution)/shard_map/pallas_call | solution.py:220
  (148 shorter events, 36.1 us)
Async XLA Ops:
  2.4 7.8 %collective-permute-start.4 = (bf16[16,1792]{1,0:T(8,128)(2,1)}, bf16[16,1792]{1,0:T(8,128)(2,1)S(1)}, u32[]{:S(2)}, u32[]{:S(2)}) collective-permute-start(bf16[16,1792]{1,0:T(8,128)(2,1)} %get-tuple-element.88.refs_0_), channel_id=1, source_target_pairs={{0,24},{1,25},{2,26},{3,27},{4,28},{5,29},{6,30},{7,31},{8,16},{9,... | collective-permute-start | bytes 172040 | tf_op jit(solution)/shard_map/ppermute | solution.py:64
  13.6 8.0 %collective-permute-start.6 = (bf16[64,1792]{1,0:T(8,128)(2,1)S(1)}, bf16[64,1792]{1,0:T(8,128)(2,1)S(1)}, u32[]{:S(2)}, u32[]{:S(2)}) collective-permute-start(bf16[64,1792]{1,0:T(8,128)(2,1)S(1)} %shard_map.361.refs_0_), channel_id=1, source_target_pairs={{0,2},{1,5},{2,0},{3,7},{4,6},{5,1},{6,4},{7,3},{8,10},{9,13},{10,... | collective-permute-start | bytes 688136 | tf_op jit(solution)/shard_map/ppermute | solution.py:64
  15.2 6.5 %collective-permute-start.5 = (bf16[64,1792]{1,0:T(8,128)(2,1)S(1)}, bf16[64,1792]{1,0:T(8,128)(2,1)S(1)}, u32[]{:S(2)}, u32[]{:S(2)}) collective-permute-start(bf16[64,1792]{1,0:T(8,128)(2,1)S(1)} %shard_map.361.refs_0_), channel_id=1, source_target_pairs={{0,4},{1,3},{2,6},{3,1},{4,0},{5,7},{6,2},{7,5},{8,12},{9,11},{10,... | collective-permute-start | bytes 688136 | tf_op jit(solution)/shard_map/ppermute | solution.py:64
  16.7 11.1 %collective-permute-start.15 = (bf16[16,3072]{1,0:T(8,128)(2,1)}, bf16[16,3072]{1,0:T(8,128)(2,1)S(1)}, u32[]{:S(2)}, u32[]{:S(2)}) collective-permute-start(bf16[16,3072]{1,0:T(8,128)(2,1)} %get-tuple-element.97.refs_0_), channel_id=1, source_target_pairs={{0,24},{1,25},{2,26},{3,27},{4,28},{5,29},{6,30},{7,31},{8,16},{9,... | collective-permute-start | bytes 294920 | tf_op jit(solution)/shard_map/ppermute | solution.py:64
  19.3 9.0 %collective-permute-start.14 = (bf16[16,3072]{1,0:T(8,128)(2,1)}, bf16[16,3072]{1,0:T(8,128)(2,1)}, u32[]{:S(2)}, u32[]{:S(2)}) collective-permute-start(bf16[16,3072]{1,0:T(8,128)(2,1)} %get-tuple-element.97.refs_0_), channel_id=1, source_target_pairs={{0,16},{1,17},{2,18},{3,19},{4,20},{5,21},{6,22},{7,23},{8,24},{9,... | collective-permute-start | bytes 294920 | tf_op jit(solution)/shard_map/ppermute | solution.py:64
  20.0 13.1 %collective-permute-start.8 = (bf16[64,1792]{1,0:T(8,128)(2,1)S(1)}, bf16[64,1792]{1,0:T(8,128)(2,1)}, u32[]{:S(2)}, u32[]{:S(2)}) collective-permute-start(bf16[64,1792]{1,0:T(8,128)(2,1)S(1)} %shard_map.361.refs_0_), channel_id=1, source_target_pairs={{0,1},{1,0},{2,3},{3,2},{4,5},{5,4},{6,7},{7,6},{8,9},{9,8},{10,11... | collective-permute-start | bytes 688136 | tf_op jit(solution)/shard_map/ppermute | solution.py:71
  21.7 11.9 %collective-permute-start.7 = (bf16[64,1792]{1,0:T(8,128)(2,1)S(1)}, bf16[64,1792]{1,0:T(8,128)(2,1)}, u32[]{:S(2)}, u32[]{:S(2)}) collective-permute-start(bf16[64,1792]{1,0:T(8,128)(2,1)S(1)} %shard_map.362.refs_4_), channel_id=1, source_target_pairs={{0,2},{1,5},{2,0},{3,7},{4,6},{5,1},{6,4},{7,3},{8,10},{9,13},{10,... | collective-permute-start | bytes 688136 | tf_op jit(solution)/shard_map/ppermute | solution.py:64
  27.8 6.9 %collective-permute-start = (bf16[2,162,512]{2,1,0:T(8,128)(2,1)}, bf16[2,162,512]{2,1,0:T(8,128)(2,1)}, u32[]{:S(2)}, u32[]{:S(2)}) collective-permute-start(bf16[2,162,512]{2,1,0:T(8,128)(2,1)} %get-tuple-element.86), channel_id=1, source_target_pairs={{0,1},{1,0},{2,3},{3,2},{4,5},{5,4},{6,7},{7,6},{8,9},{9,8},{10,11... | collective-permute-start | bytes 995336 | tf_op jit(solution)/shard_map/ppermute | solution.py:71
  27.8 7.4 %collective-permute-start.1 = (bf16[2,162,512]{2,1,0:T(8,128)(2,1)}, bf16[2,162,512]{2,1,0:T(8,128)(2,1)}, u32[]{:S(2)}, u32[]{:S(2)}) collective-permute-start(bf16[2,162,512]{2,1,0:T(8,128)(2,1)} %get-tuple-element.87), channel_id=1, source_target_pairs={{0,1},{1,0},{2,3},{3,2},{4,5},{5,4},{6,7},{7,6},{8,9},{9,8},{10,11... | collective-permute-start | bytes 995336 | tf_op jit(solution)/shard_map/ppermute | solution.py:71
  34.7 15.0 %collective-permute-start.12 = (bf16[3,162,384]{2,1,0:T(8,128)(2,1)}, bf16[3,162,384]{2,1,0:T(8,128)(2,1)S(1)}, u32[]{:S(2)}, u32[]{:S(2)}) collective-permute-start(bf16[3,162,384]{2,1,0:T(8,128)(2,1)} %copy-done.15), channel_id=1, source_target_pairs={{0,1},{1,0},{2,3},{3,2},{4,5},{5,4},{6,7},{7,6},{8,9},{9,8},{10,11... | collective-permute-start | bytes 1119752 | tf_op jit(solution)/shard_map/ppermute | solution.py:71
  35.2 19.6 %collective-permute-start.18 = (bf16[64,3072]{1,0:T(8,128)(2,1)S(1)}, bf16[64,3072]{1,0:T(8,128)(2,1)S(1)}, u32[]{:S(2)}, u32[]{:S(2)}) collective-permute-start(bf16[64,3072]{1,0:T(8,128)(2,1)S(1)} %shard_map.365.refs_0_), channel_id=1, source_target_pairs={{0,6},{1,7},{2,4},{3,5},{4,2},{5,3},{6,0},{7,1},{8,14},{9,15},{10,... | collective-permute-start | bytes 1179656 | tf_op jit(solution)/shard_map/ppermute | solution.py:64
  36.2 18.5 %collective-permute-start.17 = (bf16[64,3072]{1,0:T(8,128)(2,1)S(1)}, bf16[64,3072]{1,0:T(8,128)(2,1)S(1)}, u32[]{:S(2)}, u32[]{:S(2)}) collective-permute-start(bf16[64,3072]{1,0:T(8,128)(2,1)S(1)} %shard_map.365.refs_0_), channel_id=1, source_target_pairs={{0,2},{1,5},{2,0},{3,7},{4,6},{5,1},{6,4},{7,3},{8,10},{9,13},{10,... | collective-permute-start | bytes 1179656 | tf_op jit(solution)/shard_map/ppermute | solution.py:64
  37.1 18.3 %collective-permute-start.16 = (bf16[64,3072]{1,0:T(8,128)(2,1)S(1)}, bf16[64,3072]{1,0:T(8,128)(2,1)S(1)}, u32[]{:S(2)}, u32[]{:S(2)}) collective-permute-start(bf16[64,3072]{1,0:T(8,128)(2,1)S(1)} %shard_map.365.refs_0_), channel_id=1, source_target_pairs={{0,4},{1,3},{2,6},{3,1},{4,0},{5,7},{6,2},{7,5},{8,12},{9,11},{10,... | collective-permute-start | bytes 1179656 | tf_op jit(solution)/shard_map/ppermute | solution.py:64
  85.9 18.4 %collective-permute-start.27 = (bf16[128,3072]{1,0:T(8,128)(2,1)S(1)}, bf16[128,3072]{1,0:T(8,128)(2,1)S(1)}, u32[]{:S(2)}, u32[]{:S(2)}) collective-permute-start(bf16[128,3072]{1,0:T(8,128)(2,1)S(1)} %get-tuple-element.125), channel_id=1, source_target_pairs={{0,1},{1,0},{2,3},{3,2},{4,5},{5,4},{6,7},{7,6},{8,9},{9,8},{10,11... | collective-permute-start | bytes 2359304 | tf_op jit(solution)/shard_map/ppermute | solution.py:71
  88.3 16.0 %collective-permute-start.28 = (bf16[128,3072]{1,0:T(8,128)(2,1)S(1)}, bf16[128,3072]{1,0:T(8,128)(2,1)S(1)}, u32[]{:S(2)}, u32[]{:S(2)}) collective-permute-start(bf16[128,3072]{1,0:T(8,128)(2,1)S(1)} %shard_map.372.refs_4_), channel_id=1, source_target_pairs={{0,2},{1,5},{2,0},{3,7},{4,6},{5,1},{6,4},{7,3},{8,10},{9,13},{10,... | collective-permute-start | bytes 2359304 | tf_op jit(solution)/shard_map/ppermute | solution.py:64
  89.1 5.7 %collective-permute-start.24 = (bf16[64,768]{1,0:T(8,128)(2,1)S(1)}, bf16[64,768]{1,0:T(8,128)(2,1)S(1)}, u32[]{:S(2)}, u32[]{:S(2)}) collective-permute-start(bf16[64,768]{1,0:T(8,128)(2,1)S(1)} %shard_map.370.refs_0_), channel_id=1, source_target_pairs={{0,4},{1,3},{2,6},{3,1},{4,0},{5,7},{6,2},{7,5},{8,12},{9,11},{10,... | collective-permute-start | bytes 294920 | tf_op jit(solution)/shard_map/ppermute | solution.py:64
  90.1 11.2 %collective-permute-start.23 = (bf16[2,162,512]{2,1,0:T(8,128)(2,1)S(1)}, bf16[2,162,512]{2,1,0:T(8,128)(2,1)S(1)}, u32[]{:S(2)}, u32[]{:S(2)}) collective-permute-start(bf16[2,162,512]{2,1,0:T(8,128)(2,1)S(1)} %get-tuple-element.108), channel_id=1, source_target_pairs={{0,1},{1,0},{2,3},{3,2},{4,5},{5,4},{6,7},{7,6},{8,9},{9,8},{10,11... | collective-permute-start | bytes 995336 | tf_op jit(solution)/shard_map/ppermute | solution.py:71
  94.9 6.5 %collective-permute-start.26 = (bf16[64,768]{1,0:T(8,128)(2,1)S(1)}, bf16[64,768]{1,0:T(8,128)(2,1)S(1)}, u32[]{:S(2)}, u32[]{:S(2)}) collective-permute-start(bf16[64,768]{1,0:T(8,128)(2,1)S(1)} %get-tuple-element.121), channel_id=1, source_target_pairs={{0,8},{1,9},{2,10},{3,11},{4,12},{5,13},{6,14},{7,15},{8,0},{9,1},... | collective-permute-start | bytes 294920 | tf_op jit(solution)/shard_map/ppermute | solution.py:64
  104.5 7.8 %collective-permute-start.33 = (bf16[64,3072]{1,0:T(8,128)(2,1)S(1)}, bf16[64,3072]{1,0:T(8,128)(2,1)S(1)}, u32[]{:S(2)}, u32[]{:S(2)}) collective-permute-start(bf16[64,3072]{1,0:T(8,128)(2,1)S(1)} %shard_map.377.refs_0_), channel_id=1, source_target_pairs={{0,4},{1,3},{2,6},{3,1},{4,0},{5,7},{6,2},{7,5},{8,12},{9,11},{10,... | collective-permute-start | bytes 1179656 | tf_op jit(solution)/shard_map/ppermute | solution.py:64
  109.3 15.3 %collective-permute-start.30 = (bf16[128,1792]{1,0:T(8,128)(2,1)S(1)}, bf16[128,1792]{1,0:T(8,128)(2,1)S(1)}, u32[]{:S(2)}, u32[]{:S(2)}) collective-permute-start(bf16[128,1792]{1,0:T(8,128)(2,1)S(1)} %get-tuple-element.129), channel_id=1, source_target_pairs={{0,1},{1,0},{2,3},{3,2},{4,5},{5,4},{6,7},{7,6},{8,9},{9,8},{10,11... | collective-permute-start | bytes 1376264 | tf_op jit(solution)/shard_map/ppermute | solution.py:71
  112.6 13.0 %collective-permute-start.34 = (bf16[128,1792]{1,0:T(8,128)(2,1)S(1)}, bf16[128,1792]{1,0:T(8,128)(2,1)S(1)}, u32[]{:S(2)}, u32[]{:S(2)}) collective-permute-start(bf16[128,1792]{1,0:T(8,128)(2,1)S(1)} %shard_map.380.refs_2_), channel_id=1, source_target_pairs={{0,2},{1,5},{2,0},{3,7},{4,6},{5,1},{6,4},{7,3},{8,10},{9,13},{10,... | collective-permute-start | bytes 1376264 | tf_op jit(solution)/shard_map/ppermute | solution.py:64
  114.0 8.7 %collective-permute-start.29 = (bf16[2,162,512]{2,1,0:T(8,128)(2,1)S(1)}, bf16[2,162,512]{2,1,0:T(8,128)(2,1)S(1)}, u32[]{:S(2)}, u32[]{:S(2)}) collective-permute-start(bf16[2,162,512]{2,1,0:T(8,128)(2,1)S(1)} %get-tuple-element.127), channel_id=1, source_target_pairs={{0,1},{1,0},{2,3},{3,2},{4,5},{5,4},{6,7},{7,6},{8,9},{9,8},{10,11... | collective-permute-start | bytes 995336 | tf_op jit(solution)/shard_map/ppermute | solution.py:71
  114.1 8.4 %collective-permute-start.35 = (bf16[64,768]{1,0:T(8,128)(2,1)S(1)}, bf16[64,768]{1,0:T(8,128)(2,1)S(1)}, u32[]{:S(2)}, u32[]{:S(2)}) collective-permute-start(bf16[64,768]{1,0:T(8,128)(2,1)S(1)} %get-tuple-element.133), channel_id=1, source_target_pairs={{0,16},{1,17},{2,18},{3,19},{4,20},{5,21},{6,22},{7,23},{8,24},{9,... | collective-permute-start | bytes 294920 | tf_op jit(solution)/shard_map/ppermute | solution.py:64
  117.5 17.3 %collective-permute-start.40 = (bf16[16,3072]{1,0:T(8,128)(2,1)S(1)}, bf16[16,3072]{1,0:T(8,128)(2,1)S(1)}, u32[]{:S(2)}, u32[]{:S(2)}) collective-permute-start(bf16[16,3072]{1,0:T(8,128)(2,1)S(1)} %get-tuple-element.138), channel_id=1, source_target_pairs={{0,8},{1,9},{2,10},{3,11},{4,12},{5,13},{6,14},{7,15},{8,0},{9,1},... | collective-permute-start | bytes 294920 | tf_op jit(solution)/shard_map/ppermute | solution.py:64
  122.5 13.7 %collective-permute-start.41 = (bf16[16,3072]{1,0:T(8,128)(2,1)S(1)}, bf16[16,3072]{1,0:T(8,128)(2,1)S(1)}, u32[]{:S(2)}, u32[]{:S(2)}) collective-permute-start(bf16[16,3072]{1,0:T(8,128)(2,1)S(1)} %get-tuple-element.139), channel_id=1, source_target_pairs={{0,16},{1,17},{2,18},{3,19},{4,20},{5,21},{6,22},{7,23},{8,24},{9,... | collective-permute-start | bytes 294920 | tf_op jit(solution)/shard_map/ppermute | solution.py:64
  122.8 14.6 %collective-permute-start.42 = (bf16[16,3072]{1,0:T(8,128)(2,1)S(1)}, bf16[16,3072]{1,0:T(8,128)(2,1)S(1)}, u32[]{:S(2)}, u32[]{:S(2)}) collective-permute-start(bf16[16,3072]{1,0:T(8,128)(2,1)S(1)} %get-tuple-element.140), channel_id=1, source_target_pairs={{0,24},{1,25},{2,26},{3,27},{4,28},{5,29},{6,30},{7,31},{8,16},{9,... | collective-permute-start | bytes 294920 | tf_op jit(solution)/shard_map/ppermute | solution.py:64
  125.7 7.1 %collective-permute-start.36 = (bf16[64,1792]{1,0:T(8,128)(2,1)S(1)}, bf16[64,1792]{1,0:T(8,128)(2,1)S(1)}, u32[]{:S(2)}, u32[]{:S(2)}) collective-permute-start(bf16[64,1792]{1,0:T(8,128)(2,1)S(1)} %shard_map.382.refs_4_), channel_id=1, source_target_pairs={{0,4},{1,3},{2,6},{3,1},{4,0},{5,7},{6,2},{7,5},{8,12},{9,11},{10,... | collective-permute-start | bytes 688136 | tf_op jit(solution)/shard_map/ppermute | solution.py:64
  129.3 11.9 %collective-permute-start.44 = (bf16[64,768]{1,0:T(8,128)(2,1)S(1)}, bf16[64,768]{1,0:T(8,128)(2,1)S(1)}, u32[]{:S(2)}, u32[]{:S(2)}) collective-permute-start(bf16[64,768]{1,0:T(8,128)(2,1)S(1)} %shard_map.381.refs_3_.refs_0_), channel_id=1, source_target_pairs={{0,2},{1,5},{2,0},{3,7},{4,6},{5,1},{6,4},{7,3},{8,10},{9,13},{10,... | collective-permute-start | bytes 294920 | tf_op jit(solution)/shard_map/ppermute | solution.py:64
  132.8 8.4 %collective-permute-start.45 = (bf16[64,768]{1,0:T(8,128)(2,1)S(1)}, bf16[64,768]{1,0:T(8,128)(2,1)S(1)}, u32[]{:S(2)}, u32[]{:S(2)}) collective-permute-start(bf16[64,768]{1,0:T(8,128)(2,1)S(1)} %collective-permute-done.43.refs_1_), channel_id=1, source_target_pairs={{0,2},{1,5},{2,0},{3,7},{4,6},{5,1},{6,4},{7,3},{8,10},{9,13},{10,... | collective-permute-start | bytes 294920 | tf_op jit(solution)/shard_map/ppermute | solution.py:64
  134.7 9.4 %collective-permute-start.37 = (bf16[16,1792]{1,0:T(8,128)(2,1)S(1)}, bf16[16,1792]{1,0:T(8,128)(2,1)S(1)}, u32[]{:S(2)}, u32[]{:S(2)}) collective-permute-start(bf16[16,1792]{1,0:T(8,128)(2,1)S(1)} %get-tuple-element.135), channel_id=1, source_target_pairs={{0,8},{1,9},{2,10},{3,11},{4,12},{5,13},{6,14},{7,15},{8,0},{9,1},... | collective-permute-start | bytes 172040 | tf_op jit(solution)/shard_map/ppermute | solution.py:64
  136.2 8.0 %collective-permute-start.38 = (bf16[16,1792]{1,0:T(8,128)(2,1)S(1)}, bf16[16,1792]{1,0:T(8,128)(2,1)S(1)}, u32[]{:S(2)}, u32[]{:S(2)}) collective-permute-start(bf16[16,1792]{1,0:T(8,128)(2,1)S(1)} %get-tuple-element.136), channel_id=1, source_target_pairs={{0,16},{1,17},{2,18},{3,19},{4,20},{5,21},{6,22},{7,23},{8,24},{9,... | collective-permute-start | bytes 172040 | tf_op jit(solution)/shard_map/ppermute | solution.py:64
  137.4 6.8 %collective-permute-start.39 = (bf16[16,1792]{1,0:T(8,128)(2,1)S(1)}, bf16[16,1792]{1,0:T(8,128)(2,1)S(1)}, u32[]{:S(2)}, u32[]{:S(2)}) collective-permute-start(bf16[16,1792]{1,0:T(8,128)(2,1)S(1)} %get-tuple-element.137), channel_id=1, source_target_pairs={{0,24},{1,25},{2,26},{3,27},{4,28},{5,29},{6,30},{7,31},{8,16},{9,... | collective-permute-start | bytes 172040 | tf_op jit(solution)/shard_map/ppermute | solution.py:64
  (37 other events, 145.8 us)

commit v7 on v6

--- a/solution.py
+++ b/solution.py
@@ -643,31 +643,11 @@
     )
 
 
-def out_grads(gated, gb, after):
+def weight_grads(levels, sides, vec, gated, q, h, wl, wo, x, half, after):
     count = len(after)
 
-    def kernel(t_ref, gb_ref, *refs):
-        gwo = refs[count]
-
-        def out_tile(n, carry):
-            cols = pl.ds(pl.multiple_of(n * TILE, TILE), TILE)
-            gwo[cols, :] = dot(t_ref[:, cols], gb_ref[...], TN).astype(BF)
-            return carry
-
-        lax.fori_loop(0, HALF // TILE, out_tile, 0)
-
-    return call(
-        kernel, sds((HALF, D), BF), [VM] * 2 + [HB] * count, [], 1000000000, 5000000, gated, gb, *after, room=10
-    )
-
-
-def weight_grads(table, levels, sides, vec, gated, q, gwo, h, wl, wo, x, half, after):
-    count = len(after)
-
-    def kernel(
-        table_ref, levels_ref, sides_ref, vec_ref, t_ref, q_ref, gwo, h_ref, wl_ref, wo_ref, x_ref, *refs
-    ):
-        keep, send, send_up, stay_ref, away_ref, gh_ref, branch, gwl = refs[count:]
+    def kernel(levels_ref, sides_ref, vec_ref, t_ref, q_ref, h_ref, wl_ref, wo_ref, x_ref, *refs):
+        gwl, stay_ref, away_ref, gh_ref, branch = refs[count:]
 
         def in_tile(n, carry):
             cols = pl.ds(pl.multiple_of(n * TILE, TILE), TILE)
@@ -681,37 +661,64 @@
         live = jnp.concatenate([live_mask(levels_ref, b, D) for b in range(2)], axis=0)
         out = branch[...] + seg(vec_ref, "c2")
         split_rows(branch, stay_ref, away_ref, me, x_ref[...].astype(F32) + jnp.where(live, out, 0.0))
-        for k in range(DEVS):
-            dev = table_ref[k]
-            target = keep if k < GROUPS else send if k < GROUPS * 3 // 2 else send_up
-            r = pl.ds(k % (GROUPS if k < GROUPS else GROUPS // 2) * 16, 16)
-            target[r, 0:HALF] = gwl[pl.ds(pl.multiple_of(dev * 16, 16), 16), :]
-            for g in range(3):
-                target[r, HALF + g * D : HALF + (g + 1) * D] = gwo[pl.ds(pl.multiple_of(dev * 48 + 16 * g, 16), 16), :]
 
     pair = sds((2, half, D), BF)
-    payload = sds((D // 2, LO), BF)
-    part = sds((D // 4, LO), BF)
     return call(
         kernel,
-        (payload, part, part, pair, pair, sds((ROWS, D), F32)),
-        [SM] * 3 + [VM] * 8 + [HB] * count,
-        [pltpu.VMEM((ROWS, D), F32), pltpu.VMEM((D, HALF), BF)],
-        5000000000,
-        15000000,
-        table,
+        (sds((D, HALF), BF), pair, pair, sds((ROWS, D), F32)),
+        [SM] * 2 + [VM] * 7 + [HB] * count,
+        [pltpu.VMEM((ROWS, D), F32)],
+        4000000000,
+        12000000,
         levels,
         sides,
         vec,
         gated,
         q,
-        gwo,
         h,
         wl,
         wo,
         x,
         *after,
-        room=24,
+        room=12,
+    )
+
+
+def out_grads(table, gated, gb, gwl, after):
+    count = len(after)
+
+    def kernel(table_ref, t_ref, gb_ref, gwl_ref, *refs):
+        keep, send, send_up, gwo = refs[count:]
+
+        def out_tile(n, carry):
+            cols = pl.ds(pl.multiple_of(n * TILE, TILE), TILE)
+            gwo[cols, :] = dot(t_ref[:, cols], gb_ref[...], TN).astype(BF)
+            return carry
+
+        lax.fori_loop(0, HALF // TILE, out_tile, 0)
+        for k in range(DEVS):
+            dev = table_ref[k]
+            target = keep if k < GROUPS else send if k < GROUPS * 3 // 2 else send_up
+            r = pl.ds(k % (GROUPS if k < GROUPS else GROUPS // 2) * 16, 16)
+            target[r, 0:HALF] = gwl_ref[pl.ds(pl.multiple_of(dev * 16, 16), 16), :]
+            for g in range(3):
+                target[r, HALF + g * D : HALF + (g + 1) * D] = gwo[pl.ds(pl.multiple_of(dev * 48 + 16 * g, 16), 16), :]
+
+    payload = sds((D // 2, LO), BF)
+    part = sds((D // 4, LO), BF)
+    return call(
+        kernel,
+        (payload, part, part),
+        [SM] + [VM] * 3 + [HB] * count,
+        [pltpu.VMEM((HALF, D), BF)],
+        2000000000,
+        8000000,
+        table,
+        gated,
+        gb,
+        gwl,
+        *after,
+        room=10,
     )
 
 
@@ -1196,31 +1203,29 @@
         sp_part = add_part([sp_keep, sp_got], 128, [])
         sp_terms = [sp_keep, sp_got, route.swap(sp_part, near)]
         after[0] = [sp_part]
-    gwo = out_grads(gated, gb, after[0])
+    gwl, mixed_stay, mixed_away, gh = weight_grads(levels, sides, vec, gated, q, h, wl, wo, x, rows, after[0])
     if fits:
-        sp_part = add_part(sp_terms, 64, [gwo])
+        sp_part = add_part(sp_terms, 64, [gh])
         sp_terms.append(route.swap(sp_part, far))
         after[1] = [sp_part]
-    lo_keep, lo_send, lo_up, mixed_stay, mixed_away, gh = weight_grads(
-        ktable, levels, sides, vec, gated, q, gwo, h, wl, wo, x, rows, after[1]
-    )
+    lo_keep, lo_send, lo_up = out_grads(ktable, gated, gb, gwl, after[1])
     mixed_got = route.cross(mixed_away)
     if fits:
         lo_up = route.cross(lo_up)
         lo_terms = [lo_keep, route.cross(lo_send)]
         lo_part = add_part([lo_keep, lo_up], 128, [], [1, 0])
         lo_terms.append(route.swap(lo_part, near))
-        sp_own, sp_out = line_turn(sp_terms, 1, [lo_part])
-        sp_terms = [sp_own, route.swap(sp_out, (route.direct[0],) * 2)]
-        after[2] = [sp_own]
+        after[2] = [lo_part]
     gp, gate_sum = gate_backward(vec, gs, mm, hat, slope, scale, after[2])
     if fits:
-        sp_own, sp_out = line_turn(sp_terms, 2, [gate_sum])
-        sp_terms = [sp_own, route.swap(sp_out, (route.direct[1],) * 2)]
+        sp_own, sp_out = line_turn(sp_terms, 1, [gate_sum])
+        sp_terms = [sp_own, route.swap(sp_out, (route.direct[0],) * 2)]
         after[3] = [sp_own, mixed_got]
     gwr, ghb = in_grads(gp, h, weight_right, gh, after[3])
     if fits:
-        lo_part = add_part(lo_terms, 64, [gwr])
+        sp_own, sp_out = line_turn(sp_terms, 2, [gwr])
+        sp_terms = [sp_own, route.swap(sp_out, (route.direct[1],) * 2)]
+        lo_part = add_part(lo_terms, 64, [sp_own])
         lo_terms.append(route.swap(lo_part, far))
         after[4] = [lo_part]
     right_keep, right_send, up_a, up_b, grad_stay, grad_away = in_backward(
@@ -1234,11 +1239,11 @@
         lo_got = [route.swap(p, (m, m)) for p, m in zip(sends, route.direct)]
         right_part = add_upper(right_keep, upper, [lo_own])
         right_terms.append(route.swap(right_part, near))
-        (sp_sum,) = line_turn(sp_terms, 0, [right_part, grad_got])
+        right_part = add_part(right_terms, 64, [grad_got])
+        right_terms.append(route.swap(right_part, far))
+        (sp_sum,) = line_turn(sp_terms, 0, [right_part])
         spat_pieces = route.widen(sp_sum)
-        right_part = add_part(right_terms, 64, [sp_sum])
-        right_terms.append(route.swap(right_part, far))
-        right_own, *sends = line_parts(right_terms, [right_part])
+        right_own, *sends = line_parts(right_terms, [sp_sum])
         right_got = [route.swap(p, (m, m)) for p, m in zip(sends, route.direct)]
         left_sum, *new_out = finish_out(lo_own, lo_got, dense_out, out_first, out_second, right_own)
         korder = order

time: 147 us -> 138 us (0.939)
  waiting for transfers between devices: 37 us -> 27.7 us
    ppermute x29, waiting for transfers between devices: 30.7 us -> 21.4 us  [swap(): return lax.ppermute(block, AXES, pairs)]
  transfers between devices with their start and end apart: 46 -> 46, of which waited for: 14 -> 15; matrix products, arithmetic and copies ran while one was open for 3% -> 3% of each run, Pallas kernels for 25% -> 28%
where the time goes in v7:
time: 138 us
  Pallas kernels  59.1 us (43%)
  starting transfers between devices  41 us (30%)
  waiting for transfers between devices  27.7 us (20%)
  local copies, waits for them, and re-layouts  7.25 us (5%)
  other arithmetic  1.66 us (1%)
    pallas_call x17, Pallas kernels, call(): pl.pallas_call(kernel, out_shape=out_shape, in_specs=in_specs, out_specs=...  58 us
    ppermute x29, starting transfers between devices, swap(): return lax.ppermute(block, AXES, pairs)  37.4 us
    ppermute x29, waiting for transfers between devices, swap(): return lax.ppermute(block, AXES, pairs)  21.4 us
    unnamed x50, local copies, waits for them, and re-layouts  6.33 us
    ppermute x17, waiting for transfers between devices, cross(): return lax.ppermute(block, AXES, pairs)  6.3 us
    ppermute x17, starting transfers between devices, cross(): return lax.ppermute(block, AXES, pairs)  3.58 us
  transfers between devices with their start and end apart: 46, of which 15 were waited for; matrix products, arithmetic and copies ran while one was open for 3% of the time, Pallas kernels for 28%

profile of v7, /device:TPU:0, one launch (start us, length us, event | category | flops | bytes accessed | tf_op | source)
XLA Modules:
  0.0 137.9 jit_solution(689241792292729576)
XLA Ops:
  0.7 1.7 %shard_map.360 = (bf16[16,1792]{1,0:T(8,128)(2,1)}, bf16[16,3072]{1,0:T(8,128)(2,1)}) custom-call(f32[16,3072]{1,0:T(8,128)} %w_ref.3, f32[48,512]{1,0:T(8,128)} %w_ref.2, f32[1,240]{1,0:T(1,128)} %bitcast.7), custom_call_target="tpu_custom_call" | custom-call | flops 1000 | bytes 600000 | tf_op jit(solution)/shard_map/pallas_call | solution.py:220
  2.4 5.1 %collective-permute-start.4 = (bf16[16,1792]{1,0:T(8,128)(2,1)}, bf16[16,1792]{1,0:T(8,128)(2,1)S(1)}, u32[]{:S(2)}, u32[]{:S(2)}) collective-permute-start(bf16[16,1792]{1,0:T(8,128)(2,1)} %get-tuple-element.89.refs_0_), channel_id=1, source_target_pairs={{0,24},{1,25},{2,26},{3,27},{4,28},{5,29},{6,30},{7,31},{8,16},{9,... | collective-permute-start | bytes 172040 | tf_op jit(solution)/shard_map/ppermute | solution.py:64
  8.1 2.0 %collective-permute-done.4.refs_3_ = bf16[16,1792]{1,0:T(8,128)(2,1)S(1)} collective-permute-done((bf16[16,1792]{1,0:T(8,128)(2,1)}, bf16[16,1792]{1,0:T(8,128)(2,1)S(1)}, u32[]{:S(2)}, u32[]{:S(2)}) %collective-permute-start.4) | collective-permute-done | bytes 57376 | tf_op jit(solution)/shard_map/ppermute | solution.py:64
  10.1 2.6 %collective-permute-done.3.refs_2_ = bf16[16,1792]{1,0:T(8,128)(2,1)S(1)} collective-permute-done((bf16[16,1792]{1,0:T(8,128)(2,1)}, bf16[16,1792]{1,0:T(8,128)(2,1)S(1)}, u32[]{:S(2)}, u32[]{:S(2)}) %collective-permute-start.3) | collective-permute-done | bytes 57376 | tf_op jit(solution)/shard_map/ppermute | solution.py:64
  13.6 1.6 %collective-permute-start.6 = (bf16[64,1792]{1,0:T(8,128)(2,1)S(1)}, bf16[64,1792]{1,0:T(8,128)(2,1)S(1)}, u32[]{:S(2)}, u32[]{:S(2)}) collective-permute-start(bf16[64,1792]{1,0:T(8,128)(2,1)S(1)} %shard_map.361.refs_0_), channel_id=1, source_target_pairs={{0,2},{1,5},{2,0},{3,7},{4,6},{5,1},{6,4},{7,3},{8,10},{9,13},{10,... | collective-permute-start | bytes 688136 | tf_op jit(solution)/shard_map/ppermute | solution.py:64
  15.2 1.5 %collective-permute-start.5 = (bf16[64,1792]{1,0:T(8,128)(2,1)S(1)}, bf16[64,1792]{1,0:T(8,128)(2,1)S(1)}, u32[]{:S(2)}, u32[]{:S(2)}) collective-permute-start(bf16[64,1792]{1,0:T(8,128)(2,1)S(1)} %shard_map.361.refs_0_), channel_id=1, source_target_pairs={{0,4},{1,3},{2,6},{3,1},{4,0},{5,7},{6,2},{7,5},{8,12},{9,11},{10,... | collective-permute-start | bytes 688136 | tf_op jit(solution)/shard_map/ppermute | solution.py:64
  16.7 2.6 %collective-permute-start.15 = (bf16[16,3072]{1,0:T(8,128)(2,1)}, bf16[16,3072]{1,0:T(8,128)(2,1)S(1)}, u32[]{:S(2)}, u32[]{:S(2)}) collective-permute-start(bf16[16,3072]{1,0:T(8,128)(2,1)} %get-tuple-element.98.refs_0_), channel_id=1, source_target_pairs={{0,24},{1,25},{2,26},{3,27},{4,28},{5,29},{6,30},{7,31},{8,16},{9,... | collective-permute-start | bytes 294920 | tf_op jit(solution)/shard_map/ppermute | solution.py:64
  20.0 1.6 %collective-permute-done.6.refs_1_.refs_2_ = bf16[64,1792]{1,0:T(8,128)(2,1)S(1)} collective-permute-done((bf16[64,1792]{1,0:T(8,128)(2,1)S(1)}, bf16[64,1792]{1,0:T(8,128)(2,1)S(1)}, u32[]{:S(2)}, u32[]{:S(2)}) %collective-permute-start.6) | collective-permute-done | bytes 229408 | tf_op jit(solution)/shard_map/ppermute | solution.py:64
  21.7 1.6 %collective-permute-start.7 = (bf16[64,1792]{1,0:T(8,128)(2,1)S(1)}, bf16[64,1792]{1,0:T(8,128)(2,1)}, u32[]{:S(2)}, u32[]{:S(2)}) collective-permute-start(bf16[64,1792]{1,0:T(8,128)(2,1)S(1)} %shard_map.362.refs_4_), channel_id=1, source_target_pairs={{0,2},{1,5},{2,0},{3,7},{4,6},{5,1},{6,4},{7,3},{8,10},{9,13},{10,... | collective-permute-start | bytes 688136 | tf_op jit(solution)/shard_map/ppermute | solution.py:64
  25.5 1.5 %shard_map.359 = (bf16[3,162,384]{2,1,0:T(8,128)(2,1)S(1)}, bf16[2,162,512]{2,1,0:T(8,128)(2,1)}, bf16[2,162,512]{2,1,0:T(8,128)(2,1)}) custom-call(s32[33]{0:T(128)S(1)} %pad_add_fusion.1.sides_ref, f32[3,162,324]{2,1,0:T(8,128)S(1)} %copy-done, f32[3,162,1]{2,1,0:T(8,128)S(1)} %copy.47.b_ref, bf16[4,162,512]{2,1,0:T(8,128)(2,1)S(1)} %copy.50.x_ref.p_ref, ...), custom_call_target="tpu_custom_call" | custom-call | flops 1000 | bytes 3000000 | tf_op jit(solution)/shard_map/pallas_call | solution.py:220
  28.9 4.2 %collective-permute-done.13.refs_1_ = bf16[16,3072]{1,0:T(8,128)(2,1)S(1)} collective-permute-done((bf16[16,3072]{1,0:T(8,128)(2,1)S(1)}, bf16[16,3072]{1,0:T(8,128)(2,1)S(1)}, u32[]{:S(2)}, u32[]{:S(2)}) %collective-permute-start.13) | collective-permute-done | bytes 98336 | tf_op jit(solution)/shard_map/ppermute | solution.py:64
  37.1 1.5 %collective-permute-start.16 = (bf16[64,3072]{1,0:T(8,128)(2,1)S(1)}, bf16[64,3072]{1,0:T(8,128)(2,1)S(1)}, u32[]{:S(2)}, u32[]{:S(2)}) collective-permute-start(bf16[64,3072]{1,0:T(8,128)(2,1)S(1)} %shard_map.365.refs_0_), channel_id=1, source_target_pairs={{0,4},{1,3},{2,6},{3,1},{4,0},{5,7},{6,2},{7,5},{8,12},{9,11},{10,... | collective-permute-start | bytes 1179656 | tf_op jit(solution)/shard_map/ppermute | solution.py:64
  38.7 11.0 %shard_map.363 = (bf16[672,512]{1,0:T(8,128)(2,1)S(1)}, bf16[672,512]{1,0:T(8,128)(2,1)S(1)}, bf16[672,512]{1,0:T(8,128)(2,1)S(1)}, f32[672,1536]{1,0:T(8,128)S(...) custom-call(s32[32]{0:T(128)S(1)} %get-tuple-element.195.table_ref, ...), custom_call_target="tpu_custom_call" | custom-call | flops 10000000000 | bytes 20000000 | tf_op jit(solution)/shard_map/pallas_call | solution.py:220
  49.7 5.0 %shard_map.364 = (bf16[720,1536]{1,0:T(8,128)(2,1)S(1)}, bf16[672,1536]{1,0:T(8,128)(2,1)S(1)}, f32[672,128]{1,0:T(8,128)S(1)}, bf16[672,1536]{1,0:T(8,128)(2,1)S(1)}, bf16[2,336,384]{2,1,0:T(8,128)(2,1)S(1)}) custom-call(s32[2]{0:T(128)S(1)} %dynamic_slice.3.levels_ref, s32[33]{0:T(128)S(1)} %pad_add_fusion.1.sides_ref, ...), custom_call_target="tpu_custom_call" | custom-call | flops 6000000000 | bytes 12000000 | tf_op jit(solution)/shard_map/pallas_call | solution.py:220
  56.1 2.9 %collective-permute-done.19.refs_4_ = bf16[64,3072]{1,0:T(8,128)(2,1)S(1)} collective-permute-done((bf16[64,3072]{1,0:T(8,128)(2,1)S(1)}, bf16[64,3072]{1,0:T(8,128)(2,1)S(1)}, u32[]{:S(2)}, u32[]{:S(2)}) %collective-permute-start.19) | collective-permute-done | bytes 393248 | tf_op jit(solution)/shard_map/ppermute | solution.py:71
  59.0 14.0 %shard_map.367 = (bf16[672,1536]{1,0:T(8,128)(2,1)S(1)}, bf16[672,1536]{1,0:T(8,128)(2,1)S(1)}, bf16[672,1536]{1,0:T(8,128)(2,1)S(1)}, bf16[672,512]{1,0:T(8,128...) custom-call(s32[32]{0:T(128)S(1)} %get-tuple-element.195.table_ref, ...), custom_call_target="tpu_custom_call" | custom-call | flops 8000000000 | bytes 16000000 | tf_op jit(solution)/shard_map/pallas_call | solution.py:220
  73.2 1.6 %collective-permute-done.21.refs_1_ = bf16[256,768]{1,0:T(8,128)(2,1)S(1)} collective-permute-done((bf16[256,768]{1,0:T(8,128)(2,1)S(1)}, bf16[256,768]{1,0:T(8,128)(2,1)S(1)}, u32[]{:S(2)}, u32[]{:S(2)}) %collective-permute-start.21) | collective-permute-done | bytes 393248 | tf_op jit(solution)/shard_map/ppermute | solution.py:71
  75.6 4.9 %shard_map.369 = (bf16[512,1536]{1,0:T(8,128)(2,1)S(1)}, bf16[2,162,512]{2,1,0:T(8,128)(2,1)S(1)}, bf16[2,162,512]{2,1,0:T(8,128)(2,1)S(1)}, f32[672,512]{1,0:T(8,128)S(1)}) custom-call(s32[2]{0:T(128)S(1)} %dynamic_slice.3.levels_ref, s32[33]{0:T(128)S(1)} %pad_add_fusion.1.sides_ref, f32[1,7680]{1,0:T(1,128)S(1)} %get-tuple-element.90.vec_ref, ...), custom_call_target="tpu_custom_call" | custom-call | flops 4000000000 | bytes 12000000 | tf_op jit(solution)/shard_map/pallas_call | solution.py:220
  80.7 3.2 %shard_map.371 = (bf16[256,3072]{1,0:T(8,128)(2,1)S(1)}, bf16[128,3072]{1,0:T(8,128)(2,1)S(1)}, bf16[128,3072]{1,0:T(8,128)(2,1)S(1)}) custom-call(s32[32]{0:T(128)S(1)} %get-tuple-element.195.table_ref, bf16[672,1536]{1,0:T(8,128)(2,1)S(1)} %get-tuple-element.100.t_ref, bf16[672,512]{1,0:T(8,128)(2,1)S(1)} %get-tuple-element.114.gb_ref, ...), custom_call_target="tpu_custom_call" | custom-call | flops 2000000000 | bytes 8000000 | tf_op jit(solution)/shard_map/pallas_call | solution.py:220
  84.4 1.8 %collective-permute-done.24.refs_1_ = bf16[128,3072]{1,0:T(8,128)(2,1)S(1)} collective-permute-done((bf16[128,3072]{1,0:T(8,128)(2,1)S(1)}, bf16[128,3072]{1,0:T(8,128)(2,1)S(1)}, u32[]{:S(2)}, u32[]{:S(2)}) %collective-permute-start.24) | collective-permute-done | bytes 786464 | tf_op jit(solution)/shard_map/ppermute | solution.py:71
  88.5 5.7 %shard_map.373 = (bf16[672,1536]{1,0:T(8,128)(2,1)S(1)}, f32[1,4608]{1,0:T(1,128)S(1)}) custom-call(f32[1,7680]{1,0:T(1,128)S(1)} %get-tuple-element.90.vec_ref, bf16[672,1536]{1,0:T(8,128)(2,1)S(1)} %get-tuple-element.110.gs_ref, bf16[2,336,384]{2,1,0:T(8,128)(2,1)S(1)} %get-tuple-element.99.refs_3_.mm_ref, ...), custom_call_target="tpu_custom_call" | custom-call | flops 3000000000 | bytes 10000000 | tf_op jit(solution)/shard_map/pallas_call | solution.py:220
  95.1 2.7 %shard_map.375 = (bf16[512,1536]{1,0:T(8,128)(2,1)S(1)}, f32[672,512]{1,0:T(8,128)S(1)}) custom-call(bf16[672,1536]{1,0:T(8,128)(2,1)S(1)} %get-tuple-element.120.gp_ref, bf16[672,512]{1,0:T(8,128)(2,1)S(1)} %get-tuple-element.91.h_ref, bf16[512,1536]{1,0:T(8,128)(2,1)S(1)} %get-tuple-element.121.w_ref, f32[672,512]{1,0:T(8,128)S(1)} %get-tuple-element.116.refs_3_.gh_ref, ...), custom_call_target="tpu_custom_call" | custom-call | flops 3000000000 | bytes 8000000 | tf_op jit(solution)/shard_map/pallas_call | solution.py:220
  97.8 1.4 %collective-permute-done.28.refs_1_ = bf16[64,768]{1,0:T(8,128)(2,1)S(1)} collective-permute-done((bf16[64,768]{1,0:T(8,128)(2,1)S(1)}, bf16[64,768]{1,0:T(8,128)(2,1)S(1)}, u32[]{:S(2)}, u32[]{:S(2)}) %collective-permute-start.28) | collective-permute-done | bytes 98336 | tf_op jit(solution)/shard_map/ppermute | solution.py:64
  100.7 2.8 %shard_map.378 = (bf16[256,1792]{1,0:T(8,128)(2,1)S(1)}, bf16[128,1792]{1,0:T(8,128)(2,1)S(1)}, bf16[64,1792]{1,0:T(8,128)(2,1)S(1)}, bf16[64,1792]{1,0:T(8,128)...) custom-call(s32[32]{0:T(128)S(1)} %get-tuple-element.195.table_ref, ...), custom_call_target="tpu_custom_call" | custom-call | flops 2000000000 | bytes 6000000 | tf_op jit(solution)/shard_map/pallas_call | solution.py:220
  104.2 3.3 %collective-permute-done.33.refs_3_ = bf16[64,3072]{1,0:T(8,128)(2,1)S(1)} collective-permute-done((bf16[64,3072]{1,0:T(8,128)(2,1)S(1)}, bf16[64,3072]{1,0:T(8,128)(2,1)S(1)}, u32[]{:S(2)}, u32[]{:S(2)}) %collective-permute-start.33) | collective-permute-done | bytes 393248 | tf_op jit(solution)/shard_map/ppermute | solution.py:64
  109.2 1.4 %collective-permute-start.36 = (bf16[64,768]{1,0:T(8,128)(2,1)S(1)}, bf16[64,768]{1,0:T(8,128)(2,1)S(1)}, u32[]{:S(2)}, u32[]{:S(2)}) collective-permute-start(bf16[64,768]{1,0:T(8,128)(2,1)S(1)} %get-tuple-element.135), channel_id=1, source_target_pairs={{0,16},{1,17},{2,18},{3,19},{4,20},{5,21},{6,22},{7,23},{8,24},{9,... | collective-permute-start | bytes 294920 | tf_op jit(solution)/shard_map/ppermute | solution.py:64
  111.9 1.4 %collective-permute-start.40 = (bf16[16,3072]{1,0:T(8,128)(2,1)S(1)}, bf16[16,3072]{1,0:T(8,128)(2,1)S(1)}, u32[]{:S(2)}, u32[]{:S(2)}) collective-permute-start(bf16[16,3072]{1,0:T(8,128)(2,1)S(1)} %get-tuple-element.140), channel_id=1, source_target_pairs={{0,8},{1,9},{2,10},{3,11},{4,12},{5,13},{6,14},{7,15},{8,0},{9,1},... | collective-permute-start | bytes 294920 | tf_op jit(solution)/shard_map/ppermute | solution.py:64
  114.2 2.1 %collective-permute-start.42 = (bf16[16,3072]{1,0:T(8,128)(2,1)S(1)}, bf16[16,3072]{1,0:T(8,128)(2,1)S(1)}, u32[]{:S(2)}, u32[]{:S(2)}) collective-permute-start(bf16[16,3072]{1,0:T(8,128)(2,1)S(1)} %get-tuple-element.142), channel_id=1, source_target_pairs={{0,24},{1,25},{2,26},{3,27},{4,28},{5,29},{6,30},{7,31},{8,16},{9,... | collective-permute-start | bytes 294920 | tf_op jit(solution)/shard_map/ppermute | solution.py:64
  119.4 4.1 %collective-permute-done.43.refs_1_ = bf16[64,768]{1,0:T(8,128)(2,1)S(1)} collective-permute-done((bf16[64,768]{1,0:T(8,128)(2,1)S(1)}, bf16[64,768]{1,0:T(8,128)(2,1)S(1)}, u32[]{:S(2)}, u32[]{:S(2)}) %collective-permute-start.43) | collective-permute-done | bytes 98336 | tf_op jit(solution)/shard_map/ppermute | solution.py:64
  126.5 2.1 %collective-permute-start.38 = (bf16[16,1792]{1,0:T(8,128)(2,1)S(1)}, bf16[16,1792]{1,0:T(8,128)(2,1)S(1)}, u32[]{:S(2)}, u32[]{:S(2)}) collective-permute-start(bf16[16,1792]{1,0:T(8,128)(2,1)S(1)} %get-tuple-element.138), channel_id=1, source_target_pairs={{0,16},{1,17},{2,18},{3,19},{4,20},{5,21},{6,22},{7,23},{8,24},{9,... | collective-permute-start | bytes 172040 | tf_op jit(solution)/shard_map/ppermute | solution.py:64
  128.6 1.6 %collective-permute-start.39 = (bf16[16,1792]{1,0:T(8,128)(2,1)S(1)}, bf16[16,1792]{1,0:T(8,128)(2,1)S(1)}, u32[]{:S(2)}, u32[]{:S(2)}) collective-permute-start(bf16[16,1792]{1,0:T(8,128)(2,1)S(1)} %get-tuple-element.139), channel_id=1, source_target_pairs={{0,24},{1,25},{2,26},{3,27},{4,28},{5,29},{6,30},{7,31},{8,16},{9,... | collective-permute-start | bytes 172040 | tf_op jit(solution)/shard_map/ppermute | solution.py:64
  132.4 2.8 %shard_map.385 = (f32[3,162,324]{2,1,0:T(8,128)}, f32[3,162,324]{2,1,0:T(8,128)}, f32[3,162,324]{2,1,0:T(8,128)}, f32[3,162]{1,0:T(4,128)}, f32[3,162]{1,0:T(4,128)}, /*index=5*/f32[3,162]{1,0:T(4,128)}) custom-call(s32[16]{0:T(128)S(1)} %get-tuple-element.197.order_ref, bf16[64,768]{1,0:T(8,128)(2,1)S(1)} %shard_map.382.refs_4_.refs_0_, ...), custom_call_target="tpu_custom_call" | custom-call | flops 10000000 | bytes 6000000 | tf_op jit(solution)/shard_map/pallas_call | solution.py:220
  (148 shorter events, 33.2 us)
Async XLA Ops:
  2.4 7.8 %collective-permute-start.4 = (bf16[16,1792]{1,0:T(8,128)(2,1)}, bf16[16,1792]{1,0:T(8,128)(2,1)S(1)}, u32[]{:S(2)}, u32[]{:S(2)}) collective-permute-start(bf16[16,1792]{1,0:T(8,128)(2,1)} %get-tuple-element.89.refs_0_), channel_id=1, source_target_pairs={{0,24},{1,25},{2,26},{3,27},{4,28},{5,29},{6,30},{7,31},{8,16},{9,... | collective-permute-start | bytes 172040 | tf_op jit(solution)/shard_map/ppermute | solution.py:64
  7.5 5.3 %collective-permute-start.3 = (bf16[16,1792]{1,0:T(8,128)(2,1)}, bf16[16,1792]{1,0:T(8,128)(2,1)S(1)}, u32[]{:S(2)}, u32[]{:S(2)}) collective-permute-start(bf16[16,1792]{1,0:T(8,128)(2,1)} %get-tuple-element.89.refs_0_), channel_id=1, source_target_pairs={{0,16},{1,17},{2,18},{3,19},{4,20},{5,21},{6,22},{7,23},{8,24},{9,... | collective-permute-start | bytes 172040 | tf_op jit(solution)/shard_map/ppermute | solution.py:64
  13.6 8.0 %collective-permute-start.6 = (bf16[64,1792]{1,0:T(8,128)(2,1)S(1)}, bf16[64,1792]{1,0:T(8,128)(2,1)S(1)}, u32[]{:S(2)}, u32[]{:S(2)}) collective-permute-start(bf16[64,1792]{1,0:T(8,128)(2,1)S(1)} %shard_map.361.refs_0_), channel_id=1, source_target_pairs={{0,2},{1,5},{2,0},{3,7},{4,6},{5,1},{6,4},{7,3},{8,10},{9,13},{10,... | collective-permute-start | bytes 688136 | tf_op jit(solution)/shard_map/ppermute | solution.py:64
  15.2 6.5 %collective-permute-start.5 = (bf16[64,1792]{1,0:T(8,128)(2,1)S(1)}, bf16[64,1792]{1,0:T(8,128)(2,1)S(1)}, u32[]{:S(2)}, u32[]{:S(2)}) collective-permute-start(bf16[64,1792]{1,0:T(8,128)(2,1)S(1)} %shard_map.361.refs_0_), channel_id=1, source_target_pairs={{0,4},{1,3},{2,6},{3,1},{4,0},{5,7},{6,2},{7,5},{8,12},{9,11},{10,... | collective-permute-start | bytes 688136 | tf_op jit(solution)/shard_map/ppermute | solution.py:64
  16.7 11.1 %collective-permute-start.15 = (bf16[16,3072]{1,0:T(8,128)(2,1)}, bf16[16,3072]{1,0:T(8,128)(2,1)S(1)}, u32[]{:S(2)}, u32[]{:S(2)}) collective-permute-start(bf16[16,3072]{1,0:T(8,128)(2,1)} %get-tuple-element.98.refs_0_), channel_id=1, source_target_pairs={{0,24},{1,25},{2,26},{3,27},{4,28},{5,29},{6,30},{7,31},{8,16},{9,... | collective-permute-start | bytes 294920 | tf_op jit(solution)/shard_map/ppermute | solution.py:64
  19.3 9.0 %collective-permute-start.14 = (bf16[16,3072]{1,0:T(8,128)(2,1)}, bf16[16,3072]{1,0:T(8,128)(2,1)}, u32[]{:S(2)}, u32[]{:S(2)}) collective-permute-start(bf16[16,3072]{1,0:T(8,128)(2,1)} %get-tuple-element.98.refs_0_), channel_id=1, source_target_pairs={{0,16},{1,17},{2,18},{3,19},{4,20},{5,21},{6,22},{7,23},{8,24},{9,... | collective-permute-start | bytes 294920 | tf_op jit(solution)/shard_map/ppermute | solution.py:64
  20.0 13.1 %collective-permute-start.8 = (bf16[64,1792]{1,0:T(8,128)(2,1)S(1)}, bf16[64,1792]{1,0:T(8,128)(2,1)}, u32[]{:S(2)}, u32[]{:S(2)}) collective-permute-start(bf16[64,1792]{1,0:T(8,128)(2,1)S(1)} %shard_map.361.refs_0_), channel_id=1, source_target_pairs={{0,1},{1,0},{2,3},{3,2},{4,5},{5,4},{6,7},{7,6},{8,9},{9,8},{10,11... | collective-permute-start | bytes 688136 | tf_op jit(solution)/shard_map/ppermute | solution.py:71
  21.7 11.9 %collective-permute-start.7 = (bf16[64,1792]{1,0:T(8,128)(2,1)S(1)}, bf16[64,1792]{1,0:T(8,128)(2,1)}, u32[]{:S(2)}, u32[]{:S(2)}) collective-permute-start(bf16[64,1792]{1,0:T(8,128)(2,1)S(1)} %shard_map.362.refs_4_), channel_id=1, source_target_pairs={{0,2},{1,5},{2,0},{3,7},{4,6},{5,1},{6,4},{7,3},{8,10},{9,13},{10,... | collective-permute-start | bytes 688136 | tf_op jit(solution)/shard_map/ppermute | solution.py:64
  27.8 6.9 %collective-permute-start = (bf16[2,162,512]{2,1,0:T(8,128)(2,1)}, bf16[2,162,512]{2,1,0:T(8,128)(2,1)}, u32[]{:S(2)}, u32[]{:S(2)}) collective-permute-start(bf16[2,162,512]{2,1,0:T(8,128)(2,1)} %get-tuple-element.87), channel_id=1, source_target_pairs={{0,1},{1,0},{2,3},{3,2},{4,5},{5,4},{6,7},{7,6},{8,9},{9,8},{10,11... | collective-permute-start | bytes 995336 | tf_op jit(solution)/shard_map/ppermute | solution.py:71
  27.8 7.4 %collective-permute-start.1 = (bf16[2,162,512]{2,1,0:T(8,128)(2,1)}, bf16[2,162,512]{2,1,0:T(8,128)(2,1)}, u32[]{:S(2)}, u32[]{:S(2)}) collective-permute-start(bf16[2,162,512]{2,1,0:T(8,128)(2,1)} %get-tuple-element.88), channel_id=1, source_target_pairs={{0,1},{1,0},{2,3},{3,2},{4,5},{5,4},{6,7},{7,6},{8,9},{9,8},{10,11... | collective-permute-start | bytes 995336 | tf_op jit(solution)/shard_map/ppermute | solution.py:71
  34.7 15.0 %collective-permute-start.12 = (bf16[3,162,384]{2,1,0:T(8,128)(2,1)}, bf16[3,162,384]{2,1,0:T(8,128)(2,1)S(1)}, u32[]{:S(2)}, u32[]{:S(2)}) collective-permute-start(bf16[3,162,384]{2,1,0:T(8,128)(2,1)} %copy-done.15), channel_id=1, source_target_pairs={{0,1},{1,0},{2,3},{3,2},{4,5},{5,4},{6,7},{7,6},{8,9},{9,8},{10,11... | collective-permute-start | bytes 1119752 | tf_op jit(solution)/shard_map/ppermute | solution.py:71
  35.2 19.6 %collective-permute-start.18 = (bf16[64,3072]{1,0:T(8,128)(2,1)S(1)}, bf16[64,3072]{1,0:T(8,128)(2,1)S(1)}, u32[]{:S(2)}, u32[]{:S(2)}) collective-permute-start(bf16[64,3072]{1,0:T(8,128)(2,1)S(1)} %shard_map.365.refs_0_), channel_id=1, source_target_pairs={{0,6},{1,7},{2,4},{3,5},{4,2},{5,3},{6,0},{7,1},{8,14},{9,15},{10,... | collective-permute-start | bytes 1179656 | tf_op jit(solution)/shard_map/ppermute | solution.py:64
  36.2 18.5 %collective-permute-start.17 = (bf16[64,3072]{1,0:T(8,128)(2,1)S(1)}, bf16[64,3072]{1,0:T(8,128)(2,1)S(1)}, u32[]{:S(2)}, u32[]{:S(2)}) collective-permute-start(bf16[64,3072]{1,0:T(8,128)(2,1)S(1)} %shard_map.365.refs_0_), channel_id=1, source_target_pairs={{0,2},{1,5},{2,0},{3,7},{4,6},{5,1},{6,4},{7,3},{8,10},{9,13},{10,... | collective-permute-start | bytes 1179656 | tf_op jit(solution)/shard_map/ppermute | solution.py:64
  37.1 18.3 %collective-permute-start.16 = (bf16[64,3072]{1,0:T(8,128)(2,1)S(1)}, bf16[64,3072]{1,0:T(8,128)(2,1)S(1)}, u32[]{:S(2)}, u32[]{:S(2)}) collective-permute-start(bf16[64,3072]{1,0:T(8,128)(2,1)S(1)} %shard_map.365.refs_0_), channel_id=1, source_target_pairs={{0,4},{1,3},{2,6},{3,1},{4,0},{5,7},{6,2},{7,5},{8,12},{9,11},{10,... | collective-permute-start | bytes 1179656 | tf_op jit(solution)/shard_map/ppermute | solution.py:64
  74.9 5.7 %collective-permute-start.23 = (bf16[128,768]{1,0:T(8,128)(2,1)S(1)}, bf16[128,768]{1,0:T(8,128)(2,1)S(1)}, u32[]{:S(2)}, u32[]{:S(2)}) collective-permute-start(bf16[128,768]{1,0:T(8,128)(2,1)S(1)} %shard_map.368.refs_0_), channel_id=1, source_target_pairs={{0,2},{1,5},{2,0},{3,7},{4,6},{5,1},{6,4},{7,3},{8,10},{9,13},{10,... | collective-permute-start | bytes 589832 | tf_op jit(solution)/shard_map/ppermute | solution.py:64
  83.9 15.3 %collective-permute-start.26 = (bf16[128,3072]{1,0:T(8,128)(2,1)S(1)}, bf16[128,3072]{1,0:T(8,128)(2,1)S(1)}, u32[]{:S(2)}, u32[]{:S(2)}) collective-permute-start(bf16[128,3072]{1,0:T(8,128)(2,1)S(1)} %get-tuple-element.125), channel_id=1, source_target_pairs={{0,1},{1,0},{2,3},{3,2},{4,5},{5,4},{6,7},{7,6},{8,9},{9,8},{10,11... | collective-permute-start | bytes 2359304 | tf_op jit(solution)/shard_map/ppermute | solution.py:71
  86.4 13.1 %collective-permute-start.27 = (bf16[128,3072]{1,0:T(8,128)(2,1)S(1)}, bf16[128,3072]{1,0:T(8,128)(2,1)S(1)}, u32[]{:S(2)}, u32[]{:S(2)}) collective-permute-start(bf16[128,3072]{1,0:T(8,128)(2,1)S(1)} %shard_map.372.refs_0_), channel_id=1, source_target_pairs={{0,2},{1,5},{2,0},{3,7},{4,6},{5,1},{6,4},{7,3},{8,10},{9,13},{10,... | collective-permute-start | bytes 2359304 | tf_op jit(solution)/shard_map/ppermute | solution.py:64
  87.7 7.3 %collective-permute-start.22 = (bf16[2,162,512]{2,1,0:T(8,128)(2,1)S(1)}, bf16[2,162,512]{2,1,0:T(8,128)(2,1)S(1)}, u32[]{:S(2)}, u32[]{:S(2)}) collective-permute-start(bf16[2,162,512]{2,1,0:T(8,128)(2,1)S(1)} %get-tuple-element.108), channel_id=1, source_target_pairs={{0,1},{1,0},{2,3},{3,2},{4,5},{5,4},{6,7},{7,6},{8,9},{9,8},{10,11... | collective-permute-start | bytes 995336 | tf_op jit(solution)/shard_map/ppermute | solution.py:71
  87.7 6.4 %collective-permute-start.25 = (bf16[64,768]{1,0:T(8,128)(2,1)S(1)}, bf16[64,768]{1,0:T(8,128)(2,1)S(1)}, u32[]{:S(2)}, u32[]{:S(2)}) collective-permute-start(bf16[64,768]{1,0:T(8,128)(2,1)S(1)} %shard_map.370.refs_0_), channel_id=1, source_target_pairs={{0,4},{1,3},{2,6},{3,1},{4,0},{5,7},{6,2},{7,5},{8,12},{9,11},{10,... | collective-permute-start | bytes 294920 | tf_op jit(solution)/shard_map/ppermute | solution.py:64
  99.6 7.8 %collective-permute-start.33 = (bf16[64,3072]{1,0:T(8,128)(2,1)S(1)}, bf16[64,3072]{1,0:T(8,128)(2,1)S(1)}, u32[]{:S(2)}, u32[]{:S(2)}) collective-permute-start(bf16[64,3072]{1,0:T(8,128)(2,1)S(1)} %shard_map.377.refs_0_), channel_id=1, source_target_pairs={{0,4},{1,3},{2,6},{3,1},{4,0},{5,7},{6,2},{7,5},{8,12},{9,11},{10,... | collective-permute-start | bytes 1179656 | tf_op jit(solution)/shard_map/ppermute | solution.py:64
  104.1 10.1 %collective-permute-start.30 = (bf16[128,1792]{1,0:T(8,128)(2,1)S(1)}, bf16[128,1792]{1,0:T(8,128)(2,1)S(1)}, u32[]{:S(2)}, u32[]{:S(2)}) collective-permute-start(bf16[128,1792]{1,0:T(8,128)(2,1)S(1)} %get-tuple-element.131), channel_id=1, source_target_pairs={{0,1},{1,0},{2,3},{3,2},{4,5},{5,4},{6,7},{7,6},{8,9},{9,8},{10,11... | collective-permute-start | bytes 1376264 | tf_op jit(solution)/shard_map/ppermute | solution.py:71
  107.8 8.5 %collective-permute-start.34 = (bf16[128,1792]{1,0:T(8,128)(2,1)S(1)}, bf16[128,1792]{1,0:T(8,128)(2,1)S(1)}, u32[]{:S(2)}, u32[]{:S(2)}) collective-permute-start(bf16[128,1792]{1,0:T(8,128)(2,1)S(1)} %shard_map.380), channel_id=1, source_target_pairs={{0,2},{1,5},{2,0},{3,7},{4,6},{5,1},{6,4},{7,3},{8,10},{9,13},{10,... | collective-permute-start | bytes 1376264 | tf_op jit(solution)/shard_map/ppermute | solution.py:64
  109.2 9.2 %collective-permute-start.36 = (bf16[64,768]{1,0:T(8,128)(2,1)S(1)}, bf16[64,768]{1,0:T(8,128)(2,1)S(1)}, u32[]{:S(2)}, u32[]{:S(2)}) collective-permute-start(bf16[64,768]{1,0:T(8,128)(2,1)S(1)} %get-tuple-element.135), channel_id=1, source_target_pairs={{0,16},{1,17},{2,18},{3,19},{4,20},{5,21},{6,22},{7,23},{8,24},{9,... | collective-permute-start | bytes 294920 | tf_op jit(solution)/shard_map/ppermute | solution.py:64
  111.9 13.9 %collective-permute-start.40 = (bf16[16,3072]{1,0:T(8,128)(2,1)S(1)}, bf16[16,3072]{1,0:T(8,128)(2,1)S(1)}, u32[]{:S(2)}, u32[]{:S(2)}) collective-permute-start(bf16[16,3072]{1,0:T(8,128)(2,1)S(1)} %get-tuple-element.140), channel_id=1, source_target_pairs={{0,8},{1,9},{2,10},{3,11},{4,12},{5,13},{6,14},{7,15},{8,0},{9,1},... | collective-permute-start | bytes 294920 | tf_op jit(solution)/shard_map/ppermute | solution.py:64
  113.3 13.2 %collective-permute-start.41 = (bf16[16,3072]{1,0:T(8,128)(2,1)S(1)}, bf16[16,3072]{1,0:T(8,128)(2,1)S(1)}, u32[]{:S(2)}, u32[]{:S(2)}) collective-permute-start(bf16[16,3072]{1,0:T(8,128)(2,1)S(1)} %get-tuple-element.141), channel_id=1, source_target_pairs={{0,16},{1,17},{2,18},{3,19},{4,20},{5,21},{6,22},{7,23},{8,24},{9,... | collective-permute-start | bytes 294920 | tf_op jit(solution)/shard_map/ppermute | solution.py:64
  114.2 14.4 %collective-permute-start.42 = (bf16[16,3072]{1,0:T(8,128)(2,1)S(1)}, bf16[16,3072]{1,0:T(8,128)(2,1)S(1)}, u32[]{:S(2)}, u32[]{:S(2)}) collective-permute-start(bf16[16,3072]{1,0:T(8,128)(2,1)S(1)} %get-tuple-element.142), channel_id=1, source_target_pairs={{0,24},{1,25},{2,26},{3,27},{4,28},{5,29},{6,30},{7,31},{8,16},{9,... | collective-permute-start | bytes 294920 | tf_op jit(solution)/shard_map/ppermute | solution.py:64
  116.4 8.4 %collective-permute-start.35 = (bf16[64,1792]{1,0:T(8,128)(2,1)S(1)}, bf16[64,1792]{1,0:T(8,128)(2,1)S(1)}, u32[]{:S(2)}, u32[]{:S(2)}) collective-permute-start(bf16[64,1792]{1,0:T(8,128)(2,1)S(1)} %shard_map.381.refs_2_), channel_id=1, source_target_pairs={{0,4},{1,3},{2,6},{3,1},{4,0},{5,7},{6,2},{7,5},{8,12},{9,11},{10,... | collective-permute-start | bytes 688136 | tf_op jit(solution)/shard_map/ppermute | solution.py:64
  123.6 8.7 %collective-permute-start.44 = (bf16[64,768]{1,0:T(8,128)(2,1)S(1)}, bf16[64,768]{1,0:T(8,128)(2,1)S(1)}, u32[]{:S(2)}, u32[]{:S(2)}) collective-permute-start(bf16[64,768]{1,0:T(8,128)(2,1)S(1)} %shard_map.382.refs_4_.refs_0_), channel_id=1, source_target_pairs={{0,2},{1,5},{2,0},{3,7},{4,6},{5,1},{6,4},{7,3},{8,10},{9,13},{10,... | collective-permute-start | bytes 294920 | tf_op jit(solution)/shard_map/ppermute | solution.py:64
  124.9 7.4 %collective-permute-start.45 = (bf16[64,768]{1,0:T(8,128)(2,1)S(1)}, bf16[64,768]{1,0:T(8,128)(2,1)S(1)}, u32[]{:S(2)}, u32[]{:S(2)}) collective-permute-start(bf16[64,768]{1,0:T(8,128)(2,1)S(1)} %collective-permute-done.43.refs_1_), channel_id=1, source_target_pairs={{0,2},{1,5},{2,0},{3,7},{4,6},{5,1},{6,4},{7,3},{8,10},{9,13},{10,... | collective-permute-start | bytes 294920 | tf_op jit(solution)/shard_map/ppermute | solution.py:64
  125.8 9.4 %collective-permute-start.37 = (bf16[16,1792]{1,0:T(8,128)(2,1)S(1)}, bf16[16,1792]{1,0:T(8,128)(2,1)S(1)}, u32[]{:S(2)}, u32[]{:S(2)}) collective-permute-start(bf16[16,1792]{1,0:T(8,128)(2,1)S(1)} %get-tuple-element.137), channel_id=1, source_target_pairs={{0,8},{1,9},{2,10},{3,11},{4,12},{5,13},{6,14},{7,15},{8,0},{9,1},... | collective-permute-start | bytes 172040 | tf_op jit(solution)/shard_map/ppermute | solution.py:64
  126.5 8.7 %collective-permute-start.38 = (bf16[16,1792]{1,0:T(8,128)(2,1)S(1)}, bf16[16,1792]{1,0:T(8,128)(2,1)S(1)}, u32[]{:S(2)}, u32[]{:S(2)}) collective-permute-start(bf16[16,1792]{1,0:T(8,128)(2,1)S(1)} %get-tuple-element.138), channel_id=1, source_target_pairs={{0,16},{1,17},{2,18},{3,19},{4,20},{5,21},{6,22},{7,23},{8,24},{9,... | collective-permute-start | bytes 172040 | tf_op jit(solution)/shard_map/ppermute | solution.py:64
  128.6 6.6 %collective-permute-start.39 = (bf16[16,1792]{1,0:T(8,128)(2,1)S(1)}, bf16[16,1792]{1,0:T(8,128)(2,1)S(1)}, u32[]{:S(2)}, u32[]{:S(2)}) collective-permute-start(bf16[16,1792]{1,0:T(8,128)(2,1)S(1)} %get-tuple-element.139), channel_id=1, source_target_pairs={{0,24},{1,25},{2,26},{3,27},{4,28},{5,29},{6,30},{7,31},{8,16},{9,... | collective-permute-start | bytes 172040 | tf_op jit(solution)/shard_map/ppermute | solution.py:64
  (37 other events, 145.1 us)

commit v8 on v7

--- a/solution.py
+++ b/solution.py
@@ -14,7 +14,8 @@
 PPAD = 336
 P_MID = 196
 P_LOW = 100
-VCOLS = 256
+VCOLS = 128
+VSUB = 120
 ROWS = 2 * PPAD
 GROUPS = 16
 DEVS = 2 * GROUPS
@@ -286,7 +287,9 @@
         for c in copies:
             c.wait()
         out_ref[:, 0:HALF] = w_ref[:, HALF:].astype(BF)
-        row[0:1, 0:per] = v_ref[...]
+        for i in range(-(-per // VSUB)):
+            size = min(VSUB, per - i * VSUB)
+            row[i : i + 1, 0:size] = v_ref[:, i * VSUB : i * VSUB + size]
         out_ref[:, HALF : HALF + VCOLS] = row[...].astype(BF)
         lo_ref[:, 0:HALF] = w_ref[:, 0:HALF].astype(BF)
         for g in range(3):
@@ -462,8 +465,10 @@
         for c in vcopies:
             c.wait()
         for s in range(DEVS):
-            row = vblk[16 * s : 16 * s + 16, :].astype(F32)[0:1, :VPER]
-            vec_ref[0:1, VPER * s : VPER * s + VPER] = row
+            rows = vblk[16 * s : 16 * s + 16, :].astype(F32)
+            for i in range(VPER // VSUB):
+                at = VPER * s + VSUB * i
+                vec_ref[0:1, at : at + VSUB] = rows[i : i + 1, :VSUB]
 
         def norm_one(r):
             hat, _ = norm_parts(xbuf[pl.ds(r, STRIPE), :])
@@ -862,7 +867,9 @@
         split_rows(pgb, stay_ref, away_ref, sides_ref[0], pgb[...])
         blocks[...] = jnp.zeros_like(blocks)
         for s in range(DEVS):
-            blocks[s, 0:1, 0:VPER] = gvec[0:1, VPER * s : VPER * s + VPER]
+            for i in range(VPER // VSUB):
+                at = VPER * s + VSUB * i
+                blocks[s, i : i + 1, 0:VSUB] = gvec[0:1, at : at + VSUB]
         for k in range(DEVS):
             dev = table_ref[k]
             target, first = next((t, f) for t, f in ((up_b, 28), (up_a, 24), (send, GROUPS), (keep, 0)) if k >= f)
@@ -1040,7 +1047,8 @@
     def kernel(own_ref, a_ref, b_ref, c_ref, l_ref, w_ref, m_ref, s_ref, after_ref, nw, nm, ns, vec_ref):
         total = own_ref[...] + a_ref[...].astype(F32)
         total = total + (b_ref[...].astype(F32) + c_ref[...].astype(F32))
-        vec_ref[...] = total[0:1, HALF:]
+        for i in range(VPER // VSUB):
+            vec_ref[0:1, i * VSUB : (i + 1) * VSUB] = total[i : i + 1, HALF : HALF + VSUB]
         for cols, grad in ((slice(0, HALF), l_ref[...]), (slice(HALF, FF), total[:, 0:HALF])):
             new = adamw(w_ref[:, cols], grad, m_ref[:, cols], s_ref[:, cols], DENSE_RATE, DENSE_DECAY)
             nw[:, cols] = new[0]
@@ -1050,7 +1058,7 @@
     same = sds(weight.shape, F32)
     return call(
         kernel,
-        (same, same, same, sds((1, VCOLS), F32)),
+        (same, same, same, sds((1, VPER), F32)),
         [VM] * 8 + [HB],
         [],
         1000000,
@@ -1181,8 +1189,8 @@
         lo_blocks = lo_blocks + [route.cross(b) for b in lo_blocks]
     if not fits:
         whole = in_order(right_blocks, table, in_rows)
-        all_vec = whole[:, 0, HALF : HALF + vec_len].reshape(DEVS, 1, VPER)
-        all_vec = jnp.pad(all_vec, ((0, 0), (0, 15), (0, VCOLS - VPER))).reshape(D, VCOLS)
+        all_vec = whole[:, 0, HALF : HALF + vec_len].reshape(DEVS, VPER // VSUB, VSUB)
+        all_vec = jnp.pad(all_vec, ((0, 0), (0, 16 - VPER // VSUB), (0, VCOLS - VSUB))).reshape(D, VCOLS)
         right_blocks = [jnp.concatenate([whole[:, :, :HALF].reshape(D, HALF), all_vec], axis=1)]
         whole = in_order(lo_blocks, table, in_rows)
         outs = whole[:, :, HALF:].reshape(ndev, in_rows, 3, D).transpose(0, 2, 1, 3).reshape(DEVS, 3, 16, D)
@@ -1242,7 +1250,7 @@
         right_part = add_part(right_terms, 64, [grad_got])
         right_terms.append(route.swap(right_part, far))
         (sp_sum,) = line_turn(sp_terms, 0, [right_part])
-        spat_pieces = route.widen(sp_sum)
+        spat_pieces = route.widen_direct(sp_sum)
         right_own, *sends = line_parts(right_terms, [sp_sum])
         right_got = [route.swap(p, (m, m)) for p, m in zip(sends, route.direct)]
         left_sum, *new_out = finish_out(lo_own, lo_got, dense_out, out_first, out_second, right_own)
@@ -1267,7 +1275,8 @@
         korder = jnp.arange(GROUPS, dtype=jnp.int32)
         after = []
         both = jnp.concatenate([right_keep, right_send, up_a, up_b])
-        vecs = jnp.take(both[::16, HALF : HALF + VPER].reshape(ndev, vec_len), table, axis=0)
+        vecs = both.reshape(DEVS, 16, -1)[:, : VPER // VSUB, HALF : HALF + VSUB]
+        vecs = jnp.take(vecs.reshape(ndev, vec_len), table, axis=0)
         vec_sum = route.scatter(vecs[: route.n], vecs[route.n :]).reshape(vec_len)
         rights = jnp.take(both[:, :HALF].reshape(ndev, in_rows, HALF), table, axis=0).reshape(D, HALF)
         right_sum = route.scatter(rights[: D // 2], rights[D // 2 :])

time: 138 us -> 145 us (1.051)
  local copies, waits for them, and re-layouts: 7.25 us -> 12.1 us
    unnamed x50 -> x56, local copies, waits for them, and re-layouts: 6.33 us -> 10.6 us
  transfers between devices with their start and end apart: 46 -> 46, of which waited for: 15 -> 10; matrix products, arithmetic and copies ran while one was open for 3% -> 6% of each run, Pallas kernels for 28% -> 27%
where the time goes in v8:
time: 145 us; the launch traced here: 144 us
  Pallas kernels  58.5 us (40%)
  starting transfers between devices  40.9 us (28%)
  waiting for transfers between devices  29.1 us (20%)
  local copies, waits for them, and re-layouts  12.1 us (8%)
  other arithmetic  2.67 us (2%)
    pallas_call x17, Pallas kernels, call(): pl.pallas_call(kernel, out_shape=out_shape, in_specs=in_specs, out_specs=...  57.5 us
    ppermute x29, starting transfers between devices, swap(): return lax.ppermute(block, AXES, pairs)  37.3 us
    ppermute x29, waiting for transfers between devices, swap(): return lax.ppermute(block, AXES, pairs)  22.8 us
    unnamed x56, local copies, waits for them, and re-layouts  10.6 us
    ppermute x17, waiting for transfers between devices, cross(): return lax.ppermute(block, AXES, pairs)  6.3 us
    ppermute x17, starting transfers between devices, cross(): return lax.ppermute(block, AXES, pairs)  3.6 us
  transfers between devices with their start and end apart: 46, of which 10 were waited for; matrix products, arithmetic and copies ran while one was open for 6% of the time, Pallas kernels for 27%

profile of v8, /device:TPU:0, one launch (start us, length us, event | category | flops | bytes accessed | tf_op | source)
XLA Modules:
  0.0 144.5 jit_solution(11539508093551739347)
XLA Ops:
  0.7 1.7 %shard_map.360 = (bf16[16,1664]{1,0:T(8,128)(2,1)}, bf16[16,3072]{1,0:T(8,128)(2,1)}) custom-call(f32[16,3072]{1,0:T(8,128)} %w_ref.3, f32[48,512]{1,0:T(8,128)} %w_ref.2, f32[1,240]{1,0:T(1,128)} %bitcast.6), custom_call_target="tpu_custom_call" | custom-call | flops 1000 | bytes 600000 | tf_op jit(solution)/shard_map/pallas_call | solution.py:221
  2.4 5.1 %collective-permute-start.4 = (bf16[16,1664]{1,0:T(8,128)(2,1)}, bf16[16,1664]{1,0:T(8,128)(2,1)S(1)}, u32[]{:S(2)}, u32[]{:S(2)}) collective-permute-start(bf16[16,1664]{1,0:T(8,128)(2,1)} %get-tuple-element.89.refs_0_), channel_id=1, source_target_pairs={{0,24},{1,25},{2,26},{3,27},{4,28},{5,29},{6,30},{7,31},{8,16},{9,... | collective-permute-start | bytes 159752 | tf_op jit(solution)/shard_map/ppermute | solution.py:65
  8.1 3.7 %collective-permute-start.15 = (bf16[16,3072]{1,0:T(8,128)(2,1)}, bf16[16,3072]{1,0:T(8,128)(2,1)S(1)}, u32[]{:S(2)}, u32[]{:S(2)}) collective-permute-start(bf16[16,3072]{1,0:T(8,128)(2,1)} %get-tuple-element.98.refs_0_), channel_id=1, source_target_pairs={{0,24},{1,25},{2,26},{3,27},{4,28},{5,29},{6,30},{7,31},{8,16},{9,... | collective-permute-start | bytes 294920 | tf_op jit(solution)/shard_map/ppermute | solution.py:65
  11.9 5.7 %collective-permute-done.3.refs_2_ = bf16[16,1664]{1,0:T(8,128)(2,1)S(1)} collective-permute-done((bf16[16,1664]{1,0:T(8,128)(2,1)}, bf16[16,1664]{1,0:T(8,128)(2,1)S(1)}, u32[]{:S(2)}, u32[]{:S(2)}) %collective-permute-start.3) | collective-permute-done | bytes 53280 | tf_op jit(solution)/shard_map/ppermute | solution.py:65
  18.4 1.6 %collective-permute-start.6 = (bf16[64,1664]{1,0:T(8,128)(2,1)S(1)}, bf16[64,1664]{1,0:T(8,128)(2,1)S(1)}, u32[]{:S(2)}, u32[]{:S(2)}) collective-permute-start(bf16[64,1664]{1,0:T(8,128)(2,1)S(1)} %shard_map.361.refs_0_), channel_id=1, source_target_pairs={{0,2},{1,5},{2,0},{3,7},{4,6},{5,1},{6,4},{7,3},{8,10},{9,13},{10,... | collective-permute-start | bytes 638984 | tf_op jit(solution)/shard_map/ppermute | solution.py:65
  20.0 1.5 %collective-permute-start.5 = (bf16[64,1664]{1,0:T(8,128)(2,1)S(1)}, bf16[64,1664]{1,0:T(8,128)(2,1)S(1)}, u32[]{:S(2)}, u32[]{:S(2)}) collective-permute-start(bf16[64,1664]{1,0:T(8,128)(2,1)S(1)} %shard_map.361.refs_0_), channel_id=1, source_target_pairs={{0,4},{1,3},{2,6},{3,1},{4,0},{5,7},{6,2},{7,5},{8,12},{9,11},{10,... | collective-permute-start | bytes 638984 | tf_op jit(solution)/shard_map/ppermute | solution.py:65
  27.3 1.5 %shard_map.359 = (bf16[3,162,384]{2,1,0:T(8,128)(2,1)S(1)}, bf16[2,162,512]{2,1,0:T(8,128)(2,1)}, bf16[2,162,512]{2,1,0:T(8,128)(2,1)}) custom-call(s32[33]{0:T(128)S(1)} %pad_add_fusion.1.sides_ref, f32[3,162,324]{2,1,0:T(8,128)S(1)} %copy-done, f32[3,162,1]{2,1,0:T(8,128)S(1)} %copy.47.b_ref, bf16[4,162,512]{2,1,0:T(8,128)(2,1)S(1)} %copy.50.x_ref.p_ref, ...), custom_call_target="tpu_custom_call" | custom-call | flops 1000 | bytes 3000000 | tf_op jit(solution)/shard_map/pallas_call | solution.py:221
  30.2 4.9 %collective-permute-done.13.refs_1_ = bf16[16,3072]{1,0:T(8,128)(2,1)S(1)} collective-permute-done((bf16[16,3072]{1,0:T(8,128)(2,1)S(1)}, bf16[16,3072]{1,0:T(8,128)(2,1)S(1)}, u32[]{:S(2)}, u32[]{:S(2)}) %collective-permute-start.13) | collective-permute-done | bytes 98336 | tf_op jit(solution)/shard_map/ppermute | solution.py:65
  37.6 1.5 %collective-permute-start.18 = (bf16[64,3072]{1,0:T(8,128)(2,1)S(1)}, bf16[64,3072]{1,0:T(8,128)(2,1)S(1)}, u32[]{:S(2)}, u32[]{:S(2)}) collective-permute-start(bf16[64,3072]{1,0:T(8,128)(2,1)S(1)} %shard_map.365.refs_0_), channel_id=1, source_target_pairs={{0,6},{1,7},{2,4},{3,5},{4,2},{5,3},{6,0},{7,1},{8,14},{9,15},{10,... | collective-permute-start | bytes 1179656 | tf_op jit(solution)/shard_map/ppermute | solution.py:65
  39.1 1.5 %collective-permute-start.17 = (bf16[64,3072]{1,0:T(8,128)(2,1)S(1)}, bf16[64,3072]{1,0:T(8,128)(2,1)S(1)}, u32[]{:S(2)}, u32[]{:S(2)}) collective-permute-start(bf16[64,3072]{1,0:T(8,128)(2,1)S(1)} %shard_map.365.refs_0_), channel_id=1, source_target_pairs={{0,2},{1,5},{2,0},{3,7},{4,6},{5,1},{6,4},{7,3},{8,10},{9,13},{10,... | collective-permute-start | bytes 1179656 | tf_op jit(solution)/shard_map/ppermute | solution.py:65
  43.4 11.2 %shard_map.363 = (bf16[672,512]{1,0:T(8,128)(2,1)S(1)}, bf16[672,512]{1,0:T(8,128)(2,1)S(1)}, bf16[672,512]{1,0:T(8,128)(2,1)S(1)}, f32[672,1536]{1,0:T(8,128)S(...) custom-call(s32[32]{0:T(128)S(1)} %copy-done.16, ...), custom_call_target="tpu_custom_call" | custom-call | flops 10000000000 | bytes 20000000 | tf_op jit(solution)/shard_map/pallas_call | solution.py:221
  54.6 5.1 %shard_map.364 = (bf16[720,1536]{1,0:T(8,128)(2,1)S(1)}, bf16[672,1536]{1,0:T(8,128)(2,1)S(1)}, f32[672,128]{1,0:T(8,128)S(1)}, bf16[672,1536]{1,0:T(8,128)(2,1)S(1)}, bf16[2,336,384]{2,1,0:T(8,128)(2,1)S(1)}) custom-call(s32[2]{0:T(128)S(1)} %dynamic_slice.3.levels_ref, s32[33]{0:T(128)S(1)} %copy-done.18, f32[1,7680]{1,0:T(1,128)S(1)} %get-tuple-element.90.vec_ref, ...), custom_call_target="tpu_custom_call" | custom-call | flops 6000000000 | bytes 12000000 | tf_op jit(solution)/shard_map/pallas_call | solution.py:221
  60.3 2.9 %collective-permute-done.19.refs_4_ = bf16[64,3072]{1,0:T(8,128)(2,1)S(1)} collective-permute-done((bf16[64,3072]{1,0:T(8,128)(2,1)S(1)}, bf16[64,3072]{1,0:T(8,128)(2,1)S(1)}, u32[]{:S(2)}, u32[]{:S(2)}) %collective-permute-start.19) | collective-permute-done | bytes 393248 | tf_op jit(solution)/shard_map/ppermute | solution.py:72
  63.2 14.0 %shard_map.367 = (bf16[672,1536]{1,0:T(8,128)(2,1)S(1)}, bf16[672,1536]{1,0:T(8,128)(2,1)S(1)}, bf16[672,1536]{1,0:T(8,128)(2,1)S(1)}, bf16[672,512]{1,0:T(8,128...) custom-call(s32[32]{0:T(128)S(1)} %copy-done.16, ...), custom_call_target="tpu_custom_call" | custom-call | flops 8000000000 | bytes 16000000 | tf_op jit(solution)/shard_map/pallas_call | solution.py:221
  77.5 1.6 %collective-permute-done.21.refs_1_ = bf16[256,768]{1,0:T(8,128)(2,1)S(1)} collective-permute-done((bf16[256,768]{1,0:T(8,128)(2,1)S(1)}, bf16[256,768]{1,0:T(8,128)(2,1)S(1)}, u32[]{:S(2)}, u32[]{:S(2)}) %collective-permute-start.21) | collective-permute-done | bytes 393248 | tf_op jit(solution)/shard_map/ppermute | solution.py:72
  79.1 1.4 collective-permute-start.23
  80.5 4.9 %shard_map.369 = (bf16[512,1536]{1,0:T(8,128)(2,1)S(1)}, bf16[2,162,512]{2,1,0:T(8,128)(2,1)S(1)}, bf16[2,162,512]{2,1,0:T(8,128)(2,1)S(1)}, f32[672,512]{1,0:T(8,128)S(1)}) custom-call(s32[2]{0:T(128)S(1)} %dynamic_slice.3.levels_ref, s32[33]{0:T(128)S(1)} %copy-done.18, f32[1,7680]{1,0:T(1,128)S(1)} %get-tuple-element.90.vec_ref, ...), custom_call_target="tpu_custom_call" | custom-call | flops 4000000000 | bytes 12000000 | tf_op jit(solution)/shard_map/pallas_call | solution.py:221
  85.5 3.2 %shard_map.371 = (bf16[256,3072]{1,0:T(8,128)(2,1)S(1)}, bf16[128,3072]{1,0:T(8,128)(2,1)S(1)}, bf16[128,3072]{1,0:T(8,128)(2,1)S(1)}) custom-call(s32[32]{0:T(128)S(1)} %copy-done.16, bf16[672,1536]{1,0:T(8,128)(2,1)S(1)} %get-tuple-element.100.t_ref, bf16[672,512]{1,0:T(8,128)(2,1)S(1)} %get-tuple-element.114.gb_ref, ...), custom_call_target="tpu_custom_call" | custom-call | flops 2000000000 | bytes 8000000 | tf_op jit(solution)/shard_map/pallas_call | solution.py:221
  89.3 1.8 %collective-permute-done.24.refs_1_ = bf16[128,3072]{1,0:T(8,128)(2,1)S(1)} collective-permute-done((bf16[128,3072]{1,0:T(8,128)(2,1)S(1)}, bf16[128,3072]{1,0:T(8,128)(2,1)S(1)}, u32[]{:S(2)}, u32[]{:S(2)}) %collective-permute-start.24) | collective-permute-done | bytes 786464 | tf_op jit(solution)/shard_map/ppermute | solution.py:72
  93.5 5.6 %shard_map.373 = (bf16[672,1536]{1,0:T(8,128)(2,1)S(1)}, f32[1,4608]{1,0:T(1,128)S(1)}) custom-call(f32[1,7680]{1,0:T(1,128)S(1)} %get-tuple-element.90.vec_ref, bf16[672,1536]{1,0:T(8,128)(2,1)S(1)} %get-tuple-element.110.gs_ref, bf16[2,336,384]{2,1,0:T(8,128)(2,1)S(1)} %get-tuple-element.99.refs_3_.mm_ref, ...), custom_call_target="tpu_custom_call" | custom-call | flops 3000000000 | bytes 10000000 | tf_op jit(solution)/shard_map/pallas_call | solution.py:221
  99.5 2.7 %shard_map.375 = (bf16[512,1536]{1,0:T(8,128)(2,1)S(1)}, f32[672,512]{1,0:T(8,128)S(1)}) custom-call(bf16[672,1536]{1,0:T(8,128)(2,1)S(1)} %get-tuple-element.120.gp_ref, bf16[672,512]{1,0:T(8,128)(2,1)S(1)} %get-tuple-element.91.h_ref, bf16[512,1536]{1,0:T(8,128)(2,1)S(1)} %get-tuple-element.121.w_ref, f32[672,512]{1,0:T(8,128)S(1)} %get-tuple-element.116.refs_3_.gh_ref, ...), custom_call_target="tpu_custom_call" | custom-call | flops 3000000000 | bytes 8000000 | tf_op jit(solution)/shard_map/pallas_call | solution.py:221
  102.2 1.8 %collective-permute-done.28.refs_1_ = bf16[64,768]{1,0:T(8,128)(2,1)S(1)} collective-permute-done((bf16[64,768]{1,0:T(8,128)(2,1)S(1)}, bf16[64,768]{1,0:T(8,128)(2,1)S(1)}, u32[]{:S(2)}, u32[]{:S(2)}) %collective-permute-start.28) | collective-permute-done | bytes 98336 | tf_op jit(solution)/shard_map/ppermute | solution.py:65
  105.4 2.9 %shard_map.378 = (bf16[256,1664]{1,0:T(8,128)(2,1)S(1)}, bf16[128,1664]{1,0:T(8,128)(2,1)S(1)}, bf16[64,1664]{1,0:T(8,128)(2,1)S(1)}, bf16[64,1664]{1,0:T(8,128)...) custom-call(s32[32]{0:T(128)S(1)} %copy-done.16, s32[33]{0:T(128)S(1)} %copy-done.18, ...), custom_call_target="tpu_custom_call" | custom-call | flops 2000000000 | bytes 6000000 | tf_op jit(solution)/shard_map/pallas_call | solution.py:221
  109.0 3.3 %collective-permute-done.33.refs_3_ = bf16[64,3072]{1,0:T(8,128)(2,1)S(1)} collective-permute-done((bf16[64,3072]{1,0:T(8,128)(2,1)S(1)}, bf16[64,3072]{1,0:T(8,128)(2,1)S(1)}, u32[]{:S(2)}, u32[]{:S(2)}) %collective-permute-start.33) | collective-permute-done | bytes 393248 | tf_op jit(solution)/shard_map/ppermute | solution.py:65
  116.0 1.7 %collective-permute-start.40 = (bf16[16,3072]{1,0:T(8,128)(2,1)S(1)}, bf16[16,3072]{1,0:T(8,128)(2,1)S(1)}, u32[]{:S(2)}, u32[]{:S(2)}) collective-permute-start(bf16[16,3072]{1,0:T(8,128)(2,1)S(1)} %get-tuple-element.140), channel_id=1, source_target_pairs={{0,8},{1,9},{2,10},{3,11},{4,12},{5,13},{6,14},{7,15},{8,0},{9,1},... | collective-permute-start | bytes 294920 | tf_op jit(solution)/shard_map/ppermute | solution.py:65
  118.0 2.4 %collective-permute-start.42 = (bf16[16,3072]{1,0:T(8,128)(2,1)S(1)}, bf16[16,3072]{1,0:T(8,128)(2,1)S(1)}, u32[]{:S(2)}, u32[]{:S(2)}) collective-permute-start(bf16[16,3072]{1,0:T(8,128)(2,1)S(1)} %get-tuple-element.142), channel_id=1, source_target_pairs={{0,24},{1,25},{2,26},{3,27},{4,28},{5,29},{6,30},{7,31},{8,16},{9,... | collective-permute-start | bytes 294920 | tf_op jit(solution)/shard_map/ppermute | solution.py:65
  122.0 1.5 %collective-permute-start.45 = (bf16[64,768]{1,0:T(8,128)(2,1)S(1)}, bf16[64,768]{1,0:T(8,128)(2,1)S(1)}, u32[]{:S(2)}, u32[]{:S(2)}) collective-permute-start(bf16[64,768]{1,0:T(8,128)(2,1)S(1)} %shard_map.382.refs_4_.refs_0_), channel_id=1, source_target_pairs={{0,6},{1,7},{2,4},{3,5},{4,2},{5,3},{6,0},{7,1},{8,14},{9,15},{10,... | collective-permute-start | bytes 294920 | tf_op jit(solution)/shard_map/ppermute | solution.py:65
  123.5 6.4 %collective-permute-done.35.refs_3_ = bf16[64,1664]{1,0:T(8,128)(2,1)S(1)} collective-permute-done((bf16[64,1664]{1,0:T(8,128)(2,1)S(1)}, bf16[64,1664]{1,0:T(8,128)(2,1)S(1)}, u32[]{:S(2)}, u32[]{:S(2)}) %collective-permute-start.35) | collective-permute-done | bytes 213024 | tf_op jit(solution)/shard_map/ppermute | solution.py:65
  130.9 1.5 %collective-permute-start.43 = (bf16[64,768]{1,0:T(8,128)(2,1)S(1)}, bf16[64,768]{1,0:T(8,128)(2,1)S(1)}, u32[]{:S(2)}, u32[]{:S(2)}) collective-permute-start(bf16[64,768]{1,0:T(8,128)(2,1)S(1)} %shard_map.382.refs_4_.refs_0_), channel_id=1, source_target_pairs={{0,4},{1,3},{2,6},{3,1},{4,0},{5,7},{6,2},{7,5},{8,12},{9,11},{10,... | collective-permute-start | bytes 294920 | tf_op jit(solution)/shard_map/ppermute | solution.py:65
  132.6 2.7 %collective-permute-start.38 = (bf16[16,1664]{1,0:T(8,128)(2,1)S(1)}, bf16[16,1664]{1,0:T(8,128)(2,1)S(1)}, u32[]{:S(2)}, u32[]{:S(2)}) collective-permute-start(bf16[16,1664]{1,0:T(8,128)(2,1)S(1)} %get-tuple-element.138), channel_id=1, source_target_pairs={{0,16},{1,17},{2,18},{3,19},{4,20},{5,21},{6,22},{7,23},{8,24},{9,... | collective-permute-start | bytes 159752 | tf_op jit(solution)/shard_map/ppermute | solution.py:65
  135.3 1.5 %collective-permute-start.39 = (bf16[16,1664]{1,0:T(8,128)(2,1)S(1)}, bf16[16,1664]{1,0:T(8,128)(2,1)S(1)}, u32[]{:S(2)}, u32[]{:S(2)}) collective-permute-start(bf16[16,1664]{1,0:T(8,128)(2,1)S(1)} %get-tuple-element.139), channel_id=1, source_target_pairs={{0,24},{1,25},{2,26},{3,27},{4,28},{5,29},{6,30},{7,31},{8,16},{9,... | collective-permute-start | bytes 159752 | tf_op jit(solution)/shard_map/ppermute | solution.py:65
  139.0 2.8 %shard_map.385 = (f32[3,162,324]{2,1,0:T(8,128)}, f32[3,162,324]{2,1,0:T(8,128)}, f32[3,162,324]{2,1,0:T(8,128)}, f32[3,162]{1,0:T(4,128)}, f32[3,162]{1,0:T(4,128)}, /*index=5*/f32[3,162]{1,0:T(4,128)}) custom-call(s32[16]{0:T(128)S(1)} %copy-done.15, bf16[64,768]{1,0:T(8,128)(2,1)S(1)} %shard_map.382.refs_4_.refs_0_, ...), custom_call_target="tpu_custom_call" | custom-call | flops 10000000 | bytes 6000000 | tf_op jit(solution)/shard_map/pallas_call | solution.py:221
  (154 shorter events, 31.7 us)
Async XLA Ops:
  2.4 9.5 %collective-permute-start.4 = (bf16[16,1664]{1,0:T(8,128)(2,1)}, bf16[16,1664]{1,0:T(8,128)(2,1)S(1)}, u32[]{:S(2)}, u32[]{:S(2)}) collective-permute-start(bf16[16,1664]{1,0:T(8,128)(2,1)} %get-tuple-element.89.refs_0_), channel_id=1, source_target_pairs={{0,24},{1,25},{2,26},{3,27},{4,28},{5,29},{6,30},{7,31},{8,16},{9,... | collective-permute-start | bytes 159752 | tf_op jit(solution)/shard_map/ppermute | solution.py:65
  7.5 10.1 %collective-permute-start.3 = (bf16[16,1664]{1,0:T(8,128)(2,1)}, bf16[16,1664]{1,0:T(8,128)(2,1)S(1)}, u32[]{:S(2)}, u32[]{:S(2)}) collective-permute-start(bf16[16,1664]{1,0:T(8,128)(2,1)} %get-tuple-element.89.refs_0_), channel_id=1, source_target_pairs={{0,16},{1,17},{2,18},{3,19},{4,20},{5,21},{6,22},{7,23},{8,24},{9,... | collective-permute-start | bytes 159752 | tf_op jit(solution)/shard_map/ppermute | solution.py:65
  7.5 10.1 %collective-permute-start.2 = (bf16[16,1664]{1,0:T(8,128)(2,1)}, bf16[16,1664]{1,0:T(8,128)(2,1)S(1)}, u32[]{:S(2)}, u32[]{:S(2)}) collective-permute-start(bf16[16,1664]{1,0:T(8,128)(2,1)} %get-tuple-element.89.refs_0_), channel_id=1, source_target_pairs={{0,8},{1,9},{2,10},{3,11},{4,12},{5,13},{6,14},{7,15},{8,0},{9,1},... | collective-permute-start | bytes 159752 | tf_op jit(solution)/shard_map/ppermute | solution.py:65
  8.1 21.7 %collective-permute-start.15 = (bf16[16,3072]{1,0:T(8,128)(2,1)}, bf16[16,3072]{1,0:T(8,128)(2,1)S(1)}, u32[]{:S(2)}, u32[]{:S(2)}) collective-permute-start(bf16[16,3072]{1,0:T(8,128)(2,1)} %get-tuple-element.98.refs_0_), channel_id=1, source_target_pairs={{0,24},{1,25},{2,26},{3,27},{4,28},{5,29},{6,30},{7,31},{8,16},{9,... | collective-permute-start | bytes 294920 | tf_op jit(solution)/shard_map/ppermute | solution.py:65
  11.9 18.3 %collective-permute-start.14 = (bf16[16,3072]{1,0:T(8,128)(2,1)}, bf16[16,3072]{1,0:T(8,128)(2,1)S(1)}, u32[]{:S(2)}, u32[]{:S(2)}) collective-permute-start(bf16[16,3072]{1,0:T(8,128)(2,1)} %get-tuple-element.98.refs_0_), channel_id=1, source_target_pairs={{0,16},{1,17},{2,18},{3,19},{4,20},{5,21},{6,22},{7,23},{8,24},{9,... | collective-permute-start | bytes 294920 | tf_op jit(solution)/shard_map/ppermute | solution.py:65
  18.4 8.2 %collective-permute-start.6 = (bf16[64,1664]{1,0:T(8,128)(2,1)S(1)}, bf16[64,1664]{1,0:T(8,128)(2,1)S(1)}, u32[]{:S(2)}, u32[]{:S(2)}) collective-permute-start(bf16[64,1664]{1,0:T(8,128)(2,1)S(1)} %shard_map.361.refs_0_), channel_id=1, source_target_pairs={{0,2},{1,5},{2,0},{3,7},{4,6},{5,1},{6,4},{7,3},{8,10},{9,13},{10,... | collective-permute-start | bytes 638984 | tf_op jit(solution)/shard_map/ppermute | solution.py:65
  20.0 6.7 %collective-permute-start.5 = (bf16[64,1664]{1,0:T(8,128)(2,1)S(1)}, bf16[64,1664]{1,0:T(8,128)(2,1)S(1)}, u32[]{:S(2)}, u32[]{:S(2)}) collective-permute-start(bf16[64,1664]{1,0:T(8,128)(2,1)S(1)} %shard_map.361.refs_0_), channel_id=1, source_target_pairs={{0,4},{1,3},{2,6},{3,1},{4,0},{5,7},{6,2},{7,5},{8,12},{9,11},{10,... | collective-permute-start | bytes 638984 | tf_op jit(solution)/shard_map/ppermute | solution.py:65
  26.6 8.4 %collective-permute-start.8 = (bf16[64,1664]{1,0:T(8,128)(2,1)S(1)}, bf16[64,1664]{1,0:T(8,128)(2,1)S(1)}, u32[]{:S(2)}, u32[]{:S(2)}) collective-permute-start(bf16[64,1664]{1,0:T(8,128)(2,1)S(1)} %shard_map.361.refs_0_), channel_id=1, source_target_pairs={{0,1},{1,0},{2,3},{3,2},{4,5},{5,4},{6,7},{7,6},{8,9},{9,8},{10,11... | collective-permute-start | bytes 638984 | tf_op jit(solution)/shard_map/ppermute | solution.py:72
  26.7 9.6 %collective-permute-start.7 = (bf16[64,1664]{1,0:T(8,128)(2,1)S(1)}, bf16[64,1664]{1,0:T(8,128)(2,1)}, u32[]{:S(2)}, u32[]{:S(2)}) collective-permute-start(bf16[64,1664]{1,0:T(8,128)(2,1)S(1)} %shard_map.362.refs_4_), channel_id=1, source_target_pairs={{0,2},{1,5},{2,0},{3,7},{4,6},{5,1},{6,4},{7,3},{8,10},{9,13},{10,... | collective-permute-start | bytes 638984 | tf_op jit(solution)/shard_map/ppermute | solution.py:65
  29.6 7.4 %collective-permute-start = (bf16[2,162,512]{2,1,0:T(8,128)(2,1)}, bf16[2,162,512]{2,1,0:T(8,128)(2,1)}, u32[]{:S(2)}, u32[]{:S(2)}) collective-permute-start(bf16[2,162,512]{2,1,0:T(8,128)(2,1)} %get-tuple-element.87), channel_id=1, source_target_pairs={{0,1},{1,0},{2,3},{3,2},{4,5},{5,4},{6,7},{7,6},{8,9},{9,8},{10,11... | collective-permute-start | bytes 995336 | tf_op jit(solution)/shard_map/ppermute | solution.py:72
  29.8 7.8 %collective-permute-start.1 = (bf16[2,162,512]{2,1,0:T(8,128)(2,1)}, bf16[2,162,512]{2,1,0:T(8,128)(2,1)}, u32[]{:S(2)}, u32[]{:S(2)}) collective-permute-start(bf16[2,162,512]{2,1,0:T(8,128)(2,1)} %get-tuple-element.88), channel_id=1, source_target_pairs={{0,1},{1,0},{2,3},{3,2},{4,5},{5,4},{6,7},{7,6},{8,9},{9,8},{10,11... | collective-permute-start | bytes 995336 | tf_op jit(solution)/shard_map/ppermute | solution.py:72
  37.1 17.5 %collective-permute-start.12 = (bf16[3,162,384]{2,1,0:T(8,128)(2,1)}, bf16[3,162,384]{2,1,0:T(8,128)(2,1)S(1)}, u32[]{:S(2)}, u32[]{:S(2)}) collective-permute-start(bf16[3,162,384]{2,1,0:T(8,128)(2,1)} %copy-done.19), channel_id=1, source_target_pairs={{0,1},{1,0},{2,3},{3,2},{4,5},{5,4},{6,7},{7,6},{8,9},{9,8},{10,11... | collective-permute-start | bytes 1119752 | tf_op jit(solution)/shard_map/ppermute | solution.py:72
  37.6 22.0 %collective-permute-start.18 = (bf16[64,3072]{1,0:T(8,128)(2,1)S(1)}, bf16[64,3072]{1,0:T(8,128)(2,1)S(1)}, u32[]{:S(2)}, u32[]{:S(2)}) collective-permute-start(bf16[64,3072]{1,0:T(8,128)(2,1)S(1)} %shard_map.365.refs_0_), channel_id=1, source_target_pairs={{0,6},{1,7},{2,4},{3,5},{4,2},{5,3},{6,0},{7,1},{8,14},{9,15},{10,... | collective-permute-start | bytes 1179656 | tf_op jit(solution)/shard_map/ppermute | solution.py:65
  39.1 20.5 %collective-permute-start.17 = (bf16[64,3072]{1,0:T(8,128)(2,1)S(1)}, bf16[64,3072]{1,0:T(8,128)(2,1)S(1)}, u32[]{:S(2)}, u32[]{:S(2)}) collective-permute-start(bf16[64,3072]{1,0:T(8,128)(2,1)S(1)} %shard_map.365.refs_0_), channel_id=1, source_target_pairs={{0,2},{1,5},{2,0},{3,7},{4,6},{5,1},{6,4},{7,3},{8,10},{9,13},{10,... | collective-permute-start | bytes 1179656 | tf_op jit(solution)/shard_map/ppermute | solution.py:65
  40.6 19.0 %collective-permute-start.16 = (bf16[64,3072]{1,0:T(8,128)(2,1)S(1)}, bf16[64,3072]{1,0:T(8,128)(2,1)S(1)}, u32[]{:S(2)}, u32[]{:S(2)}) collective-permute-start(bf16[64,3072]{1,0:T(8,128)(2,1)S(1)} %shard_map.365.refs_0_), channel_id=1, source_target_pairs={{0,4},{1,3},{2,6},{3,1},{4,0},{5,7},{6,2},{7,5},{8,12},{9,11},{10,... | collective-permute-start | bytes 1179656 | tf_op jit(solution)/shard_map/ppermute | solution.py:65
  88.8 15.3 %collective-permute-start.26 = (bf16[128,3072]{1,0:T(8,128)(2,1)S(1)}, bf16[128,3072]{1,0:T(8,128)(2,1)S(1)}, u32[]{:S(2)}, u32[]{:S(2)}) collective-permute-start(bf16[128,3072]{1,0:T(8,128)(2,1)S(1)} %get-tuple-element.125), channel_id=1, source_target_pairs={{0,1},{1,0},{2,3},{3,2},{4,5},{5,4},{6,7},{7,6},{8,9},{9,8},{10,11... | collective-permute-start | bytes 2359304 | tf_op jit(solution)/shard_map/ppermute | solution.py:72
  91.2 13.1 %collective-permute-start.27 = (bf16[128,3072]{1,0:T(8,128)(2,1)S(1)}, bf16[128,3072]{1,0:T(8,128)(2,1)S(1)}, u32[]{:S(2)}, u32[]{:S(2)}) collective-permute-start(bf16[128,3072]{1,0:T(8,128)(2,1)S(1)} %shard_map.372.refs_0_), channel_id=1, source_target_pairs={{0,2},{1,5},{2,0},{3,7},{4,6},{5,1},{6,4},{7,3},{8,10},{9,13},{10,... | collective-permute-start | bytes 2359304 | tf_op jit(solution)/shard_map/ppermute | solution.py:65
  92.0 7.5 %collective-permute-start.22 = (bf16[2,162,512]{2,1,0:T(8,128)(2,1)S(1)}, bf16[2,162,512]{2,1,0:T(8,128)(2,1)S(1)}, u32[]{:S(2)}, u32[]{:S(2)}) collective-permute-start(bf16[2,162,512]{2,1,0:T(8,128)(2,1)S(1)} %get-tuple-element.108), channel_id=1, source_target_pairs={{0,1},{1,0},{2,3},{3,2},{4,5},{5,4},{6,7},{7,6},{8,9},{9,8},{10,11... | collective-permute-start | bytes 995336 | tf_op jit(solution)/shard_map/ppermute | solution.py:72
  92.0 7.1 %collective-permute-start.25 = (bf16[64,768]{1,0:T(8,128)(2,1)S(1)}, bf16[64,768]{1,0:T(8,128)(2,1)S(1)}, u32[]{:S(2)}, u32[]{:S(2)}) collective-permute-start(bf16[64,768]{1,0:T(8,128)(2,1)S(1)} %shard_map.370.refs_0_), channel_id=1, source_target_pairs={{0,4},{1,3},{2,6},{3,1},{4,0},{5,7},{6,2},{7,5},{8,12},{9,11},{10,... | collective-permute-start | bytes 294920 | tf_op jit(solution)/shard_map/ppermute | solution.py:65
  104.5 7.8 %collective-permute-start.33 = (bf16[64,3072]{1,0:T(8,128)(2,1)S(1)}, bf16[64,3072]{1,0:T(8,128)(2,1)S(1)}, u32[]{:S(2)}, u32[]{:S(2)}) collective-permute-start(bf16[64,3072]{1,0:T(8,128)(2,1)S(1)} %shard_map.377.refs_0_), channel_id=1, source_target_pairs={{0,4},{1,3},{2,6},{3,1},{4,0},{5,7},{6,2},{7,5},{8,12},{9,11},{10,... | collective-permute-start | bytes 1179656 | tf_op jit(solution)/shard_map/ppermute | solution.py:65
  108.9 9.1 %collective-permute-start.30 = (bf16[128,1664]{1,0:T(8,128)(2,1)S(1)}, bf16[128,1664]{1,0:T(8,128)(2,1)S(1)}, u32[]{:S(2)}, u32[]{:S(2)}) collective-permute-start(bf16[128,1664]{1,0:T(8,128)(2,1)S(1)} %get-tuple-element.131), channel_id=1, source_target_pairs={{0,1},{1,0},{2,3},{3,2},{4,5},{5,4},{6,7},{7,6},{8,9},{9,8},{10,11... | collective-permute-start | bytes 1277960 | tf_op jit(solution)/shard_map/ppermute | solution.py:72
  112.7 8.2 %collective-permute-start.34 = (bf16[128,1664]{1,0:T(8,128)(2,1)S(1)}, bf16[128,1664]{1,0:T(8,128)(2,1)S(1)}, u32[]{:S(2)}, u32[]{:S(2)}) collective-permute-start(bf16[128,1664]{1,0:T(8,128)(2,1)S(1)} %shard_map.380), channel_id=1, source_target_pairs={{0,2},{1,5},{2,0},{3,7},{4,6},{5,1},{6,4},{7,3},{8,10},{9,13},{10,... | collective-permute-start | bytes 1277960 | tf_op jit(solution)/shard_map/ppermute | solution.py:65
  113.5 8.5 %collective-permute-start.36 = (bf16[64,768]{1,0:T(8,128)(2,1)S(1)}, bf16[64,768]{1,0:T(8,128)(2,1)S(1)}, u32[]{:S(2)}, u32[]{:S(2)}) collective-permute-start(bf16[64,768]{1,0:T(8,128)(2,1)S(1)} %get-tuple-element.135), channel_id=1, source_target_pairs={{0,16},{1,17},{2,18},{3,19},{4,20},{5,21},{6,22},{7,23},{8,24},{9,... | collective-permute-start | bytes 294920 | tf_op jit(solution)/shard_map/ppermute | solution.py:65
  116.0 14.9 %collective-permute-start.40 = (bf16[16,3072]{1,0:T(8,128)(2,1)S(1)}, bf16[16,3072]{1,0:T(8,128)(2,1)S(1)}, u32[]{:S(2)}, u32[]{:S(2)}) collective-permute-start(bf16[16,3072]{1,0:T(8,128)(2,1)S(1)} %get-tuple-element.140), channel_id=1, source_target_pairs={{0,8},{1,9},{2,10},{3,11},{4,12},{5,13},{6,14},{7,15},{8,0},{9,1},... | collective-permute-start | bytes 294920 | tf_op jit(solution)/shard_map/ppermute | solution.py:65
  117.8 14.6 %collective-permute-start.41 = (bf16[16,3072]{1,0:T(8,128)(2,1)S(1)}, bf16[16,3072]{1,0:T(8,128)(2,1)S(1)}, u32[]{:S(2)}, u32[]{:S(2)}) collective-permute-start(bf16[16,3072]{1,0:T(8,128)(2,1)S(1)} %get-tuple-element.141), channel_id=1, source_target_pairs={{0,16},{1,17},{2,18},{3,19},{4,20},{5,21},{6,22},{7,23},{8,24},{9,... | collective-permute-start | bytes 294920 | tf_op jit(solution)/shard_map/ppermute | solution.py:65
  118.0 14.6 %collective-permute-start.42 = (bf16[16,3072]{1,0:T(8,128)(2,1)S(1)}, bf16[16,3072]{1,0:T(8,128)(2,1)S(1)}, u32[]{:S(2)}, u32[]{:S(2)}) collective-permute-start(bf16[16,3072]{1,0:T(8,128)(2,1)S(1)} %get-tuple-element.142), channel_id=1, source_target_pairs={{0,24},{1,25},{2,26},{3,27},{4,28},{5,29},{6,30},{7,31},{8,16},{9,... | collective-permute-start | bytes 294920 | tf_op jit(solution)/shard_map/ppermute | solution.py:65
  120.9 9.0 %collective-permute-start.35 = (bf16[64,1664]{1,0:T(8,128)(2,1)S(1)}, bf16[64,1664]{1,0:T(8,128)(2,1)S(1)}, u32[]{:S(2)}, u32[]{:S(2)}) collective-permute-start(bf16[64,1664]{1,0:T(8,128)(2,1)S(1)} %shard_map.381.refs_2_), channel_id=1, source_target_pairs={{0,4},{1,3},{2,6},{3,1},{4,0},{5,7},{6,2},{7,5},{8,12},{9,11},{10,... | collective-permute-start | bytes 638984 | tf_op jit(solution)/shard_map/ppermute | solution.py:65
  122.0 13.3 %collective-permute-start.45 = (bf16[64,768]{1,0:T(8,128)(2,1)S(1)}, bf16[64,768]{1,0:T(8,128)(2,1)S(1)}, u32[]{:S(2)}, u32[]{:S(2)}) collective-permute-start(bf16[64,768]{1,0:T(8,128)(2,1)S(1)} %shard_map.382.refs_4_.refs_0_), channel_id=1, source_target_pairs={{0,6},{1,7},{2,4},{3,5},{4,2},{5,3},{6,0},{7,1},{8,14},{9,15},{10,... | collective-permute-start | bytes 294920 | tf_op jit(solution)/shard_map/ppermute | solution.py:65
  129.9 9.0 %collective-permute-start.44 = (bf16[64,768]{1,0:T(8,128)(2,1)S(1)}, bf16[64,768]{1,0:T(8,128)(2,1)S(1)}, u32[]{:S(2)}, u32[]{:S(2)}) collective-permute-start(bf16[64,768]{1,0:T(8,128)(2,1)S(1)} %shard_map.382.refs_4_.refs_0_), channel_id=1, source_target_pairs={{0,2},{1,5},{2,0},{3,7},{4,6},{5,1},{6,4},{7,3},{8,10},{9,13},{10,... | collective-permute-start | bytes 294920 | tf_op jit(solution)/shard_map/ppermute | solution.py:65
  130.9 8.0 %collective-permute-start.43 = (bf16[64,768]{1,0:T(8,128)(2,1)S(1)}, bf16[64,768]{1,0:T(8,128)(2,1)S(1)}, u32[]{:S(2)}, u32[]{:S(2)}) collective-permute-start(bf16[64,768]{1,0:T(8,128)(2,1)S(1)} %shard_map.382.refs_4_.refs_0_), channel_id=1, source_target_pairs={{0,4},{1,3},{2,6},{3,1},{4,0},{5,7},{6,2},{7,5},{8,12},{9,11},{10,... | collective-permute-start | bytes 294920 | tf_op jit(solution)/shard_map/ppermute | solution.py:65
  132.4 9.4 %collective-permute-start.37 = (bf16[16,1664]{1,0:T(8,128)(2,1)S(1)}, bf16[16,1664]{1,0:T(8,128)(2,1)S(1)}, u32[]{:S(2)}, u32[]{:S(2)}) collective-permute-start(bf16[16,1664]{1,0:T(8,128)(2,1)S(1)} %get-tuple-element.137), channel_id=1, source_target_pairs={{0,8},{1,9},{2,10},{3,11},{4,12},{5,13},{6,14},{7,15},{8,0},{9,1},... | collective-permute-start | bytes 159752 | tf_op jit(solution)/shard_map/ppermute | solution.py:65
  132.6 9.2 %collective-permute-start.38 = (bf16[16,1664]{1,0:T(8,128)(2,1)S(1)}, bf16[16,1664]{1,0:T(8,128)(2,1)S(1)}, u32[]{:S(2)}, u32[]{:S(2)}) collective-permute-start(bf16[16,1664]{1,0:T(8,128)(2,1)S(1)} %get-tuple-element.138), channel_id=1, source_target_pairs={{0,16},{1,17},{2,18},{3,19},{4,20},{5,21},{6,22},{7,23},{8,24},{9,... | collective-permute-start | bytes 159752 | tf_op jit(solution)/shard_map/ppermute | solution.py:65
  (40 other events, 148.9 us)

commit v9 on v7

--- a/solution.py
+++ b/solution.py
@@ -1243,9 +1243,9 @@
         right_terms.append(route.swap(right_part, far))
         (sp_sum,) = line_turn(sp_terms, 0, [right_part])
         spat_pieces = route.widen(sp_sum)
-        right_own, *sends = line_parts(right_terms, [sp_sum])
+        left_sum, *new_out = finish_out(lo_own, lo_got, dense_out, out_first, out_second, sp_sum)
+        right_own, *sends = line_parts(right_terms, [left_sum])
         right_got = [route.swap(p, (m, m)) for p, m in zip(sends, route.direct)]
-        left_sum, *new_out = finish_out(lo_own, lo_got, dense_out, out_first, out_second, right_own)
         korder = order
         after = [left_sum]
     else:

time: 138 us -> 138 us (level)
  no operation moved by 1% of the time
where the time goes in v9:
time: 138 us
  Pallas kernels  59.1 us (43%)
  starting transfers between devices  40.9 us (30%)
  waiting for transfers between devices  28 us (20%)
  local copies, waits for them, and re-layouts  7.25 us (5%)
  other arithmetic  1.66 us (1%)
    pallas_call x17, Pallas kernels, call(): pl.pallas_call(kernel, out_shape=out_shape, in_specs=in_specs, out_specs=...  58.1 us
    ppermute x29, starting transfers between devices, swap(): return lax.ppermute(block, AXES, pairs)  37.3 us
    ppermute x29, waiting for transfers between devices, swap(): return lax.ppermute(block, AXES, pairs)  21.7 us
    unnamed x50, local copies, waits for them, and re-layouts  6.33 us
    ppermute x17, waiting for transfers between devices, cross(): return lax.ppermute(block, AXES, pairs)  6.31 us
    ppermute x17, starting transfers between devices, cross(): return lax.ppermute(block, AXES, pairs)  3.58 us
  transfers between devices with their start and end apart: 46, of which 15 were waited for; matrix products, arithmetic and copies ran while one was open for 3% of the time, Pallas kernels for 28%

profile of v9, /device:TPU:0, one launch (start us, length us, event | category | flops | bytes accessed | tf_op | source)
XLA Modules:
  0.0 138.1 jit_solution(11139849968603584611)
XLA Ops:
  0.7 1.7 %shard_map.360 = (bf16[16,1792]{1,0:T(8,128)(2,1)}, bf16[16,3072]{1,0:T(8,128)(2,1)}) custom-call(f32[16,3072]{1,0:T(8,128)} %w_ref.3, f32[48,512]{1,0:T(8,128)} %w_ref.2, f32[1,240]{1,0:T(1,128)} %bitcast.7), custom_call_target="tpu_custom_call" | custom-call | flops 1000 | bytes 600000 | tf_op jit(solution)/shard_map/pallas_call | solution.py:220
  2.4 5.1 %collective-permute-start.4 = (bf16[16,1792]{1,0:T(8,128)(2,1)}, bf16[16,1792]{1,0:T(8,128)(2,1)S(1)}, u32[]{:S(2)}, u32[]{:S(2)}) collective-permute-start(bf16[16,1792]{1,0:T(8,128)(2,1)} %get-tuple-element.89.refs_0_), channel_id=1, source_target_pairs={{0,24},{1,25},{2,26},{3,27},{4,28},{5,29},{6,30},{7,31},{8,16},{9,... | collective-permute-start | bytes 172040 | tf_op jit(solution)/shard_map/ppermute | solution.py:64
  8.1 2.0 %collective-permute-done.4.refs_3_ = bf16[16,1792]{1,0:T(8,128)(2,1)S(1)} collective-permute-done((bf16[16,1792]{1,0:T(8,128)(2,1)}, bf16[16,1792]{1,0:T(8,128)(2,1)S(1)}, u32[]{:S(2)}, u32[]{:S(2)}) %collective-permute-start.4) | collective-permute-done | bytes 57376 | tf_op jit(solution)/shard_map/ppermute | solution.py:64
  10.1 2.6 %collective-permute-done.3.refs_2_ = bf16[16,1792]{1,0:T(8,128)(2,1)S(1)} collective-permute-done((bf16[16,1792]{1,0:T(8,128)(2,1)}, bf16[16,1792]{1,0:T(8,128)(2,1)S(1)}, u32[]{:S(2)}, u32[]{:S(2)}) %collective-permute-start.3) | collective-permute-done | bytes 57376 | tf_op jit(solution)/shard_map/ppermute | solution.py:64
  13.6 1.6 %collective-permute-start.6 = (bf16[64,1792]{1,0:T(8,128)(2,1)S(1)}, bf16[64,1792]{1,0:T(8,128)(2,1)S(1)}, u32[]{:S(2)}, u32[]{:S(2)}) collective-permute-start(bf16[64,1792]{1,0:T(8,128)(2,1)S(1)} %shard_map.361.refs_0_), channel_id=1, source_target_pairs={{0,2},{1,5},{2,0},{3,7},{4,6},{5,1},{6,4},{7,3},{8,10},{9,13},{10,... | collective-permute-start | bytes 688136 | tf_op jit(solution)/shard_map/ppermute | solution.py:64
  15.2 1.5 %collective-permute-start.5 = (bf16[64,1792]{1,0:T(8,128)(2,1)S(1)}, bf16[64,1792]{1,0:T(8,128)(2,1)S(1)}, u32[]{:S(2)}, u32[]{:S(2)}) collective-permute-start(bf16[64,1792]{1,0:T(8,128)(2,1)S(1)} %shard_map.361.refs_0_), channel_id=1, source_target_pairs={{0,4},{1,3},{2,6},{3,1},{4,0},{5,7},{6,2},{7,5},{8,12},{9,11},{10,... | collective-permute-start | bytes 688136 | tf_op jit(solution)/shard_map/ppermute | solution.py:64
  16.7 2.6 %collective-permute-start.15 = (bf16[16,3072]{1,0:T(8,128)(2,1)}, bf16[16,3072]{1,0:T(8,128)(2,1)S(1)}, u32[]{:S(2)}, u32[]{:S(2)}) collective-permute-start(bf16[16,3072]{1,0:T(8,128)(2,1)} %get-tuple-element.98.refs_0_), channel_id=1, source_target_pairs={{0,24},{1,25},{2,26},{3,27},{4,28},{5,29},{6,30},{7,31},{8,16},{9,... | collective-permute-start | bytes 294920 | tf_op jit(solution)/shard_map/ppermute | solution.py:64
  20.0 1.6 %collective-permute-done.6.refs_1_.refs_2_ = bf16[64,1792]{1,0:T(8,128)(2,1)S(1)} collective-permute-done((bf16[64,1792]{1,0:T(8,128)(2,1)S(1)}, bf16[64,1792]{1,0:T(8,128)(2,1)S(1)}, u32[]{:S(2)}, u32[]{:S(2)}) %collective-permute-start.6) | collective-permute-done | bytes 229408 | tf_op jit(solution)/shard_map/ppermute | solution.py:64
  21.7 1.6 %collective-permute-start.7 = (bf16[64,1792]{1,0:T(8,128)(2,1)S(1)}, bf16[64,1792]{1,0:T(8,128)(2,1)}, u32[]{:S(2)}, u32[]{:S(2)}) collective-permute-start(bf16[64,1792]{1,0:T(8,128)(2,1)S(1)} %shard_map.362.refs_4_), channel_id=1, source_target_pairs={{0,2},{1,5},{2,0},{3,7},{4,6},{5,1},{6,4},{7,3},{8,10},{9,13},{10,... | collective-permute-start | bytes 688136 | tf_op jit(solution)/shard_map/ppermute | solution.py:64
  25.5 1.5 %shard_map.359 = (bf16[3,162,384]{2,1,0:T(8,128)(2,1)S(1)}, bf16[2,162,512]{2,1,0:T(8,128)(2,1)}, bf16[2,162,512]{2,1,0:T(8,128)(2,1)}) custom-call(s32[33]{0:T(128)S(1)} %pad_add_fusion.1.sides_ref, f32[3,162,324]{2,1,0:T(8,128)S(1)} %copy-done, f32[3,162,1]{2,1,0:T(8,128)S(1)} %copy.47.b_ref, bf16[4,162,512]{2,1,0:T(8,128)(2,1)S(1)} %copy.50.x_ref.p_ref, ...), custom_call_target="tpu_custom_call" | custom-call | flops 1000 | bytes 3000000 | tf_op jit(solution)/shard_map/pallas_call | solution.py:220
  28.9 4.2 %collective-permute-done.13.refs_1_ = bf16[16,3072]{1,0:T(8,128)(2,1)S(1)} collective-permute-done((bf16[16,3072]{1,0:T(8,128)(2,1)S(1)}, bf16[16,3072]{1,0:T(8,128)(2,1)S(1)}, u32[]{:S(2)}, u32[]{:S(2)}) %collective-permute-start.13) | collective-permute-done | bytes 98336 | tf_op jit(solution)/shard_map/ppermute | solution.py:64
  37.1 1.5 %collective-permute-start.16 = (bf16[64,3072]{1,0:T(8,128)(2,1)S(1)}, bf16[64,3072]{1,0:T(8,128)(2,1)S(1)}, u32[]{:S(2)}, u32[]{:S(2)}) collective-permute-start(bf16[64,3072]{1,0:T(8,128)(2,1)S(1)} %shard_map.365.refs_0_), channel_id=1, source_target_pairs={{0,4},{1,3},{2,6},{3,1},{4,0},{5,7},{6,2},{7,5},{8,12},{9,11},{10,... | collective-permute-start | bytes 1179656 | tf_op jit(solution)/shard_map/ppermute | solution.py:64
  38.7 11.0 %shard_map.363 = (bf16[672,512]{1,0:T(8,128)(2,1)S(1)}, bf16[672,512]{1,0:T(8,128)(2,1)S(1)}, bf16[672,512]{1,0:T(8,128)(2,1)S(1)}, f32[672,1536]{1,0:T(8,128)S(...) custom-call(s32[32]{0:T(128)S(1)} %get-tuple-element.195.table_ref, ...), custom_call_target="tpu_custom_call" | custom-call | flops 10000000000 | bytes 20000000 | tf_op jit(solution)/shard_map/pallas_call | solution.py:220
  49.7 5.0 %shard_map.364 = (bf16[720,1536]{1,0:T(8,128)(2,1)S(1)}, bf16[672,1536]{1,0:T(8,128)(2,1)S(1)}, f32[672,128]{1,0:T(8,128)S(1)}, bf16[672,1536]{1,0:T(8,128)(2,1)S(1)}, bf16[2,336,384]{2,1,0:T(8,128)(2,1)S(1)}) custom-call(s32[2]{0:T(128)S(1)} %dynamic_slice.3.levels_ref, s32[33]{0:T(128)S(1)} %pad_add_fusion.1.sides_ref, ...), custom_call_target="tpu_custom_call" | custom-call | flops 6000000000 | bytes 12000000 | tf_op jit(solution)/shard_map/pallas_call | solution.py:220
  56.1 2.9 %collective-permute-done.19.refs_4_ = bf16[64,3072]{1,0:T(8,128)(2,1)S(1)} collective-permute-done((bf16[64,3072]{1,0:T(8,128)(2,1)S(1)}, bf16[64,3072]{1,0:T(8,128)(2,1)S(1)}, u32[]{:S(2)}, u32[]{:S(2)}) %collective-permute-start.19) | collective-permute-done | bytes 393248 | tf_op jit(solution)/shard_map/ppermute | solution.py:71
  59.0 14.1 %shard_map.367 = (bf16[672,1536]{1,0:T(8,128)(2,1)S(1)}, bf16[672,1536]{1,0:T(8,128)(2,1)S(1)}, bf16[672,1536]{1,0:T(8,128)(2,1)S(1)}, bf16[672,512]{1,0:T(8,128...) custom-call(s32[32]{0:T(128)S(1)} %get-tuple-element.195.table_ref, ...), custom_call_target="tpu_custom_call" | custom-call | flops 8000000000 | bytes 16000000 | tf_op jit(solution)/shard_map/pallas_call | solution.py:220
  73.3 1.6 %collective-permute-done.21.refs_1_ = bf16[256,768]{1,0:T(8,128)(2,1)S(1)} collective-permute-done((bf16[256,768]{1,0:T(8,128)(2,1)S(1)}, bf16[256,768]{1,0:T(8,128)(2,1)S(1)}, u32[]{:S(2)}, u32[]{:S(2)}) %collective-permute-start.21) | collective-permute-done | bytes 393248 | tf_op jit(solution)/shard_map/ppermute | solution.py:71
  75.7 4.9 %shard_map.369 = (bf16[512,1536]{1,0:T(8,128)(2,1)S(1)}, bf16[2,162,512]{2,1,0:T(8,128)(2,1)S(1)}, bf16[2,162,512]{2,1,0:T(8,128)(2,1)S(1)}, f32[672,512]{1,0:T(8,128)S(1)}) custom-call(s32[2]{0:T(128)S(1)} %dynamic_slice.3.levels_ref, s32[33]{0:T(128)S(1)} %pad_add_fusion.1.sides_ref, f32[1,7680]{1,0:T(1,128)S(1)} %get-tuple-element.90.vec_ref, ...), custom_call_target="tpu_custom_call" | custom-call | flops 4000000000 | bytes 12000000 | tf_op jit(solution)/shard_map/pallas_call | solution.py:220
  80.7 3.2 %shard_map.371 = (bf16[256,3072]{1,0:T(8,128)(2,1)S(1)}, bf16[128,3072]{1,0:T(8,128)(2,1)S(1)}, bf16[128,3072]{1,0:T(8,128)(2,1)S(1)}) custom-call(s32[32]{0:T(128)S(1)} %get-tuple-element.195.table_ref, bf16[672,1536]{1,0:T(8,128)(2,1)S(1)} %get-tuple-element.100.t_ref, bf16[672,512]{1,0:T(8,128)(2,1)S(1)} %get-tuple-element.114.gb_ref, ...), custom_call_target="tpu_custom_call" | custom-call | flops 2000000000 | bytes 8000000 | tf_op jit(solution)/shard_map/pallas_call | solution.py:220
  84.5 1.8 %collective-permute-done.24.refs_1_ = bf16[128,3072]{1,0:T(8,128)(2,1)S(1)} collective-permute-done((bf16[128,3072]{1,0:T(8,128)(2,1)S(1)}, bf16[128,3072]{1,0:T(8,128)(2,1)S(1)}, u32[]{:S(2)}, u32[]{:S(2)}) %collective-permute-start.24) | collective-permute-done | bytes 786464 | tf_op jit(solution)/shard_map/ppermute | solution.py:71
  88.5 5.7 %shard_map.373 = (bf16[672,1536]{1,0:T(8,128)(2,1)S(1)}, f32[1,4608]{1,0:T(1,128)S(1)}) custom-call(f32[1,7680]{1,0:T(1,128)S(1)} %get-tuple-element.90.vec_ref, bf16[672,1536]{1,0:T(8,128)(2,1)S(1)} %get-tuple-element.110.gs_ref, bf16[2,336,384]{2,1,0:T(8,128)(2,1)S(1)} %get-tuple-element.99.refs_3_.mm_ref, ...), custom_call_target="tpu_custom_call" | custom-call | flops 3000000000 | bytes 10000000 | tf_op jit(solution)/shard_map/pallas_call | solution.py:220
  95.1 2.7 %shard_map.375 = (bf16[512,1536]{1,0:T(8,128)(2,1)S(1)}, f32[672,512]{1,0:T(8,128)S(1)}) custom-call(bf16[672,1536]{1,0:T(8,128)(2,1)S(1)} %get-tuple-element.120.gp_ref, bf16[672,512]{1,0:T(8,128)(2,1)S(1)} %get-tuple-element.91.h_ref, bf16[512,1536]{1,0:T(8,128)(2,1)S(1)} %get-tuple-element.121.w_ref, f32[672,512]{1,0:T(8,128)S(1)} %get-tuple-element.116.refs_3_.gh_ref, ...), custom_call_target="tpu_custom_call" | custom-call | flops 3000000000 | bytes 8000000 | tf_op jit(solution)/shard_map/pallas_call | solution.py:220
  97.8 1.5 %collective-permute-done.28.refs_1_ = bf16[64,768]{1,0:T(8,128)(2,1)S(1)} collective-permute-done((bf16[64,768]{1,0:T(8,128)(2,1)S(1)}, bf16[64,768]{1,0:T(8,128)(2,1)S(1)}, u32[]{:S(2)}, u32[]{:S(2)}) %collective-permute-start.28) | collective-permute-done | bytes 98336 | tf_op jit(solution)/shard_map/ppermute | solution.py:64
  100.7 2.8 %shard_map.378 = (bf16[256,1792]{1,0:T(8,128)(2,1)S(1)}, bf16[128,1792]{1,0:T(8,128)(2,1)S(1)}, bf16[64,1792]{1,0:T(8,128)(2,1)S(1)}, bf16[64,1792]{1,0:T(8,128)...) custom-call(s32[32]{0:T(128)S(1)} %get-tuple-element.195.table_ref, ...), custom_call_target="tpu_custom_call" | custom-call | flops 2000000000 | bytes 6000000 | tf_op jit(solution)/shard_map/pallas_call | solution.py:220
  104.2 3.3 %collective-permute-done.33.refs_3_ = bf16[64,3072]{1,0:T(8,128)(2,1)S(1)} collective-permute-done((bf16[64,3072]{1,0:T(8,128)(2,1)S(1)}, bf16[64,3072]{1,0:T(8,128)(2,1)S(1)}, u32[]{:S(2)}, u32[]{:S(2)}) %collective-permute-start.33) | collective-permute-done | bytes 393248 | tf_op jit(solution)/shard_map/ppermute | solution.py:64
  109.3 1.4 %collective-permute-start.39 = (bf16[64,768]{1,0:T(8,128)(2,1)S(1)}, bf16[64,768]{1,0:T(8,128)(2,1)S(1)}, u32[]{:S(2)}, u32[]{:S(2)}) collective-permute-start(bf16[64,768]{1,0:T(8,128)(2,1)S(1)} %get-tuple-element.138), channel_id=1, source_target_pairs={{0,16},{1,17},{2,18},{3,19},{4,20},{5,21},{6,22},{7,23},{8,24},{9,... | collective-permute-start | bytes 294920 | tf_op jit(solution)/shard_map/ppermute | solution.py:64
  111.9 1.4 %collective-permute-start.36 = (bf16[16,3072]{1,0:T(8,128)(2,1)S(1)}, bf16[16,3072]{1,0:T(8,128)(2,1)S(1)}, u32[]{:S(2)}, u32[]{:S(2)}) collective-permute-start(bf16[16,3072]{1,0:T(8,128)(2,1)S(1)} %get-tuple-element.135), channel_id=1, source_target_pairs={{0,8},{1,9},{2,10},{3,11},{4,12},{5,13},{6,14},{7,15},{8,0},{9,1},... | collective-permute-start | bytes 294920 | tf_op jit(solution)/shard_map/ppermute | solution.py:64
  114.2 2.2 %collective-permute-start.38 = (bf16[16,3072]{1,0:T(8,128)(2,1)S(1)}, bf16[16,3072]{1,0:T(8,128)(2,1)S(1)}, u32[]{:S(2)}, u32[]{:S(2)}) collective-permute-start(bf16[16,3072]{1,0:T(8,128)(2,1)S(1)} %get-tuple-element.137), channel_id=1, source_target_pairs={{0,24},{1,25},{2,26},{3,27},{4,28},{5,29},{6,30},{7,31},{8,16},{9,... | collective-permute-start | bytes 294920 | tf_op jit(solution)/shard_map/ppermute | solution.py:64
  120.2 4.0 %collective-permute-done.37.b_ref = bf16[16,3072]{1,0:T(8,128)(2,1)S(1)} collective-permute-done((bf16[16,3072]{1,0:T(8,128)(2,1)S(1)}, bf16[16,3072]{1,0:T(8,128)(2,1)S(1)}, u32[]{:S(2)}, u32[]{:S(2)}) %collective-permute-start.37) | collective-permute-done | bytes 98336 | tf_op jit(solution)/shard_map/ppermute | solution.py:64
  126.2 2.2 %collective-permute-start.40 = (bf16[16,1792]{1,0:T(8,128)(2,1)S(1)}, bf16[16,1792]{1,0:T(8,128)(2,1)S(1)}, u32[]{:S(2)}, u32[]{:S(2)}) collective-permute-start(bf16[16,1792]{1,0:T(8,128)(2,1)S(1)} %get-tuple-element.141), channel_id=1, source_target_pairs={{0,8},{1,9},{2,10},{3,11},{4,12},{5,13},{6,14},{7,15},{8,0},{9,1},... | collective-permute-start | bytes 172040 | tf_op jit(solution)/shard_map/ppermute | solution.py:64
  129.2 1.6 %collective-permute-start.42 = (bf16[16,1792]{1,0:T(8,128)(2,1)S(1)}, bf16[16,1792]{1,0:T(8,128)(2,1)S(1)}, u32[]{:S(2)}, u32[]{:S(2)}) collective-permute-start(bf16[16,1792]{1,0:T(8,128)(2,1)S(1)} %get-tuple-element.143), channel_id=1, source_target_pairs={{0,24},{1,25},{2,26},{3,27},{4,28},{5,29},{6,30},{7,31},{8,16},{9,... | collective-permute-start | bytes 172040 | tf_op jit(solution)/shard_map/ppermute | solution.py:64
  132.1 2.8 %shard_map.385 = (f32[3,162,324]{2,1,0:T(8,128)}, f32[3,162,324]{2,1,0:T(8,128)}, f32[3,162,324]{2,1,0:T(8,128)}, f32[3,162]{1,0:T(4,128)}, f32[3,162]{1,0:T(4,128)}, /*index=5*/f32[3,162]{1,0:T(4,128)}) custom-call(s32[16]{0:T(128)S(1)} %get-tuple-element.197.order_ref, bf16[64,768]{1,0:T(8,128)(2,1)S(1)} %shard_map.382.after_ref.refs_0_, ...), custom_call_target="tpu_custom_call" | custom-call | flops 10000000 | bytes 6000000 | tf_op jit(solution)/shard_map/pallas_call | solution.py:220
  (148 shorter events, 33.3 us)
Async XLA Ops:
  2.4 7.8 %collective-permute-start.4 = (bf16[16,1792]{1,0:T(8,128)(2,1)}, bf16[16,1792]{1,0:T(8,128)(2,1)S(1)}, u32[]{:S(2)}, u32[]{:S(2)}) collective-permute-start(bf16[16,1792]{1,0:T(8,128)(2,1)} %get-tuple-element.89.refs_0_), channel_id=1, source_target_pairs={{0,24},{1,25},{2,26},{3,27},{4,28},{5,29},{6,30},{7,31},{8,16},{9,... | collective-permute-start | bytes 172040 | tf_op jit(solution)/shard_map/ppermute | solution.py:64
  13.6 8.0 %collective-permute-start.6 = (bf16[64,1792]{1,0:T(8,128)(2,1)S(1)}, bf16[64,1792]{1,0:T(8,128)(2,1)S(1)}, u32[]{:S(2)}, u32[]{:S(2)}) collective-permute-start(bf16[64,1792]{1,0:T(8,128)(2,1)S(1)} %shard_map.361.refs_0_), channel_id=1, source_target_pairs={{0,2},{1,5},{2,0},{3,7},{4,6},{5,1},{6,4},{7,3},{8,10},{9,13},{10,... | collective-permute-start | bytes 688136 | tf_op jit(solution)/shard_map/ppermute | solution.py:64
  15.2 6.5 %collective-permute-start.5 = (bf16[64,1792]{1,0:T(8,128)(2,1)S(1)}, bf16[64,1792]{1,0:T(8,128)(2,1)S(1)}, u32[]{:S(2)}, u32[]{:S(2)}) collective-permute-start(bf16[64,1792]{1,0:T(8,128)(2,1)S(1)} %shard_map.361.refs_0_), channel_id=1, source_target_pairs={{0,4},{1,3},{2,6},{3,1},{4,0},{5,7},{6,2},{7,5},{8,12},{9,11},{10,... | collective-permute-start | bytes 688136 | tf_op jit(solution)/shard_map/ppermute | solution.py:64
  16.7 11.1 %collective-permute-start.15 = (bf16[16,3072]{1,0:T(8,128)(2,1)}, bf16[16,3072]{1,0:T(8,128)(2,1)S(1)}, u32[]{:S(2)}, u32[]{:S(2)}) collective-permute-start(bf16[16,3072]{1,0:T(8,128)(2,1)} %get-tuple-element.98.refs_0_), channel_id=1, source_target_pairs={{0,24},{1,25},{2,26},{3,27},{4,28},{5,29},{6,30},{7,31},{8,16},{9,... | collective-permute-start | bytes 294920 | tf_op jit(solution)/shard_map/ppermute | solution.py:64
  19.3 9.0 %collective-permute-start.14 = (bf16[16,3072]{1,0:T(8,128)(2,1)}, bf16[16,3072]{1,0:T(8,128)(2,1)}, u32[]{:S(2)}, u32[]{:S(2)}) collective-permute-start(bf16[16,3072]{1,0:T(8,128)(2,1)} %get-tuple-element.98.refs_0_), channel_id=1, source_target_pairs={{0,16},{1,17},{2,18},{3,19},{4,20},{5,21},{6,22},{7,23},{8,24},{9,... | collective-permute-start | bytes 294920 | tf_op jit(solution)/shard_map/ppermute | solution.py:64
  20.0 13.1 %collective-permute-start.8 = (bf16[64,1792]{1,0:T(8,128)(2,1)S(1)}, bf16[64,1792]{1,0:T(8,128)(2,1)}, u32[]{:S(2)}, u32[]{:S(2)}) collective-permute-start(bf16[64,1792]{1,0:T(8,128)(2,1)S(1)} %shard_map.361.refs_0_), channel_id=1, source_target_pairs={{0,1},{1,0},{2,3},{3,2},{4,5},{5,4},{6,7},{7,6},{8,9},{9,8},{10,11... | collective-permute-start | bytes 688136 | tf_op jit(solution)/shard_map/ppermute | solution.py:71
  21.7 11.9 %collective-permute-start.7 = (bf16[64,1792]{1,0:T(8,128)(2,1)S(1)}, bf16[64,1792]{1,0:T(8,128)(2,1)}, u32[]{:S(2)}, u32[]{:S(2)}) collective-permute-start(bf16[64,1792]{1,0:T(8,128)(2,1)S(1)} %shard_map.362.refs_4_), channel_id=1, source_target_pairs={{0,2},{1,5},{2,0},{3,7},{4,6},{5,1},{6,4},{7,3},{8,10},{9,13},{10,... | collective-permute-start | bytes 688136 | tf_op jit(solution)/shard_map/ppermute | solution.py:64
  27.8 6.9 %collective-permute-start = (bf16[2,162,512]{2,1,0:T(8,128)(2,1)}, bf16[2,162,512]{2,1,0:T(8,128)(2,1)}, u32[]{:S(2)}, u32[]{:S(2)}) collective-permute-start(bf16[2,162,512]{2,1,0:T(8,128)(2,1)} %get-tuple-element.87), channel_id=1, source_target_pairs={{0,1},{1,0},{2,3},{3,2},{4,5},{5,4},{6,7},{7,6},{8,9},{9,8},{10,11... | collective-permute-start | bytes 995336 | tf_op jit(solution)/shard_map/ppermute | solution.py:71
  27.8 7.4 %collective-permute-start.1 = (bf16[2,162,512]{2,1,0:T(8,128)(2,1)}, bf16[2,162,512]{2,1,0:T(8,128)(2,1)}, u32[]{:S(2)}, u32[]{:S(2)}) collective-permute-start(bf16[2,162,512]{2,1,0:T(8,128)(2,1)} %get-tuple-element.88), channel_id=1, source_target_pairs={{0,1},{1,0},{2,3},{3,2},{4,5},{5,4},{6,7},{7,6},{8,9},{9,8},{10,11... | collective-permute-start | bytes 995336 | tf_op jit(solution)/shard_map/ppermute | solution.py:71
  34.7 15.0 %collective-permute-start.12 = (bf16[3,162,384]{2,1,0:T(8,128)(2,1)}, bf16[3,162,384]{2,1,0:T(8,128)(2,1)S(1)}, u32[]{:S(2)}, u32[]{:S(2)}) collective-permute-start(bf16[3,162,384]{2,1,0:T(8,128)(2,1)} %copy-done.15), channel_id=1, source_target_pairs={{0,1},{1,0},{2,3},{3,2},{4,5},{5,4},{6,7},{7,6},{8,9},{9,8},{10,11... | collective-permute-start | bytes 1119752 | tf_op jit(solution)/shard_map/ppermute | solution.py:71
  35.2 19.6 %collective-permute-start.18 = (bf16[64,3072]{1,0:T(8,128)(2,1)S(1)}, bf16[64,3072]{1,0:T(8,128)(2,1)S(1)}, u32[]{:S(2)}, u32[]{:S(2)}) collective-permute-start(bf16[64,3072]{1,0:T(8,128)(2,1)S(1)} %shard_map.365.refs_0_), channel_id=1, source_target_pairs={{0,6},{1,7},{2,4},{3,5},{4,2},{5,3},{6,0},{7,1},{8,14},{9,15},{10,... | collective-permute-start | bytes 1179656 | tf_op jit(solution)/shard_map/ppermute | solution.py:64
  36.2 18.5 %collective-permute-start.17 = (bf16[64,3072]{1,0:T(8,128)(2,1)S(1)}, bf16[64,3072]{1,0:T(8,128)(2,1)S(1)}, u32[]{:S(2)}, u32[]{:S(2)}) collective-permute-start(bf16[64,3072]{1,0:T(8,128)(2,1)S(1)} %shard_map.365.refs_0_), channel_id=1, source_target_pairs={{0,2},{1,5},{2,0},{3,7},{4,6},{5,1},{6,4},{7,3},{8,10},{9,13},{10,... | collective-permute-start | bytes 1179656 | tf_op jit(solution)/shard_map/ppermute | solution.py:64
  37.1 18.3 %collective-permute-start.16 = (bf16[64,3072]{1,0:T(8,128)(2,1)S(1)}, bf16[64,3072]{1,0:T(8,128)(2,1)S(1)}, u32[]{:S(2)}, u32[]{:S(2)}) collective-permute-start(bf16[64,3072]{1,0:T(8,128)(2,1)S(1)} %shard_map.365.refs_0_), channel_id=1, source_target_pairs={{0,4},{1,3},{2,6},{3,1},{4,0},{5,7},{6,2},{7,5},{8,12},{9,11},{10,... | collective-permute-start | bytes 1179656 | tf_op jit(solution)/shard_map/ppermute | solution.py:64
  75.0 5.7 %collective-permute-start.23 = (bf16[128,768]{1,0:T(8,128)(2,1)S(1)}, bf16[128,768]{1,0:T(8,128)(2,1)S(1)}, u32[]{:S(2)}, u32[]{:S(2)}) collective-permute-start(bf16[128,768]{1,0:T(8,128)(2,1)S(1)} %shard_map.368.refs_0_), channel_id=1, source_target_pairs={{0,2},{1,5},{2,0},{3,7},{4,6},{5,1},{6,4},{7,3},{8,10},{9,13},{10,... | collective-permute-start | bytes 589832 | tf_op jit(solution)/shard_map/ppermute | solution.py:64
  84.0 15.3 %collective-permute-start.26 = (bf16[128,3072]{1,0:T(8,128)(2,1)S(1)}, bf16[128,3072]{1,0:T(8,128)(2,1)S(1)}, u32[]{:S(2)}, u32[]{:S(2)}) collective-permute-start(bf16[128,3072]{1,0:T(8,128)(2,1)S(1)} %get-tuple-element.125), channel_id=1, source_target_pairs={{0,1},{1,0},{2,3},{3,2},{4,5},{5,4},{6,7},{7,6},{8,9},{9,8},{10,11... | collective-permute-start | bytes 2359304 | tf_op jit(solution)/shard_map/ppermute | solution.py:71
  86.4 13.1 %collective-permute-start.27 = (bf16[128,3072]{1,0:T(8,128)(2,1)S(1)}, bf16[128,3072]{1,0:T(8,128)(2,1)S(1)}, u32[]{:S(2)}, u32[]{:S(2)}) collective-permute-start(bf16[128,3072]{1,0:T(8,128)(2,1)S(1)} %shard_map.372.refs_0_), channel_id=1, source_target_pairs={{0,2},{1,5},{2,0},{3,7},{4,6},{5,1},{6,4},{7,3},{8,10},{9,13},{10,... | collective-permute-start | bytes 2359304 | tf_op jit(solution)/shard_map/ppermute | solution.py:64
  87.8 7.3 %collective-permute-start.22 = (bf16[2,162,512]{2,1,0:T(8,128)(2,1)S(1)}, bf16[2,162,512]{2,1,0:T(8,128)(2,1)S(1)}, u32[]{:S(2)}, u32[]{:S(2)}) collective-permute-start(bf16[2,162,512]{2,1,0:T(8,128)(2,1)S(1)} %get-tuple-element.108), channel_id=1, source_target_pairs={{0,1},{1,0},{2,3},{3,2},{4,5},{5,4},{6,7},{7,6},{8,9},{9,8},{10,11... | collective-permute-start | bytes 995336 | tf_op jit(solution)/shard_map/ppermute | solution.py:71
  87.8 6.4 %collective-permute-start.25 = (bf16[64,768]{1,0:T(8,128)(2,1)S(1)}, bf16[64,768]{1,0:T(8,128)(2,1)S(1)}, u32[]{:S(2)}, u32[]{:S(2)}) collective-permute-start(bf16[64,768]{1,0:T(8,128)(2,1)S(1)} %shard_map.370.refs_0_), channel_id=1, source_target_pairs={{0,4},{1,3},{2,6},{3,1},{4,0},{5,7},{6,2},{7,5},{8,12},{9,11},{10,... | collective-permute-start | bytes 294920 | tf_op jit(solution)/shard_map/ppermute | solution.py:64
  99.7 7.8 %collective-permute-start.33 = (bf16[64,3072]{1,0:T(8,128)(2,1)S(1)}, bf16[64,3072]{1,0:T(8,128)(2,1)S(1)}, u32[]{:S(2)}, u32[]{:S(2)}) collective-permute-start(bf16[64,3072]{1,0:T(8,128)(2,1)S(1)} %shard_map.377.refs_0_), channel_id=1, source_target_pairs={{0,4},{1,3},{2,6},{3,1},{4,0},{5,7},{6,2},{7,5},{8,12},{9,11},{10,... | collective-permute-start | bytes 1179656 | tf_op jit(solution)/shard_map/ppermute | solution.py:64
  104.1 10.1 %collective-permute-start.30 = (bf16[128,1792]{1,0:T(8,128)(2,1)S(1)}, bf16[128,1792]{1,0:T(8,128)(2,1)S(1)}, u32[]{:S(2)}, u32[]{:S(2)}) collective-permute-start(bf16[128,1792]{1,0:T(8,128)(2,1)S(1)} %get-tuple-element.131), channel_id=1, source_target_pairs={{0,1},{1,0},{2,3},{3,2},{4,5},{5,4},{6,7},{7,6},{8,9},{9,8},{10,11... | collective-permute-start | bytes 1376264 | tf_op jit(solution)/shard_map/ppermute | solution.py:71
  107.9 8.5 %collective-permute-start.34 = (bf16[128,1792]{1,0:T(8,128)(2,1)S(1)}, bf16[128,1792]{1,0:T(8,128)(2,1)S(1)}, u32[]{:S(2)}, u32[]{:S(2)}) collective-permute-start(bf16[128,1792]{1,0:T(8,128)(2,1)S(1)} %shard_map.380), channel_id=1, source_target_pairs={{0,2},{1,5},{2,0},{3,7},{4,6},{5,1},{6,4},{7,3},{8,10},{9,13},{10,... | collective-permute-start | bytes 1376264 | tf_op jit(solution)/shard_map/ppermute | solution.py:64
  109.3 9.2 %collective-permute-start.39 = (bf16[64,768]{1,0:T(8,128)(2,1)S(1)}, bf16[64,768]{1,0:T(8,128)(2,1)S(1)}, u32[]{:S(2)}, u32[]{:S(2)}) collective-permute-start(bf16[64,768]{1,0:T(8,128)(2,1)S(1)} %get-tuple-element.138), channel_id=1, source_target_pairs={{0,16},{1,17},{2,18},{3,19},{4,20},{5,21},{6,22},{7,23},{8,24},{9,... | collective-permute-start | bytes 294920 | tf_op jit(solution)/shard_map/ppermute | solution.py:64
  111.9 7.5 %collective-permute-start.36 = (bf16[16,3072]{1,0:T(8,128)(2,1)S(1)}, bf16[16,3072]{1,0:T(8,128)(2,1)S(1)}, u32[]{:S(2)}, u32[]{:S(2)}) collective-permute-start(bf16[16,3072]{1,0:T(8,128)(2,1)S(1)} %get-tuple-element.135), channel_id=1, source_target_pairs={{0,8},{1,9},{2,10},{3,11},{4,12},{5,13},{6,14},{7,15},{8,0},{9,1},... | collective-permute-start | bytes 294920 | tf_op jit(solution)/shard_map/ppermute | solution.py:64
  113.3 10.8 %collective-permute-start.37 = (bf16[16,3072]{1,0:T(8,128)(2,1)S(1)}, bf16[16,3072]{1,0:T(8,128)(2,1)S(1)}, u32[]{:S(2)}, u32[]{:S(2)}) collective-permute-start(bf16[16,3072]{1,0:T(8,128)(2,1)S(1)} %get-tuple-element.136), channel_id=1, source_target_pairs={{0,16},{1,17},{2,18},{3,19},{4,20},{5,21},{6,22},{7,23},{8,24},{9,... | collective-permute-start | bytes 294920 | tf_op jit(solution)/shard_map/ppermute | solution.py:64
  114.2 9.9 %collective-permute-start.38 = (bf16[16,3072]{1,0:T(8,128)(2,1)S(1)}, bf16[16,3072]{1,0:T(8,128)(2,1)S(1)}, u32[]{:S(2)}, u32[]{:S(2)}) collective-permute-start(bf16[16,3072]{1,0:T(8,128)(2,1)S(1)} %get-tuple-element.137), channel_id=1, source_target_pairs={{0,24},{1,25},{2,26},{3,27},{4,28},{5,29},{6,30},{7,31},{8,16},{9,... | collective-permute-start | bytes 294920 | tf_op jit(solution)/shard_map/ppermute | solution.py:64
  116.5 9.5 %collective-permute-start.35 = (bf16[64,1792]{1,0:T(8,128)(2,1)S(1)}, bf16[64,1792]{1,0:T(8,128)(2,1)S(1)}, u32[]{:S(2)}, u32[]{:S(2)}) collective-permute-start(bf16[64,1792]{1,0:T(8,128)(2,1)S(1)} %shard_map.381.refs_2_), channel_id=1, source_target_pairs={{0,4},{1,3},{2,6},{3,1},{4,0},{5,7},{6,2},{7,5},{8,12},{9,11},{10,... | collective-permute-start | bytes 688136 | tf_op jit(solution)/shard_map/ppermute | solution.py:64
  118.5 6.4 %collective-permute-start.43 = (bf16[64,768]{1,0:T(8,128)(2,1)S(1)}, bf16[64,768]{1,0:T(8,128)(2,1)S(1)}, u32[]{:S(2)}, u32[]{:S(2)}) collective-permute-start(bf16[64,768]{1,0:T(8,128)(2,1)S(1)} %shard_map.382.after_ref.refs_0_), channel_id=1, source_target_pairs={{0,4},{1,3},{2,6},{3,1},{4,0},{5,7},{6,2},{7,5},{8,12},{9,11},{10,... | collective-permute-start | bytes 294920 | tf_op jit(solution)/shard_map/ppermute | solution.py:64
  119.5 12.6 %collective-permute-start.44 = (bf16[64,768]{1,0:T(8,128)(2,1)S(1)}, bf16[64,768]{1,0:T(8,128)(2,1)S(1)}, u32[]{:S(2)}, u32[]{:S(2)}) collective-permute-start(bf16[64,768]{1,0:T(8,128)(2,1)S(1)} %shard_map.382.after_ref.refs_0_), channel_id=1, source_target_pairs={{0,2},{1,5},{2,0},{3,7},{4,6},{5,1},{6,4},{7,3},{8,10},{9,13},{10,... | collective-permute-start | bytes 294920 | tf_op jit(solution)/shard_map/ppermute | solution.py:64
  124.9 7.1 %collective-permute-start.45 = (bf16[64,768]{1,0:T(8,128)(2,1)S(1)}, bf16[64,768]{1,0:T(8,128)(2,1)S(1)}, u32[]{:S(2)}, u32[]{:S(2)}) collective-permute-start(bf16[64,768]{1,0:T(8,128)(2,1)S(1)} %collective-permute-done.43.refs_1_), channel_id=1, source_target_pairs={{0,2},{1,5},{2,0},{3,7},{4,6},{5,1},{6,4},{7,3},{8,10},{9,13},{10,... | collective-permute-start | bytes 294920 | tf_op jit(solution)/shard_map/ppermute | solution.py:64
  126.2 8.8 %collective-permute-start.40 = (bf16[16,1792]{1,0:T(8,128)(2,1)S(1)}, bf16[16,1792]{1,0:T(8,128)(2,1)S(1)}, u32[]{:S(2)}, u32[]{:S(2)}) collective-permute-start(bf16[16,1792]{1,0:T(8,128)(2,1)S(1)} %get-tuple-element.141), channel_id=1, source_target_pairs={{0,8},{1,9},{2,10},{3,11},{4,12},{5,13},{6,14},{7,15},{8,0},{9,1},... | collective-permute-start | bytes 172040 | tf_op jit(solution)/shard_map/ppermute | solution.py:64
  128.3 7.1 %collective-permute-start.41 = (bf16[16,1792]{1,0:T(8,128)(2,1)S(1)}, bf16[16,1792]{1,0:T(8,128)(2,1)S(1)}, u32[]{:S(2)}, u32[]{:S(2)}) collective-permute-start(bf16[16,1792]{1,0:T(8,128)(2,1)S(1)} %get-tuple-element.142), channel_id=1, source_target_pairs={{0,16},{1,17},{2,18},{3,19},{4,20},{5,21},{6,22},{7,23},{8,24},{9,... | collective-permute-start | bytes 172040 | tf_op jit(solution)/shard_map/ppermute | solution.py:64
  129.2 6.3 %collective-permute-start.42 = (bf16[16,1792]{1,0:T(8,128)(2,1)S(1)}, bf16[16,1792]{1,0:T(8,128)(2,1)S(1)}, u32[]{:S(2)}, u32[]{:S(2)}) collective-permute-start(bf16[16,1792]{1,0:T(8,128)(2,1)S(1)} %get-tuple-element.143), channel_id=1, source_target_pairs={{0,24},{1,25},{2,26},{3,27},{4,28},{5,29},{6,30},{7,31},{8,16},{9,... | collective-permute-start | bytes 172040 | tf_op jit(solution)/shard_map/ppermute | solution.py:64
  (37 other events, 174.0 us)

commit v10 on v9

--- a/solution.py
+++ b/solution.py
@@ -1284,7 +1284,7 @@
         korder, spat_pieces, spatial, spat_first, spat_second, spatial_bias, bias_first, bias_second, after
     )
     if fits:
-        *new_in, vec_sum = finish_in(right_own, right_got, left_sum, dense_in, in_first, in_second, spat_new[0])
+        *new_in, vec_sum = finish_in(right_own, right_got, left_sum, dense_in, in_first, in_second, left_sum)
         vec_sum = vec_sum[0, :vec_len]
     new_vec = adamw(vectors, vec_sum, vec_first, vec_second, SMALL_RATE, 0.0)
     return (mixed, patches_grad) + tuple(new_in) + tuple(new_out) + new_vec + tuple(spat_new)

time: 138 us -> 137 us (level)
    unnamed x50 -> x48, local copies, waits for them, and re-layouts: 6.33 us -> 5.21 us
where the time goes in v10:
time: 137 us
  Pallas kernels  59.1 us (43%)
  starting transfers between devices  41.2 us (30%)
  waiting for transfers between devices  27.7 us (20%)
  local copies, waits for them, and re-layouts  6.13 us (4%)
  other arithmetic  1.66 us (1%)
    pallas_call x17, Pallas kernels, call(): pl.pallas_call(kernel, out_shape=out_shape, in_specs=in_specs, out_specs=...  58.1 us
    ppermute x29, starting transfers between devices, swap(): return lax.ppermute(block, AXES, pairs)  37.6 us
    ppermute x29, waiting for transfers between devices, swap(): return lax.ppermute(block, AXES, pairs)  21.4 us
    ppermute x17, waiting for transfers between devices, cross(): return lax.ppermute(block, AXES, pairs)  6.29 us
    unnamed x48, local copies, waits for them, and re-layouts  5.21 us
    ppermute x17, starting transfers between devices, cross(): return lax.ppermute(block, AXES, pairs)  3.59 us
  transfers between devices with their start and end apart: 46, of which 15 were waited for; matrix products, arithmetic and copies ran while one was open for 3% of the time, Pallas kernels for 28%

profile of v10, /device:TPU:0, one launch (start us, length us, event | category | flops | bytes accessed | tf_op | source)
XLA Modules:
  0.0 136.9 jit_solution(4797744298467650223)
XLA Ops:
  0.7 1.7 %shard_map.360 = (bf16[16,1792]{1,0:T(8,128)(2,1)}, bf16[16,3072]{1,0:T(8,128)(2,1)}) custom-call(f32[16,3072]{1,0:T(8,128)} %w_ref.3, f32[48,512]{1,0:T(8,128)} %w_ref.2, f32[1,240]{1,0:T(1,128)} %bitcast.7), custom_call_target="tpu_custom_call" | custom-call | flops 1000 | bytes 600000 | tf_op jit(solution)/shard_map/pallas_call | solution.py:220
  2.4 5.1 %collective-permute-start.4 = (bf16[16,1792]{1,0:T(8,128)(2,1)}, bf16[16,1792]{1,0:T(8,128)(2,1)S(1)}, u32[]{:S(2)}, u32[]{:S(2)}) collective-permute-start(bf16[16,1792]{1,0:T(8,128)(2,1)} %get-tuple-element.89.refs_0_), channel_id=1, source_target_pairs={{0,24},{1,25},{2,26},{3,27},{4,28},{5,29},{6,30},{7,31},{8,16},{9,... | collective-permute-start | bytes 172040 | tf_op jit(solution)/shard_map/ppermute | solution.py:64
  8.1 2.0 %collective-permute-done.4.refs_3_ = bf16[16,1792]{1,0:T(8,128)(2,1)S(1)} collective-permute-done((bf16[16,1792]{1,0:T(8,128)(2,1)}, bf16[16,1792]{1,0:T(8,128)(2,1)S(1)}, u32[]{:S(2)}, u32[]{:S(2)}) %collective-permute-start.4) | collective-permute-done | bytes 57376 | tf_op jit(solution)/shard_map/ppermute | solution.py:64
  10.1 2.6 %collective-permute-done.3.refs_2_ = bf16[16,1792]{1,0:T(8,128)(2,1)S(1)} collective-permute-done((bf16[16,1792]{1,0:T(8,128)(2,1)}, bf16[16,1792]{1,0:T(8,128)(2,1)S(1)}, u32[]{:S(2)}, u32[]{:S(2)}) %collective-permute-start.3) | collective-permute-done | bytes 57376 | tf_op jit(solution)/shard_map/ppermute | solution.py:64
  13.6 1.6 %collective-permute-start.6 = (bf16[64,1792]{1,0:T(8,128)(2,1)S(1)}, bf16[64,1792]{1,0:T(8,128)(2,1)S(1)}, u32[]{:S(2)}, u32[]{:S(2)}) collective-permute-start(bf16[64,1792]{1,0:T(8,128)(2,1)S(1)} %shard_map.361.refs_0_), channel_id=1, source_target_pairs={{0,2},{1,5},{2,0},{3,7},{4,6},{5,1},{6,4},{7,3},{8,10},{9,13},{10,... | collective-permute-start | bytes 688136 | tf_op jit(solution)/shard_map/ppermute | solution.py:64
  15.2 1.5 %collective-permute-start.5 = (bf16[64,1792]{1,0:T(8,128)(2,1)S(1)}, bf16[64,1792]{1,0:T(8,128)(2,1)S(1)}, u32[]{:S(2)}, u32[]{:S(2)}) collective-permute-start(bf16[64,1792]{1,0:T(8,128)(2,1)S(1)} %shard_map.361.refs_0_), channel_id=1, source_target_pairs={{0,4},{1,3},{2,6},{3,1},{4,0},{5,7},{6,2},{7,5},{8,12},{9,11},{10,... | collective-permute-start | bytes 688136 | tf_op jit(solution)/shard_map/ppermute | solution.py:64
  16.7 2.6 %collective-permute-start.15 = (bf16[16,3072]{1,0:T(8,128)(2,1)}, bf16[16,3072]{1,0:T(8,128)(2,1)S(1)}, u32[]{:S(2)}, u32[]{:S(2)}) collective-permute-start(bf16[16,3072]{1,0:T(8,128)(2,1)} %get-tuple-element.98.refs_0_), channel_id=1, source_target_pairs={{0,24},{1,25},{2,26},{3,27},{4,28},{5,29},{6,30},{7,31},{8,16},{9,... | collective-permute-start | bytes 294920 | tf_op jit(solution)/shard_map/ppermute | solution.py:64
  20.0 1.6 %collective-permute-done.6.refs_1_.refs_2_ = bf16[64,1792]{1,0:T(8,128)(2,1)S(1)} collective-permute-done((bf16[64,1792]{1,0:T(8,128)(2,1)S(1)}, bf16[64,1792]{1,0:T(8,128)(2,1)S(1)}, u32[]{:S(2)}, u32[]{:S(2)}) %collective-permute-start.6) | collective-permute-done | bytes 229408 | tf_op jit(solution)/shard_map/ppermute | solution.py:64
  21.7 1.6 %collective-permute-start.7 = (bf16[64,1792]{1,0:T(8,128)(2,1)S(1)}, bf16[64,1792]{1,0:T(8,128)(2,1)}, u32[]{:S(2)}, u32[]{:S(2)}) collective-permute-start(bf16[64,1792]{1,0:T(8,128)(2,1)S(1)} %shard_map.362.refs_4_), channel_id=1, source_target_pairs={{0,2},{1,5},{2,0},{3,7},{4,6},{5,1},{6,4},{7,3},{8,10},{9,13},{10,... | collective-permute-start | bytes 688136 | tf_op jit(solution)/shard_map/ppermute | solution.py:64
  25.5 1.5 %shard_map.359 = (bf16[3,162,384]{2,1,0:T(8,128)(2,1)S(1)}, bf16[2,162,512]{2,1,0:T(8,128)(2,1)}, bf16[2,162,512]{2,1,0:T(8,128)(2,1)}) custom-call(s32[33]{0:T(128)S(1)} %pad_add_fusion.1.sides_ref, f32[3,162,324]{2,1,0:T(8,128)S(1)} %copy-done, f32[3,162,1]{2,1,0:T(8,128)S(1)} %copy.47.b_ref, bf16[4,162,512]{2,1,0:T(8,128)(2,1)S(1)} %copy.50.x_ref.p_ref, ...), custom_call_target="tpu_custom_call" | custom-call | flops 1000 | bytes 3000000 | tf_op jit(solution)/shard_map/pallas_call | solution.py:220
  28.9 4.2 %collective-permute-done.13.refs_1_ = bf16[16,3072]{1,0:T(8,128)(2,1)S(1)} collective-permute-done((bf16[16,3072]{1,0:T(8,128)(2,1)S(1)}, bf16[16,3072]{1,0:T(8,128)(2,1)S(1)}, u32[]{:S(2)}, u32[]{:S(2)}) %collective-permute-start.13) | collective-permute-done | bytes 98336 | tf_op jit(solution)/shard_map/ppermute | solution.py:64
  37.1 1.5 %collective-permute-start.16 = (bf16[64,3072]{1,0:T(8,128)(2,1)S(1)}, bf16[64,3072]{1,0:T(8,128)(2,1)S(1)}, u32[]{:S(2)}, u32[]{:S(2)}) collective-permute-start(bf16[64,3072]{1,0:T(8,128)(2,1)S(1)} %shard_map.365.refs_0_), channel_id=1, source_target_pairs={{0,4},{1,3},{2,6},{3,1},{4,0},{5,7},{6,2},{7,5},{8,12},{9,11},{10,... | collective-permute-start | bytes 1179656 | tf_op jit(solution)/shard_map/ppermute | solution.py:64
  38.7 11.0 %shard_map.363 = (bf16[672,512]{1,0:T(8,128)(2,1)S(1)}, bf16[672,512]{1,0:T(8,128)(2,1)S(1)}, bf16[672,512]{1,0:T(8,128)(2,1)S(1)}, f32[672,1536]{1,0:T(8,128)S(...) custom-call(s32[32]{0:T(128)S(1)} %get-tuple-element.195.table_ref, ...), custom_call_target="tpu_custom_call" | custom-call | flops 10000000000 | bytes 20000000 | tf_op jit(solution)/shard_map/pallas_call | solution.py:220
  49.7 5.0 %shard_map.364 = (bf16[720,1536]{1,0:T(8,128)(2,1)S(1)}, bf16[672,1536]{1,0:T(8,128)(2,1)S(1)}, f32[672,128]{1,0:T(8,128)S(1)}, bf16[672,1536]{1,0:T(8,128)(2,1)S(1)}, bf16[2,336,384]{2,1,0:T(8,128)(2,1)S(1)}) custom-call(s32[2]{0:T(128)S(1)} %dynamic_slice.3.levels_ref, s32[33]{0:T(128)S(1)} %pad_add_fusion.1.sides_ref, ...), custom_call_target="tpu_custom_call" | custom-call | flops 6000000000 | bytes 12000000 | tf_op jit(solution)/shard_map/pallas_call | solution.py:220
  56.1 2.9 %collective-permute-done.19.refs_4_ = bf16[64,3072]{1,0:T(8,128)(2,1)S(1)} collective-permute-done((bf16[64,3072]{1,0:T(8,128)(2,1)S(1)}, bf16[64,3072]{1,0:T(8,128)(2,1)S(1)}, u32[]{:S(2)}, u32[]{:S(2)}) %collective-permute-start.19) | collective-permute-done | bytes 393248 | tf_op jit(solution)/shard_map/ppermute | solution.py:71
  59.0 14.0 %shard_map.367 = (bf16[672,1536]{1,0:T(8,128)(2,1)S(1)}, bf16[672,1536]{1,0:T(8,128)(2,1)S(1)}, bf16[672,1536]{1,0:T(8,128)(2,1)S(1)}, bf16[672,512]{1,0:T(8,128...) custom-call(s32[32]{0:T(128)S(1)} %get-tuple-element.195.table_ref, ...), custom_call_target="tpu_custom_call" | custom-call | flops 8000000000 | bytes 16000000 | tf_op jit(solution)/shard_map/pallas_call | solution.py:220
  73.3 1.6 %collective-permute-done.21.refs_1_ = bf16[256,768]{1,0:T(8,128)(2,1)S(1)} collective-permute-done((bf16[256,768]{1,0:T(8,128)(2,1)S(1)}, bf16[256,768]{1,0:T(8,128)(2,1)S(1)}, u32[]{:S(2)}, u32[]{:S(2)}) %collective-permute-start.21) | collective-permute-done | bytes 393248 | tf_op jit(solution)/shard_map/ppermute | solution.py:71
  75.6 4.9 %shard_map.369 = (bf16[512,1536]{1,0:T(8,128)(2,1)S(1)}, bf16[2,162,512]{2,1,0:T(8,128)(2,1)S(1)}, bf16[2,162,512]{2,1,0:T(8,128)(2,1)S(1)}, f32[672,512]{1,0:T(8,128)S(1)}) custom-call(s32[2]{0:T(128)S(1)} %dynamic_slice.3.levels_ref, s32[33]{0:T(128)S(1)} %pad_add_fusion.1.sides_ref, f32[1,7680]{1,0:T(1,128)S(1)} %get-tuple-element.90.vec_ref, ...), custom_call_target="tpu_custom_call" | custom-call | flops 4000000000 | bytes 12000000 | tf_op jit(solution)/shard_map/pallas_call | solution.py:220
  80.7 3.2 %shard_map.371 = (bf16[256,3072]{1,0:T(8,128)(2,1)S(1)}, bf16[128,3072]{1,0:T(8,128)(2,1)S(1)}, bf16[128,3072]{1,0:T(8,128)(2,1)S(1)}) custom-call(s32[32]{0:T(128)S(1)} %get-tuple-element.195.table_ref, bf16[672,1536]{1,0:T(8,128)(2,1)S(1)} %get-tuple-element.100.t_ref, bf16[672,512]{1,0:T(8,128)(2,1)S(1)} %get-tuple-element.114.gb_ref, ...), custom_call_target="tpu_custom_call" | custom-call | flops 2000000000 | bytes 8000000 | tf_op jit(solution)/shard_map/pallas_call | solution.py:220
  84.4 1.8 %collective-permute-done.24.refs_1_ = bf16[128,3072]{1,0:T(8,128)(2,1)S(1)} collective-permute-done((bf16[128,3072]{1,0:T(8,128)(2,1)S(1)}, bf16[128,3072]{1,0:T(8,128)(2,1)S(1)}, u32[]{:S(2)}, u32[]{:S(2)}) %collective-permute-start.24) | collective-permute-done | bytes 786464 | tf_op jit(solution)/shard_map/ppermute | solution.py:71
  88.5 5.7 %shard_map.373 = (bf16[672,1536]{1,0:T(8,128)(2,1)S(1)}, f32[1,4608]{1,0:T(1,128)S(1)}) custom-call(f32[1,7680]{1,0:T(1,128)S(1)} %get-tuple-element.90.vec_ref, bf16[672,1536]{1,0:T(8,128)(2,1)S(1)} %get-tuple-element.110.gs_ref, bf16[2,336,384]{2,1,0:T(8,128)(2,1)S(1)} %get-tuple-element.99.refs_3_.mm_ref, ...), custom_call_target="tpu_custom_call" | custom-call | flops 3000000000 | bytes 10000000 | tf_op jit(solution)/shard_map/pallas_call | solution.py:220
  95.1 2.7 %shard_map.375 = (bf16[512,1536]{1,0:T(8,128)(2,1)S(1)}, f32[672,512]{1,0:T(8,128)S(1)}) custom-call(bf16[672,1536]{1,0:T(8,128)(2,1)S(1)} %get-tuple-element.120.gp_ref, bf16[672,512]{1,0:T(8,128)(2,1)S(1)} %get-tuple-element.91.h_ref, bf16[512,1536]{1,0:T(8,128)(2,1)S(1)} %get-tuple-element.121.w_ref, f32[672,512]{1,0:T(8,128)S(1)} %get-tuple-element.116.refs_3_.gh_ref, ...), custom_call_target="tpu_custom_call" | custom-call | flops 3000000000 | bytes 8000000 | tf_op jit(solution)/shard_map/pallas_call | solution.py:220
  97.8 1.4 %collective-permute-done.28.refs_1_ = bf16[64,768]{1,0:T(8,128)(2,1)S(1)} collective-permute-done((bf16[64,768]{1,0:T(8,128)(2,1)S(1)}, bf16[64,768]{1,0:T(8,128)(2,1)S(1)}, u32[]{:S(2)}, u32[]{:S(2)}) %collective-permute-start.28) | collective-permute-done | bytes 98336 | tf_op jit(solution)/shard_map/ppermute | solution.py:64
  100.7 2.8 %shard_map.378 = (bf16[256,1792]{1,0:T(8,128)(2,1)S(1)}, bf16[128,1792]{1,0:T(8,128)(2,1)S(1)}, bf16[64,1792]{1,0:T(8,128)(2,1)S(1)}, bf16[64,1792]{1,0:T(8,128)...) custom-call(s32[32]{0:T(128)S(1)} %get-tuple-element.195.table_ref, ...), custom_call_target="tpu_custom_call" | custom-call | flops 2000000000 | bytes 6000000 | tf_op jit(solution)/shard_map/pallas_call | solution.py:220
  104.2 3.3 %collective-permute-done.33.refs_3_ = bf16[64,3072]{1,0:T(8,128)(2,1)S(1)} collective-permute-done((bf16[64,3072]{1,0:T(8,128)(2,1)S(1)}, bf16[64,3072]{1,0:T(8,128)(2,1)S(1)}, u32[]{:S(2)}, u32[]{:S(2)}) %collective-permute-start.33) | collective-permute-done | bytes 393248 | tf_op jit(solution)/shard_map/ppermute | solution.py:64
  109.2 1.4 %collective-permute-start.39 = (bf16[64,768]{1,0:T(8,128)(2,1)S(1)}, bf16[64,768]{1,0:T(8,128)(2,1)S(1)}, u32[]{:S(2)}, u32[]{:S(2)}) collective-permute-start(bf16[64,768]{1,0:T(8,128)(2,1)S(1)} %get-tuple-element.138), channel_id=1, source_target_pairs={{0,16},{1,17},{2,18},{3,19},{4,20},{5,21},{6,22},{7,23},{8,24},{9,... | collective-permute-start | bytes 294920 | tf_op jit(solution)/shard_map/ppermute | solution.py:64
  111.9 1.4 %collective-permute-start.36 = (bf16[16,3072]{1,0:T(8,128)(2,1)S(1)}, bf16[16,3072]{1,0:T(8,128)(2,1)S(1)}, u32[]{:S(2)}, u32[]{:S(2)}) collective-permute-start(bf16[16,3072]{1,0:T(8,128)(2,1)S(1)} %get-tuple-element.135), channel_id=1, source_target_pairs={{0,8},{1,9},{2,10},{3,11},{4,12},{5,13},{6,14},{7,15},{8,0},{9,1},... | collective-permute-start | bytes 294920 | tf_op jit(solution)/shard_map/ppermute | solution.py:64
  114.2 2.2 %collective-permute-start.38 = (bf16[16,3072]{1,0:T(8,128)(2,1)S(1)}, bf16[16,3072]{1,0:T(8,128)(2,1)S(1)}, u32[]{:S(2)}, u32[]{:S(2)}) collective-permute-start(bf16[16,3072]{1,0:T(8,128)(2,1)S(1)} %get-tuple-element.137), channel_id=1, source_target_pairs={{0,24},{1,25},{2,26},{3,27},{4,28},{5,29},{6,30},{7,31},{8,16},{9,... | collective-permute-start | bytes 294920 | tf_op jit(solution)/shard_map/ppermute | solution.py:64
  120.3 3.8 %collective-permute-done.37.b_ref = bf16[16,3072]{1,0:T(8,128)(2,1)S(1)} collective-permute-done((bf16[16,3072]{1,0:T(8,128)(2,1)S(1)}, bf16[16,3072]{1,0:T(8,128)(2,1)S(1)}, u32[]{:S(2)}, u32[]{:S(2)}) %collective-permute-start.37) | collective-permute-done | bytes 98336 | tf_op jit(solution)/shard_map/ppermute | solution.py:64
  126.1 2.2 %collective-permute-start.40 = (bf16[16,1792]{1,0:T(8,128)(2,1)S(1)}, bf16[16,1792]{1,0:T(8,128)(2,1)S(1)}, u32[]{:S(2)}, u32[]{:S(2)}) collective-permute-start(bf16[16,1792]{1,0:T(8,128)(2,1)S(1)} %get-tuple-element.141), channel_id=1, source_target_pairs={{0,8},{1,9},{2,10},{3,11},{4,12},{5,13},{6,14},{7,15},{8,0},{9,1},... | collective-permute-start | bytes 172040 | tf_op jit(solution)/shard_map/ppermute | solution.py:64
  129.1 1.6 %collective-permute-start.42 = (bf16[16,1792]{1,0:T(8,128)(2,1)S(1)}, bf16[16,1792]{1,0:T(8,128)(2,1)S(1)}, u32[]{:S(2)}, u32[]{:S(2)}) collective-permute-start(bf16[16,1792]{1,0:T(8,128)(2,1)S(1)} %get-tuple-element.143), channel_id=1, source_target_pairs={{0,24},{1,25},{2,26},{3,27},{4,28},{5,29},{6,30},{7,31},{8,16},{9,... | collective-permute-start | bytes 172040 | tf_op jit(solution)/shard_map/ppermute | solution.py:64
  132.1 2.8 %shard_map.386 = (f32[3,162,324]{2,1,0:T(8,128)}, f32[3,162,324]{2,1,0:T(8,128)}, f32[3,162,324]{2,1,0:T(8,128)}, f32[3,162]{1,0:T(4,128)}, f32[3,162]{1,0:T(4,128)}, /*index=5*/f32[3,162]{1,0:T(4,128)}) custom-call(s32[16]{0:T(128)S(1)} %get-tuple-element.197.order_ref, bf16[64,768]{1,0:T(8,128)(2,1)S(1)} %shard_map.382.after_ref.refs_0_, ...), custom_call_target="tpu_custom_call" | custom-call | flops 10000000 | bytes 6000000 | tf_op jit(solution)/shard_map/pallas_call | solution.py:220
  (146 shorter events, 32.4 us)
Async XLA Ops:
  2.4 7.8 %collective-permute-start.4 = (bf16[16,1792]{1,0:T(8,128)(2,1)}, bf16[16,1792]{1,0:T(8,128)(2,1)S(1)}, u32[]{:S(2)}, u32[]{:S(2)}) collective-permute-start(bf16[16,1792]{1,0:T(8,128)(2,1)} %get-tuple-element.89.refs_0_), channel_id=1, source_target_pairs={{0,24},{1,25},{2,26},{3,27},{4,28},{5,29},{6,30},{7,31},{8,16},{9,... | collective-permute-start | bytes 172040 | tf_op jit(solution)/shard_map/ppermute | solution.py:64
  13.6 8.0 %collective-permute-start.6 = (bf16[64,1792]{1,0:T(8,128)(2,1)S(1)}, bf16[64,1792]{1,0:T(8,128)(2,1)S(1)}, u32[]{:S(2)}, u32[]{:S(2)}) collective-permute-start(bf16[64,1792]{1,0:T(8,128)(2,1)S(1)} %shard_map.361.refs_0_), channel_id=1, source_target_pairs={{0,2},{1,5},{2,0},{3,7},{4,6},{5,1},{6,4},{7,3},{8,10},{9,13},{10,... | collective-permute-start | bytes 688136 | tf_op jit(solution)/shard_map/ppermute | solution.py:64
  15.2 6.5 %collective-permute-start.5 = (bf16[64,1792]{1,0:T(8,128)(2,1)S(1)}, bf16[64,1792]{1,0:T(8,128)(2,1)S(1)}, u32[]{:S(2)}, u32[]{:S(2)}) collective-permute-start(bf16[64,1792]{1,0:T(8,128)(2,1)S(1)} %shard_map.361.refs_0_), channel_id=1, source_target_pairs={{0,4},{1,3},{2,6},{3,1},{4,0},{5,7},{6,2},{7,5},{8,12},{9,11},{10,... | collective-permute-start | bytes 688136 | tf_op jit(solution)/shard_map/ppermute | solution.py:64
  16.7 11.1 %collective-permute-start.15 = (bf16[16,3072]{1,0:T(8,128)(2,1)}, bf16[16,3072]{1,0:T(8,128)(2,1)S(1)}, u32[]{:S(2)}, u32[]{:S(2)}) collective-permute-start(bf16[16,3072]{1,0:T(8,128)(2,1)} %get-tuple-element.98.refs_0_), channel_id=1, source_target_pairs={{0,24},{1,25},{2,26},{3,27},{4,28},{5,29},{6,30},{7,31},{8,16},{9,... | collective-permute-start | bytes 294920 | tf_op jit(solution)/shard_map/ppermute | solution.py:64
  19.3 9.0 %collective-permute-start.14 = (bf16[16,3072]{1,0:T(8,128)(2,1)}, bf16[16,3072]{1,0:T(8,128)(2,1)}, u32[]{:S(2)}, u32[]{:S(2)}) collective-permute-start(bf16[16,3072]{1,0:T(8,128)(2,1)} %get-tuple-element.98.refs_0_), channel_id=1, source_target_pairs={{0,16},{1,17},{2,18},{3,19},{4,20},{5,21},{6,22},{7,23},{8,24},{9,... | collective-permute-start | bytes 294920 | tf_op jit(solution)/shard_map/ppermute | solution.py:64
  20.0 13.1 %collective-permute-start.8 = (bf16[64,1792]{1,0:T(8,128)(2,1)S(1)}, bf16[64,1792]{1,0:T(8,128)(2,1)}, u32[]{:S(2)}, u32[]{:S(2)}) collective-permute-start(bf16[64,1792]{1,0:T(8,128)(2,1)S(1)} %shard_map.361.refs_0_), channel_id=1, source_target_pairs={{0,1},{1,0},{2,3},{3,2},{4,5},{5,4},{6,7},{7,6},{8,9},{9,8},{10,11... | collective-permute-start | bytes 688136 | tf_op jit(solution)/shard_map/ppermute | solution.py:71
  21.7 11.9 %collective-permute-start.7 = (bf16[64,1792]{1,0:T(8,128)(2,1)S(1)}, bf16[64,1792]{1,0:T(8,128)(2,1)}, u32[]{:S(2)}, u32[]{:S(2)}) collective-permute-start(bf16[64,1792]{1,0:T(8,128)(2,1)S(1)} %shard_map.362.refs_4_), channel_id=1, source_target_pairs={{0,2},{1,5},{2,0},{3,7},{4,6},{5,1},{6,4},{7,3},{8,10},{9,13},{10,... | collective-permute-start | bytes 688136 | tf_op jit(solution)/shard_map/ppermute | solution.py:64
  27.8 6.9 %collective-permute-start = (bf16[2,162,512]{2,1,0:T(8,128)(2,1)}, bf16[2,162,512]{2,1,0:T(8,128)(2,1)}, u32[]{:S(2)}, u32[]{:S(2)}) collective-permute-start(bf16[2,162,512]{2,1,0:T(8,128)(2,1)} %get-tuple-element.87), channel_id=1, source_target_pairs={{0,1},{1,0},{2,3},{3,2},{4,5},{5,4},{6,7},{7,6},{8,9},{9,8},{10,11... | collective-permute-start | bytes 995336 | tf_op jit(solution)/shard_map/ppermute | solution.py:71
  27.8 7.4 %collective-permute-start.1 = (bf16[2,162,512]{2,1,0:T(8,128)(2,1)}, bf16[2,162,512]{2,1,0:T(8,128)(2,1)}, u32[]{:S(2)}, u32[]{:S(2)}) collective-permute-start(bf16[2,162,512]{2,1,0:T(8,128)(2,1)} %get-tuple-element.88), channel_id=1, source_target_pairs={{0,1},{1,0},{2,3},{3,2},{4,5},{5,4},{6,7},{7,6},{8,9},{9,8},{10,11... | collective-permute-start | bytes 995336 | tf_op jit(solution)/shard_map/ppermute | solution.py:71
  34.7 15.0 %collective-permute-start.12 = (bf16[3,162,384]{2,1,0:T(8,128)(2,1)}, bf16[3,162,384]{2,1,0:T(8,128)(2,1)S(1)}, u32[]{:S(2)}, u32[]{:S(2)}) collective-permute-start(bf16[3,162,384]{2,1,0:T(8,128)(2,1)} %copy-done.14), channel_id=1, source_target_pairs={{0,1},{1,0},{2,3},{3,2},{4,5},{5,4},{6,7},{7,6},{8,9},{9,8},{10,11... | collective-permute-start | bytes 1119752 | tf_op jit(solution)/shard_map/ppermute | solution.py:71
  35.2 19.6 %collective-permute-start.18 = (bf16[64,3072]{1,0:T(8,128)(2,1)S(1)}, bf16[64,3072]{1,0:T(8,128)(2,1)S(1)}, u32[]{:S(2)}, u32[]{:S(2)}) collective-permute-start(bf16[64,3072]{1,0:T(8,128)(2,1)S(1)} %shard_map.365.refs_0_), channel_id=1, source_target_pairs={{0,6},{1,7},{2,4},{3,5},{4,2},{5,3},{6,0},{7,1},{8,14},{9,15},{10,... | collective-permute-start | bytes 1179656 | tf_op jit(solution)/shard_map/ppermute | solution.py:64
  36.2 18.5 %collective-permute-start.17 = (bf16[64,3072]{1,0:T(8,128)(2,1)S(1)}, bf16[64,3072]{1,0:T(8,128)(2,1)S(1)}, u32[]{:S(2)}, u32[]{:S(2)}) collective-permute-start(bf16[64,3072]{1,0:T(8,128)(2,1)S(1)} %shard_map.365.refs_0_), channel_id=1, source_target_pairs={{0,2},{1,5},{2,0},{3,7},{4,6},{5,1},{6,4},{7,3},{8,10},{9,13},{10,... | collective-permute-start | bytes 1179656 | tf_op jit(solution)/shard_map/ppermute | solution.py:64
  37.1 18.3 %collective-permute-start.16 = (bf16[64,3072]{1,0:T(8,128)(2,1)S(1)}, bf16[64,3072]{1,0:T(8,128)(2,1)S(1)}, u32[]{:S(2)}, u32[]{:S(2)}) collective-permute-start(bf16[64,3072]{1,0:T(8,128)(2,1)S(1)} %shard_map.365.refs_0_), channel_id=1, source_target_pairs={{0,4},{1,3},{2,6},{3,1},{4,0},{5,7},{6,2},{7,5},{8,12},{9,11},{10,... | collective-permute-start | bytes 1179656 | tf_op jit(solution)/shard_map/ppermute | solution.py:64
  74.9 5.7 %collective-permute-start.23 = (bf16[128,768]{1,0:T(8,128)(2,1)S(1)}, bf16[128,768]{1,0:T(8,128)(2,1)S(1)}, u32[]{:S(2)}, u32[]{:S(2)}) collective-permute-start(bf16[128,768]{1,0:T(8,128)(2,1)S(1)} %shard_map.368.refs_0_), channel_id=1, source_target_pairs={{0,2},{1,5},{2,0},{3,7},{4,6},{5,1},{6,4},{7,3},{8,10},{9,13},{10,... | collective-permute-start | bytes 589832 | tf_op jit(solution)/shard_map/ppermute | solution.py:64
  83.9 15.3 %collective-permute-start.26 = (bf16[128,3072]{1,0:T(8,128)(2,1)S(1)}, bf16[128,3072]{1,0:T(8,128)(2,1)S(1)}, u32[]{:S(2)}, u32[]{:S(2)}) collective-permute-start(bf16[128,3072]{1,0:T(8,128)(2,1)S(1)} %get-tuple-element.125), channel_id=1, source_target_pairs={{0,1},{1,0},{2,3},{3,2},{4,5},{5,4},{6,7},{7,6},{8,9},{9,8},{10,11... | collective-permute-start | bytes 2359304 | tf_op jit(solution)/shard_map/ppermute | solution.py:71
  86.4 13.1 %collective-permute-start.27 = (bf16[128,3072]{1,0:T(8,128)(2,1)S(1)}, bf16[128,3072]{1,0:T(8,128)(2,1)S(1)}, u32[]{:S(2)}, u32[]{:S(2)}) collective-permute-start(bf16[128,3072]{1,0:T(8,128)(2,1)S(1)} %shard_map.372.refs_0_), channel_id=1, source_target_pairs={{0,2},{1,5},{2,0},{3,7},{4,6},{5,1},{6,4},{7,3},{8,10},{9,13},{10,... | collective-permute-start | bytes 2359304 | tf_op jit(solution)/shard_map/ppermute | solution.py:64
  87.7 7.3 %collective-permute-start.22 = (bf16[2,162,512]{2,1,0:T(8,128)(2,1)S(1)}, bf16[2,162,512]{2,1,0:T(8,128)(2,1)S(1)}, u32[]{:S(2)}, u32[]{:S(2)}) collective-permute-start(bf16[2,162,512]{2,1,0:T(8,128)(2,1)S(1)} %get-tuple-element.108), channel_id=1, source_target_pairs={{0,1},{1,0},{2,3},{3,2},{4,5},{5,4},{6,7},{7,6},{8,9},{9,8},{10,11... | collective-permute-start | bytes 995336 | tf_op jit(solution)/shard_map/ppermute | solution.py:71
  87.7 6.4 %collective-permute-start.25 = (bf16[64,768]{1,0:T(8,128)(2,1)S(1)}, bf16[64,768]{1,0:T(8,128)(2,1)S(1)}, u32[]{:S(2)}, u32[]{:S(2)}) collective-permute-start(bf16[64,768]{1,0:T(8,128)(2,1)S(1)} %shard_map.370.refs_0_), channel_id=1, source_target_pairs={{0,4},{1,3},{2,6},{3,1},{4,0},{5,7},{6,2},{7,5},{8,12},{9,11},{10,... | collective-permute-start | bytes 294920 | tf_op jit(solution)/shard_map/ppermute | solution.py:64
  99.6 7.8 %collective-permute-start.33 = (bf16[64,3072]{1,0:T(8,128)(2,1)S(1)}, bf16[64,3072]{1,0:T(8,128)(2,1)S(1)}, u32[]{:S(2)}, u32[]{:S(2)}) collective-permute-start(bf16[64,3072]{1,0:T(8,128)(2,1)S(1)} %shard_map.377.refs_0_), channel_id=1, source_target_pairs={{0,4},{1,3},{2,6},{3,1},{4,0},{5,7},{6,2},{7,5},{8,12},{9,11},{10,... | collective-permute-start | bytes 1179656 | tf_op jit(solution)/shard_map/ppermute | solution.py:64
  104.1 10.1 %collective-permute-start.30 = (bf16[128,1792]{1,0:T(8,128)(2,1)S(1)}, bf16[128,1792]{1,0:T(8,128)(2,1)S(1)}, u32[]{:S(2)}, u32[]{:S(2)}) collective-permute-start(bf16[128,1792]{1,0:T(8,128)(2,1)S(1)} %get-tuple-element.131), channel_id=1, source_target_pairs={{0,1},{1,0},{2,3},{3,2},{4,5},{5,4},{6,7},{7,6},{8,9},{9,8},{10,11... | collective-permute-start | bytes 1376264 | tf_op jit(solution)/shard_map/ppermute | solution.py:71
  107.8 8.6 %collective-permute-start.34 = (bf16[128,1792]{1,0:T(8,128)(2,1)S(1)}, bf16[128,1792]{1,0:T(8,128)(2,1)S(1)}, u32[]{:S(2)}, u32[]{:S(2)}) collective-permute-start(bf16[128,1792]{1,0:T(8,128)(2,1)S(1)} %shard_map.380), channel_id=1, source_target_pairs={{0,2},{1,5},{2,0},{3,7},{4,6},{5,1},{6,4},{7,3},{8,10},{9,13},{10,... | collective-permute-start | bytes 1376264 | tf_op jit(solution)/shard_map/ppermute | solution.py:64
  109.2 9.2 %collective-permute-start.39 = (bf16[64,768]{1,0:T(8,128)(2,1)S(1)}, bf16[64,768]{1,0:T(8,128)(2,1)S(1)}, u32[]{:S(2)}, u32[]{:S(2)}) collective-permute-start(bf16[64,768]{1,0:T(8,128)(2,1)S(1)} %get-tuple-element.138), channel_id=1, source_target_pairs={{0,16},{1,17},{2,18},{3,19},{4,20},{5,21},{6,22},{7,23},{8,24},{9,... | collective-permute-start | bytes 294920 | tf_op jit(solution)/shard_map/ppermute | solution.py:64
  111.9 7.6 %collective-permute-start.36 = (bf16[16,3072]{1,0:T(8,128)(2,1)S(1)}, bf16[16,3072]{1,0:T(8,128)(2,1)S(1)}, u32[]{:S(2)}, u32[]{:S(2)}) collective-permute-start(bf16[16,3072]{1,0:T(8,128)(2,1)S(1)} %get-tuple-element.135), channel_id=1, source_target_pairs={{0,8},{1,9},{2,10},{3,11},{4,12},{5,13},{6,14},{7,15},{8,0},{9,1},... | collective-permute-start | bytes 294920 | tf_op jit(solution)/shard_map/ppermute | solution.py:64
  113.3 10.8 %collective-permute-start.37 = (bf16[16,3072]{1,0:T(8,128)(2,1)S(1)}, bf16[16,3072]{1,0:T(8,128)(2,1)S(1)}, u32[]{:S(2)}, u32[]{:S(2)}) collective-permute-start(bf16[16,3072]{1,0:T(8,128)(2,1)S(1)} %get-tuple-element.136), channel_id=1, source_target_pairs={{0,16},{1,17},{2,18},{3,19},{4,20},{5,21},{6,22},{7,23},{8,24},{9,... | collective-permute-start | bytes 294920 | tf_op jit(solution)/shard_map/ppermute | solution.py:64
  114.2 9.9 %collective-permute-start.38 = (bf16[16,3072]{1,0:T(8,128)(2,1)S(1)}, bf16[16,3072]{1,0:T(8,128)(2,1)S(1)}, u32[]{:S(2)}, u32[]{:S(2)}) collective-permute-start(bf16[16,3072]{1,0:T(8,128)(2,1)S(1)} %get-tuple-element.137), channel_id=1, source_target_pairs={{0,24},{1,25},{2,26},{3,27},{4,28},{5,29},{6,30},{7,31},{8,16},{9,... | collective-permute-start | bytes 294920 | tf_op jit(solution)/shard_map/ppermute | solution.py:64
  116.4 9.5 %collective-permute-start.35 = (bf16[64,1792]{1,0:T(8,128)(2,1)S(1)}, bf16[64,1792]{1,0:T(8,128)(2,1)S(1)}, u32[]{:S(2)}, u32[]{:S(2)}) collective-permute-start(bf16[64,1792]{1,0:T(8,128)(2,1)S(1)} %shard_map.381.refs_2_), channel_id=1, source_target_pairs={{0,4},{1,3},{2,6},{3,1},{4,0},{5,7},{6,2},{7,5},{8,12},{9,11},{10,... | collective-permute-start | bytes 688136 | tf_op jit(solution)/shard_map/ppermute | solution.py:64
  118.4 6.4 %collective-permute-start.43 = (bf16[64,768]{1,0:T(8,128)(2,1)S(1)}, bf16[64,768]{1,0:T(8,128)(2,1)S(1)}, u32[]{:S(2)}, u32[]{:S(2)}) collective-permute-start(bf16[64,768]{1,0:T(8,128)(2,1)S(1)} %shard_map.382.after_ref.refs_0_), channel_id=1, source_target_pairs={{0,4},{1,3},{2,6},{3,1},{4,0},{5,7},{6,2},{7,5},{8,12},{9,11},{10,... | collective-permute-start | bytes 294920 | tf_op jit(solution)/shard_map/ppermute | solution.py:64
  119.4 12.6 %collective-permute-start.44 = (bf16[64,768]{1,0:T(8,128)(2,1)S(1)}, bf16[64,768]{1,0:T(8,128)(2,1)S(1)}, u32[]{:S(2)}, u32[]{:S(2)}) collective-permute-start(bf16[64,768]{1,0:T(8,128)(2,1)S(1)} %shard_map.382.after_ref.refs_0_), channel_id=1, source_target_pairs={{0,2},{1,5},{2,0},{3,7},{4,6},{5,1},{6,4},{7,3},{8,10},{9,13},{10,... | collective-permute-start | bytes 294920 | tf_op jit(solution)/shard_map/ppermute | solution.py:64
  124.9 7.1 %collective-permute-start.45 = (bf16[64,768]{1,0:T(8,128)(2,1)S(1)}, bf16[64,768]{1,0:T(8,128)(2,1)S(1)}, u32[]{:S(2)}, u32[]{:S(2)}) collective-permute-start(bf16[64,768]{1,0:T(8,128)(2,1)S(1)} %collective-permute-done.43.refs_1_), channel_id=1, source_target_pairs={{0,2},{1,5},{2,0},{3,7},{4,6},{5,1},{6,4},{7,3},{8,10},{9,13},{10,... | collective-permute-start | bytes 294920 | tf_op jit(solution)/shard_map/ppermute | solution.py:64
  126.1 8.8 %collective-permute-start.40 = (bf16[16,1792]{1,0:T(8,128)(2,1)S(1)}, bf16[16,1792]{1,0:T(8,128)(2,1)S(1)}, u32[]{:S(2)}, u32[]{:S(2)}) collective-permute-start(bf16[16,1792]{1,0:T(8,128)(2,1)S(1)} %get-tuple-element.141), channel_id=1, source_target_pairs={{0,8},{1,9},{2,10},{3,11},{4,12},{5,13},{6,14},{7,15},{8,0},{9,1},... | collective-permute-start | bytes 172040 | tf_op jit(solution)/shard_map/ppermute | solution.py:64
  128.3 7.1 %collective-permute-start.41 = (bf16[16,1792]{1,0:T(8,128)(2,1)S(1)}, bf16[16,1792]{1,0:T(8,128)(2,1)S(1)}, u32[]{:S(2)}, u32[]{:S(2)}) collective-permute-start(bf16[16,1792]{1,0:T(8,128)(2,1)S(1)} %get-tuple-element.142), channel_id=1, source_target_pairs={{0,16},{1,17},{2,18},{3,19},{4,20},{5,21},{6,22},{7,23},{8,24},{9,... | collective-permute-start | bytes 172040 | tf_op jit(solution)/shard_map/ppermute | solution.py:64
  129.1 6.2 %collective-permute-start.42 = (bf16[16,1792]{1,0:T(8,128)(2,1)S(1)}, bf16[16,1792]{1,0:T(8,128)(2,1)S(1)}, u32[]{:S(2)}, u32[]{:S(2)}) collective-permute-start(bf16[16,1792]{1,0:T(8,128)(2,1)S(1)} %get-tuple-element.143), channel_id=1, source_target_pairs={{0,24},{1,25},{2,26},{3,27},{4,28},{5,29},{6,30},{7,31},{8,16},{9,... | collective-permute-start | bytes 172040 | tf_op jit(solution)/shard_map/ppermute | solution.py:64
  (36 other events, 177.9 us)
